TPU v7x, 32 devices: a whole 2x2x4 slice. The times are simulated.
32 devices in a mesh: seq: 8 (over y, x, core), head: 4 (over z).
Axes of the slice: x: 2, y: 2, z: 4, core: 2. Of those that a mesh axis runs over, the one named last changes fastest.
Arguments:
- inputs: bfloat16 [32768, 512], P(('seq', 'head')), may hold values from -6 to 6
- attn_gain: bfloat16 [512], P(('seq', 'head')), may hold values from 0.099609375 to 1.8984375
- attn_shift: bfloat16 [512], P(('seq', 'head')), may hold values from -3 to 3
- query_weight: bfloat16 [512, 512], P(None, 'head'), may hold values from -1 to 1
- key_weight: bfloat16 [512, 512], P(None, 'head'), may hold values from -0.25 to 0.25
- value_weight: bfloat16 [512, 512], P(None, 'head'), may hold values from -0.25 to 0.25
- control_weight: bfloat16 [512, 512], P(None, 'head'), may hold values from -0.5 to 0.5
- output_weight: bfloat16 [512, 512], P('head'), may hold values from -1 to 1
- ffn_gain: bfloat16 [512], P(('seq', 'head')), may hold values from 0.099609375 to 1.8984375
- ffn_shift: bfloat16 [512], P(('seq', 'head')), may hold values from -3 to 3
- expand_weight: bfloat16 [512, 2048], P(None, ('seq', 'head')), may hold values from -0.25 to 0.25
- expand_bias: bfloat16 [2048], P(('seq', 'head')), may hold values from -3 to 3
- shrink_weight: bfloat16 [2048, 512], P(None, ('seq', 'head')), may hold values from -0.125 to 0.125
- shrink_bias: bfloat16 [512], P(('seq', 'head')), may hold values from -3 to 3
- cotangent: bfloat16 [32768, 512], P(('seq', 'head')), may hold values from -6 to 6
Outputs:
- result: bfloat16 [32768, 512], P(('seq', 'head'))
- grad_inputs: bfloat16 [32768, 512], P(('seq', 'head'))
- grad_attn_gain: float32 [512], P(('seq', 'head'))
- grad_attn_shift: float32 [512], P(('seq', 'head'))
- grad_query_weight: float32 [512, 512], P('seq', 'head')
- grad_key_weight: float32 [512, 512], P('seq', 'head')
- grad_value_weight: float32 [512, 512], P('seq', 'head')
- grad_control_weight: float32 [512, 512], P('seq', 'head')
- grad_output_weight: float32 [512, 512], P('head', 'seq')
- grad_ffn_gain: float32 [512], P(('seq', 'head'))
- grad_ffn_shift: float32 [512], P(('seq', 'head'))
- grad_expand_weight: float32 [512, 2048], P(None, ('seq', 'head'))
- grad_expand_bias: float32 [2048], P(('seq', 'head'))
- grad_shrink_weight: float32 [2048, 512], P(None, ('seq', 'head'))
- grad_shrink_bias: float32 [512], P(('seq', 'head'))
All inputs are finite; a program needn't handle non-finite values.
Results may differ from a plain program's by a relative error of at most 0.025.
The roundings to bfloat16 on the way count: a program that leaves them out, or rounds other values in their place, can miss the bound.
Values may be sent and summed in bfloat16 or wider, within the bound.
No kernel may reach another device: no remote copies, remote signals or barrier semaphores. Data moves between devices by JAX's collectives and lax.ppermute only.
A program may use at most 128 MiB of HBM per device.

v0:
```python
import jax
import jax.numpy as jnp
from jax import lax
from jax.sharding import PartitionSpec as P

D = 512
H = 8
SLOTS = 64
LEN = 1024


EPSILON = 1e-05


def scale_norm(tokens, scaling):
    average = jnp.mean(tokens, axis=-1, keepdims=True)
    centred = tokens - average
    spread = jnp.mean(centred * centred, axis=-1, keepdims=True)
    return centred * lax.rsqrt(spread + EPSILON) * scaling


def causal_mask(length):
    places = jnp.arange(length)
    return places[:, None] >= places[None, :]


def smooth_gate(hidden):
    return jax.nn.gelu(hidden, approximate=True)


def slot_forward(packed):
    queries, key_rows, value_rows, control = packed
    causal = causal_mask(queries.shape[0])
    powers = jnp.exp(control)
    running = jnp.cumsum(powers, axis=0)
    powers_low = powers.astype(jnp.bfloat16)
    affinity = jnp.einsum("thd,ihd->hti", queries, key_rows, preferred_element_type=jnp.float32)
    scored = jnp.where(causal, affinity * 0.125, 0.0).astype(jnp.bfloat16)
    summed = jnp.einsum("hti,ihs->ths", scored, powers_low, preferred_element_type=jnp.float32)
    slot_score = summed / running
    highest = jnp.max(slot_score, axis=-1, keepdims=True)
    lifted = jnp.exp(slot_score - highest)
    slot_prob = lifted / jnp.sum(lifted, axis=-1, keepdims=True)
    reading = (slot_prob / running).astype(jnp.bfloat16)
    mixing = jnp.einsum("ths,ihs->hti", reading, powers_low, preferred_element_type=jnp.float32)
    mixing = jnp.where(causal, mixing, 0.0).astype(jnp.bfloat16)
    output = jnp.einsum("hti,ihd->thd", mixing, value_rows, preferred_element_type=jnp.float32)
    return (output.astype(jnp.bfloat16), powers, running, slot_score, slot_prob)


def slot_backward(packed):
    grad_output, queries, key_rows, value_rows, powers, running, slot_score, slot_prob = packed
    causal = causal_mask(queries.shape[0])
    powers_low = powers.astype(jnp.bfloat16)
    reading = (slot_prob / running).astype(jnp.bfloat16)
    affinity = jnp.einsum("thd,ihd->hti", queries, key_rows, preferred_element_type=jnp.float32)
    scored = jnp.where(causal, affinity * 0.125, 0.0).astype(jnp.bfloat16)
    mixing = jnp.einsum("ths,ihs->hti", reading, powers_low, preferred_element_type=jnp.float32)
    mixing = jnp.where(causal, mixing, 0.0).astype(jnp.bfloat16)
    grad_value = jnp.einsum("hti,thd->ihd", mixing, grad_output, preferred_element_type=jnp.float32)
    grad_mixing = jnp.einsum(
        "thd,ihd->hti", grad_output, value_rows, preferred_element_type=jnp.float32
    )
    grad_mixing = jnp.where(causal, grad_mixing, 0.0).astype(jnp.bfloat16)
    grad_reading = jnp.einsum(
        "hti,ihs->ths", grad_mixing, powers_low, preferred_element_type=jnp.float32
    )
    grad_powers = jnp.einsum(
        "hti,ths->ihs", grad_mixing, reading, preferred_element_type=jnp.float32
    )
    grad_prob = grad_reading / running
    grad_running = -grad_reading * slot_prob / (running * running)
    grad_slots = slot_prob * (grad_prob - jnp.sum(slot_prob * grad_prob, axis=-1, keepdims=True))
    grad_running = grad_running - grad_slots * slot_score / running
    grad_summed = (grad_slots / running).astype(jnp.bfloat16)
    grad_scored = jnp.einsum(
        "ths,ihs->hti", grad_summed, powers_low, preferred_element_type=jnp.float32
    )
    grad_scored = jnp.where(causal, grad_scored, 0.0).astype(jnp.bfloat16)
    grad_powers = grad_powers + jnp.einsum(
        "hti,ths->ihs", scored, grad_summed, preferred_element_type=jnp.float32
    )
    grad_queries = 0.125 * jnp.einsum(
        "hti,ihd->thd", grad_scored, key_rows, preferred_element_type=jnp.float32
    )
    grad_keys = 0.125 * jnp.einsum(
        "hti,thd->ihd", grad_scored, queries, preferred_element_type=jnp.float32
    )
    carried = jnp.flip(jnp.cumsum(jnp.flip(grad_running, 0), axis=0), 0)
    grad_control = (grad_powers + carried) * powers
    return (
        grad_queries.astype(jnp.bfloat16),
        grad_keys.astype(jnp.bfloat16),
        grad_value.astype(jnp.bfloat16),
        grad_control.astype(jnp.bfloat16),
    )


def body(
    inputs,
    attn_gain,
    attn_shift,
    query_weight,
    key_weight,
    value_weight,
    control_weight,
    output_weight,
    ffn_gain,
    ffn_shift,
    expand_weight,
    expand_bias,
    shrink_weight,
    shrink_bias,
    cotangent,
):
    gathered = (
        lax.all_gather(expand_weight, ("seq", "head"), axis=1, tiled=True),
        lax.all_gather(shrink_weight, ("seq", "head"), axis=1, tiled=True),
        lax.all_gather(attn_gain, ("seq", "head"), axis=0, tiled=True),
        lax.all_gather(attn_shift, ("seq", "head"), axis=0, tiled=True),
        lax.all_gather(ffn_gain, ("seq", "head"), axis=0, tiled=True),
        lax.all_gather(ffn_shift, ("seq", "head"), axis=0, tiled=True),
        lax.all_gather(expand_bias, ("seq", "head"), axis=0, tiled=True),
        lax.all_gather(shrink_bias, ("seq", "head"), axis=0, tiled=True),
    )
    expand_full = gathered[0]
    shrink_full = gathered[1]
    gain_attn, shift_attn, gain_ffn, shift_ffn, bias_expand, bias_shrink = tuple(
        (member.astype(jnp.float32) for member in gathered[2:])
    )
    head_size = D // H
    head_count = query_weight.shape[1] // head_size
    tokens = inputs.astype(jnp.float32)
    normed_low = (scale_norm(tokens, gain_attn) + shift_attn).astype(jnp.bfloat16)
    group_rows = lax.all_gather(normed_low, "head", axis=0, tiled=True)
    group_size = group_rows.shape[0]
    seq_count = group_size // LEN

    def split_heads(matrix, columns):
        return matrix.reshape(seq_count, LEN, head_count, columns)

    queries = split_heads(
        jnp.dot(group_rows, query_weight, preferred_element_type=jnp.float32).astype(jnp.bfloat16),
        head_size,
    )
    key_rows = split_heads(
        jnp.dot(group_rows, key_weight, preferred_element_type=jnp.float32).astype(jnp.bfloat16),
        head_size,
    )
    value_rows = split_heads(
        jnp.dot(group_rows, value_weight, preferred_element_type=jnp.float32).astype(jnp.bfloat16),
        head_size,
    )
    control = split_heads(
        jnp.dot(group_rows, control_weight, preferred_element_type=jnp.float32), SLOTS
    )
    outputs, powers, running, slot_score, slot_prob = lax.map(
        slot_forward, (queries, key_rows, value_rows, control)
    )
    heads_out = outputs.reshape(group_size, head_count * head_size)
    branch = lax.psum_scatter(
        jnp.dot(heads_out, output_weight, preferred_element_type=jnp.float32).astype(jnp.bfloat16),
        "head",
        scatter_dimension=0,
        tiled=True,
    ).astype(jnp.float32)
    residual = tokens + branch
    second_low = (scale_norm(residual, gain_ffn) + shift_ffn).astype(jnp.bfloat16)
    hidden = jnp.dot(second_low, expand_full, preferred_element_type=jnp.float32) + bias_expand
    activated = smooth_gate(hidden).astype(jnp.bfloat16)
    result = (
        residual + jnp.dot(activated, shrink_full, preferred_element_type=jnp.float32) + bias_shrink
    )
    upstream = cotangent.astype(jnp.float32)
    outbias_grad = jnp.sum(upstream, axis=0)
    shrink_wgrad = jnp.einsum("tf,td->fd", activated, cotangent, preferred_element_type=jnp.float32)
    fresh = (
        lax.all_gather(expand_weight, ("seq", "head"), axis=1, tiled=True),
        lax.all_gather(shrink_weight, ("seq", "head"), axis=1, tiled=True),
        lax.all_gather(attn_gain, ("seq", "head"), axis=0, tiled=True),
        lax.all_gather(ffn_gain, ("seq", "head"), axis=0, tiled=True),
    )
    expand_full = fresh[0]
    shrink_full = fresh[1]
    gain_attn = fresh[2].astype(jnp.float32)
    gain_ffn = fresh[3].astype(jnp.float32)
    active_grad = jnp.einsum(
        "td,fd->tf", cotangent, shrink_full, preferred_element_type=jnp.float32
    )
    gate_pull = jax.vjp(smooth_gate, hidden)[1]
    hidden_grad = gate_pull(active_grad)[0].astype(jnp.bfloat16)
    inbias_grad = jnp.sum(hidden_grad.astype(jnp.float32), axis=0)
    expand_wgrad = jnp.einsum(
        "tc,tf->cf", second_low, hidden_grad, preferred_element_type=jnp.float32
    )
    second_grad = jnp.einsum(
        "tf,cf->tc", hidden_grad, expand_full, preferred_element_type=jnp.float32
    )
    ffn_pull = jax.vjp(scale_norm, residual, gain_ffn)[1]
    residual_part, ffngain_grad = ffn_pull(second_grad)
    ffnshift_grad = jnp.sum(second_grad, axis=0)
    residual_grad = upstream + residual_part
    branch_low = residual_grad.astype(jnp.bfloat16)
    branch_rows = lax.all_gather(branch_low, "head", axis=0, tiled=True)
    heads_grad = jnp.einsum(
        "gd,cd->gc", branch_rows, output_weight, preferred_element_type=jnp.float32
    ).astype(jnp.bfloat16)
    output_wgrad = jnp.einsum(
        "gd,gc->dc", branch_rows, heads_out, preferred_element_type=jnp.float32
    )
    backs = lax.map(
        slot_backward,
        (
            split_heads(heads_grad, head_size),
            queries,
            key_rows,
            value_rows,
            powers,
            running,
            slot_score,
            slot_prob,
        ),
    )
    query_back = backs[0].reshape(group_size, -1)
    key_back = backs[1].reshape(group_size, -1)
    value_back = backs[2].reshape(group_size, -1)
    control_back = backs[3].reshape(group_size, -1)
    summed_back = jnp.einsum(
        "gc,dc->gd", query_back, query_weight, preferred_element_type=jnp.float32
    )
    summed_back = summed_back + jnp.einsum(
        "gc,dc->gd", key_back, key_weight, preferred_element_type=jnp.float32
    )
    summed_back = summed_back + jnp.einsum(
        "gc,dc->gd", value_back, value_weight, preferred_element_type=jnp.float32
    )
    normed_grad = lax.psum_scatter(
        (
            summed_back
            + jnp.einsum(
                "gc,dc->gd", control_back, control_weight, preferred_element_type=jnp.float32
            )
        ).astype(jnp.bfloat16),
        "head",
        scatter_dimension=0,
        tiled=True,
    ).astype(jnp.float32)
    query_wgrad = jnp.einsum(
        "gd,gc->dc", group_rows, query_back, preferred_element_type=jnp.float32
    )
    key_wgrad = jnp.einsum("gd,gc->dc", group_rows, key_back, preferred_element_type=jnp.float32)
    value_wgrad = jnp.einsum(
        "gd,gc->dc", group_rows, value_back, preferred_element_type=jnp.float32
    )
    control_wgrad = jnp.einsum(
        "gd,gc->dc", group_rows, control_back, preferred_element_type=jnp.float32
    )
    attn_pull = jax.vjp(scale_norm, tokens, gain_attn)[1]
    tokens_part, attngain_grad = attn_pull(normed_grad)
    attnshift_grad = jnp.sum(normed_grad, axis=0)
    input_grad = (residual_grad + tokens_part).astype(jnp.bfloat16)
    attn_sums = (
        lax.psum_scatter(query_wgrad, "seq", scatter_dimension=0, tiled=True),
        lax.psum_scatter(key_wgrad, "seq", scatter_dimension=0, tiled=True),
        lax.psum_scatter(value_wgrad, "seq", scatter_dimension=0, tiled=True),
        lax.psum_scatter(control_wgrad, "seq", scatter_dimension=0, tiled=True),
        lax.psum_scatter(output_wgrad, "seq", scatter_dimension=0, tiled=True),
    )
    ffn_sums = (
        lax.psum_scatter(expand_wgrad, ("seq", "head"), scatter_dimension=1, tiled=True),
        lax.psum_scatter(shrink_wgrad, ("seq", "head"), scatter_dimension=1, tiled=True),
        lax.psum_scatter(attngain_grad, ("seq", "head"), scatter_dimension=0, tiled=True),
        lax.psum_scatter(attnshift_grad, ("seq", "head"), scatter_dimension=0, tiled=True),
        lax.psum_scatter(ffngain_grad, ("seq", "head"), scatter_dimension=0, tiled=True),
        lax.psum_scatter(ffnshift_grad, ("seq", "head"), scatter_dimension=0, tiled=True),
        lax.psum_scatter(inbias_grad, ("seq", "head"), scatter_dimension=0, tiled=True),
        lax.psum_scatter(outbias_grad, ("seq", "head"), scatter_dimension=0, tiled=True),
    )
    return (
        result.astype(jnp.bfloat16),
        input_grad,
        ffn_sums[2],
        ffn_sums[3],
        attn_sums[0],
        attn_sums[1],
        attn_sums[2],
        attn_sums[3],
        attn_sums[4].T,
        ffn_sums[4],
        ffn_sums[5],
        ffn_sums[0],
        ffn_sums[6],
        ffn_sums[1],
        ffn_sums[7],
    )


def solution(mesh):
    placed = (
        P(("seq", "head"), None),
        P(("seq", "head")),
        P(("seq", "head")),
        P(None, "head"),
        P(None, "head"),
        P(None, "head"),
        P(None, "head"),
        P("head", None),
        P(("seq", "head")),
        P(("seq", "head")),
        P(None, ("seq", "head")),
        P(("seq", "head")),
        P(None, ("seq", "head")),
        P(("seq", "head")),
        P(("seq", "head"), None),
    )
    return jax.shard_map(
        body,
        mesh=mesh,
        in_specs=placed,
        out_specs=(
            P(("seq", "head"), None),
            P(("seq", "head"), None),
            P(("seq", "head")),
            P(("seq", "head")),
            P("seq", "head"),
            P("seq", "head"),
            P("seq", "head"),
            P("seq", "head"),
            P("head", "seq"),
            P(("seq", "head")),
            P(("seq", "head")),
            P(None, ("seq", "head")),
            P(("seq", "head")),
            P(None, ("seq", "head")),
            P(("seq", "head")),
        ),
        check_vma=False,
    )
```

profile of v0, /device:TPU:0, one launch (start us, length us, event | category | flops | bytes accessed | tf_op | source)
XLA Modules:
  0.0 1541.5 jit_solution(1341142543980459345)
XLA Ops:
  13.5 42.2 %all-reduce.13 = (bf16[512]{0:T(512)(128)(2,1)S(1)}, bf16[512]{0:T(512)(128)(2,1)S(1)}, bf16[512]{0:T(512)(128)(2,1)S(1)}, bf16[512]{0:T(512)(128)(2,1)S(1)}, bf...) all-reduce(bf16[512]{0:T(512)(128)(2,1)S(1)} %dynamic-update-slice., ...), channel_id=1, replica_groups=mesh['seq'=8,'head'=4] {'seq','head'}, use_global_device_ids=true, to_apply=%add.1 | all-reduce | flops 4608 | bytes 18432
  58.3 80.5 %all-gather.5.cloned.1.call-done = bf16[4096,512]{1,0:T(8,128)(2,1)} async-done(((bf16[1024,512]{1,0:T(8,128)(2,1)}), bf16[4096,512]{1,0:T(8,128)(2,1)}) %all-gather.5.cloned.1.call-update) | async-done | bytes 4194320 | tf_op jit(solution)/shard_map/all_gather | solution.py:135
  138.9 4.4 convolution_convert_fusion.2
  143.3 3.9 reshape.171
  147.2 3.6 copy.81
  150.7 4.4 convolution_convert_fusion.3
  155.1 3.9 reshape.170
  159.0 3.6 copy.80
  162.6 4.4 convolution_convert_fusion.4
  167.0 3.9 reshape.169
  170.9 3.5 copy.78
  174.4 3.7 fusion.137
  181.6 212.9 %while.34 = (s32[]{:T(128)}, bf16[4,1024,2,64]{1,3,2,0:T(8,128)(2,1)}, f32[4,1024,2,64]{1,3,2,0:T(8,128)}, f32[4,1024,2,64]{1,3,2,0:T(8,128)}, f32[4,1024,2,64]{...) while((s32[]{:T(128)}, ...), condition=%wide.region_7.8_spmd, body=%wide.region_2.7_spmd.sunk | while | flops 1103372288 | bytes 18947216 | solution.py:157
  186.3 36.0 %reduce-window.36 = f32[64,2,8,128]{3,2,1,0:T(8,128)S(1)} reduce-window(f32[64,2,8,128]{3,2,1,0:T(8,128)S(1)} %copy.150, f32[]{:T(128)} %constant.63.clone.12..sunk), window={size=1x1x1x128 pad=0_0x0_0x0_0x127_0}, to_apply=%region_3.3 | reduce-window | flops 16646144 | bytes 1048580 | tf_op jit(solution)/shard_map/reduce-window
  223.5 4.9 bitcast_dynamic-update-slice_fusion.5
  229.1 4.6 fusion.236
  239.5 36.0 %reduce-window.36 = f32[64,2,8,128]{3,2,1,0:T(8,128)S(1)} reduce-window(f32[64,2,8,128]{3,2,1,0:T(8,128)S(1)} %copy.150, f32[]{:T(128)} %constant.63.clone.12..sunk), window={size=1x1x1x128 pad=0_0x0_0x0_0x127_0}, to_apply=%region_3.3 | reduce-window | flops 16646144 | bytes 1048580 | tf_op jit(solution)/shard_map/reduce-window
  276.6 4.9 bitcast_dynamic-update-slice_fusion.5
  282.3 4.6 fusion.236
  292.6 36.0 %reduce-window.36 = f32[64,2,8,128]{3,2,1,0:T(8,128)S(1)} reduce-window(f32[64,2,8,128]{3,2,1,0:T(8,128)S(1)} %copy.150, f32[]{:T(128)} %constant.63.clone.12..sunk), window={size=1x1x1x128 pad=0_0x0_0x0_0x127_0}, to_apply=%region_3.3 | reduce-window | flops 16646144 | bytes 1048580 | tf_op jit(solution)/shard_map/reduce-window
  329.7 4.9 bitcast_dynamic-update-slice_fusion.5
  335.5 4.6 fusion.236
  345.8 36.0 %reduce-window.36 = f32[64,2,8,128]{3,2,1,0:T(8,128)S(1)} reduce-window(f32[64,2,8,128]{3,2,1,0:T(8,128)S(1)} %copy.150, f32[]{:T(128)} %constant.63.clone.12..sunk), window={size=1x1x1x128 pad=0_0x0_0x0_0x127_0}, to_apply=%region_3.3 | reduce-window | flops 16646144 | bytes 1048580 | tf_op jit(solution)/shard_map/reduce-window
  382.9 4.9 bitcast_dynamic-update-slice_fusion.5
  388.6 4.6 fusion.236
  402.5 75.3 %reduce-scatter.10.cloned.1.call-done = bf16[1024,512]{1,0:T(8,128)(2,1)} async-done(((bf16[4096,512]{1,0:T(8,128)(2,1)}), bf16[1024,512]{1,0:T(8,128)(2,1)}) %reduce-scatter.10.cloned.1.call-update) | async-done | bytes 1048592 | tf_op jit(solution)/shard_map/reduce_scatter | solution.py:161
  480.1 34.5 %all-gather.7.cloned.1.call-done = bf16[512,2048]{0,1:T(8,128)(2,1)} async-done(((bf16[512,64]{0,1:T(8,128)(2,1)}), bf16[512,2048]{0,1:T(8,128)(2,1)}) %all-gather.7.cloned.1.call-update) | async-done | bytes 2097168 | tf_op jit(solution)/shard_map/all_gather | solution.py:117
  514.6 8.7 multiply_convert_fusion
  523.3 50.0 %all-gather.9.cloned.1.call-done = bf16[2048,512]{0,1:T(8,128)(2,1)} async-done(((bf16[2048,16]{0,1:T(8,128)(2,1)}), bf16[2048,512]{0,1:T(8,128)(2,1)}) %all-gather.9.cloned.1.call-update) | async-done | bytes 2097168 | tf_op jit(solution)/shard_map/all_gather | solution.py:118
  573.3 10.8 convert_reduce_fusion
  591.4 79.7 %all-gather.11.cloned.1.call-done = bf16[4096,512]{1,0:T(8,128)(2,1)} async-done(((bf16[1024,512]{1,0:T(8,128)(2,1)}), bf16[4096,512]{1,0:T(8,128)(2,1)}) %all-gather.11.cloned.1.call-update) | async-done | bytes 4194320 | tf_op jit(solution)/shard_map/all_gather | solution.py:204
  681.4 267.5 %while.35 = (s32[]{:T(128)}, bf16[4,1024,2,64]{1,3,2,0:T(8,128)(2,1)}, bf16[4,1024,2,64]{1,3,2,0:T(8,128)(2,1)}, bf16[4,1024,2,64]{1,3,2,0:T(8,128)(2,1)}, bf16[...) while((s32[]{:T(128)}, ...), condition=%wide.region_17.18_spmd, body=%wide.region_13.17_spmd.sunk | while | flops 2724341760 | bytes 101763944 | solution.py:211
  692.1 36.0 %reduce-window.38 = f32[64,2,8,128]{3,2,1,0:T(8,128)S(1)} reduce-window(f32[64,2,8,128]{3,2,1,0:T(8,128)S(1)} %copy.154, f32[]{:T(128)} %constant.63.clone.12..sunk.1), window={size=1x1x1x128 pad=0_0x0_0x0_0x127_0}, to_apply=%region_15.15 | reduce-window | flops 16646144 | bytes 1048580 | tf_op jit(solution)/shard_map/reduce-window.2
  733.6 3.9 fusion.260
  737.5 4.3 fusion.258
  758.8 36.0 %reduce-window.38 = f32[64,2,8,128]{3,2,1,0:T(8,128)S(1)} reduce-window(f32[64,2,8,128]{3,2,1,0:T(8,128)S(1)} %copy.154, f32[]{:T(128)} %constant.63.clone.12..sunk.1), window={size=1x1x1x128 pad=0_0x0_0x0_0x127_0}, to_apply=%region_15.15 | reduce-window | flops 16646144 | bytes 1048580 | tf_op jit(solution)/shard_map/reduce-window.2
  796.8 3.5 fusion.259
  800.3 3.9 fusion.260
  804.2 4.3 fusion.258
  825.5 36.0 %reduce-window.38 = f32[64,2,8,128]{3,2,1,0:T(8,128)S(1)} reduce-window(f32[64,2,8,128]{3,2,1,0:T(8,128)S(1)} %copy.154, f32[]{:T(128)} %constant.63.clone.12..sunk.1), window={size=1x1x1x128 pad=0_0x0_0x0_0x127_0}, to_apply=%region_15.15 | reduce-window | flops 16646144 | bytes 1048580 | tf_op jit(solution)/shard_map/reduce-window.2
  867.0 3.9 fusion.260
  870.9 4.3 fusion.258
  892.3 36.0 %reduce-window.38 = f32[64,2,8,128]{3,2,1,0:T(8,128)S(1)} reduce-window(f32[64,2,8,128]{3,2,1,0:T(8,128)S(1)} %copy.154, f32[]{:T(128)} %constant.63.clone.12..sunk.1), window={size=1x1x1x128 pad=0_0x0_0x0_0x127_0}, to_apply=%region_15.15 | reduce-window | flops 16646144 | bytes 1048580 | tf_op jit(solution)/shard_map/reduce-window.2
  930.3 3.5 fusion.259
  933.8 3.9 fusion.260
  937.7 4.3 fusion.258
  959.0 4.6 fusion.138
  963.6 7.6 add_convert_fusion
  972.5 4.2 fusion.145
  977.0 4.2 fusion.144
  981.3 4.3 fusion.141
  985.6 4.2 fusion.142
  990.0 4.3 fusion.143
  994.4 6.5 fusion.146
  1002.5 6.9 fusion.129
  1010.0 6.3 add_convert_fusion.2
  1016.3 30.4 %reduce-scatter.12.cloned.1.call-done = bf16[1024,512]{1,0:T(8,128)(2,1)} async-done(((bf16[4096,512]{1,0:T(8,128)(2,1)}), bf16[1024,512]{1,0:T(8,128)(2,1)}) %reduce-scatter.12.cloned.1.call-update) | async-done | bytes 1048592 | tf_op jit(solution)/shard_map/reduce_scatter | solution.py:237
  1053.5 41.1 %all-reduce.12 = (f32[512]{0:T(512)S(1)}, f32[512]{0:T(512)S(1)}, f32[512]{0:T(512)S(1)}, f32[512]{0:T(512)S(1)}, f32[2048]{0:T(1024)S(1)}, /*index=5*/f32[512]{0:T(512)S(1)}) all-reduce(f32[512]{0:T(512)S(1)} %get-tuple-element.221, f32[512]{0:T(512)S(1)} %get-tuple-element.224, ...), channel_id=4, replica_groups=mesh['seq'=8,'head'=4] {'seq','head'}, use_global_device_ids=true, to_apply=%region_22.23.clone | all-reduce | flops 4608 | bytes 36864
  1098.1 23.6 %reduce-scatter.20.cloned.1.call-done = f32[64,128]{1,0:T(8,128)} async-done(((f32[512,128]{1,0:T(8,128)}), f32[64,128]{1,0:T(8,128)}) %reduce-scatter.20.cloned.1.call-update) | async-done | bytes 32784 | tf_op jit(solution)/shard_map/reduce_scatter | solution.py:266
  1121.7 37.3 %reduce-scatter.14.cloned.1.call-done = f32[64,128]{1,0:T(8,128)} async-done(((f32[512,128]{1,0:T(8,128)}), f32[64,128]{1,0:T(8,128)}) %reduce-scatter.14.cloned.1.call-update) | async-done | bytes 32784 | tf_op jit(solution)/shard_map/reduce_scatter | solution.py:263
  1158.9 37.5 %reduce-scatter.16.cloned.1.call-done = f32[64,128]{1,0:T(8,128)} async-done(((f32[512,128]{1,0:T(8,128)}), f32[64,128]{1,0:T(8,128)}) %reduce-scatter.16.cloned.1.call-update) | async-done | bytes 32784 | tf_op jit(solution)/shard_map/reduce_scatter | solution.py:264
  1196.4 37.3 %reduce-scatter.18.cloned.1.call-done = f32[64,128]{1,0:T(8,128)} async-done(((f32[512,128]{1,0:T(8,128)}), f32[64,128]{1,0:T(8,128)}) %reduce-scatter.18.cloned.1.call-update) | async-done | bytes 32784 | tf_op jit(solution)/shard_map/reduce_scatter | solution.py:265
  1233.7 150.9 %reduce-scatter.26.cloned.1.call-done = f32[2048,16]{0,1:T(8,128)} async-done(((f32[2048,512]{0,1:T(8,128)}), f32[2048,16]{0,1:T(8,128)}) %reduce-scatter.26.cloned.1.call-update) | async-done | bytes 131088 | tf_op jit(solution)/shard_map/reduce_scatter | solution.py:271
  1384.6 149.5 %reduce-scatter.24.cloned.1.call-done = f32[512,64]{0,1:T(8,128)} async-done(((f32[512,2048]{0,1:T(8,128)}), f32[512,64]{0,1:T(8,128)}) %reduce-scatter.24.cloned.1.call-update) | async-done | bytes 131088 | tf_op jit(solution)/shard_map/reduce_scatter | solution.py:270
  (414 shorter events, 176.3 us)
Async XLA Ops:
  8.0 389.9 %copy-start = (bf16[128,512]{1,0:T(8,128)(2,1)S(1)}, bf16[128,512]{1,0:T(8,128)(2,1)}, u32[]{:S(2)}) copy-start(bf16[128,512]{1,0:T(8,128)(2,1)} %param.26) | copy-start | bytes 393220
  8.0 48.3 %copy-start.3 = (bf16[1024,512]{1,0:T(8,128)(2,1)S(1)}, bf16[1024,512]{1,0:T(8,128)(2,1)}, u32[]{:S(2)}) copy-start(bf16[1024,512]{1,0:T(8,128)(2,1)} %param.19) | copy-start | bytes 3145732
  8.0 4.0 copy-start.62
  8.1 4.2 copy-start.63
  8.1 4.5 copy-start.64
  8.1 4.7 copy-start.65
  8.1 5.0 copy-start.66
  8.1 5.2 copy-start.67
  8.1 130.8 %all-gather.5.cloned.1.call-start = ((), (), s32[]{:S(2)}) async-start(), calls=%async_computation.9 | async-start | bytes 5242880 | tf_op jit(solution)/shard_map/all_gather | solution.py:135
  9.7 48.0 %copy-start.37 = (f32[1024]{0:T(1024)}, f32[1024]{0:T(1024)S(1)}, u32[]{:S(2)}) copy-start(f32[1024]{0:T(1024)S(1)} %broadcast_multiply_fusion.1) | copy-start | bytes 12292
  9.7 129.2 %copy-start.31 = (bf16[512,128]{1,0:T(8,128)(2,1)S(1)}, bf16[512,128]{1,0:T(8,128)(2,1)}, u32[]{:S(2)}) copy-start(bf16[512,128]{1,0:T(8,128)(2,1)} %param.23) | copy-start | bytes 393220
  12.0 126.8 %copy-start.39 = (f32[1024]{0:T(1024)}, f32[1024]{0:T(1024)S(1)}, u32[]{:S(2)}) copy-start(f32[1024]{0:T(1024)S(1)} %fusion.127) | copy-start | bytes 12292
  57.7 420.1 %reduce-scatter.10.cloned.1.call-start = ((), (), s32[]{:S(2)}) async-start(), calls=%async_computation.10 | async-start | bytes 5242880 | tf_op jit(solution)/shard_map/reduce_scatter | solution.py:161
  147.1 3.6 copy-start.33
  159.0 3.6 copy-start.29
  170.9 3.5 copy-start.35
  401.2 113.4 %all-gather.7.cloned.1.call-start = ((), (), s32[]{:S(2)}) async-start(), calls=%async_computation.11 | async-start | bytes 2162688 | tf_op jit(solution)/shard_map/all_gather | solution.py:117
  401.8 171.5 %all-gather.9.cloned.1.call-start = ((), (), s32[]{:S(2)}) async-start(), calls=%async_computation.12 | async-start | bytes 2162688 | tf_op jit(solution)/shard_map/all_gather | solution.py:118
  402.4 268.7 %all-gather.11.cloned.1.call-start = ((), (), s32[]{:S(2)}) async-start(), calls=%async_computation.13 | async-start | bytes 5242880 | tf_op jit(solution)/shard_map/all_gather | solution.py:204
  402.4 185.0 %copy-start.51 = (f32[512]{0:T(512)}, f32[512]{0:T(512)S(1)}, u32[]{:S(2)}) copy-start(f32[512]{0:T(512)S(1)} %convert_element_type.143) | copy-start | bytes 6148
  402.5 112.1 %copy-start.56 = (f32[512]{0:T(512)}, f32[512]{0:T(512)S(1)}, u32[]{:S(2)}) copy-start(f32[512]{0:T(512)S(1)} %convert_element_type.144) | copy-start | bytes 6148
  479.5 107.9 %copy-start.47 = (f32[1024]{0:T(1024)}, f32[1024]{0:T(1024)S(1)}, u32[]{:S(2)}) copy-start(f32[1024]{0:T(1024)S(1)} %broadcast_multiply_fusion) | copy-start | bytes 12292
  480.1 107.4 %copy-start.49 = (f32[1024]{0:T(1024)}, f32[1024]{0:T(1024)S(1)}, u32[]{:S(2)}) copy-start(f32[1024]{0:T(1024)S(1)} %fusion.128) | copy-start | bytes 12292
  480.1 93.2 %copy-start.19 = (bf16[1024,512]{1,0:T(8,128)(2,1)S(1)}, bf16[1024,512]{1,0:T(8,128)(2,1)}, u32[]{:S(2)}) copy-start(bf16[1024,512]{1,0:T(8,128)(2,1)} %param.33) | copy-start | bytes 3145732
  573.3 10.8 copy-start.59
  591.3 455.4 %reduce-scatter.12.cloned.1.call-start = ((), (), s32[]{:S(2)}) async-start(), calls=%async_computation.14 | async-start | bytes 5242880 | tf_op jit(solution)/shard_map/reduce_scatter | solution.py:237
  681.7 4.3 copy-start.27
  686.1 3.7 copy-start.61
  745.1 3.4 copy-start.24
  745.1 3.4 copy-start.28
  748.5 4.3 copy-start.27
  752.8 3.7 copy-start.61
  811.9 3.4 copy-start.24
  811.9 3.4 copy-start.28
  815.2 4.3 copy-start.27
  819.5 3.7 copy-start.61
  878.6 3.4 copy-start.24
  882.0 4.3 copy-start.27
  886.3 3.7 copy-start.61
  945.3 3.4 copy-start.24
  948.9 3.5 copy-start.26
  953.5 5.5 copy-start.13
  959.0 4.6 copy-start.36
  971.3 5.7 copy-start.18
  971.3 126.8 %reduce-scatter.22.cloned.1.call-start = ((), (), s32[]{:S(2)}) async-start(), calls=%async_computation.19 | async-start | bytes 294912 | tf_op jit(solution)/shard_map/reduce_scatter | solution.py:267
  976.7 4.6 copy-start.14
  976.7 145.0 %reduce-scatter.20.cloned.1.call-start = ((), (), s32[]{:S(2)}) async-start(), calls=%async_computation.18 | async-start | bytes 294912 | tf_op jit(solution)/shard_map/reduce_scatter | solution.py:266
  981.2 4.4 copy-start.12
  981.2 177.7 %reduce-scatter.14.cloned.1.call-start = ((), (), s32[]{:S(2)}) async-start(), calls=%async_computation.15 | async-start | bytes 294912 | tf_op jit(solution)/shard_map/reduce_scatter | solution.py:263
  985.6 4.4 copy-start.10
  985.6 210.9 %reduce-scatter.16.cloned.1.call-start = ((), (), s32[]{:S(2)}) async-start(), calls=%async_computation.16 | async-start | bytes 294912 | tf_op jit(solution)/shard_map/reduce_scatter | solution.py:264
  989.9 4.5 copy-start.20
  989.9 243.8 %reduce-scatter.18.cloned.1.call-start = ((), (), s32[]{:S(2)}) async-start(), calls=%async_computation.17 | async-start | bytes 294912 | tf_op jit(solution)/shard_map/reduce_scatter | solution.py:265
  994.3 390.3 %reduce-scatter.26.cloned.1.call-start = ((), (), s32[]{:S(2)}) async-start(), calls=%async_computation.21 | async-start | bytes 4325376 | tf_op jit(solution)/shard_map/reduce_scatter | solution.py:271
  1001.0 533.2 %reduce-scatter.24.cloned.1.call-start = ((), (), s32[]{:S(2)}) async-start(), calls=%async_computation.20 | async-start | bytes 4325376 | tf_op jit(solution)/shard_map/reduce_scatter | solution.py:270
  1010.0 36.7 %copy-start.38 = (f32[1024]{0:T(1024)S(1)}, f32[1024]{0:T(1024)}, u32[]{:S(2)}) copy-start(f32[1024]{0:T(1024)} %copy-done.37) | copy-start | bytes 12292
  1010.0 36.7 %copy-start.42 = (f32[512]{0:T(512)S(1)}, f32[512]{0:T(512)}, u32[]{:S(2)}) copy-start(f32[512]{0:T(512)} %copy-done.41) | copy-start | bytes 6148
  1016.3 32.6 %copy-start.46 = (f32[1024]{0:T(1024)S(1)}, f32[1024]{0:T(1024)}, u32[]{:S(2)}) copy-start(f32[1024]{0:T(1024)} %copy-done.45) | copy-start | bytes 12292
  1016.3 32.6 %copy-start.40 = (f32[1024]{0:T(1024)S(1)}, f32[1024]{0:T(1024)}, u32[]{:S(2)}) copy-start(f32[1024]{0:T(1024)} %copy-done.39) | copy-start | bytes 12292
  1016.3 35.1 %copy-start.6 = (f32[1024,512]{1,0:T(8,128)S(1)}, f32[1024,512]{1,0:T(8,128)}, u32[]{:S(2)}) copy-start(f32[1024,512]{1,0:T(8,128)} %copy-done.5) | copy-start | bytes 6291460
  1016.3 35.1 %copy-start.44 = (f32[1024]{0:T(1024)S(1)}, f32[1024]{0:T(1024)}, u32[]{:S(2)}) copy-start(f32[1024]{0:T(1024)} %copy-done.43) | copy-start | bytes 12292
  1046.7 4.7 copy-start.17
  1046.7 4.7 copy-start.21
  1051.4 482.8 %copy-start.1 = (bf16[128,512]{1,0:T(8,128)(2,1)S(1)}, bf16[128,512]{1,0:T(8,128)(2,1)}, u32[]{:S(2)}) copy-start(bf16[128,512]{1,0:T(8,128)(2,1)} %param.26) | copy-start | bytes 393220
  (39 other events, 71.7 us)
Sparse Core Ops, SparseCore 0:
  57.8 80.9 all-gather.4
  401.3 76.4 reduce-scatter.9
  591.4 79.6 all-gather.10
  971.4 75.2 reduce-scatter.11
  1050.1 34.1 reduce-scatter.21
  1088.0 33.6 reduce-scatter.19
  1125.3 33.6 reduce-scatter.13
  1162.8 33.5 reduce-scatter.15
  1200.0 33.6 reduce-scatter.17
  1236.5 148.0 reduce-scatter.25
  1387.6 146.5 reduce-scatter.23
Sparse Core Ops, SparseCore 1:
  405.0 109.5 all-gather.6
  517.8 55.4 all-gather.8
where the time goes:
time: 1550 us; the launch traced here: 1540 us
  waiting for transfers between devices  788 us (51%)
  other arithmetic  326 us (21%)
  matrix products  229 us (15%)
  local copies, waits for them, and re-layouts  96 us (6%)
  blocking collectives  83.2 us (5%)
  between operations  16.4 us (1%)
    another operation x28, other arithmetic  290 us
    reduce_scatter x1, waiting for transfers between devices, body(): lax.psum_scatter(shrink_wgrad, ('seq', 'head'), scatter_dimension=1, tile...  151 us
    reduce_scatter x1, waiting for transfers between devices, body(): lax.psum_scatter(expand_wgrad, ('seq', 'head'), scatter_dimension=1, tile...  150 us
    unnamed x2, blocking collectives  83.2 us
    all_gather x1, waiting for transfers between devices, body(): group_rows = lax.all_gather(normed_low, 'head', axis=0, tiled=True)  80.5 us
    all_gather x1, waiting for transfers between devices, body(): branch_rows = lax.all_gather(branch_low, 'head', axis=0, tiled=True)  79.7 us
    reduce_scatter x1, waiting for transfers between devices, body(): lax.psum_scatter(jnp.dot(heads_out, output_weight, preferred_element_type...  75.3 us
    all_gather x1, waiting for transfers between devices, body(): lax.all_gather(shrink_weight, ('seq', 'head'), axis=1, tiled=True)  50 us
  transfers between devices with their start and end apart: 13, of which 12 were waited for; matrix products, arithmetic and copies ran while one was open for 4% of the time, Pallas kernels for 0%

commit v1 on v0

v1 whole, which is shorter than its diff:
```python
import functools

import jax
import jax.numpy as jnp
from jax import lax
from jax.experimental import pallas as pl
from jax.experimental.pallas import tpu as pltpu
from jax.sharding import PartitionSpec as P

EPSILON = 1e-5
CHUNK = 128
PAIR = 128
F32 = jnp.float32
BF16 = jnp.bfloat16
LIMIT = 56 * 1024 * 1024


def nn(a, b):
    return lax.dot_general(a, b, (((1,), (0,)), ((), ())), preferred_element_type=F32)


def nt(a, b):
    return lax.dot_general(a, b, (((1,), (1,)), ((), ())), preferred_element_type=F32)


def tn(a, b):
    return lax.dot_general(a, b, (((0,), (0,)), ((), ())), preferred_element_type=F32)


def low(v):
    return v.astype(BF16)


def iota(shape, axis):
    return lax.broadcasted_iota(jnp.int32, shape, axis)


def first_half(shape):
    return iota(shape, 1) < PAIR // 2


def stacked(block):
    left = first_half(block.shape)
    zero = jnp.zeros_like(block)
    return jnp.concatenate([jnp.where(left, block, zero), jnp.where(left, zero, block)], axis=0)


def parts(v):
    high = low(v)
    return jnp.concatenate([high, low(v - high.astype(F32))], axis=1)


def whole(v):
    return v[:, :PAIR] + v[:, PAIR:]


def head_block(shape=(PAIR, PAIR)):
    return (iota(shape, 0) < PAIR // 2) == (iota(shape, 1) < PAIR // 2)


def causal_pair():
    return iota((CHUNK, 2 * CHUNK), 0) >= (iota((CHUNK, 2 * CHUNK), 1) & (CHUNK - 1))


def causal_pair_t():
    return iota((CHUNK, 2 * CHUNK), 0) <= (iota((CHUNK, 2 * CHUNK), 1) & (CHUNK - 1))


def ones_where(mask):
    return low(jnp.where(mask, 1.0, 0.0))


def norm_parts(tokens):
    average = jnp.mean(tokens, axis=-1, keepdims=True)
    centred = tokens - average
    rate = lax.rsqrt(jnp.mean(centred * centred, axis=-1, keepdims=True) + EPSILON)
    return centred * rate, rate


def norm_back(grad, normal, rate, gain):
    w = grad * gain
    return rate * (
        w
        - jnp.mean(w, axis=-1, keepdims=True)
        - normal * jnp.mean(w * normal, axis=-1, keepdims=True)
    )


def chunks(length):
    return [slice(c * CHUNK, (c + 1) * CHUNK) for c in range(length // CHUNK)]


def attend_forward(normed, weight, keep):
    q_ref, k_ref, v_ref, powers_ref, inverse_ref, score_ref, prob_ref, key_state, value_state, heads_ref = keep
    length = normed.shape[0]
    cuts = chunks(length)
    for rows in [slice(r, r + 256) for r in range(0, length, 256)]:
        made = nn(normed[rows, :], weight)
        q_ref[rows, :] = low(low(made[:, :PAIR]).astype(F32) * 0.125)
        k_ref[rows, :] = low(made[:, PAIR : 2 * PAIR])
        v_ref[rows, :] = low(made[:, 2 * PAIR : 3 * PAIR])
        powers_ref[rows, :] = jnp.exp(made[:, 3 * PAIR :])
    tri = ones_where(iota((CHUNK, CHUNK), 0) >= iota((CHUNK, CHUNK), 1))
    same = head_block()
    both = jnp.concatenate([ones_where(same)] * 2, axis=0)
    causal = causal_pair()
    carried = jnp.zeros((1, PAIR), F32)
    local = [whole(nn(tri, parts(powers_ref[rows, :]))) for rows in cuts]
    for rows, sums in zip(cuts, local):
        running = sums + carried
        carried = running[CHUNK - 1 :, :]
        inverse_ref[rows, :] = 1.0 / running
    key_sum = jnp.zeros((PAIR, PAIR), F32)
    value_sum = jnp.zeros((PAIR, PAIR), F32)
    for c, rows in enumerate(cuts):
        key_state[c, :, :] = low(jnp.where(same, key_sum, 0.0))
        value_state[c, :, :] = low(jnp.where(same, value_sum, 0.0))
        if c + 1 < len(cuts):
            powers_low = low(powers_ref[rows, :])
            key_sum = key_sum + tn(k_ref[rows, :], powers_low)
            value_sum = value_sum + tn(powers_low, v_ref[rows, :])
    left = first_half((CHUNK, PAIR))
    scored = [
        low(jnp.where(causal, nt(q_ref[rows, :], stacked(k_ref[rows, :])), 0.0)) for rows in cuts
    ]
    for c, rows in enumerate(cuts):
        summed = nn(scored[c], stacked(low(powers_ref[rows, :]))) + nn(q_ref[rows, :], key_state[c, :, :])
        score_ref[rows, :] = summed * inverse_ref[rows, :]
    for c, rows in enumerate(cuts):
        score = score_ref[rows, :]
        top_a = jnp.max(jnp.where(left, score, -jnp.inf), axis=-1, keepdims=True)
        top_b = jnp.max(jnp.where(left, -jnp.inf, score), axis=-1, keepdims=True)
        lifted = jnp.exp(score - jnp.where(left, top_a, top_b))
        prob_ref[rows, :] = lifted / nn(parts(lifted), both)
    reading = [low(prob_ref[rows, :] * inverse_ref[rows, :]) for rows in cuts]
    mixing = [
        low(jnp.where(causal, nt(reading[c], stacked(low(powers_ref[rows, :]))), 0.0))
        for c, rows in enumerate(cuts)
    ]
    for c, rows in enumerate(cuts):
        heads_ref[rows, :] = low(
            nn(mixing[c], stacked(v_ref[rows, :])) + nn(reading[c], value_state[c, :, :])
        )


def attend_backward(heads_grad, kept, backs):
    q_ref, k_ref, v_ref, powers_ref, inverse_ref, score_ref, prob_ref, key_state, value_state = kept
    cuts = chunks(heads_grad.shape[0])
    same = head_block()
    both = jnp.concatenate([ones_where(same)] * 2, axis=0)
    causal = causal_pair()
    causal_t = causal_pair_t()
    tri_t = ones_where(iota((CHUNK, CHUNK), 0) <= iota((CHUNK, CHUNK), 1))
    after = jnp.zeros((1, PAIR), F32)
    read_sum = jnp.zeros((PAIR, PAIR), F32)
    score_sum = jnp.zeros((PAIR, PAIR), F32)
    for c in reversed(range(len(cuts))):
        rows = cuts[c]
        q, k, v = q_ref[rows, :], k_ref[rows, :], v_ref[rows, :]
        grad = heads_grad[rows, :]
        inverse = inverse_ref[rows, :]
        prob = prob_ref[rows, :]
        powers = powers_ref[rows, :]
        powers_low = low(powers)
        reading = low(prob * inverse)
        powers_two, values_two, keys_two = stacked(powers_low), stacked(v), stacked(k)
        queries_two, grad_two, reading_two = stacked(q), stacked(grad), stacked(reading)
        read_state = low(jnp.where(same, read_sum, 0.0))
        score_state = low(jnp.where(same, score_sum, 0.0))
        mixing_t = low(jnp.where(causal_t, nt(powers_low, reading_two), 0.0))
        mixing_grad = low(jnp.where(causal, nt(grad, values_two), 0.0))
        mixing_grad_t = low(jnp.where(causal_t, nt(v, grad_two), 0.0))
        scored_t = low(jnp.where(causal_t, nt(k, queries_two), 0.0))
        values_grad = nn(mixing_t, grad_two) + nn(powers_low, read_state)
        reading_grad = nn(mixing_grad, powers_two) + nt(grad, value_state[c, :, :])
        powers_grad = nn(mixing_grad_t, reading_two) + nt(v, read_state)
        prob_grad = reading_grad * inverse
        weighed = prob * prob_grad
        slots_grad = weighed - prob * nn(parts(weighed), both)
        running_grad = -inverse * (weighed + slots_grad * score_ref[rows, :])
        summed_grad = low(slots_grad * inverse)
        summed_two = stacked(summed_grad)
        scored_grad = low(jnp.where(causal, nt(summed_grad, powers_two), 0.0))
        scored_grad_t = low(jnp.where(causal_t, nt(powers_low, summed_two), 0.0))
        powers_grad = powers_grad + nn(scored_t, summed_two) + nn(k, score_state)
        backs[rows, :PAIR] = low(
            0.125 * (nn(scored_grad, keys_two) + nt(summed_grad, key_state[c, :, :]))
        )
        backs[rows, PAIR : 2 * PAIR] = low(
            nn(scored_grad_t, queries_two) + nt(powers_low, score_state)
        )
        backs[rows, 2 * PAIR : 3 * PAIR] = low(values_grad)
        later = whole(nn(tri_t, parts(running_grad))) + after
        after = later[:1, :]
        backs[rows, 3 * PAIR :] = low((powers_grad + later) * powers)
        if c:
            read_sum = read_sum + tn(reading, grad)
            score_sum = score_sum + tn(q, summed_grad)


def kept_shapes(length, lead=()):
    n = length // CHUNK
    shape = jax.ShapeDtypeStruct
    return (
        [shape(lead + (length, PAIR), BF16)] * 3
        + [shape(lead + (length, PAIR), F32)] * 4
        + [shape(lead + (n, PAIR, PAIR), BF16)] * 2
        + [shape(lead + (length, PAIR), BF16)]
    )


def vmem(n):
    return [pl.BlockSpec(memory_space=pltpu.VMEM)] * n


def by_slot(shapes):
    return [
        pl.BlockSpec((None,) + s.shape[1:], lambda a, rank=len(s.shape): (a,) + (0,) * (rank - 1))
        for s in shapes
    ]


def fixed(shape):
    return pl.BlockSpec(shape, lambda a: (0,) * len(shape))


def cost(micros):
    return pl.CostEstimate(flops=int(micros * 1e9), bytes_accessed=int(micros * 1e6), transcendentals=0)


def params():
    return pltpu.CompilerParams(vmem_limit_bytes=LIMIT)


def select(width, offset, share, total):
    return ones_where(
        iota((width, total), 0) == offset + (iota((width, total), 1) & (share - 1))
    )


def owned(devices, share, total):
    return iota((devices, total), 0) == lax.shift_right_logical(
        iota((devices, total), 1), share.bit_length() - 1
    )


def spread(rows, offset, share, total):
    each = nn(rows, select(rows.shape[1], offset, share, total))
    return jnp.sum(jnp.where(owned(rows.shape[0], share, total), each, 0.0), axis=0, keepdims=True)


def collect(row, devices, offset, share):
    total = row.shape[1]
    rest = jnp.where(owned(devices, share, total), row, 0.0)
    chosen = select(128, offset, share, total)
    out = jnp.zeros((devices, 128), F32)
    for _ in range(3):
        part = low(rest)
        out = out + nt(part, chosen)
        rest = rest - part.astype(F32)
    return out


def fill(weight, pieces):
    if len(pieces) == 1:
        weight[...] = pieces[0][...]
        return
    mine = lax.axis_index("seq")
    rows = pieces[0].shape[0]
    for r, piece in enumerate(pieces):
        weight[pl.ds(pl.multiple_of((mine ^ r) * rows, rows), rows), :] = piece[...]


def first_kernel(tokens_ref, vectors_ref, weight_ref, normed_ref, residual_ref, *keep):
    tokens = tokens_ref[...].astype(F32)
    normal, _ = norm_parts(tokens)
    width = tokens.shape[1]
    share = width // vectors_ref.shape[0]
    small = vectors_ref[:, :128]
    gain = spread(small, 0, share, width)
    shift = spread(small, share, share, width)
    normed_ref[...] = low(normal * gain + shift)
    attend_forward(normed_ref, weight_ref[:width, :], keep)
    residual_ref[...] = tokens + nn(keep[-1][...], weight_ref[width:, :])


def forward_first(tokens, vectors, weight):
    length, width = tokens.shape
    outs = [jax.ShapeDtypeStruct((length, width), BF16), jax.ShapeDtypeStruct((length, width), F32)]
    outs += kept_shapes(length)
    made = pl.pallas_call(
        first_kernel,
        out_shape=outs,
        in_specs=vmem(3),
        out_specs=vmem(len(outs)),
        compiler_params=params(),
        cost_estimate=cost(6),
        name="attend_first",
    )(tokens, vectors, weight)
    return made[0], made[1], made[2:]


def rest_kernel(count, normed_ref, before_ref, *refs):
    pieces, residual_ref, keep, weight = refs[:count], refs[count], refs[count + 1 : -1], refs[-1]
    width = normed_ref.shape[1]
    fill(weight, pieces)

    @pl.when(pl.program_id(0) == 0)
    def _():
        residual_ref[...] = before_ref[...]

    attend_forward(normed_ref, weight[:width, :], keep)
    residual_ref[...] += nn(keep[-1][...], weight[width:, :])


def forward_rest(normed, residual, pieces):
    length, width = normed.shape
    slots = pieces[0].shape[0]
    keep = kept_shapes(length, (slots,))
    made = pl.pallas_call(
        functools.partial(rest_kernel, len(pieces)),
        grid=(slots,),
        out_shape=[jax.ShapeDtypeStruct((length, width), F32)] + keep,
        in_specs=[fixed((length, width))] * 2 + by_slot(pieces),
        out_specs=[fixed((length, width))] + by_slot(keep),
        scratch_shapes=[pltpu.VMEM((width + PAIR, 4 * PAIR), BF16)],
        compiler_params=params(),
        cost_estimate=cost(17),
        name="attend_rest",
    )(normed, residual, *pieces)
    return made[0], made[1:]


GELU_A = 0.7978845608028654
GELU_B = 0.044715


def gelu_both(u):
    square = u * u
    bend = jnp.tanh(GELU_A * (u + GELU_B * (square * u)))
    half = 0.5 * (1.0 + bend)
    slope = half + 0.5 * u * (1.0 - bend * bend) * (GELU_A * (1.0 + 3.0 * GELU_B * square))
    return u * half, slope


def place(core, chip, turn, slots):
    seq = lax.axis_index("seq") ^ (2 * chip + core)
    return seq * slots + lax.rem(lax.axis_index("head") + turn, slots)


def weight_copies(pieces, expand, shrink, sems):
    if len(pieces) == 2:
        return [
            pltpu.make_async_copy(pieces[0], expand, sems.at[0]),
            pltpu.make_async_copy(pieces[1], shrink, sems.at[1]),
        ]
    copies = []
    for r, piece in enumerate(pieces):
        slots = piece.shape[0]
        for a in range(slots):
            source = place(r % 2, r // 2, slots - a, slots)
            n = len(copies)
            copies.append(
                pltpu.make_async_copy(
                    piece.at[a, pl.ds(0, 4)], expand.at[pl.ds(source * 4, 4)], sems.at[n]
                )
            )
            copies.append(
                pltpu.make_async_copy(
                    piece.at[a, pl.ds(4, 4)], shrink.at[:, source], sems.at[n + 1]
                )
            )
    return copies


def grad_copies(expand, shrink, outs, sems):
    if len(outs) == 2 and outs[0].shape == expand.shape:
        return [
            pltpu.make_async_copy(expand, outs[0], sems.at[0]),
            pltpu.make_async_copy(shrink, outs[1], sems.at[1]),
        ]
    copies = []
    for core, out in enumerate(outs):
        for chip in range(out.shape[0]):
            slots = out.shape[1]
            for a in range(slots):
                target = place(core, chip, a, slots)
                n = len(copies)
                copies.append(
                    pltpu.make_async_copy(
                        expand.at[pl.ds(target * 4, 4)], out.at[chip, a, pl.ds(0, 4)], sems.at[n]
                    )
                )
                copies.append(
                    pltpu.make_async_copy(
                        shrink.at[:, target], out.at[chip, a, pl.ds(4, 4)], sems.at[n + 1]
                    )
                )
    return copies


def ffn_kernel(count, residual_ref, vectors_ref, cotangent_ref, *refs):
    pieces = refs[:count]
    result_ref, grad_ref, branch_ref, sums_ref = refs[count : count + 4]
    grads = refs[count + 4 : count + 6]
    (expand_all, shrink_all, expand_grad, shrink_grad, second, normal_ref, rate_ref, total, back,
     gains, bias_row, bias_grads, sems) = refs[count + 6 :]
    k = pl.program_id(0)
    steps = pl.num_programs(0)
    length, width = residual_ref.shape
    devices = vectors_ref.shape[0]
    share = width // devices
    tiles = [slice(r, r + 256) for r in range(0, length, 256)]
    step = expand_all.shape[0] * 16 // 4
    hidden_share = 4 * step // devices

    @pl.when(k == 0)
    def _():
        copies = weight_copies(pieces, expand_all, shrink_all, sems)
        for copy in copies:
            copy.start()
        small = vectors_ref[:, :128]
        for i in range(3):
            gains[i : i + 1, :] = spread(small, (2 + i) * share, share, width)
        wide = spread(vectors_ref[:, 128:], 0, hidden_share, 4 * step)
        for i in range(4):
            bias_row[i, 0:1, :] = wide[:, i * step : (i + 1) * step]
        for rows in tiles:
            normal, rate = norm_parts(residual_ref[rows, :])
            normal_ref[rows, :] = normal
            rate_ref[rows, :] = rate
            second[rows, :] = low(normal * gains[0:1, :] + gains[1:2, :])
            total[rows, :] = residual_ref[rows, :] + gains[2:3, :]
            back[rows, :] = jnp.zeros((256, width), F32)
        for copy in copies:
            copy.wait()

    blocks = step // 16
    expand = expand_all[pl.ds(k * blocks, blocks)].reshape(step, width)
    shrink = shrink_all[k].reshape(width, step)
    bias = bias_row[k][0:1, :]
    bias_grad = jnp.zeros((1, step), F32)
    acts, hids = [], []
    for rows in tiles:
        hidden = nt(second[rows, :], expand) + bias
        pull = nn(cotangent_ref[rows, :], shrink)
        value, slope = gelu_both(hidden)
        activated = low(value)
        hidden_grad = low(pull * slope)
        bias_grad = bias_grad + jnp.sum(hidden_grad.astype(F32), axis=0, keepdims=True)
        total[rows, :] = total[rows, :] + nt(activated, shrink)
        back[rows, :] = back[rows, :] + nn(hidden_grad, expand)
        acts.append(activated)
        hids.append(hidden_grad)
    bias_grads[k, 0:1, :] = bias_grad
    shrink_grad[k] = low(tn(cotangent_ref[...], jnp.concatenate(acts, axis=0))).reshape(
        width // 16, 16, step
    )
    expand_grad[pl.ds(k * blocks, blocks)] = low(
        tn(jnp.concatenate(hids, axis=0), second[...])
    ).reshape(blocks, 16, width)

    @pl.when(k == steps - 1)
    def _():
        copies = grad_copies(expand_grad, shrink_grad, grads, sems)
        for copy in copies:
            copy.start()
        gain = gains[0:1, :]
        gain_grad = jnp.zeros((1, width), F32)
        shift_grad = jnp.zeros((1, width), F32)
        outer = jnp.zeros((1, width), F32)
        for rows in tiles:
            result_ref[rows, :] = low(total[rows, :])
            grad = back[rows, :]
            normal = normal_ref[rows, :]
            upstream = cotangent_ref[rows, :].astype(F32)
            gain_grad = gain_grad + jnp.sum(grad * normal, axis=0, keepdims=True)
            shift_grad = shift_grad + jnp.sum(grad, axis=0, keepdims=True)
            outer = outer + jnp.sum(upstream, axis=0, keepdims=True)
            full = upstream + norm_back(grad, normal, rate_ref[rows, :], gain)
            grad_ref[rows, :] = full
            branch_ref[rows, :] = low(full)
        sums_ref[:, :128] = (
            collect(gain_grad, devices, 2 * share, share)
            + collect(shift_grad, devices, 3 * share, share)
            + collect(outer, devices, 4 * share, share)
        )
        wide = jnp.concatenate([bias_grads[i][0:1, :] for i in range(4)], axis=1)
        sums_ref[:, 128:] = collect(wide, devices, 0, hidden_share)
        for copy in copies:
            copy.wait()


def feed_forward(residual, vectors, cotangent, pieces, grad_shapes, hidden):
    length, width = residual.shape
    step = hidden // 4
    shape = jax.ShapeDtypeStruct
    anywhere = pl.BlockSpec(memory_space=pl.ANY)
    return pl.pallas_call(
        functools.partial(ffn_kernel, len(pieces)),
        grid=(4,),
        out_shape=[
            shape((length, width), BF16),
            shape((length, width), F32),
            shape((length, width), BF16),
            shape(vectors.shape, F32),
        ]
        + [shape(s, BF16) for s in grad_shapes],
        in_specs=[fixed((length, width)), fixed(vectors.shape), fixed((length, width))]
        + [anywhere] * len(pieces),
        out_specs=[fixed((length, width))] * 3 + [fixed(vectors.shape)] + [anywhere] * len(grad_shapes),
        scratch_shapes=[
            pltpu.VMEM((hidden // 16, 16, width), BF16),
            pltpu.VMEM((4, width // 16, 16, step), BF16),
            pltpu.VMEM((hidden // 16, 16, width), BF16),
            pltpu.VMEM((4, width // 16, 16, step), BF16),
            pltpu.VMEM((length, width), BF16),
            pltpu.VMEM((length, width), F32),
            pltpu.VMEM((length, 1), F32),
            pltpu.VMEM((length, width), F32),
            pltpu.VMEM((length, width), F32),
            pltpu.VMEM((8, width), F32),
            pltpu.VMEM((4, 8, step), F32),
            pltpu.VMEM((4, 8, step), F32),
            pltpu.SemaphoreType.DMA((max(2, 2 * vectors.shape[0]),)),
        ],
        compiler_params=params(),
        cost_estimate=cost(27),
        name="feed_forward",
    )(residual, vectors, cotangent, *pieces)


def pair_grads(branch_ref, normed_ref, weight_in, weight_out, kept, heads_ref, outs, grad, backs, made):
    grad[...] = low(nt(branch_ref[...], weight_out))
    attend_backward(grad, kept, backs)
    made[:, : 4 * PAIR] = low(tn(normed_ref[...], backs[...]))
    made[:, 4 * PAIR :] = low(tn(branch_ref[...], heads_ref[...]))
    if len(outs) == 1:
        outs[0][...] = made[...]
        return
    seq = lax.axis_index("seq")
    for core, out in enumerate(outs):
        rows = out.shape[1]
        for chip in range(out.shape[0]):
            start = pl.multiple_of((seq ^ (2 * chip + core)) * rows, rows)
            out[chip] = made[pl.ds(start, rows), :]


def back_rest_kernel(count, parts_out, branch_ref, normed_ref, *refs):
    pieces, refs = refs[:count], refs[count:]
    kept, heads_ref, refs = refs[:9], refs[9], refs[10:]
    sum_ref, outs = refs[0], refs[1 : 1 + parts_out]
    weight, grad, backs, made = refs[1 + parts_out :]
    width = normed_ref.shape[1]
    fill(weight, pieces)
    pair_grads(
        branch_ref, normed_ref, None, weight[width:, :], kept, heads_ref, outs, grad, backs, made
    )

    @pl.when(pl.program_id(0) == 0)
    def _():
        sum_ref[...] = jnp.zeros_like(sum_ref)

    sum_ref[...] += nt(backs[...], weight[:width, :])


def back_scratch(length, width):
    return [
        pltpu.VMEM((length, PAIR), BF16),
        pltpu.VMEM((length, 4 * PAIR), BF16),
        pltpu.VMEM((width, 5 * PAIR), BF16),
    ]


def backward_rest(branch, normed, pieces, kept, grad_shapes):
    length, width = branch.shape
    slots = pieces[0].shape[0]
    shape = jax.ShapeDtypeStruct
    grads = [shape((slots,) + s, BF16) for s in grad_shapes]
    return pl.pallas_call(
        functools.partial(back_rest_kernel, len(pieces), len(grads)),
        grid=(slots,),
        out_shape=[shape((length, width), F32)] + grads,
        in_specs=[fixed((length, width))] * 2 + by_slot(pieces) + by_slot(kept),
        out_specs=[fixed((length, width))] + by_slot(grads),
        scratch_shapes=[pltpu.VMEM((width + PAIR, 4 * PAIR), BF16)] + back_scratch(length, width),
        compiler_params=params(),
        cost_estimate=cost(36),
        name="attend_back_rest",
    )(branch, normed, *pieces, *kept)


def back_first_kernel(parts_out, branch_ref, normed_ref, weight_ref, *refs):
    kept, heads_ref, refs = refs[:9], refs[9], refs[10:]
    backs, outs = refs[0], refs[1 : 1 + parts_out]
    grad, made = refs[1 + parts_out :]
    width = normed_ref.shape[1]
    pair_grads(
        branch_ref, normed_ref, None, weight_ref[width:, :], kept, heads_ref, outs, grad, backs, made
    )


def backward_first(branch, normed, weight, kept, grad_shapes):
    length, width = branch.shape
    shape = jax.ShapeDtypeStruct
    outs = [shape((length, 4 * PAIR), BF16)] + [shape(s, BF16) for s in grad_shapes]
    scratch = back_scratch(length, width)
    return pl.pallas_call(
        functools.partial(back_first_kernel, len(grad_shapes)),
        out_shape=outs,
        in_specs=vmem(13),
        out_specs=vmem(len(outs)),
        scratch_shapes=[scratch[0], scratch[2]],
        compiler_params=params(),
        cost_estimate=cost(11),
        name="attend_back_first",
    )(branch, normed, weight, *kept)


def last_kernel(tokens_ref, vectors_ref, backs_ref, weight_ref, total_ref, grad_ref, before_ref, out_ref, sums_ref):
    length, width = tokens_ref.shape
    devices = vectors_ref.shape[0]
    share = width // devices
    gain = spread(vectors_ref[:, :128], 0, share, width)
    gain_grad = jnp.zeros((1, width), F32)
    shift_grad = jnp.zeros((1, width), F32)
    for rows in [slice(r, r + 256) for r in range(0, length, 256)]:
        grad = total_ref[rows, :] + nt(backs_ref[rows, :], weight_ref[:width, :])
        normal, rate = norm_parts(tokens_ref[rows, :].astype(F32))
        gain_grad = gain_grad + jnp.sum(grad * normal, axis=0, keepdims=True)
        shift_grad = shift_grad + jnp.sum(grad, axis=0, keepdims=True)
        out_ref[rows, :] = low(grad_ref[rows, :] + norm_back(grad, normal, rate, gain))
    sums_ref[:, :128] = (
        before_ref[:, :128]
        + collect(gain_grad, devices, 0, share)
        + collect(shift_grad, devices, share, share)
    )
    sums_ref[:, 128:] = before_ref[:, 128:]


def finish(tokens, vectors, backs, weight, total, grad, before):
    shape = jax.ShapeDtypeStruct
    return pl.pallas_call(
        last_kernel,
        out_shape=[shape(tokens.shape, BF16), shape(before.shape, F32)],
        in_specs=vmem(7),
        out_specs=vmem(2),
        compiler_params=params(),
        cost_estimate=cost(5),
        name="norm_back",
    )(tokens, vectors, backs, weight, total, grad, before)


def flip(count, bit):
    return [(i, i ^ bit) for i in range(count)]


def turn(count, by):
    return [(i, (i + by) % count) for i in range(count)]


def add(*members):
    return functools.reduce(lambda a, b: a + b, [m.astype(F32) for m in members])


def across(shares, chips, seqs):
    held = [shares] + [lax.ppermute(shares, "seq", flip(seqs, 2 * r)) for r in range(1, chips)]
    mates = [lax.ppermute(h, "seq", flip(seqs, 1)) for h in held]
    return [member for both in zip(held, mates) for member in both]


def back_across(keep, send, chips, seqs):
    other = lax.ppermute(send, "seq", flip(seqs, 1))
    made = [add(keep[r], other[r]) for r in range(chips)]
    came = [lax.ppermute(low(made[r]), "seq", flip(seqs, 2 * r)) for r in range(1, chips)]
    return add(made[0], *came)


def body(
    inputs,
    attn_gain,
    attn_shift,
    query_weight,
    key_weight,
    value_weight,
    control_weight,
    output_weight,
    ffn_gain,
    ffn_shift,
    expand_weight,
    expand_bias,
    shrink_weight,
    shrink_bias,
    cotangent,
):
    seqs, slots = lax.axis_size("seq"), lax.axis_size("head")
    devices = seqs * slots
    chips = seqs // 2
    width = inputs.shape[1]
    share = width // devices
    hidden_share = expand_weight.shape[1]
    hidden = hidden_share * devices
    z = lax.axis_index("head")
    direct = share % 16 == 0 and hidden_share == 4 * share and (width + PAIR) % (16 * seqs) == 0

    own = jnp.concatenate(
        [
            jnp.concatenate([query_weight, key_weight, value_weight, control_weight], axis=1),
            output_weight,
        ],
        axis=0,
    )
    small = jnp.concatenate([attn_gain, attn_shift, ffn_gain, ffn_shift, shrink_bias])
    row = jnp.concatenate(
        [
            small,
            jnp.zeros((128 - small.shape[0],), BF16),
            expand_bias,
            jnp.zeros((128 - expand_bias.shape[0],), BF16),
        ]
    )
    vectors = lax.all_to_all(
        jnp.broadcast_to(row[None, :], (devices, 256)), ("seq", "head"), 0, 0, tiled=True
    )
    expand_t = expand_weight.T
    shrink_t = shrink_weight.T
    if direct:
        rows = own.shape[0] // seqs
        piece = lax.dynamic_slice_in_dim(own, lax.axis_index("seq") * rows, rows, axis=0)
        near = jnp.stack([lax.ppermute(piece, "head", turn(slots, a)) for a in range(1, slots)])
        pieces = across(near, chips, seqs)
        load = jnp.concatenate(
            [expand_t.reshape(4, 16, width)]
            + [shrink_t[None, :, k * width : (k + 1) * width] for k in range(4)],
            axis=0,
        )
        near = jnp.stack([load] + [lax.ppermute(load, "head", turn(slots, a)) for a in range(1, slots)])
        ffn_pieces = across(near, chips, seqs)
        pair_shapes = [(chips, width // seqs, 5 * PAIR)] * 2
        ffn_shapes = [(chips, slots, 8, 16, width)] * 2
    else:
        every = lax.all_gather(own, "head", axis=0, tiled=False)
        pieces = [jnp.stack([every[(z + slots - a) % slots] for a in range(1, slots)])]
        ffn_pieces = [
            lax.all_gather(expand_t, ("seq", "head"), axis=0, tiled=True).reshape(hidden // 16, 16, width),
            lax.all_gather(shrink_t, ("seq", "head"), axis=0, tiled=True)
            .reshape(width // 16, 16, 4, hidden // 4)
            .transpose(2, 0, 1, 3),
        ]
        pair_shapes = [(width, 5 * PAIR)]
        ffn_shapes = [(hidden // 16, 16, width), (4, width // 16, 16, hidden // 4)]

    normed, residual, kept_first = forward_first(inputs, vectors, own)
    residual, kept_rest = forward_rest(normed, residual, pieces)
    result, residual_grad, branch, sums, *ffn_grads = feed_forward(
        residual, vectors, cotangent, ffn_pieces, ffn_shapes, hidden
    )
    total, *rest_grads = backward_rest(branch, normed, pieces, kept_rest, pair_shapes)
    backs, *first_grads = backward_first(branch, normed, own, kept_first, pair_shapes)
    input_grad, sums = finish(inputs, vectors, backs, own, total, residual_grad, sums)

    if direct:
        mine = back_across(*ffn_grads, chips, seqs)
        came = [lax.ppermute(low(mine[a]), "head", turn(slots, a)) for a in range(1, slots)]
        ffn_sum = add(mine[0], *came)
        expand_grad = ffn_sum[:4].reshape(hidden_share, width)
        shrink_grad = jnp.concatenate([ffn_sum[4 + k] for k in range(4)], axis=1)
        keep, send = [jnp.swapaxes(g, 0, 1) for g in rest_grads]
        rest = back_across(keep, send, chips, seqs)
        came = [
            lax.ppermute(low(rest[a - 1]), "head", turn(slots, slots - a)) for a in range(1, slots)
        ]
        pair_sum = add(back_across(*first_grads, chips, seqs), *came)
    else:
        expand_grad = lax.psum_scatter(
            ffn_grads[0].reshape(hidden, width).astype(F32), ("seq", "head"), scatter_dimension=0, tiled=True
        )
        shrink_grad = lax.psum_scatter(
            ffn_grads[1].transpose(1, 2, 0, 3).reshape(width, hidden).astype(F32),
            ("seq", "head"),
            scatter_dimension=0,
            tiled=True,
        )
        every = jnp.concatenate([first_grads[0][None], rest_grads[0]], axis=0).astype(F32)
        every = jnp.stack([every[(z + slots - p) % slots] for p in range(slots)])
        pair_sum = lax.psum_scatter(every, "head", scatter_dimension=0, tiled=False)
        pair_sum = lax.psum_scatter(pair_sum, "seq", scatter_dimension=0, tiled=True)

    sums = jnp.sum(lax.all_to_all(sums, ("seq", "head"), 0, 0, tiled=True), axis=0)
    vector = [sums[i * share : (i + 1) * share] for i in range(5)]
    return (
        result,
        input_grad,
        vector[0],
        vector[1],
        pair_sum[:, :PAIR],
        pair_sum[:, PAIR : 2 * PAIR],
        pair_sum[:, 2 * PAIR : 3 * PAIR],
        pair_sum[:, 3 * PAIR : 4 * PAIR],
        pair_sum[:, 4 * PAIR :].T,
        vector[2],
        vector[3],
        expand_grad.T,
        sums[128 : 128 + hidden_share],
        shrink_grad.T,
        vector[4],
    )


def solution(mesh):
    placed = (
        P(("seq", "head"), None),
        P(("seq", "head")),
        P(("seq", "head")),
        P(None, "head"),
        P(None, "head"),
        P(None, "head"),
        P(None, "head"),
        P("head", None),
        P(("seq", "head")),
        P(("seq", "head")),
        P(None, ("seq", "head")),
        P(("seq", "head")),
        P(None, ("seq", "head")),
        P(("seq", "head")),
        P(("seq", "head"), None),
    )
    return jax.shard_map(
        body,
        mesh=mesh,
        in_specs=placed,
        out_specs=(
            P(("seq", "head"), None),
            P(("seq", "head"), None),
            P(("seq", "head")),
            P(("seq", "head")),
            P("seq", "head"),
            P("seq", "head"),
            P("seq", "head"),
            P("seq", "head"),
            P("head", "seq"),
            P(("seq", "head")),
            P(("seq", "head")),
            P(None, ("seq", "head")),
            P(("seq", "head")),
            P(None, ("seq", "head")),
            P(("seq", "head")),
        ),
        check_vma=False,
    )
```

time: 1550 us -> 219 us (0.14)
  waiting for transfers between devices: 788 us -> 55.3 us
  other arithmetic: 326 us -> 13.7 us
  matrix products: 229 us -> 0 us
  Pallas kernels: 0 us -> 89.2 us
  local copies, waits for them, and re-layouts: 96 us -> 8.99 us
  blocking collectives: 83.2 us -> 8.87 us
  starting transfers between devices: 1.53 us -> 41.4 us
    reduce_scatter x9 -> x0, waiting for transfers between devices: 542 us -> none  [the longest x1 151 us: body(): lax.psum_scatter(shrink_wgrad, ('seq', 'head'), scatter_dimension=1, tile...]
    another operation x28 -> x4, other arithmetic: 290 us -> 3.56 us
    all_gather x4 -> x0, waiting for transfers between devices: 245 us -> none  [the longest x1 80.5 us: body(): group_rows = lax.all_gather(normed_low, 'head', axis=0, tiled=True)]
    dot_general x61 -> x0, matrix products: 229 us -> none  [the longest x4 19.6 us: slot_forward(): jnp.einsum('hti,ihs->ths', scored, powers_low, preferred_element_type=jnp...]
    pallas_call x0 -> x6, Pallas kernels: none -> 89.2 us  [the longest x1 29.5 us: backward_rest(): pl.pallas_call(functools.partial(back_rest_kernel, len(pieces), len(grads...]
    unnamed x2 -> x0, blocking collectives: 83.2 us -> none
    ppermute x0 -> x38, waiting for transfers between devices: none -> 55.3 us  [the longest x9 15.3 us: back_across(): lax.ppermute(low(made[r]), 'seq', flip(seqs, 2 * r))]
    ppermute x0 -> x38, starting transfers between devices: none -> 38.8 us  [the longest x9 10.5 us: back_across(): lax.ppermute(low(made[r]), 'seq', flip(seqs, 2 * r))]
  transfers between devices with their start and end apart: 13 -> 39, of which waited for: 12 -> 12; matrix products, arithmetic and copies ran while one was open for 4% -> 7% of each run, Pallas kernels for 0% -> 15%
where the time goes in v1:
time: 219 us
  Pallas kernels  89.2 us (41%)
  waiting for transfers between devices  55.3 us (25%)
  starting transfers between devices  41.4 us (19%)
  other arithmetic  13.7 us (6%)
  local copies, waits for them, and re-layouts  8.99 us (4%)
  blocking collectives  8.87 us (4%)
    pallas_call x1, Pallas kernels, backward_rest(): pl.pallas_call(functools.partial(back_rest_kernel, len(pieces), len(grads...  29.5 us
    pallas_call x1, Pallas kernels, feed_forward(): pl.pallas_call(functools.partial(ffn_kernel, len(pieces)), grid=(4,), out...  26 us
    ppermute x9, waiting for transfers between devices, back_across(): lax.ppermute(low(made[r]), 'seq', flip(seqs, 2 * r))  15.3 us
    ppermute x6, waiting for transfers between devices, across(): lax.ppermute(shares, 'seq', flip(seqs, 2 * r))  15.2 us
    pallas_call x1, Pallas kernels, forward_rest(): pl.pallas_call(functools.partial(rest_kernel, len(pieces)), grid=(slots,)...  11.5 us
    pallas_call x1, Pallas kernels, backward_first(): pl.pallas_call(functools.partial(back_first_kernel, len(grad_shapes)), ou...  10.7 us
    ppermute x9, starting transfers between devices, back_across(): lax.ppermute(low(made[r]), 'seq', flip(seqs, 2 * r))  10.5 us
    all_to_all x1, blocking collectives, body(): lax.all_to_all(jnp.broadcast_to(row[None, :], (devices, 256)), ('seq', 'h...  8.87 us
  transfers between devices with their start and end apart: 39, of which 12 were waited for; matrix products, arithmetic and copies ran while one was open for 7% of the time, Pallas kernels for 15%

profile of v1, /device:TPU:0, one launch (start us, length us, event | category | flops | bytes accessed | tf_op | source)
XLA Modules:
  0.0 218.6 jit_solution(6126451284389074691)
XLA Ops:
  0.7 1.3 pad_maximum_fusion.weight_ref
  2.0 5.1 %collective-permute-start.2 = (bf16[80,512]{1,0:T(8,128)(2,1)S(1)}, bf16[80,512]{1,0:T(8,128)(2,1)S(1)}, u32[]{:S(2)}, u32[]{:S(2)}) collective-permute-start(bf16[80,512]{1,0:T(8,128)(2,1)S(1)} %constant_dynamic-slice_fusion), channel_id=1, source_target_pairs={{0,3},{1,0},{2,1},{3,2},{4,7},{5,4},{6,5},{7,6},{8,11},{9,8},{10,9... | collective-permute-start | bytes 245768 | tf_op jit(solution)/shard_map/ppermute | solution.py:730
  7.1 1.0 collective-permute-start
  8.2 0.8 constant_dynamic-update-slice_fusion
  9.0 1.0 collective-permute-done.2
  10.0 4.7 %collective-permute-done.1 = bf16[80,512]{1,0:T(8,128)(2,1)S(1)} collective-permute-done((bf16[80,512]{1,0:T(8,128)(2,1)S(1)}, bf16[80,512]{1,0:T(8,128)(2,1)S(1)}, u32[]{:S(2)}, u32[]{:S(2)}) %collective-permute-start.1) | collective-permute-done | bytes 81952 | tf_op jit(solution)/shard_map/ppermute | solution.py:730
  14.7 2.5 %collective-permute-start.8 = (bf16[3,80,512]{2,1,0:T(8,128)(2,1)S(1)}, bf16[3,80,512]{2,1,0:T(8,128)(2,1)S(1)}, u32[]{:S(2)}, u32[]{:S(2)}) collective-permute-start(bf16[3,80,512]{2,1,0:T(8,128)(2,1)S(1)} %pad_maximum_fusion.2.refs_0_), channel_id=1, source_target_pairs={{0,24},{4,28},{8,16},{12,20},{16,8},{20,12},{24,0},{28,4},{1,25},{... | collective-permute-start | bytes 737288 | tf_op jit(solution)/shard_map/ppermute | solution.py:667
  17.2 2.1 collective-permute-start.12
  19.3 2.0 collective-permute-start.10
  21.3 0.5 collective-permute-start.6
  21.9 1.2 collective-permute-done.12
  23.1 0.5 collective-permute-start.4
  23.6 6.5 %collective-permute-done.11 = bf16[8,16,512]{2,1,0:T(8,128)(2,1)S(1)} collective-permute-done((bf16[8,16,512]{2,1,0:T(8,128)(2,1)S(1)}, bf16[8,16,512]{2,1,0:T(8,128)(2,1)S(1)}, u32[]{:S(2)}, u32[]{:S(2)}) %collective-permute-start.11) | collective-permute-done | bytes 131104 | tf_op jit(solution)/shard_map/ppermute | solution.py:737
  30.1 0.5 collective-permute-start.9
  30.8 0.5 broadcast.3
  31.3 0.7 reduce.1
  32.1 8.9 %all_to_all.17 = bf16[32,2,128]{2,1,0:T(2,128)(2,1)S(1)} all-to-all(bf16[32,2,128]{2,1,0:T(2,128)(2,1)S(1)} %reshape.97), channel_id=1, replica_groups=mesh['seq'=8,'head'=4] {'seq','head'}, dimensions={0} | all-to-all | bytes 32768 | tf_op jit(solution)/shard_map/all_to_all | solution.py:722
  40.9 0.6 copy.54
  41.6 0.6 collective-permute-start.18
  42.3 1.5 collective-permute-start.16
  43.8 1.4 collective-permute-start.14
  45.7 5.7 %attend_first.1 = (bf16[1024,512]{1,0:T(8,128)(2,1)}, f32[1024,512]{1,0:T(8,128)}, bf16[1024,128]{1,0:T(8,128)(2,1)}, bf16[1024,128]{1,0:T(8,128)(2,1)}, bf16[10...) custom-call(bf16[1024,512]{1,0:T(8,128)(2,1)} %tokens_ref.3, ...), custom_call_target="tpu_custom_call" | custom-call | flops 6000000000 | bytes 6000000 | tf_op jit(solution)/shard_map/attend_first/pallas_call | solution.py:291
  51.6 5.8 %collective-permute-done.18.refs_6_ = bf16[4,8,16,512]{3,2,1,0:T(8,128)(2,1)S(1)} collective-permute-done((bf16[4,8,16,512]{3,2,1,0:T(8,128)(2,1)S(1)}, bf16[4,8,16,512]{3,2,1,0:T(8,128)(2,1)S(1)}, u32[]{:S(2)}, u32[]{:S(2)}) %collective-permute-start.18) | collective-permute-done | bytes 524320 | tf_op jit(solution)/shard_map/ppermute | solution.py:667
  57.4 9.4 %collective-permute-done.16.refs_4_ = bf16[4,8,16,512]{3,2,1,0:T(8,128)(2,1)S(1)} collective-permute-done((bf16[4,8,16,512]{3,2,1,0:T(8,128)(2,1)S(1)}, bf16[4,8,16,512]{3,2,1,0:T(8,128)(2,1)S(1)}, u32[]{:S(2)}, u32[]{:S(2)}) %collective-permute-start.16) | collective-permute-done | bytes 524320 | tf_op jit(solution)/shard_map/ppermute | solution.py:667
  66.8 0.5 collective-permute-start.15
  67.3 0.7 copy-done.27
  68.0 11.5 %attend_rest.1 = (f32[1024,512]{1,0:T(8,128)}, bf16[3,1024,128]{2,1,0:T(8,128)(2,1)}, bf16[3,1024,128]{2,1,0:T(8,128)(2,1)}, bf16[3,1024,128]{2,1,0:T(8,128)(2,1...) custom-call(bf16[1024,512]{1,0:T(8,128)(2,1)} %get-tuple-element.52., ...), custom_call_target="tpu_custom_call" | custom-call | flops 16999999488 | bytes 17000000 | tf_op jit(solution)/shard_map/attend_rest/pallas_call | solution.py:320
  79.6 0.7 copy-done.17
  80.8 26.0 %feed_forward.1 = (bf16[1024,512]{1,0:T(8,128)(2,1)}, f32[1024,512]{1,0:T(8,128)}, bf16[1024,512]{1,0:T(8,128)(2,1)}, f32[32,256]{1,0:T(8,128)}, bf16[4,4,8,16,5...) custom-call(f32[1024,512]{1,0:T(8,128)} %get-tuple-element.54.residual_ref, bf16[32,256]{1,0:T(8,128)(2,1)} %bitcast.150, ...), custom_call_target="tpu_custom_call" | custom-call | flops 27000000512 | bytes 27000000 | tf_op jit(solution)/shard_map/feed_forward/pallas_call | solution.py:499
  106.9 29.5 %attend_back_rest.1 = (f32[1024,512]{1,0:T(8,128)}, bf16[3,4,64,640]{3,2,1,0:T(8,128)(2,1)}, bf16[3,4,64,640]{3,2,1,0:T(8,128)(2,1)}) custom-call(bf16[1024,512]{1,0:T(8,128)(2,1)} %get-tuple-element.56.branch_ref, bf16[1024,512]{1,0:T(8,128)(2,1)} %get-tuple-element.52.normed_ref, bf16[3,80,512]{2,1,0:T(8,128)(2,1)} %copy-done.6, ...), custom_call_target="tpu_custom_call" | custom-call | flops 35999997952 | bytes 36000000 | tf_op jit(solution)/shard_map/attend_back_rest/pallas_call | solution.py:580
  137.0 10.7 %attend_back_first.1 = (bf16[1024,512]{1,0:T(8,128)(2,1)}, bf16[4,64,640]{2,1,0:T(8,128)(2,1)}, bf16[4,64,640]{2,1,0:T(8,128)(2,1)}) custom-call(bf16[1024,512]{1,0:T(8,128)(2,1)} %get-tuple-element.56.branch_ref, bf16[1024,512]{1,0:T(8,128)(2,1)} %get-tuple-element.52.normed_ref, bf16[640,512]{1,0:T(8,128)(2,1)} %copy-done.3, ...), custom_call_target="tpu_custom_call" | custom-call | flops 11000000512 | bytes 11000000 | tf_op jit(solution)/shard_map/attend_back_first/pallas_call | solution.py:608
  148.0 0.9 fusion.14
  148.8 1.2 collective-permute-start.27
  150.0 0.9 fusion.12
  150.9 1.5 collective-permute-start.25
  152.4 0.8 collective-permute-start.26
  153.2 5.8 %norm_back.1 = (bf16[1024,512]{1,0:T(8,128)(2,1)}, f32[32,256]{1,0:T(8,128)}) custom-call(bf16[1024,512]{1,0:T(8,128)(2,1)} %tokens_ref.3, bf16[32,256]{1,0:T(8,128)(2,1)} %bitcast.151, bf16[1024,512]{1,0:T(8,128)(2,1)} %get-tuple-element.67.backs_ref, bf16[640,512]{1,0:T(8,128)(2,1)} %copy-done.3, f32[1024,512]{1,0:T(8,128)} %get-tuple-element.78.total_ref, ...), custom_call_target="tpu_custom_call" | custom-call | flops 5000000000 | bytes 5000000 | tf_op jit(solution)/shard_map/norm_back/pallas_call | solution.py:643
  159.0 1.6 copy.41
  160.6 2.6 %all-to-all-start.1 = ((f32[32,1,256]{2,1,0:T(1,128)}), f32[32,1,256]{2,1,0:T(1,128)S(1)}, u32[]{:S(2)}, u32[]{:S(2)}) async-start(f32[32,1,256]{2,1,0:T(1,128)} %copy.41), calls=%async_computation.1 | async-start | bytes 65536 | tf_op jit(solution)/shard_map/all_to_all | solution.py:789
  163.2 1.7 fusion.20
  164.8 1.6 collective-permute-start.21
  166.5 1.5 collective-permute-start.23
  168.3 1.5 fusion.8
  169.8 0.7 slice_bitcast_fusion.10
  170.5 3.6 %collective-permute-start.28 = (bf16[64,640]{1,0:T(8,128)(2,1)}, bf16[64,640]{1,0:T(8,128)(2,1)}, u32[]{:S(2)}, u32[]{:S(2)}) collective-permute-start(bf16[64,640]{1,0:T(8,128)(2,1)} %get-tuple-element.106), channel_id=1, source_target_pairs={{0,3},{1,0},{2,1},{3,2},{4,7},{5,4},{6,5},{7,6},{8,11},{9,8},{10,9... | collective-permute-start | bytes 245768 | tf_op jit(solution)/shard_map/ppermute | solution.py:771
  174.1 2.8 %fusion.2 = (bf16[4,8,16,512]{3,2,1,0:T(8,128)(2,1)}, bf16[4,8,16,512]{3,2,1,0:T(8,128)(2,1)S(1)}, bf16[4,8,16,512]{3,2,1,0:T(8,128)(2,1)S(1)}) fusion(bf16[4,4,8,16,512]{4,3,2,1,0:T(8,128)(2,1)} %collective-permute-done.31, bf16[4,4,8,16,512]{4,3,2,1,0:T(8,128)(2,1)S(1)} %copy-done), kind=kLoop, calls=%fused_computation.8 | loop fusion | flops 3145728 | bytes 4718592 | tf_op jit(solution)/shard_map/convert_element_type | solution.py:31
  176.9 1.5 collective-permute-start.32
  178.4 1.5 collective-permute-start.34
  179.9 0.5 collective-permute-start.33
  180.6 1.0 collective-permute-start.29
  181.6 0.6 fusion.29
  182.2 0.5 slice.204
  182.7 4.3 %collective-permute-done.30 = bf16[64,640]{1,0:T(8,128)(2,1)S(1)} collective-permute-done((bf16[64,640]{1,0:T(8,128)(2,1)}, bf16[64,640]{1,0:T(8,128)(2,1)S(1)}, u32[]{:S(2)}, u32[]{:S(2)}) %collective-permute-start.30) | collective-permute-done | bytes 81952 | tf_op jit(solution)/shard_map/ppermute | solution.py:771
  187.1 1.1 fusion.19
  188.2 3.9 %collective-permute-done.32 = bf16[4,8,16,512]{3,2,1,0:T(8,128)(2,1)} collective-permute-done((bf16[4,8,16,512]{3,2,1,0:T(8,128)(2,1)}, bf16[4,8,16,512]{3,2,1,0:T(8,128)(2,1)}, u32[]{:S(2)}, u32[]{:S(2)}) %collective-permute-start.32) | collective-permute-done | bytes 524320 | tf_op jit(solution)/shard_map/ppermute | solution.py:675
  192.1 10.3 %collective-permute-done.34 = bf16[4,8,16,512]{3,2,1,0:T(8,128)(2,1)} collective-permute-done((bf16[4,8,16,512]{3,2,1,0:T(8,128)(2,1)S(1)}, bf16[4,8,16,512]{3,2,1,0:T(8,128)(2,1)}, u32[]{:S(2)}, u32[]{:S(2)}) %collective-permute-start.34) | collective-permute-done | bytes 524320 | tf_op jit(solution)/shard_map/ppermute | solution.py:675
  202.4 1.2 collective-permute-done.33
  203.5 2.0 fusion.27
  205.6 3.8 %collective-permute-start.37 = (bf16[8,16,512]{2,1,0:T(8,128)(2,1)S(1)}, bf16[8,16,512]{2,1,0:T(8,128)(2,1)S(1)}, u32[]{:S(2)}, u32[]{:S(2)}) collective-permute-start(bf16[8,16,512]{2,1,0:T(8,128)(2,1)S(1)} %get-tuple-element.100), channel_id=1, source_target_pairs={{0,3},{1,0},{2,1},{3,2},{4,7},{5,4},{6,5},{7,6},{8,11},{9,8},{10,9... | collective-permute-start | bytes 393224 | tf_op jit(solution)/shard_map/ppermute | solution.py:764
  209.5 0.7 slice_bitcast_fusion.15
  210.1 2.5 %collective-permute-done.35 = bf16[8,16,512]{2,1,0:T(8,128)(2,1)S(1)} collective-permute-done((bf16[8,16,512]{2,1,0:T(8,128)(2,1)S(1)}, bf16[8,16,512]{2,1,0:T(8,128)(2,1)S(1)}, u32[]{:S(2)}, u32[]{:S(2)}) %collective-permute-start.35) | collective-permute-done | bytes 131104 | tf_op jit(solution)/shard_map/ppermute | solution.py:764
  212.6 4.5 %collective-permute-done.36 = bf16[8,16,512]{2,1,0:T(8,128)(2,1)S(1)} collective-permute-done((bf16[8,16,512]{2,1,0:T(8,128)(2,1)S(1)}, bf16[8,16,512]{2,1,0:T(8,128)(2,1)S(1)}, u32[]{:S(2)}, u32[]{:S(2)}) %collective-permute-start.36) | collective-permute-done | bytes 131104 | tf_op jit(solution)/shard_map/ppermute | solution.py:764
  217.2 0.7 slice.242
  217.9 0.7 maximum_bitcast_fusion
  (114 shorter events, 3.1 us)
Async XLA Ops:
  0.7 8.3 %copy-start.7 = (bf16[2048,16]{0,1:T(8,128)(2,1)S(1)}, bf16[2048,16]{0,1:T(8,128)(2,1)}, u32[]{:S(2)}) copy-start(bf16[2048,16]{0,1:T(8,128)(2,1)} %param.27) | copy-start | bytes 196612
  0.7 29.9 %copy-start.12 = (bf16[16]{0:T(256)(128)(2,1)S(1)}, bf16[16]{0:T(256)(128)(2,1)}, u32[]{:S(2)}) copy-start(bf16[16]{0:T(256)(128)(2,1)} %param.28) | copy-start | bytes 100
  0.7 29.9 %copy-start.13 = (bf16[64]{0:T(256)(128)(2,1)S(1)}, bf16[64]{0:T(256)(128)(2,1)}, u32[]{:S(2)}) copy-start(bf16[64]{0:T(256)(128)(2,1)} %param.26) | copy-start | bytes 388
  0.7 29.9 %copy-start.11 = (bf16[16]{0:T(256)(128)(2,1)S(1)}, bf16[16]{0:T(256)(128)(2,1)}, u32[]{:S(2)}) copy-start(bf16[16]{0:T(256)(128)(2,1)} %param.24) | copy-start | bytes 100
  0.7 29.9 %copy-start.10 = (bf16[16]{0:T(256)(128)(2,1)S(1)}, bf16[16]{0:T(256)(128)(2,1)}, u32[]{:S(2)}) copy-start(bf16[16]{0:T(256)(128)(2,1)} %param.23) | copy-start | bytes 100
  0.7 29.9 %copy-start.9 = (bf16[16]{0:T(256)(128)(2,1)S(1)}, bf16[16]{0:T(256)(128)(2,1)}, u32[]{:S(2)}) copy-start(bf16[16]{0:T(256)(128)(2,1)} %param.17) | copy-start | bytes 100
  0.7 29.9 %copy-start.8 = (bf16[16]{0:T(256)(128)(2,1)S(1)}, bf16[16]{0:T(256)(128)(2,1)}, u32[]{:S(2)}) copy-start(bf16[16]{0:T(256)(128)(2,1)} %param.16) | copy-start | bytes 100
  2.0 43.7 %copy-start.3 = (bf16[640,512]{1,0:T(8,128)(2,1)}, bf16[640,512]{1,0:T(8,128)(2,1)S(1)}, u32[]{:S(2)}) copy-start(bf16[640,512]{1,0:T(8,128)(2,1)S(1)} %pad_maximum_fusion.weight_ref) | copy-start | bytes 1966084
  2.0 8.0 %collective-permute-start.2 = (bf16[80,512]{1,0:T(8,128)(2,1)S(1)}, bf16[80,512]{1,0:T(8,128)(2,1)S(1)}, u32[]{:S(2)}, u32[]{:S(2)}) collective-permute-start(bf16[80,512]{1,0:T(8,128)(2,1)S(1)} %constant_dynamic-slice_fusion), channel_id=1, source_target_pairs={{0,3},{1,0},{2,1},{3,2},{4,7},{5,4},{6,5},{7,6},{8,11},{9,8},{10,9... | collective-permute-start | bytes 245768 | tf_op jit(solution)/shard_map/ppermute | solution.py:730
  7.1 7.5 %collective-permute-start.1 = (bf16[80,512]{1,0:T(8,128)(2,1)S(1)}, bf16[80,512]{1,0:T(8,128)(2,1)S(1)}, u32[]{:S(2)}, u32[]{:S(2)}) collective-permute-start(bf16[80,512]{1,0:T(8,128)(2,1)S(1)} %constant_dynamic-slice_fusion), channel_id=1, source_target_pairs={{0,2},{1,3},{2,0},{3,1},{4,6},{5,7},{6,4},{7,5},{8,10},{9,11},{10,... | collective-permute-start | bytes 245768 | tf_op jit(solution)/shard_map/ppermute | solution.py:730
  7.1 7.5 %collective-permute-start = (bf16[80,512]{1,0:T(8,128)(2,1)S(1)}, bf16[80,512]{1,0:T(8,128)(2,1)S(1)}, u32[]{:S(2)}, u32[]{:S(2)}) collective-permute-start(bf16[80,512]{1,0:T(8,128)(2,1)S(1)} %constant_dynamic-slice_fusion), channel_id=1, source_target_pairs={{0,1},{1,2},{2,3},{3,0},{4,5},{5,6},{6,7},{7,4},{8,9},{9,10},{10,1... | collective-permute-start | bytes 245768 | tf_op jit(solution)/shard_map/ppermute | solution.py:730
  14.7 36.7 %copy-start.6 = (bf16[3,80,512]{2,1,0:T(8,128)(2,1)}, bf16[3,80,512]{2,1,0:T(8,128)(2,1)S(1)}, u32[]{:S(2)}) copy-start(bf16[3,80,512]{2,1,0:T(8,128)(2,1)S(1)} %pad_maximum_fusion.2.refs_0_) | copy-start | bytes 737284
  14.7 15.4 %collective-permute-start.8 = (bf16[3,80,512]{2,1,0:T(8,128)(2,1)S(1)}, bf16[3,80,512]{2,1,0:T(8,128)(2,1)S(1)}, u32[]{:S(2)}, u32[]{:S(2)}) collective-permute-start(bf16[3,80,512]{2,1,0:T(8,128)(2,1)S(1)} %pad_maximum_fusion.2.refs_0_), channel_id=1, source_target_pairs={{0,24},{4,28},{8,16},{12,20},{16,8},{20,12},{24,0},{28,4},{1,25},{... | collective-permute-start | bytes 737288 | tf_op jit(solution)/shard_map/ppermute | solution.py:667
  17.2 5.9 %collective-permute-start.12 = (bf16[8,16,512]{2,1,0:T(8,128)(2,1)S(1)}, bf16[8,16,512]{2,1,0:T(8,128)(2,1)S(1)}, u32[]{:S(2)}, u32[]{:S(2)}) collective-permute-start(bf16[8,16,512]{2,1,0:T(8,128)(2,1)S(1)} %fusion.23), channel_id=1, source_target_pairs={{0,3},{1,0},{2,1},{3,2},{4,7},{5,4},{6,5},{7,6},{8,11},{9,8},{10,9... | collective-permute-start | bytes 393224 | tf_op jit(solution)/shard_map/ppermute | solution.py:737
  19.3 10.7 %collective-permute-start.11 = (bf16[8,16,512]{2,1,0:T(8,128)(2,1)S(1)}, bf16[8,16,512]{2,1,0:T(8,128)(2,1)S(1)}, u32[]{:S(2)}, u32[]{:S(2)}) collective-permute-start(bf16[8,16,512]{2,1,0:T(8,128)(2,1)S(1)} %fusion.23), channel_id=1, source_target_pairs={{0,2},{1,3},{2,0},{3,1},{4,6},{5,7},{6,4},{7,5},{8,10},{9,11},{10,... | collective-permute-start | bytes 393224 | tf_op jit(solution)/shard_map/ppermute | solution.py:737
  19.3 22.2 %collective-permute-start.10 = (bf16[8,16,512]{2,1,0:T(8,128)(2,1)S(1)}, bf16[8,16,512]{2,1,0:T(8,128)(2,1)S(1)}, u32[]{:S(2)}, u32[]{:S(2)}) collective-permute-start(bf16[8,16,512]{2,1,0:T(8,128)(2,1)S(1)} %fusion.23), channel_id=1, source_target_pairs={{0,1},{1,2},{2,3},{3,0},{4,5},{5,6},{6,7},{7,4},{8,9},{9,10},{10,1... | collective-permute-start | bytes 393224 | tf_op jit(solution)/shard_map/ppermute | solution.py:737
  21.3 20.9 %collective-permute-start.6 = (bf16[3,80,512]{2,1,0:T(8,128)(2,1)S(1)}, bf16[3,80,512]{2,1,0:T(8,128)(2,1)S(1)}, u32[]{:S(2)}, u32[]{:S(2)}) collective-permute-start(bf16[3,80,512]{2,1,0:T(8,128)(2,1)S(1)} %pad_maximum_fusion.2.refs_0_), channel_id=1, source_target_pairs={{0,16},{4,20},{8,24},{12,28},{16,0},{20,4},{24,8},{28,12},{1,17},{... | collective-permute-start | bytes 737288 | tf_op jit(solution)/shard_map/ppermute | solution.py:667
  23.1 20.7 %collective-permute-start.4 = (bf16[3,80,512]{2,1,0:T(8,128)(2,1)S(1)}, bf16[3,80,512]{2,1,0:T(8,128)(2,1)S(1)}, u32[]{:S(2)}, u32[]{:S(2)}) collective-permute-start(bf16[3,80,512]{2,1,0:T(8,128)(2,1)S(1)} %pad_maximum_fusion.2.refs_0_), channel_id=1, source_target_pairs={{0,8},{4,12},{8,0},{12,4},{16,24},{20,28},{24,16},{28,20},{1,9},{5... | collective-permute-start | bytes 737288 | tf_op jit(solution)/shard_map/ppermute | solution.py:667
  30.1 15.1 %collective-permute-start.3 = (bf16[3,80,512]{2,1,0:T(8,128)(2,1)S(1)}, bf16[3,80,512]{2,1,0:T(8,128)(2,1)S(1)}, u32[]{:S(2)}, u32[]{:S(2)}) collective-permute-start(bf16[3,80,512]{2,1,0:T(8,128)(2,1)S(1)} %pad_maximum_fusion.2.refs_0_), channel_id=1, source_target_pairs={{0,4},{4,0},{8,12},{12,8},{16,20},{20,16},{24,28},{28,24},{1,5},{5... | collective-permute-start | bytes 737288 | tf_op jit(solution)/shard_map/ppermute | solution.py:668
  30.1 21.3 %copy-start.21 = (bf16[3,80,512]{2,1,0:T(8,128)(2,1)}, bf16[3,80,512]{2,1,0:T(8,128)(2,1)S(1)}, u32[]{:S(2)}) copy-start(bf16[3,80,512]{2,1,0:T(8,128)(2,1)S(1)} %collective-permute-done.8.refs_6_) | copy-start | bytes 737284
  30.1 15.1 %collective-permute-start.9 = (bf16[3,80,512]{2,1,0:T(8,128)(2,1)S(1)}, bf16[3,80,512]{2,1,0:T(8,128)(2,1)S(1)}, u32[]{:S(2)}, u32[]{:S(2)}) collective-permute-start(bf16[3,80,512]{2,1,0:T(8,128)(2,1)S(1)} %collective-permute-done.8.refs_6_), channel_id=1, source_target_pairs={{0,4},{4,0},{8,12},{12,8},{16,20},{20,16},{24,28},{28,24},{1,5},{5... | collective-permute-start | bytes 737288 | tf_op jit(solution)/shard_map/ppermute | solution.py:668
  41.6 9.8 %copy-start.4 = (bf16[4,8,16,512]{3,2,1,0:T(8,128)(2,1)}, bf16[4,8,16,512]{3,2,1,0:T(8,128)(2,1)S(1)}, u32[]{:S(2)}) copy-start(bf16[4,8,16,512]{3,2,1,0:T(8,128)(2,1)S(1)} %pad_maximum_fusion.1.refs_0_) | copy-start | bytes 1572868
  41.6 15.8 %collective-permute-start.18 = (bf16[4,8,16,512]{3,2,1,0:T(8,128)(2,1)S(1)}, bf16[4,8,16,512]{3,2,1,0:T(8,128)(2,1)S(1)}, u32[]{:S(2)}, u32[]{:S(2)}) collective-permute-start(bf16[4,8,16,512]{3,2,1,0:T(8,128)(2,1)S(1)} %pad_maximum_fusion.1.refs_0_), channel_id=1, source_target_pairs={{0,24},{4,28},{8,16},{12,20},{16,8},{20,12},{24,0},{28,4},{1,25},{... | collective-permute-start | bytes 1572872 | tf_op jit(solution)/shard_map/ppermute | solution.py:667
  42.3 9.2 %copy-start.22 = (bf16[3,80,512]{2,1,0:T(8,128)(2,1)}, bf16[3,80,512]{2,1,0:T(8,128)(2,1)S(1)}, u32[]{:S(2)}) copy-start(bf16[3,80,512]{2,1,0:T(8,128)(2,1)S(1)} %collective-permute-done.6.refs_4_) | copy-start | bytes 737284
  42.3 24.6 %collective-permute-start.16 = (bf16[4,8,16,512]{3,2,1,0:T(8,128)(2,1)S(1)}, bf16[4,8,16,512]{3,2,1,0:T(8,128)(2,1)S(1)}, u32[]{:S(2)}, u32[]{:S(2)}) collective-permute-start(bf16[4,8,16,512]{3,2,1,0:T(8,128)(2,1)S(1)} %pad_maximum_fusion.1.refs_0_), channel_id=1, source_target_pairs={{0,16},{4,20},{8,24},{12,28},{16,0},{20,4},{24,8},{28,12},{1,17},{... | collective-permute-start | bytes 1572872 | tf_op jit(solution)/shard_map/ppermute | solution.py:667
  43.8 7.7 %copy-start.23 = (bf16[3,80,512]{2,1,0:T(8,128)(2,1)}, bf16[3,80,512]{2,1,0:T(8,128)(2,1)S(1)}, u32[]{:S(2)}) copy-start(bf16[3,80,512]{2,1,0:T(8,128)(2,1)S(1)} %collective-permute-done.4.refs_2_) | copy-start | bytes 737284
  43.8 23.1 %collective-permute-start.14 = (bf16[4,8,16,512]{3,2,1,0:T(8,128)(2,1)S(1)}, bf16[4,8,16,512]{3,2,1,0:T(8,128)(2,1)S(1)}, u32[]{:S(2)}, u32[]{:S(2)}) collective-permute-start(bf16[4,8,16,512]{3,2,1,0:T(8,128)(2,1)S(1)} %pad_maximum_fusion.1.refs_0_), channel_id=1, source_target_pairs={{0,8},{4,12},{8,0},{12,4},{16,24},{20,28},{24,16},{28,20},{1,9},{5... | collective-permute-start | bytes 1572872 | tf_op jit(solution)/shard_map/ppermute | solution.py:667
  45.2 6.2 %copy-start.24 = (bf16[3,80,512]{2,1,0:T(8,128)(2,1)}, bf16[3,80,512]{2,1,0:T(8,128)(2,1)S(1)}, u32[]{:S(2)}) copy-start(bf16[3,80,512]{2,1,0:T(8,128)(2,1)S(1)} %collective-permute-done.3.refs_1_) | copy-start | bytes 737284
  45.2 6.2 %collective-permute-start.7 = (bf16[3,80,512]{2,1,0:T(8,128)(2,1)S(1)}, bf16[3,80,512]{2,1,0:T(8,128)(2,1)S(1)}, u32[]{:S(2)}, u32[]{:S(2)}) collective-permute-start(bf16[3,80,512]{2,1,0:T(8,128)(2,1)S(1)} %collective-permute-done.6.refs_4_), channel_id=1, source_target_pairs={{0,4},{4,0},{8,12},{12,8},{16,20},{20,16},{24,28},{28,24},{1,5},{5... | collective-permute-start | bytes 737288 | tf_op jit(solution)/shard_map/ppermute | solution.py:668
  45.2 6.2 %copy-start.25 = (bf16[3,80,512]{2,1,0:T(8,128)(2,1)}, bf16[3,80,512]{2,1,0:T(8,128)(2,1)S(1)}, u32[]{:S(2)}) copy-start(bf16[3,80,512]{2,1,0:T(8,128)(2,1)S(1)} %collective-permute-done.9.refs_7_) | copy-start | bytes 737284
  45.2 22.1 %collective-permute-start.5 = (bf16[3,80,512]{2,1,0:T(8,128)(2,1)S(1)}, bf16[3,80,512]{2,1,0:T(8,128)(2,1)S(1)}, u32[]{:S(2)}, u32[]{:S(2)}) collective-permute-start(bf16[3,80,512]{2,1,0:T(8,128)(2,1)S(1)} %collective-permute-done.4.refs_2_), channel_id=1, source_target_pairs={{0,4},{4,0},{8,12},{12,8},{16,20},{20,16},{24,28},{28,24},{1,5},{5... | collective-permute-start | bytes 737288 | tf_op jit(solution)/shard_map/ppermute | solution.py:668
  51.5 15.9 %copy-start.26 = (bf16[3,80,512]{2,1,0:T(8,128)(2,1)}, bf16[3,80,512]{2,1,0:T(8,128)(2,1)S(1)}, u32[]{:S(2)}) copy-start(bf16[3,80,512]{2,1,0:T(8,128)(2,1)S(1)} %collective-permute-done.7.refs_5_) | copy-start | bytes 737284
  51.5 28.0 %collective-permute-start.13 = (bf16[4,8,16,512]{3,2,1,0:T(8,128)(2,1)S(1)}, bf16[4,8,16,512]{3,2,1,0:T(8,128)(2,1)S(1)}, u32[]{:S(2)}, u32[]{:S(2)}) collective-permute-start(bf16[4,8,16,512]{3,2,1,0:T(8,128)(2,1)S(1)} %pad_maximum_fusion.1.refs_0_), channel_id=1, source_target_pairs={{0,4},{4,0},{8,12},{12,8},{16,20},{20,16},{24,28},{28,24},{1,5},{5... | collective-permute-start | bytes 1572872 | tf_op jit(solution)/shard_map/ppermute | solution.py:668
  57.4 22.1 %copy-start.14 = (bf16[4,8,16,512]{3,2,1,0:T(8,128)(2,1)}, bf16[4,8,16,512]{3,2,1,0:T(8,128)(2,1)S(1)}, u32[]{:S(2)}) copy-start(bf16[4,8,16,512]{3,2,1,0:T(8,128)(2,1)S(1)} %collective-permute-done.18.refs_6_) | copy-start | bytes 1572868
  57.4 22.1 %collective-permute-start.19 = (bf16[4,8,16,512]{3,2,1,0:T(8,128)(2,1)S(1)}, bf16[4,8,16,512]{3,2,1,0:T(8,128)(2,1)S(1)}, u32[]{:S(2)}, u32[]{:S(2)}) collective-permute-start(bf16[4,8,16,512]{3,2,1,0:T(8,128)(2,1)S(1)} %collective-permute-done.18.refs_6_), channel_id=1, source_target_pairs={{0,4},{4,0},{8,12},{12,8},{16,20},{20,16},{24,28},{28,24},{1,5},{5... | collective-permute-start | bytes 1572872 | tf_op jit(solution)/shard_map/ppermute | solution.py:668
  66.8 12.7 %copy-start.15 = (bf16[4,8,16,512]{3,2,1,0:T(8,128)(2,1)}, bf16[4,8,16,512]{3,2,1,0:T(8,128)(2,1)S(1)}, u32[]{:S(2)}) copy-start(bf16[4,8,16,512]{3,2,1,0:T(8,128)(2,1)S(1)} %collective-permute-done.16.refs_4_) | copy-start | bytes 1572868
  66.8 12.8 %collective-permute-start.17 = (bf16[4,8,16,512]{3,2,1,0:T(8,128)(2,1)S(1)}, bf16[4,8,16,512]{3,2,1,0:T(8,128)(2,1)S(1)}, u32[]{:S(2)}, u32[]{:S(2)}) collective-permute-start(bf16[4,8,16,512]{3,2,1,0:T(8,128)(2,1)S(1)} %collective-permute-done.16.refs_4_), channel_id=1, source_target_pairs={{0,4},{4,0},{8,12},{12,8},{16,20},{20,16},{24,28},{28,24},{1,5},{5... | collective-permute-start | bytes 1572872 | tf_op jit(solution)/shard_map/ppermute | solution.py:668
  66.8 12.7 %copy-start.16 = (bf16[4,8,16,512]{3,2,1,0:T(8,128)(2,1)}, bf16[4,8,16,512]{3,2,1,0:T(8,128)(2,1)S(1)}, u32[]{:S(2)}) copy-start(bf16[4,8,16,512]{3,2,1,0:T(8,128)(2,1)S(1)} %collective-permute-done.14.refs_2_) | copy-start | bytes 1572868
  66.8 12.8 %collective-permute-start.15 = (bf16[4,8,16,512]{3,2,1,0:T(8,128)(2,1)S(1)}, bf16[4,8,16,512]{3,2,1,0:T(8,128)(2,1)S(1)}, u32[]{:S(2)}, u32[]{:S(2)}) collective-permute-start(bf16[4,8,16,512]{3,2,1,0:T(8,128)(2,1)S(1)} %collective-permute-done.14.refs_2_), channel_id=1, source_target_pairs={{0,4},{4,0},{8,12},{12,8},{16,20},{20,16},{24,28},{28,24},{1,5},{5... | collective-permute-start | bytes 1572872 | tf_op jit(solution)/shard_map/ppermute | solution.py:668
  79.6 1.1 copy-start.19
  79.6 1.2 copy-start.20
  136.4 11.5 %collective-permute-start.24 = (bf16[4,3,64,640]{3,2,0,1:T(8,128)(2,1)}, bf16[4,3,64,640]{3,2,0,1:T(8,128)(2,1)S(1)}, u32[]{:S(2)}, u32[]{:S(2)}) collective-permute-start(bf16[4,3,64,640]{3,2,0,1:T(8,128)(2,1)} %bitcast.152), channel_id=1, source_target_pairs={{0,4},{4,0},{8,12},{12,8},{16,20},{20,16},{24,28},{28,24},{1,5},{5... | collective-permute-start | bytes 2949128 | tf_op jit(solution)/shard_map/ppermute | solution.py:673
  136.7 37.5 %collective-permute-start.31 = (bf16[4,4,8,16,512]{4,3,2,1,0:T(8,128)(2,1)}, bf16[4,4,8,16,512]{4,3,2,1,0:T(8,128)(2,1)}, u32[]{:S(2)}, u32[]{:S(2)}) collective-permute-start(bf16[4,4,8,16,512]{4,3,2,1,0:T(8,128)(2,1)} %get-tuple-element.88), channel_id=1, source_target_pairs={{0,4},{4,0},{8,12},{12,8},{16,20},{20,16},{24,28},{28,24},{1,5},{5... | collective-permute-start | bytes 6291464 | tf_op jit(solution)/shard_map/ppermute | solution.py:673
  137.0 10.9 %copy-start.2 = (bf16[3,4,64,640]{3,2,1,0:T(8,128)(2,1)S(1)}, bf16[3,4,64,640]{3,2,1,0:T(8,128)(2,1)}, u32[]{:S(2)}) copy-start(bf16[3,4,64,640]{3,2,1,0:T(8,128)(2,1)} %get-tuple-element.85) | copy-start | bytes 2949124
  147.7 15.5 %collective-permute-start.20 = (bf16[4,64,640]{2,1,0:T(8,128)(2,1)}, bf16[4,64,640]{2,1,0:T(8,128)(2,1)}, u32[]{:S(2)}, u32[]{:S(2)}) collective-permute-start(bf16[4,64,640]{2,1,0:T(8,128)(2,1)} %get-tuple-element.84), channel_id=1, source_target_pairs={{0,4},{4,0},{8,12},{12,8},{16,20},{20,16},{24,28},{28,24},{1,5},{5... | collective-permute-start | bytes 983048 | tf_op jit(solution)/shard_map/ppermute | solution.py:673
  147.9 11.1 %copy-start.1 = (bf16[4,3,64,640]{3,2,0,1:T(8,128)(2,1)}, bf16[4,3,64,640]{3,2,0,1:T(8,128)(2,1)S(1)}, u32[]{:S(2)}) copy-start(bf16[4,3,64,640]{3,2,0,1:T(8,128)(2,1)S(1)} %collective-permute-done.24) | copy-start | bytes 2949124
  148.8 17.7 %collective-permute-start.27 = (bf16[3,64,640]{2,1,0:T(8,128)(2,1)}, bf16[3,64,640]{2,1,0:T(8,128)(2,1)}, u32[]{:S(2)}, u32[]{:S(2)}) collective-permute-start(bf16[3,64,640]{2,1,0:T(8,128)(2,1)} %fusion.14), channel_id=1, source_target_pairs={{0,24},{4,28},{8,16},{12,20},{16,8},{20,12},{24,0},{28,4},{1,25},{... | collective-permute-start | bytes 737288 | tf_op jit(solution)/shard_map/ppermute | solution.py:675
  150.9 17.1 %collective-permute-start.25 = (bf16[3,64,640]{2,1,0:T(8,128)(2,1)}, bf16[3,64,640]{2,1,0:T(8,128)(2,1)}, u32[]{:S(2)}, u32[]{:S(2)}) collective-permute-start(bf16[3,64,640]{2,1,0:T(8,128)(2,1)} %get-tuple-element.94), channel_id=1, source_target_pairs={{0,8},{4,12},{8,0},{12,4},{16,24},{20,28},{24,16},{28,20},{1,9},{5... | collective-permute-start | bytes 737288 | tf_op jit(solution)/shard_map/ppermute | solution.py:675
  152.4 16.0 %collective-permute-start.26 = (bf16[3,64,640]{2,1,0:T(8,128)(2,1)}, bf16[3,64,640]{2,1,0:T(8,128)(2,1)}, u32[]{:S(2)}, u32[]{:S(2)}) collective-permute-start(bf16[3,64,640]{2,1,0:T(8,128)(2,1)} %get-tuple-element.95), channel_id=1, source_target_pairs={{0,16},{4,20},{8,24},{12,28},{16,0},{20,4},{24,8},{28,12},{1,17},{... | collective-permute-start | bytes 737288 | tf_op jit(solution)/shard_map/ppermute | solution.py:675
  153.2 10.0 %copy-start.5 = (bf16[4,64,640]{2,1,0:T(8,128)(2,1)S(1)}, bf16[4,64,640]{2,1,0:T(8,128)(2,1)}, u32[]{:S(2)}) copy-start(bf16[4,64,640]{2,1,0:T(8,128)(2,1)} %get-tuple-element.83) | copy-start | bytes 983044
  159.0 15.1 %copy-start = (bf16[4,4,8,16,512]{4,3,2,1,0:T(8,128)(2,1)S(1)}, bf16[4,4,8,16,512]{4,3,2,1,0:T(8,128)(2,1)}, u32[]{:S(2)}) copy-start(bf16[4,4,8,16,512]{4,3,2,1,0:T(8,128)(2,1)} %get-tuple-element.87) | copy-start | bytes 6291460
  160.6 19.9 %all-to-all-start.1 = ((f32[32,1,256]{2,1,0:T(1,128)}), f32[32,1,256]{2,1,0:T(1,128)S(1)}, u32[]{:S(2)}, u32[]{:S(2)}) async-start(f32[32,1,256]{2,1,0:T(1,128)} %copy.41), calls=%async_computation.1 | async-start | bytes 65536 | tf_op jit(solution)/shard_map/all_to_all | solution.py:789
  164.8 13.6 %collective-permute-start.21 = (bf16[64,640]{1,0:T(8,128)(2,1)S(1)}, bf16[64,640]{1,0:T(8,128)(2,1)}, u32[]{:S(2)}, u32[]{:S(2)}) collective-permute-start(bf16[64,640]{1,0:T(8,128)(2,1)S(1)} %get-tuple-element.96), channel_id=1, source_target_pairs={{0,8},{4,12},{8,0},{12,4},{16,24},{20,28},{24,16},{28,20},{1,9},{5... | collective-permute-start | bytes 245768 | tf_op jit(solution)/shard_map/ppermute | solution.py:675
  166.5 13.4 %collective-permute-start.23 = (bf16[64,640]{1,0:T(8,128)(2,1)S(1)}, bf16[64,640]{1,0:T(8,128)(2,1)}, u32[]{:S(2)}, u32[]{:S(2)}) collective-permute-start(bf16[64,640]{1,0:T(8,128)(2,1)S(1)} %get-tuple-element.97), channel_id=1, source_target_pairs={{0,24},{4,28},{8,16},{12,20},{16,8},{20,12},{24,0},{28,4},{1,25},{... | collective-permute-start | bytes 245768 | tf_op jit(solution)/shard_map/ppermute | solution.py:675
  168.0 12.5 %collective-permute-start.22 = (bf16[64,640]{1,0:T(8,128)(2,1)}, bf16[64,640]{1,0:T(8,128)(2,1)}, u32[]{:S(2)}, u32[]{:S(2)}) collective-permute-start(bf16[64,640]{1,0:T(8,128)(2,1)} %get-tuple-element.98), channel_id=1, source_target_pairs={{0,16},{4,20},{8,24},{12,28},{16,0},{20,4},{24,8},{28,12},{1,17},{... | collective-permute-start | bytes 245768 | tf_op jit(solution)/shard_map/ppermute | solution.py:675
  170.5 10.1 %collective-permute-start.28 = (bf16[64,640]{1,0:T(8,128)(2,1)}, bf16[64,640]{1,0:T(8,128)(2,1)}, u32[]{:S(2)}, u32[]{:S(2)}) collective-permute-start(bf16[64,640]{1,0:T(8,128)(2,1)} %get-tuple-element.106), channel_id=1, source_target_pairs={{0,3},{1,0},{2,1},{3,2},{4,7},{5,4},{6,5},{7,6},{8,11},{9,8},{10,9... | collective-permute-start | bytes 245768 | tf_op jit(solution)/shard_map/ppermute | solution.py:771
  176.9 15.2 %collective-permute-start.32 = (bf16[4,8,16,512]{3,2,1,0:T(8,128)(2,1)}, bf16[4,8,16,512]{3,2,1,0:T(8,128)(2,1)}, u32[]{:S(2)}, u32[]{:S(2)}) collective-permute-start(bf16[4,8,16,512]{3,2,1,0:T(8,128)(2,1)} %get-tuple-element.91), channel_id=1, source_target_pairs={{0,8},{4,12},{8,0},{12,4},{16,24},{20,28},{24,16},{28,20},{1,9},{5... | collective-permute-start | bytes 1572872 | tf_op jit(solution)/shard_map/ppermute | solution.py:675
  178.4 24.0 %collective-permute-start.34 = (bf16[4,8,16,512]{3,2,1,0:T(8,128)(2,1)S(1)}, bf16[4,8,16,512]{3,2,1,0:T(8,128)(2,1)}, u32[]{:S(2)}, u32[]{:S(2)}) collective-permute-start(bf16[4,8,16,512]{3,2,1,0:T(8,128)(2,1)S(1)} %get-tuple-element.92), channel_id=1, source_target_pairs={{0,24},{4,28},{8,16},{12,20},{16,8},{20,12},{24,0},{28,4},{1,25},{... | collective-permute-start | bytes 1572872 | tf_op jit(solution)/shard_map/ppermute | solution.py:675
  179.9 23.6 %collective-permute-start.33 = (bf16[4,8,16,512]{3,2,1,0:T(8,128)(2,1)S(1)}, bf16[4,8,16,512]{3,2,1,0:T(8,128)(2,1)}, u32[]{:S(2)}, u32[]{:S(2)}) collective-permute-start(bf16[4,8,16,512]{3,2,1,0:T(8,128)(2,1)S(1)} %get-tuple-element.93), channel_id=1, source_target_pairs={{0,16},{4,20},{8,24},{12,28},{16,0},{20,4},{24,8},{28,12},{1,17},{... | collective-permute-start | bytes 1572872 | tf_op jit(solution)/shard_map/ppermute | solution.py:675
  180.5 6.6 %collective-permute-start.30 = (bf16[64,640]{1,0:T(8,128)(2,1)}, bf16[64,640]{1,0:T(8,128)(2,1)S(1)}, u32[]{:S(2)}, u32[]{:S(2)}) collective-permute-start(bf16[64,640]{1,0:T(8,128)(2,1)} %get-tuple-element.107), channel_id=1, source_target_pairs={{0,1},{1,2},{2,3},{3,0},{4,5},{5,6},{6,7},{7,4},{8,9},{9,10},{10,1... | collective-permute-start | bytes 245768 | tf_op jit(solution)/shard_map/ppermute | solution.py:771
  180.6 6.5 %collective-permute-start.29 = (bf16[64,640]{1,0:T(8,128)(2,1)}, bf16[64,640]{1,0:T(8,128)(2,1)S(1)}, u32[]{:S(2)}, u32[]{:S(2)}) collective-permute-start(bf16[64,640]{1,0:T(8,128)(2,1)} %get-tuple-element.108), channel_id=1, source_target_pairs={{0,2},{1,3},{2,0},{3,1},{4,6},{5,7},{6,4},{7,5},{8,10},{9,11},{10,... | collective-permute-start | bytes 245768 | tf_op jit(solution)/shard_map/ppermute | solution.py:771
  205.6 7.1 %collective-permute-start.35 = (bf16[8,16,512]{2,1,0:T(8,128)(2,1)S(1)}, bf16[8,16,512]{2,1,0:T(8,128)(2,1)S(1)}, u32[]{:S(2)}, u32[]{:S(2)}) collective-permute-start(bf16[8,16,512]{2,1,0:T(8,128)(2,1)S(1)} %get-tuple-element.99), channel_id=1, source_target_pairs={{0,1},{1,2},{2,3},{3,0},{4,5},{5,6},{6,7},{7,4},{8,9},{9,10},{10,1... | collective-permute-start | bytes 393224 | tf_op jit(solution)/shard_map/ppermute | solution.py:764
  205.6 7.0 %collective-permute-start.37 = (bf16[8,16,512]{2,1,0:T(8,128)(2,1)S(1)}, bf16[8,16,512]{2,1,0:T(8,128)(2,1)S(1)}, u32[]{:S(2)}, u32[]{:S(2)}) collective-permute-start(bf16[8,16,512]{2,1,0:T(8,128)(2,1)S(1)} %get-tuple-element.100), channel_id=1, source_target_pairs={{0,3},{1,0},{2,1},{3,2},{4,7},{5,4},{6,5},{7,6},{8,11},{9,8},{10,9... | collective-permute-start | bytes 393224 | tf_op jit(solution)/shard_map/ppermute | solution.py:764
  209.5 7.7 %collective-permute-start.36 = (bf16[8,16,512]{2,1,0:T(8,128)(2,1)S(1)}, bf16[8,16,512]{2,1,0:T(8,128)(2,1)S(1)}, u32[]{:S(2)}, u32[]{:S(2)}) collective-permute-start(bf16[8,16,512]{2,1,0:T(8,128)(2,1)S(1)} %get-tuple-element.101), channel_id=1, source_target_pairs={{0,2},{1,3},{2,0},{3,1},{4,6},{5,7},{6,4},{7,5},{8,10},{9,11},{10,... | collective-permute-start | bytes 393224 | tf_op jit(solution)/shard_map/ppermute | solution.py:764
  (3 other events, 2.5 us)

commit v2 on v1

--- a/solution.py
+++ b/solution.py
@@ -261,74 +261,80 @@
     return out
 
 
-def fill(weight, pieces):
-    if len(pieces) == 1:
-        weight[...] = pieces[0][...]
-        return
-    mine = lax.axis_index("seq")
-    rows = pieces[0].shape[0]
+def fill(weight, own_ref, pieces, slot):
+    rows = weight.shape[0] // len(pieces)
+    stride = rows + 16 if len(pieces) > 1 else rows
+
+    @pl.when(slot == 0)
+    def _():
+        weight[...] = own_ref[...]
+
+    @pl.when(slot > 0)
+    def _():
+        first = pl.multiple_of((slot - 1) * stride, 16)
+        mine = lax.axis_index("seq") if len(pieces) > 1 else 0
+        for r, piece in enumerate(pieces):
+            weight[pl.ds(pl.multiple_of((mine ^ r) * rows, 16), rows), :] = piece[pl.ds(first, rows), :]
+
+
+def gather_vectors(pieces, rows, slots, vectors, staged):
     for r, piece in enumerate(pieces):
-        weight[pl.ds(pl.multiple_of((mine ^ r) * rows, rows), rows), :] = piece[...]
-
-
-def first_kernel(tokens_ref, vectors_ref, weight_ref, normed_ref, residual_ref, *keep):
-    tokens = tokens_ref[...].astype(F32)
-    normal, _ = norm_parts(tokens)
-    width = tokens.shape[1]
+        for a in range(slots):
+            first = a * (rows + 16) - 16 if a else (slots - 1) * (rows + 16)
+            source = place(r % 2, r // 2, slots - a, slots)
+            staged[pl.ds(source, 1), :] = piece[first : first + 16, :256].astype(F32)[0:1, :]
+    vectors[...] = low(staged[...])
+
+
+def forward_kernel(count, slots, tokens_ref, own_ref, *refs):
+    pieces, refs = refs[:count], refs[count:]
+    if count == 1:
+        given, refs = refs[0], refs[1:]
+    normed_ref, residual_ref, vectors_ref, keep = refs[0], refs[1], refs[2], refs[3:-2]
+    weight, staged = refs[-2:]
+    slot = pl.program_id(0)
+    length, width = tokens_ref.shape
     share = width // vectors_ref.shape[0]
-    small = vectors_ref[:, :128]
-    gain = spread(small, 0, share, width)
-    shift = spread(small, share, share, width)
-    normed_ref[...] = low(normal * gain + shift)
-    attend_forward(normed_ref, weight_ref[:width, :], keep)
-    residual_ref[...] = tokens + nn(keep[-1][...], weight_ref[width:, :])
-
-
-def forward_first(tokens, vectors, weight):
-    length, width = tokens.shape
-    outs = [jax.ShapeDtypeStruct((length, width), BF16), jax.ShapeDtypeStruct((length, width), F32)]
-    outs += kept_shapes(length)
-    made = pl.pallas_call(
-        first_kernel,
-        out_shape=outs,
-        in_specs=vmem(3),
-        out_specs=vmem(len(outs)),
-        compiler_params=params(),
-        cost_estimate=cost(6),
-        name="attend_first",
-    )(tokens, vectors, weight)
-    return made[0], made[1], made[2:]
-
-
-def rest_kernel(count, normed_ref, before_ref, *refs):
-    pieces, residual_ref, keep, weight = refs[:count], refs[count], refs[count + 1 : -1], refs[-1]
-    width = normed_ref.shape[1]
-    fill(weight, pieces)
-
-    @pl.when(pl.program_id(0) == 0)
+
+    @pl.when(slot == 0)
     def _():
-        residual_ref[...] = before_ref[...]
-
+        if count == 1:
+            vectors_ref[...] = given[...]
+        else:
+            gather_vectors(pieces, weight.shape[0] // count, slots, vectors_ref, staged)
+        small = vectors_ref[:, :128]
+        gain = spread(small, 0, share, width)
+        shift = spread(small, share, share, width)
+        for rows in [slice(r, r + 256) for r in range(0, length, 256)]:
+            tokens = tokens_ref[rows, :].astype(F32)
+            normal, _ = norm_parts(tokens)
+            normed_ref[rows, :] = low(normal * gain + shift)
+            residual_ref[rows, :] = tokens
+
+    fill(weight, own_ref, pieces, slot)
     attend_forward(normed_ref, weight[:width, :], keep)
     residual_ref[...] += nn(keep[-1][...], weight[width:, :])
 
 
-def forward_rest(normed, residual, pieces):
-    length, width = normed.shape
-    slots = pieces[0].shape[0]
+def forward(tokens, own, pieces, vectors, devices, slots):
+    length, width = tokens.shape
+    shape = jax.ShapeDtypeStruct
     keep = kept_shapes(length, (slots,))
+    given = [] if vectors is None else [vectors]
+    operands = [tokens, own, *pieces, *given]
+    outs = [shape((length, width), BF16), shape((length, width), F32), shape((devices, 256), BF16)]
     made = pl.pallas_call(
-        functools.partial(rest_kernel, len(pieces)),
+        functools.partial(forward_kernel, len(pieces), slots),
         grid=(slots,),
-        out_shape=[jax.ShapeDtypeStruct((length, width), F32)] + keep,
-        in_specs=[fixed((length, width))] * 2 + by_slot(pieces),
-        out_specs=[fixed((length, width))] + by_slot(keep),
-        scratch_shapes=[pltpu.VMEM((width + PAIR, 4 * PAIR), BF16)],
+        out_shape=outs + keep,
+        in_specs=[fixed(o.shape) for o in operands],
+        out_specs=[fixed(o.shape) for o in outs] + by_slot(keep),
+        scratch_shapes=[pltpu.VMEM(own.shape, BF16), pltpu.VMEM((devices, 256), F32)],
         compiler_params=params(),
-        cost_estimate=cost(17),
-        name="attend_rest",
-    )(normed, residual, *pieces)
-    return made[0], made[1:]
+        cost_estimate=cost(18),
+        name="attend_forward",
+    )(*operands)
+    return made[0], made[1], made[2], made[3:]
 
 
 GELU_A = 0.7978845608028654
@@ -495,7 +501,6 @@
     length, width = residual.shape
     step = hidden // 4
     shape = jax.ShapeDtypeStruct
-    anywhere = pl.BlockSpec(memory_space=pl.ANY)
     return pl.pallas_call(
         functools.partial(ffn_kernel, len(pieces)),
         grid=(4,),
@@ -507,8 +512,8 @@
         ]
         + [shape(s, BF16) for s in grad_shapes],
         in_specs=[fixed((length, width)), fixed(vectors.shape), fixed((length, width))]
-        + [anywhere] * len(pieces),
-        out_specs=[fixed((length, width))] * 3 + [fixed(vectors.shape)] + [anywhere] * len(grad_shapes),
+        + anywhere(pieces),
+        out_specs=[fixed((length, width))] * 3 + [fixed(vectors.shape)] + anywhere(grad_shapes),
         scratch_shapes=[
             pltpu.VMEM((hidden // 16, 16, width), BF16),
             pltpu.VMEM((4, width // 16, 16, step), BF16),
@@ -546,13 +551,13 @@
             out[chip] = made[pl.ds(start, rows), :]
 
 
-def back_rest_kernel(count, parts_out, branch_ref, normed_ref, *refs):
-    pieces, refs = refs[:count], refs[count:]
+def back_rest_kernel(count, waits, parts_out, branch_ref, normed_ref, own_ref, *refs):
+    pieces, refs = refs[:count], refs[count + waits :]
     kept, heads_ref, refs = refs[:9], refs[9], refs[10:]
     sum_ref, outs = refs[0], refs[1 : 1 + parts_out]
     weight, grad, backs, made = refs[1 + parts_out :]
     width = normed_ref.shape[1]
-    fill(weight, pieces)
+    fill(weight, own_ref, pieces, pl.program_id(0) + 1)
     pair_grads(
         branch_ref, normed_ref, None, weight[width:, :], kept, heads_ref, outs, grad, backs, made
     )
@@ -572,25 +577,39 @@
     ]
 
 
-def backward_rest(branch, normed, pieces, kept, grad_shapes):
+def later_slots(shapes, first):
+    return [
+        pl.BlockSpec((None,) + s.shape[1:], lambda a, rank=len(s.shape): (a + first,) + (0,) * (rank - 1))
+        for s in shapes
+    ]
+
+
+def anywhere(members):
+    return [pl.BlockSpec(memory_space=pl.ANY)] * len(members)
+
+
+def backward_rest(branch, normed, own, pieces, waits, kept, grad_shapes):
     length, width = branch.shape
-    slots = pieces[0].shape[0]
+    slots = kept[0].shape[0] - 1
     shape = jax.ShapeDtypeStruct
     grads = [shape((slots,) + s, BF16) for s in grad_shapes]
     return pl.pallas_call(
-        functools.partial(back_rest_kernel, len(pieces), len(grads)),
+        functools.partial(back_rest_kernel, len(pieces), len(waits), len(grads)),
         grid=(slots,),
         out_shape=[shape((length, width), F32)] + grads,
-        in_specs=[fixed((length, width))] * 2 + by_slot(pieces) + by_slot(kept),
+        in_specs=[fixed(o.shape) for o in (branch, normed, own, *pieces)]
+        + anywhere(waits)
+        + later_slots(kept, 1),
         out_specs=[fixed((length, width))] + by_slot(grads),
-        scratch_shapes=[pltpu.VMEM((width + PAIR, 4 * PAIR), BF16)] + back_scratch(length, width),
+        scratch_shapes=[pltpu.VMEM(own.shape, BF16)] + back_scratch(length, width),
         compiler_params=params(),
-        cost_estimate=cost(36),
+        cost_estimate=cost(30),
         name="attend_back_rest",
-    )(branch, normed, *pieces, *kept)
-
-
-def back_first_kernel(parts_out, branch_ref, normed_ref, weight_ref, *refs):
+    )(branch, normed, own, *pieces, *waits, *kept)
+
+
+def back_first_kernel(waits, parts_out, branch_ref, normed_ref, weight_ref, *refs):
+    refs = refs[waits:]
     kept, heads_ref, refs = refs[:9], refs[9], refs[10:]
     backs, outs = refs[0], refs[1 : 1 + parts_out]
     grad, made = refs[1 + parts_out :]
@@ -600,21 +619,24 @@
     )
 
 
-def backward_first(branch, normed, weight, kept, grad_shapes):
+def backward_first(branch, normed, weight, waits, kept):
     length, width = branch.shape
     shape = jax.ShapeDtypeStruct
-    outs = [shape((length, 4 * PAIR), BF16)] + [shape(s, BF16) for s in grad_shapes]
+    outs = [shape((length, 4 * PAIR), BF16), shape((width, 5 * PAIR), BF16)]
     scratch = back_scratch(length, width)
     return pl.pallas_call(
-        functools.partial(back_first_kernel, len(grad_shapes)),
+        functools.partial(back_first_kernel, len(waits), 1),
+        grid=(1,),
         out_shape=outs,
-        in_specs=vmem(13),
-        out_specs=vmem(len(outs)),
+        in_specs=[fixed(o.shape) for o in (branch, normed, weight)]
+        + anywhere(waits)
+        + later_slots(kept, 0),
+        out_specs=[fixed(o.shape) for o in outs],
         scratch_shapes=[scratch[0], scratch[2]],
         compiler_params=params(),
         cost_estimate=cost(11),
         name="attend_back_first",
-    )(branch, normed, weight, *kept)
+    )(branch, normed, weight, *waits, *kept)
 
 
 def last_kernel(tokens_ref, vectors_ref, backs_ref, weight_ref, total_ref, grad_ref, before_ref, out_ref, sums_ref):
@@ -669,11 +691,15 @@
     return [member for both in zip(held, mates) for member in both]
 
 
-def back_across(keep, send, chips, seqs):
+def join_cores(keep, send, chips, seqs):
     other = lax.ppermute(send, "seq", flip(seqs, 1))
     made = [add(keep[r], other[r]) for r in range(chips)]
-    came = [lax.ppermute(low(made[r]), "seq", flip(seqs, 2 * r)) for r in range(1, chips)]
-    return add(made[0], *came)
+    return made[0], [low(m) for m in made[1:]]
+
+
+def join_chips(held, sends, seqs):
+    came = [lax.ppermute(m, "seq", flip(seqs, 2 * r + 2)) for r, m in enumerate(sends)]
+    return add(held, *came)
 
 
 def body(
@@ -719,16 +745,16 @@
             jnp.zeros((128 - expand_bias.shape[0],), BF16),
         ]
     )
-    vectors = lax.all_to_all(
-        jnp.broadcast_to(row[None, :], (devices, 256)), ("seq", "head"), 0, 0, tiled=True
-    )
     expand_t = expand_weight.T
     shrink_t = shrink_weight.T
+    vectors = None
     if direct:
         rows = own.shape[0] // seqs
         piece = lax.dynamic_slice_in_dim(own, lax.axis_index("seq") * rows, rows, axis=0)
-        near = jnp.stack([lax.ppermute(piece, "head", turn(slots, a)) for a in range(1, slots)])
-        pieces = across(near, chips, seqs)
+        block = jnp.pad(row[None, :], ((0, 15), (0, width - 256)))
+        piece = jnp.concatenate([piece, block], axis=0)
+        came = [lax.ppermute(piece, "head", turn(slots, a)) for a in range(1, slots)]
+        pieces = across(jnp.concatenate(came + [block], axis=0), chips, seqs)
         load = jnp.concatenate(
             [expand_t.reshape(4, 16, width)]
             + [shrink_t[None, :, k * width : (k + 1) * width] for k in range(4)],
@@ -740,7 +766,10 @@
         ffn_shapes = [(chips, slots, 8, 16, width)] * 2
     else:
         every = lax.all_gather(own, "head", axis=0, tiled=False)
-        pieces = [jnp.stack([every[(z + slots - a) % slots] for a in range(1, slots)])]
+        pieces = [jnp.concatenate([every[(z + slots - a) % slots] for a in range(1, slots)], axis=0)]
+        vectors = lax.all_to_all(
+            jnp.broadcast_to(row[None, :], (devices, 256)), ("seq", "head"), 0, 0, tiled=True
+        )
         ffn_pieces = [
             lax.all_gather(expand_t, ("seq", "head"), axis=0, tiled=True).reshape(hidden // 16, 16, width),
             lax.all_gather(shrink_t, ("seq", "head"), axis=0, tiled=True)
@@ -750,27 +779,34 @@
         pair_shapes = [(width, 5 * PAIR)]
         ffn_shapes = [(hidden // 16, 16, width), (4, width // 16, 16, hidden // 4)]
 
-    normed, residual, kept_first = forward_first(inputs, vectors, own)
-    residual, kept_rest = forward_rest(normed, residual, pieces)
+    normed, residual, vectors, kept = forward(inputs, own, pieces, vectors, devices, slots)
     result, residual_grad, branch, sums, *ffn_grads = feed_forward(
         residual, vectors, cotangent, ffn_pieces, ffn_shapes, hidden
     )
-    total, *rest_grads = backward_rest(branch, normed, pieces, kept_rest, pair_shapes)
-    backs, *first_grads = backward_first(branch, normed, own, kept_first, pair_shapes)
+    waits, later = [], []
+    if direct:
+        ffn_held, waits = join_cores(*ffn_grads, chips, seqs)
+    total, *rest_grads = backward_rest(branch, normed, own, pieces, waits, kept, pair_shapes)
+    if direct:
+        ffn_mine = join_chips(ffn_held, waits, seqs)
+        ffn_sends = [low(ffn_mine[a]) for a in range(1, slots)]
+        rest_held, rest_sends = join_cores(*[jnp.swapaxes(g, 0, 1) for g in rest_grads], chips, seqs)
+        later = ffn_sends + rest_sends
+    backs, first_grad = backward_first(branch, normed, own, later, kept)
     input_grad, sums = finish(inputs, vectors, backs, own, total, residual_grad, sums)
 
     if direct:
-        mine = back_across(*ffn_grads, chips, seqs)
-        came = [lax.ppermute(low(mine[a]), "head", turn(slots, a)) for a in range(1, slots)]
-        ffn_sum = add(mine[0], *came)
+        first_all = lax.all_to_all(first_grad, "seq", 0, 0, tiled=True)
+        ffn_came = [lax.ppermute(m, "head", turn(slots, a + 1)) for a, m in enumerate(ffn_sends)]
+        ffn_sum = add(ffn_mine[0], *ffn_came)
         expand_grad = ffn_sum[:4].reshape(hidden_share, width)
         shrink_grad = jnp.concatenate([ffn_sum[4 + k] for k in range(4)], axis=1)
-        keep, send = [jnp.swapaxes(g, 0, 1) for g in rest_grads]
-        rest = back_across(keep, send, chips, seqs)
-        came = [
+        rest = join_chips(rest_held, rest_sends, seqs)
+        rest_came = [
             lax.ppermute(low(rest[a - 1]), "head", turn(slots, slots - a)) for a in range(1, slots)
         ]
-        pair_sum = add(back_across(*first_grads, chips, seqs), *came)
+        first_all = first_all.reshape((seqs,) + rest.shape[1:])
+        pair_sum = add(*[first_all[i] for i in range(seqs)], *rest_came)
     else:
         expand_grad = lax.psum_scatter(
             ffn_grads[0].reshape(hidden, width).astype(F32), ("seq", "head"), scatter_dimension=0, tiled=True
@@ -781,7 +817,7 @@
             scatter_dimension=0,
             tiled=True,
         )
-        every = jnp.concatenate([first_grads[0][None], rest_grads[0]], axis=0).astype(F32)
+        every = jnp.concatenate([first_grad[None], rest_grads[0]], axis=0).astype(F32)
         every = jnp.stack([every[(z + slots - p) % slots] for p in range(slots)])
         pair_sum = lax.psum_scatter(every, "head", scatter_dimension=0, tiled=False)
         pair_sum = lax.psum_scatter(pair_sum, "seq", scatter_dimension=0, tiled=True)

time: 219 us -> 216 us (0.986)
  blocking collectives: 8.87 us -> 0 us
  local copies, waits for them, and re-layouts: 8.99 us -> 15.9 us
  waiting for transfers between devices: 55.3 us -> 61.8 us
  other arithmetic: 13.7 us -> 7.93 us
    ppermute x6, waiting for transfers between devices: 15.2 us -> 26.2 us  [across(): lax.ppermute(shares, 'seq', flip(seqs, 2 * r))]
    all_to_all x1 -> x0, blocking collectives: 8.87 us -> none  [body(): lax.all_to_all(jnp.broadcast_to(row[None, :], (devices, 256)), ('seq', 'h...]
    ppermute x15 -> x11, waiting for transfers between devices: 22.4 us -> 14.7 us  [the longest x3 10.4 us: body(): lax.ppermute(m, 'head', turn(slots, a + 1))]
    all_to_all x1, waiting for transfers between devices: 0.01 us -> 5.96 us  [body(): lax.all_to_all(sums, ('seq', 'head'), 0, 0, tiled=True)]
    ppermute x3, waiting for transfers between devices: 5.63 us -> 0.52 us  [body(): lax.ppermute(piece, 'head', turn(slots, a))]
    concatenate x1, local copies, waits for them, and re-layouts: 0.1 us -> 4.1 us  [body(): jnp.concatenate([small, jnp.zeros((128 - small.shape[0],), BF16), expand_...]
    all_to_all x0 -> x1, starting transfers between devices: none -> 3.54 us  [body(): first_all = lax.all_to_all(first_grad, 'seq', 0, 0, tiled=True)]
    convert_element_type x4 -> x2, other arithmetic: 6.21 us -> 3.02 us  [low(): return v.astype(BF16)]
  transfers between devices with their start and end apart: 39 -> 36, of which waited for: 12 -> 13; matrix products, arithmetic and copies ran while one was open for 7% -> 6% of each run, Pallas kernels for 15% -> 29%
where the time goes in v2:
time: 216 us; the launch traced here: 215 us
  Pallas kernels  88.5 us (41%)
  waiting for transfers between devices  61.8 us (29%)
  starting transfers between devices  40.1 us (19%)
  local copies, waits for them, and re-layouts  15.9 us (7%)
  other arithmetic  7.93 us (4%)
    pallas_call x1, Pallas kernels, backward_rest(): pl.pallas_call(functools.partial(back_rest_kernel, len(pieces), len(waits...  30.9 us
    ppermute x6, waiting for transfers between devices, across(): lax.ppermute(shares, 'seq', flip(seqs, 2 * r))  26.2 us
    pallas_call x1, Pallas kernels, feed_forward(): pl.pallas_call(functools.partial(ffn_kernel, len(pieces)), grid=(4,), out...  26 us
    pallas_call x1, Pallas kernels, forward(): pl.pallas_call(functools.partial(forward_kernel, len(pieces), slots), gri...  15.1 us
    pallas_call x1, Pallas kernels, backward_first(): pl.pallas_call(functools.partial(back_first_kernel, len(waits), 1), grid=...  10.6 us
    ppermute x3, waiting for transfers between devices, body(): lax.ppermute(m, 'head', turn(slots, a + 1))  10.4 us
    ppermute x6, starting transfers between devices, across(): lax.ppermute(shares, 'seq', flip(seqs, 2 * r))  8.13 us
    ppermute x3, waiting for transfers between devices, body(): lax.ppermute(load, 'head', turn(slots, a))  7.73 us
  transfers between devices with their start and end apart: 36, of which 13 were waited for; matrix products, arithmetic and copies ran while one was open for 6% of the time, Pallas kernels for 29%

profile of v2, /device:TPU:0, one launch (start us, length us, event | category | flops | bytes accessed | tf_op | source)
XLA Modules:
  0.0 215.3 jit_solution(2346251888331390893)
XLA Ops:
  0.7 4.1 %concatenate.23 = bf16[256]{0:T(256)(128)(2,1)S(1)} concatenate(bf16[16]{0:T(256)(128)(2,1)} %param.16, bf16[16]{0:T(256)(128)(2,1)} %param.17, bf16[16]{0:T(256)(128)(2,1)} %param.23, bf16[16]{0:T(256)(128)(2,1)} %param.24, bf16[16]{0:T(256)(128)(2,1)} %param.28, bf16[48]{0:T(256)(128)(2,1)S(1)} %broadcast_in_dim.21, bf16[64]{0:T(256)(128)(2,1)} %param.26, ...), dimensions={0} | concatenate | bytes 1024 | tf_op jit(solution)/shard_map/concatenate | solution.py:740
  4.8 1.2 pad_maximum_fusion.own_ref.weight_ref
  6.1 5.1 %collective-permute-start.2 = (bf16[96,512]{1,0:T(8,128)(2,1)S(1)}, bf16[96,512]{1,0:T(8,128)(2,1)S(1)}, u32[]{:S(2)}, u32[]{:S(2)}) collective-permute-start(bf16[96,512]{1,0:T(8,128)(2,1)S(1)} %pad_maximum_fusion.3), channel_id=1, source_target_pairs={{0,3},{1,0},{2,1},{3,2},{4,7},{5,4},{6,5},{7,6},{8,11},{9,8},{10,9... | collective-permute-start | bytes 294920 | tf_op jit(solution)/shard_map/ppermute | solution.py:756
  11.2 1.0 collective-permute-start
  12.2 0.8 constant_dynamic-update-slice_fusion
  13.0 0.7 fusion.19
  13.8 0.7 fusion.18
  14.5 0.7 fusion.17
  15.2 0.7 fusion.16
  15.9 2.8 %collective-permute-start.12 = (bf16[8,16,512]{2,1,0:T(8,128)(2,1)S(1)}, bf16[8,16,512]{2,1,0:T(8,128)(2,1)S(1)}, u32[]{:S(2)}, u32[]{:S(2)}) collective-permute-start(bf16[8,16,512]{2,1,0:T(8,128)(2,1)S(1)} %fusion.16), channel_id=1, source_target_pairs={{0,3},{1,0},{2,1},{3,2},{4,7},{5,4},{6,5},{7,6},{8,11},{9,8},{10,9... | collective-permute-start | bytes 393224 | tf_op jit(solution)/shard_map/ppermute | solution.py:763
  18.7 1.1 collective-permute-start.11
  19.9 0.5 collective-permute-done.1
  20.4 2.5 %collective-permute-start.8 = (bf16[304,512]{1,0:T(8,128)(2,1)S(1)}, bf16[304,512]{1,0:T(8,128)(2,1)S(1)}, u32[]{:S(2)}, u32[]{:S(2)}) collective-permute-start(bf16[304,512]{1,0:T(8,128)(2,1)S(1)} %pad_maximum_fusion.2.refs_0_), channel_id=1, source_target_pairs={{0,24},{4,28},{8,16},{12,20},{16,8},{20,12},{24,0},{28,4},{1,25},{... | collective-permute-start | bytes 933896 | tf_op jit(solution)/shard_map/ppermute | solution.py:689
  22.9 0.5 collective-permute-start.6
  23.4 7.7 %collective-permute-done.11 = bf16[8,16,512]{2,1,0:T(8,128)(2,1)S(1)} collective-permute-done((bf16[8,16,512]{2,1,0:T(8,128)(2,1)S(1)}, bf16[8,16,512]{2,1,0:T(8,128)(2,1)S(1)}, u32[]{:S(2)}, u32[]{:S(2)}) %collective-permute-start.11) | collective-permute-done | bytes 131104 | tf_op jit(solution)/shard_map/ppermute | solution.py:763
  31.2 2.5 %collective-permute-start.18 = (bf16[4,8,16,512]{3,2,1,0:T(8,128)(2,1)S(1)}, bf16[4,8,16,512]{3,2,1,0:T(8,128)(2,1)S(1)}, u32[]{:S(2)}, u32[]{:S(2)}) collective-permute-start(bf16[4,8,16,512]{3,2,1,0:T(8,128)(2,1)S(1)} %pad_maximum_fusion.1.refs_0_), channel_id=1, source_target_pairs={{0,24},{4,28},{8,16},{12,20},{16,8},{20,12},{24,0},{28,4},{1,25},{... | collective-permute-start | bytes 1572872 | tf_op jit(solution)/shard_map/ppermute | solution.py:689
  33.8 0.5 collective-permute-start.4
  34.3 0.6 collective-permute-start.16
  34.9 12.8 %collective-permute-done.6.refs_4_ = bf16[304,512]{1,0:T(8,128)(2,1)S(1)} collective-permute-done((bf16[304,512]{1,0:T(8,128)(2,1)S(1)}, bf16[304,512]{1,0:T(8,128)(2,1)S(1)}, u32[]{:S(2)}, u32[]{:S(2)}) %collective-permute-start.6) | collective-permute-done | bytes 311328 | tf_op jit(solution)/shard_map/ppermute | solution.py:689
  47.7 1.5 collective-permute-start.14
  49.2 4.5 %collective-permute-done.4.refs_2_ = bf16[304,512]{1,0:T(8,128)(2,1)S(1)} collective-permute-done((bf16[304,512]{1,0:T(8,128)(2,1)S(1)}, bf16[304,512]{1,0:T(8,128)(2,1)S(1)}, u32[]{:S(2)}, u32[]{:S(2)}) %collective-permute-start.4) | collective-permute-done | bytes 311328 | tf_op jit(solution)/shard_map/ppermute | solution.py:689
  53.7 0.5 collective-permute-start.7
  54.3 4.6 %collective-permute-done.16.refs_4_ = bf16[4,8,16,512]{3,2,1,0:T(8,128)(2,1)S(1)} collective-permute-done((bf16[4,8,16,512]{3,2,1,0:T(8,128)(2,1)S(1)}, bf16[4,8,16,512]{3,2,1,0:T(8,128)(2,1)S(1)}, u32[]{:S(2)}, u32[]{:S(2)}) %collective-permute-start.16) | collective-permute-done | bytes 524320 | tf_op jit(solution)/shard_map/ppermute | solution.py:689
  58.9 4.4 %collective-permute-done.14.refs_2_ = bf16[4,8,16,512]{3,2,1,0:T(8,128)(2,1)S(1)} collective-permute-done((bf16[4,8,16,512]{3,2,1,0:T(8,128)(2,1)S(1)}, bf16[4,8,16,512]{3,2,1,0:T(8,128)(2,1)S(1)}, u32[]{:S(2)}, u32[]{:S(2)}) %collective-permute-start.14) | collective-permute-done | bytes 524320 | tf_op jit(solution)/shard_map/ppermute | solution.py:689
  63.3 0.5 collective-permute-start.17
  64.0 0.5 copy-done.23
  64.5 0.7 copy-done.24
  65.2 15.1 %attend_forward.1 = (bf16[1024,512]{1,0:T(8,128)(2,1)}, f32[1024,512]{1,0:T(8,128)}, bf16[32,256]{1,0:T(8,128)(2,1)}, bf16[4,1024,128]{2,1,0:T(8,128)(2,1)}, bf1...) custom-call(bf16[1024,512]{1,0:T(8,128)(2,1)} %tokens_ref.3, ...), custom_call_target="tpu_custom_call" | custom-call | flops 17999998976 | bytes 18000000 | tf_op jit(solution)/shard_map/attend_forward/pallas_call | solution.py:326
  80.5 0.7 copy-done.14
  81.8 26.0 %feed_forward.1 = (bf16[1024,512]{1,0:T(8,128)(2,1)}, f32[1024,512]{1,0:T(8,128)}, bf16[1024,512]{1,0:T(8,128)(2,1)}, f32[32,256]{1,0:T(8,128)}, bf16[4,4,8,16,5...) custom-call(f32[1024,512]{1,0:T(8,128)} %get-tuple-element.41.residual_ref, ...), custom_call_target="tpu_custom_call" | custom-call | flops 27000000512 | bytes 27000000 | tf_op jit(solution)/shard_map/feed_forward/pallas_call | solution.py:504
  108.1 4.2 %collective-permute-done.20 = bf16[4,4,8,16,512]{4,3,2,1,0:T(8,128)(2,1)S(1)} collective-permute-done((bf16[4,4,8,16,512]{4,3,2,1,0:T(8,128)(2,1)}, bf16[4,4,8,16,512]{4,3,2,1,0:T(8,128)(2,1)S(1)}, u32[]{:S(2)}, u32[]{:S(2)}) %collective-permute-start.20) | collective-permute-done | bytes 2097184 | tf_op jit(solution)/shard_map/ppermute | solution.py:695
  112.3 2.0 fusion.2
  114.4 1.6 collective-permute-start.21
  116.4 1.5 collective-permute-start.22
  118.0 30.9 %attend_back_rest.1 = (f32[1024,512]{1,0:T(8,128)}, bf16[3,4,64,640]{3,2,1,0:T(8,128)(2,1)}, bf16[3,4,64,640]{3,2,1,0:T(8,128)(2,1)}) custom-call(bf16[1024,512]{1,0:T(8,128)(2,1)} %get-tuple-element.44.branch_ref, bf16[1024,512]{1,0:T(8,128)(2,1)} %get-tuple-element.45.normed_ref, bf16[640,512]{1,0:T(8,128)(2,1)} %copy-done.1, bf16[304,512]{1,0:T(8,128)(2,1)} %copy-done.6, ...), custom_call_target="tpu_custom_call" | custom-call | flops 30000001024 | bytes 30000000 | tf_op jit(solution)/shard_map/attend_back_rest/pallas_call | solution.py:596
  148.8 1.3 copy.37
  150.2 1.6 fusion.20
  151.9 0.7 collective-permute-start.33
  152.6 2.1 collective-permute-start.32
  154.6 1.9 collective-permute-start.31
  156.7 1.1 collective-permute-done.33
  157.8 9.3 %collective-permute-done.32 = bf16[8,16,512]{2,1,0:T(8,128)(2,1)S(1)} collective-permute-done((bf16[8,16,512]{2,1,0:T(8,128)(2,1)S(1)}, bf16[8,16,512]{2,1,0:T(8,128)(2,1)S(1)}, u32[]{:S(2)}, u32[]{:S(2)}) %collective-permute-start.32) | collective-permute-done | bytes 131104 | tf_op jit(solution)/shard_map/ppermute | solution.py:800
  167.2 1.0 fusion.13
  168.2 1.5 collective-permute-start.27
  169.7 1.5 collective-permute-start.26
  171.2 10.6 %attend_back_first.1 = (bf16[1024,512]{1,0:T(8,128)(2,1)}, bf16[512,640]{1,0:T(8,128)(2,1)}) custom-call(bf16[1024,512]{1,0:T(8,128)(2,1)} %get-tuple-element.44.branch_ref, bf16[1024,512]{1,0:T(8,128)(2,1)} %get-tuple-element.45.normed_ref, bf16[640,512]{1,0:T(8,128)(2,1)} %copy-done.1, bf16[8,16,512]{2,1,0:T(8,128)(2,1)} %copy-done.10, ...), custom_call_target="tpu_custom_call" | custom-call | flops 11000000512 | bytes 11000000 | tf_op jit(solution)/shard_map/attend_back_first/pallas_call | solution.py:627
  181.8 0.5 collective-permute-start.25
  182.3 5.8 %norm_back.1 = (bf16[1024,512]{1,0:T(8,128)(2,1)}, f32[32,256]{1,0:T(8,128)}) custom-call(bf16[1024,512]{1,0:T(8,128)(2,1)} %tokens_ref.3, bf16[32,256]{1,0:T(8,128)(2,1)} %get-tuple-element.42.vectors_ref, bf16[1024,512]{1,0:T(8,128)(2,1)} %get-tuple-element.60.backs_ref, bf16[640,512]{1,0:T(8,128)(2,1)} %copy-done.1, ...), custom_call_target="tpu_custom_call" | custom-call | flops 5000000000 | bytes 5000000 | tf_op jit(solution)/shard_map/norm_back/pallas_call | solution.py:665
  188.1 1.4 copy.34
  189.5 2.6 %all-to-all-start = ((f32[32,1,256]{2,1,0:T(1,128)}), f32[32,1,256]{2,1,0:T(1,128)S(1)}, u32[]{:S(2)}, u32[]{:S(2)}) async-start(f32[32,1,256]{2,1,0:T(1,128)} %copy.34), calls=%async_computation | async-start | bytes 65536 | tf_op jit(solution)/shard_map/all_to_all | solution.py:825
  192.1 0.7 maximum_bitcast_fusion
  192.8 0.7 slice.262
  193.4 6.0 %all-to-all-done = f32[32,1,256]{2,1,0:T(1,128)S(1)} async-done(((f32[32,1,256]{2,1,0:T(1,128)}), f32[32,1,256]{2,1,0:T(1,128)S(1)}, u32[]{:S(2)}, u32[]{:S(2)}) %all-to-all-start) | async-done | bytes 32800 | tf_op jit(solution)/shard_map/all_to_all | solution.py:825
  199.4 3.5 %all-to-all-start.1 = ((bf16[8,64,640]{2,1,0:T(8,128)(2,1)}), bf16[8,64,640]{2,1,0:T(8,128)(2,1)S(1)}, u32[]{:S(2)}, u32[]{:S(2)}) async-start(bf16[8,64,640]{2,1,0:T(8,128)(2,1)} %bitcast.24), calls=%async_computation.1 | async-start | bytes 1310720 | tf_op jit(solution)/shard_map/all_to_all | solution.py:799
  203.0 1.1 fusion.7
  204.2 0.5 collective-permute-start.28
  204.7 1.5 collective-permute-start.30
  206.3 0.5 collective-permute-start.29
  206.8 0.6 fusion.22
  207.4 0.5 slice.220
  207.9 1.1 collective-permute-done.28
  209.0 2.9 %collective-permute-done.30 = bf16[64,640]{1,0:T(8,128)(2,1)S(1)} collective-permute-done((bf16[64,640]{1,0:T(8,128)(2,1)S(1)}, bf16[64,640]{1,0:T(8,128)(2,1)S(1)}, u32[]{:S(2)}, u32[]{:S(2)}) %collective-permute-start.30) | collective-permute-done | bytes 81952 | tf_op jit(solution)/shard_map/ppermute | solution.py:806
  211.9 2.6 %collective-permute-done.29 = bf16[64,640]{1,0:T(8,128)(2,1)S(1)} collective-permute-done((bf16[64,640]{1,0:T(8,128)(2,1)S(1)}, bf16[64,640]{1,0:T(8,128)(2,1)S(1)}, u32[]{:S(2)}, u32[]{:S(2)}) %collective-permute-start.29) | collective-permute-done | bytes 81952 | tf_op jit(solution)/shard_map/ppermute | solution.py:806
  214.6 0.7 slice_bitcast_fusion.11
  (96 shorter events, 2.3 us)
Async XLA Ops:
  6.0 57.8 %copy-start.1 = (bf16[640,512]{1,0:T(8,128)(2,1)}, bf16[640,512]{1,0:T(8,128)(2,1)S(1)}, u32[]{:S(2)}) copy-start(bf16[640,512]{1,0:T(8,128)(2,1)S(1)} %pad_maximum_fusion.own_ref.weight_ref) | copy-start | bytes 1966084
  6.1 13.8 %collective-permute-start.2 = (bf16[96,512]{1,0:T(8,128)(2,1)S(1)}, bf16[96,512]{1,0:T(8,128)(2,1)S(1)}, u32[]{:S(2)}, u32[]{:S(2)}) collective-permute-start(bf16[96,512]{1,0:T(8,128)(2,1)S(1)} %pad_maximum_fusion.3), channel_id=1, source_target_pairs={{0,3},{1,0},{2,1},{3,2},{4,7},{5,4},{6,5},{7,6},{8,11},{9,8},{10,9... | collective-permute-start | bytes 294920 | tf_op jit(solution)/shard_map/ppermute | solution.py:756
  11.2 9.2 %collective-permute-start.1 = (bf16[96,512]{1,0:T(8,128)(2,1)S(1)}, bf16[96,512]{1,0:T(8,128)(2,1)S(1)}, u32[]{:S(2)}, u32[]{:S(2)}) collective-permute-start(bf16[96,512]{1,0:T(8,128)(2,1)S(1)} %pad_maximum_fusion.3), channel_id=1, source_target_pairs={{0,2},{1,3},{2,0},{3,1},{4,6},{5,7},{6,4},{7,5},{8,10},{9,11},{10,... | collective-permute-start | bytes 294920 | tf_op jit(solution)/shard_map/ppermute | solution.py:756
  11.2 9.2 %collective-permute-start = (bf16[96,512]{1,0:T(8,128)(2,1)S(1)}, bf16[96,512]{1,0:T(8,128)(2,1)S(1)}, u32[]{:S(2)}, u32[]{:S(2)}) collective-permute-start(bf16[96,512]{1,0:T(8,128)(2,1)S(1)} %pad_maximum_fusion.3), channel_id=1, source_target_pairs={{0,1},{1,2},{2,3},{3,0},{4,5},{5,6},{6,7},{7,4},{8,9},{9,10},{10,1... | collective-permute-start | bytes 294920 | tf_op jit(solution)/shard_map/ppermute | solution.py:756
  15.9 7.5 %collective-permute-start.12 = (bf16[8,16,512]{2,1,0:T(8,128)(2,1)S(1)}, bf16[8,16,512]{2,1,0:T(8,128)(2,1)S(1)}, u32[]{:S(2)}, u32[]{:S(2)}) collective-permute-start(bf16[8,16,512]{2,1,0:T(8,128)(2,1)S(1)} %fusion.16), channel_id=1, source_target_pairs={{0,3},{1,0},{2,1},{3,2},{4,7},{5,4},{6,5},{7,6},{8,11},{9,8},{10,9... | collective-permute-start | bytes 393224 | tf_op jit(solution)/shard_map/ppermute | solution.py:763
  18.7 12.4 %collective-permute-start.11 = (bf16[8,16,512]{2,1,0:T(8,128)(2,1)S(1)}, bf16[8,16,512]{2,1,0:T(8,128)(2,1)S(1)}, u32[]{:S(2)}, u32[]{:S(2)}) collective-permute-start(bf16[8,16,512]{2,1,0:T(8,128)(2,1)S(1)} %fusion.16), channel_id=1, source_target_pairs={{0,2},{1,3},{2,0},{3,1},{4,6},{5,7},{6,4},{7,5},{8,10},{9,11},{10,... | collective-permute-start | bytes 393224 | tf_op jit(solution)/shard_map/ppermute | solution.py:763
  19.8 11.3 %collective-permute-start.10 = (bf16[8,16,512]{2,1,0:T(8,128)(2,1)S(1)}, bf16[8,16,512]{2,1,0:T(8,128)(2,1)S(1)}, u32[]{:S(2)}, u32[]{:S(2)}) collective-permute-start(bf16[8,16,512]{2,1,0:T(8,128)(2,1)S(1)} %fusion.16), channel_id=1, source_target_pairs={{0,1},{1,2},{2,3},{3,0},{4,5},{5,6},{6,7},{7,4},{8,9},{9,10},{10,1... | collective-permute-start | bytes 393224 | tf_op jit(solution)/shard_map/ppermute | solution.py:763
  20.4 43.5 %copy-start.6 = (bf16[304,512]{1,0:T(8,128)(2,1)}, bf16[304,512]{1,0:T(8,128)(2,1)S(1)}, u32[]{:S(2)}) copy-start(bf16[304,512]{1,0:T(8,128)(2,1)S(1)} %pad_maximum_fusion.2.refs_0_) | copy-start | bytes 933892
  20.4 13.9 %collective-permute-start.8 = (bf16[304,512]{1,0:T(8,128)(2,1)S(1)}, bf16[304,512]{1,0:T(8,128)(2,1)S(1)}, u32[]{:S(2)}, u32[]{:S(2)}) collective-permute-start(bf16[304,512]{1,0:T(8,128)(2,1)S(1)} %pad_maximum_fusion.2.refs_0_), channel_id=1, source_target_pairs={{0,24},{4,28},{8,16},{12,20},{16,8},{20,12},{24,0},{28,4},{1,25},{... | collective-permute-start | bytes 933896 | tf_op jit(solution)/shard_map/ppermute | solution.py:689
  22.9 24.8 %collective-permute-start.6 = (bf16[304,512]{1,0:T(8,128)(2,1)S(1)}, bf16[304,512]{1,0:T(8,128)(2,1)S(1)}, u32[]{:S(2)}, u32[]{:S(2)}) collective-permute-start(bf16[304,512]{1,0:T(8,128)(2,1)S(1)} %pad_maximum_fusion.2.refs_0_), channel_id=1, source_target_pairs={{0,16},{4,20},{8,24},{12,28},{16,0},{20,4},{24,8},{28,12},{1,17},{... | collective-permute-start | bytes 933896 | tf_op jit(solution)/shard_map/ppermute | solution.py:689
  31.2 49.1 %copy-start.5 = (bf16[4,8,16,512]{3,2,1,0:T(8,128)(2,1)}, bf16[4,8,16,512]{3,2,1,0:T(8,128)(2,1)S(1)}, u32[]{:S(2)}) copy-start(bf16[4,8,16,512]{3,2,1,0:T(8,128)(2,1)S(1)} %pad_maximum_fusion.1.refs_0_) | copy-start | bytes 1572868
  31.2 23.0 %collective-permute-start.18 = (bf16[4,8,16,512]{3,2,1,0:T(8,128)(2,1)S(1)}, bf16[4,8,16,512]{3,2,1,0:T(8,128)(2,1)S(1)}, u32[]{:S(2)}, u32[]{:S(2)}) collective-permute-start(bf16[4,8,16,512]{3,2,1,0:T(8,128)(2,1)S(1)} %pad_maximum_fusion.1.refs_0_), channel_id=1, source_target_pairs={{0,24},{4,28},{8,16},{12,20},{16,8},{20,12},{24,0},{28,4},{1,25},{... | collective-permute-start | bytes 1572872 | tf_op jit(solution)/shard_map/ppermute | solution.py:689
  33.8 19.9 %collective-permute-start.4 = (bf16[304,512]{1,0:T(8,128)(2,1)S(1)}, bf16[304,512]{1,0:T(8,128)(2,1)S(1)}, u32[]{:S(2)}, u32[]{:S(2)}) collective-permute-start(bf16[304,512]{1,0:T(8,128)(2,1)S(1)} %pad_maximum_fusion.2.refs_0_), channel_id=1, source_target_pairs={{0,8},{4,12},{8,0},{12,4},{16,24},{20,28},{24,16},{28,20},{1,9},{5... | collective-permute-start | bytes 933896 | tf_op jit(solution)/shard_map/ppermute | solution.py:689
  34.3 19.4 %collective-permute-start.3 = (bf16[304,512]{1,0:T(8,128)(2,1)S(1)}, bf16[304,512]{1,0:T(8,128)(2,1)S(1)}, u32[]{:S(2)}, u32[]{:S(2)}) collective-permute-start(bf16[304,512]{1,0:T(8,128)(2,1)S(1)} %pad_maximum_fusion.2.refs_0_), channel_id=1, source_target_pairs={{0,4},{4,0},{8,12},{12,8},{16,20},{20,16},{24,28},{28,24},{1,5},{5... | collective-permute-start | bytes 933896 | tf_op jit(solution)/shard_map/ppermute | solution.py:690
  34.3 29.6 %copy-start.18 = (bf16[304,512]{1,0:T(8,128)(2,1)}, bf16[304,512]{1,0:T(8,128)(2,1)S(1)}, u32[]{:S(2)}) copy-start(bf16[304,512]{1,0:T(8,128)(2,1)S(1)} %collective-permute-done.8.refs_6_) | copy-start | bytes 933892
  34.3 24.6 %collective-permute-start.16 = (bf16[4,8,16,512]{3,2,1,0:T(8,128)(2,1)S(1)}, bf16[4,8,16,512]{3,2,1,0:T(8,128)(2,1)S(1)}, u32[]{:S(2)}, u32[]{:S(2)}) collective-permute-start(bf16[4,8,16,512]{3,2,1,0:T(8,128)(2,1)S(1)} %pad_maximum_fusion.1.refs_0_), channel_id=1, source_target_pairs={{0,16},{4,20},{8,24},{12,28},{16,0},{20,4},{24,8},{28,12},{1,17},{... | collective-permute-start | bytes 1572872 | tf_op jit(solution)/shard_map/ppermute | solution.py:689
  47.7 16.1 %copy-start.19 = (bf16[304,512]{1,0:T(8,128)(2,1)}, bf16[304,512]{1,0:T(8,128)(2,1)S(1)}, u32[]{:S(2)}) copy-start(bf16[304,512]{1,0:T(8,128)(2,1)S(1)} %collective-permute-done.6.refs_4_) | copy-start | bytes 933892
  47.7 15.5 %collective-permute-start.14 = (bf16[4,8,16,512]{3,2,1,0:T(8,128)(2,1)S(1)}, bf16[4,8,16,512]{3,2,1,0:T(8,128)(2,1)S(1)}, u32[]{:S(2)}, u32[]{:S(2)}) collective-permute-start(bf16[4,8,16,512]{3,2,1,0:T(8,128)(2,1)S(1)} %pad_maximum_fusion.1.refs_0_), channel_id=1, source_target_pairs={{0,8},{4,12},{8,0},{12,4},{16,24},{20,28},{24,16},{28,20},{1,9},{5... | collective-permute-start | bytes 1572872 | tf_op jit(solution)/shard_map/ppermute | solution.py:689
  53.7 10.2 %copy-start.20 = (bf16[304,512]{1,0:T(8,128)(2,1)}, bf16[304,512]{1,0:T(8,128)(2,1)S(1)}, u32[]{:S(2)}) copy-start(bf16[304,512]{1,0:T(8,128)(2,1)S(1)} %collective-permute-done.4.refs_2_) | copy-start | bytes 933892
  53.7 9.5 %collective-permute-start.9 = (bf16[304,512]{1,0:T(8,128)(2,1)S(1)}, bf16[304,512]{1,0:T(8,128)(2,1)S(1)}, u32[]{:S(2)}, u32[]{:S(2)}) collective-permute-start(bf16[304,512]{1,0:T(8,128)(2,1)S(1)} %collective-permute-done.8.refs_6_), channel_id=1, source_target_pairs={{0,4},{4,0},{8,12},{12,8},{16,20},{20,16},{24,28},{28,24},{1,5},{5... | collective-permute-start | bytes 933896 | tf_op jit(solution)/shard_map/ppermute | solution.py:690
  53.7 10.2 %copy-start.21 = (bf16[304,512]{1,0:T(8,128)(2,1)}, bf16[304,512]{1,0:T(8,128)(2,1)S(1)}, u32[]{:S(2)}) copy-start(bf16[304,512]{1,0:T(8,128)(2,1)S(1)} %collective-permute-done.3.refs_1_) | copy-start | bytes 933892
  53.7 10.0 %collective-permute-start.7 = (bf16[304,512]{1,0:T(8,128)(2,1)S(1)}, bf16[304,512]{1,0:T(8,128)(2,1)S(1)}, u32[]{:S(2)}, u32[]{:S(2)}) collective-permute-start(bf16[304,512]{1,0:T(8,128)(2,1)S(1)} %collective-permute-done.6.refs_4_), channel_id=1, source_target_pairs={{0,4},{4,0},{8,12},{12,8},{16,20},{20,16},{24,28},{28,24},{1,5},{5... | collective-permute-start | bytes 933896 | tf_op jit(solution)/shard_map/ppermute | solution.py:690
  54.2 26.2 %copy-start.11 = (bf16[4,8,16,512]{3,2,1,0:T(8,128)(2,1)}, bf16[4,8,16,512]{3,2,1,0:T(8,128)(2,1)S(1)}, u32[]{:S(2)}) copy-start(bf16[4,8,16,512]{3,2,1,0:T(8,128)(2,1)S(1)} %collective-permute-done.18.refs_6_) | copy-start | bytes 1572868
  54.2 9.6 %collective-permute-start.5 = (bf16[304,512]{1,0:T(8,128)(2,1)S(1)}, bf16[304,512]{1,0:T(8,128)(2,1)S(1)}, u32[]{:S(2)}, u32[]{:S(2)}) collective-permute-start(bf16[304,512]{1,0:T(8,128)(2,1)S(1)} %collective-permute-done.4.refs_2_), channel_id=1, source_target_pairs={{0,4},{4,0},{8,12},{12,8},{16,20},{20,16},{24,28},{28,24},{1,5},{5... | collective-permute-start | bytes 933896 | tf_op jit(solution)/shard_map/ppermute | solution.py:690
  58.9 21.5 %copy-start.12 = (bf16[4,8,16,512]{3,2,1,0:T(8,128)(2,1)}, bf16[4,8,16,512]{3,2,1,0:T(8,128)(2,1)S(1)}, u32[]{:S(2)}) copy-start(bf16[4,8,16,512]{3,2,1,0:T(8,128)(2,1)S(1)} %collective-permute-done.16.refs_4_) | copy-start | bytes 1572868
  58.9 21.5 %collective-permute-start.13 = (bf16[4,8,16,512]{3,2,1,0:T(8,128)(2,1)S(1)}, bf16[4,8,16,512]{3,2,1,0:T(8,128)(2,1)S(1)}, u32[]{:S(2)}, u32[]{:S(2)}) collective-permute-start(bf16[4,8,16,512]{3,2,1,0:T(8,128)(2,1)S(1)} %pad_maximum_fusion.1.refs_0_), channel_id=1, source_target_pairs={{0,4},{4,0},{8,12},{12,8},{16,20},{20,16},{24,28},{28,24},{1,5},{5... | collective-permute-start | bytes 1572872 | tf_op jit(solution)/shard_map/ppermute | solution.py:690
  63.2 17.2 %copy-start.13 = (bf16[4,8,16,512]{3,2,1,0:T(8,128)(2,1)}, bf16[4,8,16,512]{3,2,1,0:T(8,128)(2,1)S(1)}, u32[]{:S(2)}) copy-start(bf16[4,8,16,512]{3,2,1,0:T(8,128)(2,1)S(1)} %collective-permute-done.14.refs_2_) | copy-start | bytes 1572868
  63.2 17.2 %collective-permute-start.19 = (bf16[4,8,16,512]{3,2,1,0:T(8,128)(2,1)S(1)}, bf16[4,8,16,512]{3,2,1,0:T(8,128)(2,1)S(1)}, u32[]{:S(2)}, u32[]{:S(2)}) collective-permute-start(bf16[4,8,16,512]{3,2,1,0:T(8,128)(2,1)S(1)} %collective-permute-done.18.refs_6_), channel_id=1, source_target_pairs={{0,4},{4,0},{8,12},{12,8},{16,20},{20,16},{24,28},{28,24},{1,5},{5... | collective-permute-start | bytes 1572872 | tf_op jit(solution)/shard_map/ppermute | solution.py:690
  63.2 0.8 copy-start.22
  63.3 17.2 %collective-permute-start.17 = (bf16[4,8,16,512]{3,2,1,0:T(8,128)(2,1)S(1)}, bf16[4,8,16,512]{3,2,1,0:T(8,128)(2,1)S(1)}, u32[]{:S(2)}, u32[]{:S(2)}) collective-permute-start(bf16[4,8,16,512]{3,2,1,0:T(8,128)(2,1)S(1)} %collective-permute-done.16.refs_4_), channel_id=1, source_target_pairs={{0,4},{4,0},{8,12},{12,8},{16,20},{20,16},{24,28},{28,24},{1,5},{5... | collective-permute-start | bytes 1572872 | tf_op jit(solution)/shard_map/ppermute | solution.py:690
  63.8 0.7 copy-start.23
  63.8 16.7 %collective-permute-start.15 = (bf16[4,8,16,512]{3,2,1,0:T(8,128)(2,1)S(1)}, bf16[4,8,16,512]{3,2,1,0:T(8,128)(2,1)S(1)}, u32[]{:S(2)}, u32[]{:S(2)}) collective-permute-start(bf16[4,8,16,512]{3,2,1,0:T(8,128)(2,1)S(1)} %collective-permute-done.14.refs_2_), channel_id=1, source_target_pairs={{0,4},{4,0},{8,12},{12,8},{16,20},{20,16},{24,28},{28,24},{1,5},{5... | collective-permute-start | bytes 1572872 | tf_op jit(solution)/shard_map/ppermute | solution.py:690
  64.5 0.7 copy-start.24
  80.4 0.8 copy-start.14
  80.4 1.0 copy-start.15
  80.5 1.1 copy-start.16
  80.5 1.3 copy-start.17
  107.9 4.4 %collective-permute-start.20 = (bf16[4,4,8,16,512]{4,3,2,1,0:T(8,128)(2,1)}, bf16[4,4,8,16,512]{4,3,2,1,0:T(8,128)(2,1)S(1)}, u32[]{:S(2)}, u32[]{:S(2)}) collective-permute-start(bf16[4,4,8,16,512]{4,3,2,1,0:T(8,128)(2,1)} %get-tuple-element.47), channel_id=1, source_target_pairs={{0,4},{4,0},{8,12},{12,8},{16,20},{20,16},{24,28},{28,24},{1,5},{5... | collective-permute-start | bytes 6291464 | tf_op jit(solution)/shard_map/ppermute | solution.py:695
  114.4 3.6 %copy-start.2 = (bf16[4,8,16,512]{3,2,1,0:T(8,128)(2,1)}, bf16[4,8,16,512]{3,2,1,0:T(8,128)(2,1)S(1)}, u32[]{:S(2)}) copy-start(bf16[4,8,16,512]{3,2,1,0:T(8,128)(2,1)S(1)} %get-tuple-element.71.refs_9_) | copy-start | bytes 1572868
  114.4 3.6 %copy-start.3 = (bf16[4,8,16,512]{3,2,1,0:T(8,128)(2,1)}, bf16[4,8,16,512]{3,2,1,0:T(8,128)(2,1)S(1)}, u32[]{:S(2)}) copy-start(bf16[4,8,16,512]{3,2,1,0:T(8,128)(2,1)S(1)} %get-tuple-element.70.refs_10_) | copy-start | bytes 1572868
  114.4 3.6 %copy-start.4 = (bf16[4,8,16,512]{3,2,1,0:T(8,128)(2,1)}, bf16[4,8,16,512]{3,2,1,0:T(8,128)(2,1)S(1)}, u32[]{:S(2)}) copy-start(bf16[4,8,16,512]{3,2,1,0:T(8,128)(2,1)S(1)} %get-tuple-element.69.refs_8_) | copy-start | bytes 1572868
  114.4 35.8 %collective-permute-start.21 = (bf16[4,8,16,512]{3,2,1,0:T(8,128)(2,1)S(1)}, bf16[4,8,16,512]{3,2,1,0:T(8,128)(2,1)S(1)}, u32[]{:S(2)}, u32[]{:S(2)}) collective-permute-start(bf16[4,8,16,512]{3,2,1,0:T(8,128)(2,1)S(1)} %get-tuple-element.69.refs_8_), channel_id=1, source_target_pairs={{0,8},{4,12},{8,0},{12,4},{16,24},{20,28},{24,16},{28,20},{1,9},{5... | collective-permute-start | bytes 1572872 | tf_op jit(solution)/shard_map/ppermute | solution.py:701
  115.9 34.3 %collective-permute-start.23 = (bf16[4,8,16,512]{3,2,1,0:T(8,128)(2,1)S(1)}, bf16[4,8,16,512]{3,2,1,0:T(8,128)(2,1)S(1)}, u32[]{:S(2)}, u32[]{:S(2)}) collective-permute-start(bf16[4,8,16,512]{3,2,1,0:T(8,128)(2,1)S(1)} %get-tuple-element.70.refs_10_), channel_id=1, source_target_pairs={{0,24},{4,28},{8,16},{12,20},{16,8},{20,12},{24,0},{28,4},{1,25},{... | collective-permute-start | bytes 1572872 | tf_op jit(solution)/shard_map/ppermute | solution.py:701
  116.4 33.8 %collective-permute-start.22 = (bf16[4,8,16,512]{3,2,1,0:T(8,128)(2,1)S(1)}, bf16[4,8,16,512]{3,2,1,0:T(8,128)(2,1)S(1)}, u32[]{:S(2)}, u32[]{:S(2)}) collective-permute-start(bf16[4,8,16,512]{3,2,1,0:T(8,128)(2,1)S(1)} %get-tuple-element.71.refs_9_), channel_id=1, source_target_pairs={{0,16},{4,20},{8,24},{12,28},{16,0},{20,4},{24,8},{28,12},{1,17},{... | collective-permute-start | bytes 1572872 | tf_op jit(solution)/shard_map/ppermute | solution.py:701
  150.1 6.5 %copy-start = (bf16[3,4,64,640]{3,2,1,0:T(8,128)(2,1)S(1)}, bf16[3,4,64,640]{3,2,1,0:T(8,128)(2,1)}, u32[]{:S(2)}) copy-start(bf16[3,4,64,640]{3,2,1,0:T(8,128)(2,1)} %get-tuple-element.58) | copy-start | bytes 2949124
  150.1 17.0 %collective-permute-start.24 = (bf16[4,3,64,640]{3,2,1,0:T(8,128)(2,1)S(1)}, bf16[4,3,64,640]{3,2,1,0:T(8,128)(2,1)S(1)}, u32[]{:S(2)}, u32[]{:S(2)}) collective-permute-start(bf16[4,3,64,640]{3,2,1,0:T(8,128)(2,1)S(1)} %bitcast.102), channel_id=1, source_target_pairs={{0,4},{4,0},{8,12},{12,8},{16,20},{20,16},{24,28},{28,24},{1,5},{5... | collective-permute-start | bytes 2949128 | tf_op jit(solution)/shard_map/ppermute | solution.py:695
  151.9 16.3 %copy-start.8 = (bf16[8,16,512]{2,1,0:T(8,128)(2,1)}, bf16[8,16,512]{2,1,0:T(8,128)(2,1)S(1)}, u32[]{:S(2)}) copy-start(bf16[8,16,512]{2,1,0:T(8,128)(2,1)S(1)} %get-tuple-element.75.refs_2_) | copy-start | bytes 393220
  151.9 16.3 %copy-start.9 = (bf16[8,16,512]{2,1,0:T(8,128)(2,1)}, bf16[8,16,512]{2,1,0:T(8,128)(2,1)S(1)}, u32[]{:S(2)}) copy-start(bf16[8,16,512]{2,1,0:T(8,128)(2,1)S(1)} %get-tuple-element.76.refs_1_) | copy-start | bytes 393220
  151.9 16.3 %copy-start.10 = (bf16[8,16,512]{2,1,0:T(8,128)(2,1)}, bf16[8,16,512]{2,1,0:T(8,128)(2,1)S(1)}, u32[]{:S(2)}) copy-start(bf16[8,16,512]{2,1,0:T(8,128)(2,1)S(1)} %get-tuple-element.77.refs_0_) | copy-start | bytes 393220
  151.9 5.9 %collective-permute-start.33 = (bf16[8,16,512]{2,1,0:T(8,128)(2,1)S(1)}, bf16[8,16,512]{2,1,0:T(8,128)(2,1)S(1)}, u32[]{:S(2)}, u32[]{:S(2)}) collective-permute-start(bf16[8,16,512]{2,1,0:T(8,128)(2,1)S(1)} %get-tuple-element.75.refs_2_), channel_id=1, source_target_pairs={{0,3},{1,0},{2,1},{3,2},{4,7},{5,4},{6,5},{7,6},{8,11},{9,8},{10,9... | collective-permute-start | bytes 393224 | tf_op jit(solution)/shard_map/ppermute | solution.py:800
  152.6 14.5 %collective-permute-start.32 = (bf16[8,16,512]{2,1,0:T(8,128)(2,1)S(1)}, bf16[8,16,512]{2,1,0:T(8,128)(2,1)S(1)}, u32[]{:S(2)}, u32[]{:S(2)}) collective-permute-start(bf16[8,16,512]{2,1,0:T(8,128)(2,1)S(1)} %get-tuple-element.76.refs_1_), channel_id=1, source_target_pairs={{0,2},{1,3},{2,0},{3,1},{4,6},{5,7},{6,4},{7,5},{8,10},{9,11},{10,... | collective-permute-start | bytes 393224 | tf_op jit(solution)/shard_map/ppermute | solution.py:800
  154.6 12.4 %collective-permute-start.31 = (bf16[8,16,512]{2,1,0:T(8,128)(2,1)S(1)}, bf16[8,16,512]{2,1,0:T(8,128)(2,1)S(1)}, u32[]{:S(2)}, u32[]{:S(2)}) collective-permute-start(bf16[8,16,512]{2,1,0:T(8,128)(2,1)S(1)} %get-tuple-element.77.refs_0_), channel_id=1, source_target_pairs={{0,1},{1,2},{2,3},{3,0},{4,5},{5,6},{6,7},{7,4},{8,9},{9,10},{10,1... | collective-permute-start | bytes 393224 | tf_op jit(solution)/shard_map/ppermute | solution.py:800
  168.2 34.9 %collective-permute-start.27 = (bf16[3,64,640]{2,1,0:T(8,128)(2,1)}, bf16[3,64,640]{2,1,0:T(8,128)(2,1)S(1)}, u32[]{:S(2)}, u32[]{:S(2)}) collective-permute-start(bf16[3,64,640]{2,1,0:T(8,128)(2,1)} %get-tuple-element.72.refs_5_), channel_id=1, source_target_pairs={{0,24},{4,28},{8,16},{12,20},{16,8},{20,12},{24,0},{28,4},{1,25},{... | collective-permute-start | bytes 737288 | tf_op jit(solution)/shard_map/ppermute | solution.py:701
  169.7 33.4 %collective-permute-start.26 = (bf16[3,64,640]{2,1,0:T(8,128)(2,1)}, bf16[3,64,640]{2,1,0:T(8,128)(2,1)S(1)}, u32[]{:S(2)}, u32[]{:S(2)}) collective-permute-start(bf16[3,64,640]{2,1,0:T(8,128)(2,1)} %get-tuple-element.73.refs_4_), channel_id=1, source_target_pairs={{0,16},{4,20},{8,24},{12,28},{16,0},{20,4},{24,8},{28,12},{1,17},{... | collective-permute-start | bytes 737288 | tf_op jit(solution)/shard_map/ppermute | solution.py:701
  171.2 10.6 %copy-start.7 = (bf16[3,64,640]{2,1,0:T(8,128)(2,1)S(1)}, bf16[3,64,640]{2,1,0:T(8,128)(2,1)}, u32[]{:S(2)}) copy-start(bf16[3,64,640]{2,1,0:T(8,128)(2,1)} %get-tuple-element.74.refs_3_) | copy-start | bytes 737284
  181.8 21.2 %collective-permute-start.25 = (bf16[3,64,640]{2,1,0:T(8,128)(2,1)S(1)}, bf16[3,64,640]{2,1,0:T(8,128)(2,1)}, u32[]{:S(2)}, u32[]{:S(2)}) collective-permute-start(bf16[3,64,640]{2,1,0:T(8,128)(2,1)S(1)} %copy-done.7), channel_id=1, source_target_pairs={{0,8},{4,12},{8,0},{12,4},{16,24},{20,28},{24,16},{28,20},{1,9},{5... | collective-permute-start | bytes 737288 | tf_op jit(solution)/shard_map/ppermute | solution.py:701
  189.5 9.9 %all-to-all-start = ((f32[32,1,256]{2,1,0:T(1,128)}), f32[32,1,256]{2,1,0:T(1,128)S(1)}, u32[]{:S(2)}, u32[]{:S(2)}) async-start(f32[32,1,256]{2,1,0:T(1,128)} %copy.34), calls=%async_computation | async-start | bytes 65536 | tf_op jit(solution)/shard_map/all_to_all | solution.py:825
  199.4 15.1 %all-to-all-start.1 = ((bf16[8,64,640]{2,1,0:T(8,128)(2,1)}), bf16[8,64,640]{2,1,0:T(8,128)(2,1)S(1)}, u32[]{:S(2)}, u32[]{:S(2)}) async-start(bf16[8,64,640]{2,1,0:T(8,128)(2,1)} %bitcast.24), calls=%async_computation.1 | async-start | bytes 1310720 | tf_op jit(solution)/shard_map/all_to_all | solution.py:799
  204.2 4.8 %collective-permute-start.28 = (bf16[64,640]{1,0:T(8,128)(2,1)S(1)}, bf16[64,640]{1,0:T(8,128)(2,1)S(1)}, u32[]{:S(2)}, u32[]{:S(2)}) collective-permute-start(bf16[64,640]{1,0:T(8,128)(2,1)S(1)} %get-tuple-element.82), channel_id=1, source_target_pairs={{0,3},{1,0},{2,1},{3,2},{4,7},{5,4},{6,5},{7,6},{8,11},{9,8},{10,9... | collective-permute-start | bytes 245768 | tf_op jit(solution)/shard_map/ppermute | solution.py:806
  204.7 7.2 %collective-permute-start.30 = (bf16[64,640]{1,0:T(8,128)(2,1)S(1)}, bf16[64,640]{1,0:T(8,128)(2,1)S(1)}, u32[]{:S(2)}, u32[]{:S(2)}) collective-permute-start(bf16[64,640]{1,0:T(8,128)(2,1)S(1)} %get-tuple-element.83), channel_id=1, source_target_pairs={{0,1},{1,2},{2,3},{3,0},{4,5},{5,6},{6,7},{7,4},{8,9},{9,10},{10,1... | collective-permute-start | bytes 245768 | tf_op jit(solution)/shard_map/ppermute | solution.py:806
  206.3 8.3 %collective-permute-start.29 = (bf16[64,640]{1,0:T(8,128)(2,1)S(1)}, bf16[64,640]{1,0:T(8,128)(2,1)S(1)}, u32[]{:S(2)}, u32[]{:S(2)}) collective-permute-start(bf16[64,640]{1,0:T(8,128)(2,1)S(1)} %get-tuple-element.84), channel_id=1, source_target_pairs={{0,2},{1,3},{2,0},{3,1},{4,6},{5,7},{6,4},{7,5},{8,10},{9,11},{10,... | collective-permute-start | bytes 245768 | tf_op jit(solution)/shard_map/ppermute | solution.py:806

commit v3 on v2

--- a/solution.py
+++ b/solution.py
@@ -209,10 +209,6 @@
     )
 
 
-def vmem(n):
-    return [pl.BlockSpec(memory_space=pltpu.VMEM)] * n
-
-
 def by_slot(shapes):
     return [
         pl.BlockSpec((None,) + s.shape[1:], lambda a, rank=len(s.shape): (a,) + (0,) * (rank - 1))
@@ -261,28 +257,56 @@
     return out
 
 
+def own_device(core, chip, z, slots):
+    return (lax.axis_index("seq") ^ (2 * chip + core)) * slots + z
+
+
+def turned(by, slots):
+    return lax.rem(lax.axis_index("head") + by, slots)
+
+
 def fill(weight, own_ref, pieces, slot):
-    rows = weight.shape[0] // len(pieces)
-    stride = rows + 16 if len(pieces) > 1 else rows
-
     @pl.when(slot == 0)
     def _():
         weight[...] = own_ref[...]
 
-    @pl.when(slot > 0)
-    def _():
-        first = pl.multiple_of((slot - 1) * stride, 16)
-        mine = lax.axis_index("seq") if len(pieces) > 1 else 0
-        for r, piece in enumerate(pieces):
-            weight[pl.ds(pl.multiple_of((mine ^ r) * rows, 16), rows), :] = piece[pl.ds(first, rows), :]
+    if len(pieces) == 1:
+        rows = weight.shape[0]
+
+        @pl.when(slot > 0)
+        def _():
+            weight[...] = pieces[0][pl.ds(pl.multiple_of((slot - 1) * rows, 16), rows), :]
+
+        return
+    rows = weight.shape[0] // 8
+    mine = lax.axis_index("seq")
+    for a in range(1, 4):
+
+        @pl.when(slot == a)
+        def _(a=a):
+            for core in range(2):
+                low_a, low_b, a_x, b_y, a_y, b_x = pieces[6 * core : 6 * core + 6]
+                if a < 3:
+                    n, start = 2 * rows, (a - 1) * rows
+                    parts = [(low_a, 0), (a_x, 0), (a_y, 0), (a_y, n)]
+                else:
+                    n, start = low_b.shape[0], 0
+                    parts = [(low_b, 0), (b_x, 0), (b_y, 0), (b_x, n)]
+                for chip, (piece, offset) in enumerate(parts):
+                    source = pl.multiple_of((mine ^ (2 * chip + core)) * rows, 16)
+                    first = offset + start
+                    weight[pl.ds(source, rows), :] = piece[first : first + rows, :]
 
 
 def gather_vectors(pieces, rows, slots, vectors, staged):
-    for r, piece in enumerate(pieces):
-        for a in range(slots):
-            first = a * (rows + 16) - 16 if a else (slots - 1) * (rows + 16)
-            source = place(r % 2, r // 2, slots - a, slots)
-            staged[pl.ds(source, 1), :] = piece[first : first + 16, :256].astype(F32)[0:1, :]
+    for core in range(2):
+        _, low_b, _, b_y, _, b_x = pieces[6 * core : 6 * core + 6]
+        n = low_b.shape[0]
+        for chip, (piece, offset) in enumerate([(low_b, 0), (b_x, 0), (b_y, 0), (b_x, n)]):
+            for a in range(slots):
+                first = offset + rows + 16 * ((a + slots - 1) % slots)
+                source = own_device(core, chip, turned(slots - a, slots), slots)
+                staged[pl.ds(source, 1), :] = piece[first : first + 16, :256].astype(F32)[0:1, :]
     vectors[...] = low(staged[...])
 
 
@@ -290,8 +314,8 @@
     pieces, refs = refs[:count], refs[count:]
     if count == 1:
         given, refs = refs[0], refs[1:]
-    normed_ref, residual_ref, vectors_ref, keep = refs[0], refs[1], refs[2], refs[3:-2]
-    weight, staged = refs[-2:]
+    normed_ref, residual_ref, vectors_ref, weight, keep = refs[0], refs[1], refs[2], refs[3], refs[4:-1]
+    staged = refs[-1]
     slot = pl.program_id(0)
     length, width = tokens_ref.shape
     share = width // vectors_ref.shape[0]
@@ -301,7 +325,7 @@
         if count == 1:
             vectors_ref[...] = given[...]
         else:
-            gather_vectors(pieces, weight.shape[0] // count, slots, vectors_ref, staged)
+            gather_vectors(pieces, own_ref.shape[0] // 8, slots, vectors_ref, staged)
         small = vectors_ref[:, :128]
         gain = spread(small, 0, share, width)
         shift = spread(small, share, share, width)
@@ -319,22 +343,22 @@
 def forward(tokens, own, pieces, vectors, devices, slots):
     length, width = tokens.shape
     shape = jax.ShapeDtypeStruct
-    keep = kept_shapes(length, (slots,))
+    stacked_outs = [shape((slots,) + own.shape, BF16)] + kept_shapes(length, (slots,))
     given = [] if vectors is None else [vectors]
     operands = [tokens, own, *pieces, *given]
     outs = [shape((length, width), BF16), shape((length, width), F32), shape((devices, 256), BF16)]
     made = pl.pallas_call(
         functools.partial(forward_kernel, len(pieces), slots),
         grid=(slots,),
-        out_shape=outs + keep,
+        out_shape=outs + stacked_outs,
         in_specs=[fixed(o.shape) for o in operands],
-        out_specs=[fixed(o.shape) for o in outs] + by_slot(keep),
-        scratch_shapes=[pltpu.VMEM(own.shape, BF16), pltpu.VMEM((devices, 256), F32)],
+        out_specs=[fixed(o.shape) for o in outs] + by_slot(stacked_outs),
+        scratch_shapes=[pltpu.VMEM((devices, 256), F32)],
         compiler_params=params(),
-        cost_estimate=cost(18),
+        cost_estimate=cost(16),
         name="attend_forward",
     )(*operands)
-    return made[0], made[1], made[2], made[3:]
+    return made[0], made[1], made[2], made[3], made[4:]
 
 
 GELU_A = 0.7978845608028654
@@ -349,57 +373,43 @@
     return u * half, slope
 
 
-def place(core, chip, turn, slots):
-    seq = lax.axis_index("seq") ^ (2 * chip + core)
-    return seq * slots + lax.rem(lax.axis_index("head") + turn, slots)
-
-
-def weight_copies(pieces, expand, shrink, sems):
-    if len(pieces) == 2:
-        return [
-            pltpu.make_async_copy(pieces[0], expand, sems.at[0]),
-            pltpu.make_async_copy(pieces[1], shrink, sems.at[1]),
+def weight_copies(pieces, weights, sems):
+    if len(pieces) == 1:
+        return [pltpu.make_async_copy(pieces[0], weights, sems.at[0])]
+    copies = []
+    for core in range(2):
+        low_a, low_b, a_x, b_y, a_y, b_x = pieces[6 * core : 6 * core + 6]
+        slots = low_a.shape[0]
+        halves = [
+            [low_a, a_x, a_y.at[0], a_y.at[1]],
+            [low_b, b_x.at[0], b_y, b_x.at[1]],
         ]
-    copies = []
-    for r, piece in enumerate(pieces):
-        slots = piece.shape[0]
-        for a in range(slots):
-            source = place(r % 2, r // 2, slots - a, slots)
-            n = len(copies)
-            copies.append(
-                pltpu.make_async_copy(
-                    piece.at[a, pl.ds(0, 4)], expand.at[pl.ds(source * 4, 4)], sems.at[n]
-                )
-            )
-            copies.append(
-                pltpu.make_async_copy(
-                    piece.at[a, pl.ds(4, 4)], shrink.at[:, source], sems.at[n + 1]
-                )
-            )
+        for half in range(2):
+            for chip in range(4):
+                for a in range(slots):
+                    source = own_device(core, chip, turned(slots - a, slots), slots)
+                    copies.append(
+                        pltpu.make_async_copy(
+                            halves[half][chip].at[a],
+                            weights.at[pl.ds(2 * half, 2), :, source],
+                            sems.at[len(copies)],
+                        )
+                    )
     return copies
 
 
-def grad_copies(expand, shrink, outs, sems):
-    if len(outs) == 2 and outs[0].shape == expand.shape:
-        return [
-            pltpu.make_async_copy(expand, outs[0], sems.at[0]),
-            pltpu.make_async_copy(shrink, outs[1], sems.at[1]),
-        ]
+def grad_copies(grads, outs, sems):
+    if len(outs) == 1:
+        return [pltpu.make_async_copy(grads, outs[0], sems.at[0])]
     copies = []
     for core, out in enumerate(outs):
-        for chip in range(out.shape[0]):
-            slots = out.shape[1]
-            for a in range(slots):
-                target = place(core, chip, a, slots)
-                n = len(copies)
+        chips, slots = out.shape[:2]
+        for chip in range(chips):
+            for z in range(slots):
+                target = own_device(core, chip, z, slots)
                 copies.append(
                     pltpu.make_async_copy(
-                        expand.at[pl.ds(target * 4, 4)], out.at[chip, a, pl.ds(0, 4)], sems.at[n]
-                    )
-                )
-                copies.append(
-                    pltpu.make_async_copy(
-                        shrink.at[:, target], out.at[chip, a, pl.ds(4, 4)], sems.at[n + 1]
+                        grads.at[:, :, target], out.at[chip, z], sems.at[len(copies)]
                     )
                 )
     return copies
@@ -408,29 +418,24 @@
 def ffn_kernel(count, residual_ref, vectors_ref, cotangent_ref, *refs):
     pieces = refs[:count]
     result_ref, grad_ref, branch_ref, sums_ref = refs[count : count + 4]
-    grads = refs[count + 4 : count + 6]
-    (expand_all, shrink_all, expand_grad, shrink_grad, second, normal_ref, rate_ref, total, back,
-     gains, bias_row, bias_grads, sems) = refs[count + 6 :]
+    outs = refs[count + 4 : -11]
+    (weights, grads, second, normal_ref, rate_ref, total, back, gains, bias_row, bias_grads, sems) = refs[-11:]
     k = pl.program_id(0)
-    steps = pl.num_programs(0)
     length, width = residual_ref.shape
     devices = vectors_ref.shape[0]
     share = width // devices
     tiles = [slice(r, r + 256) for r in range(0, length, 256)]
-    step = expand_all.shape[0] * 16 // 4
-    hidden_share = 4 * step // devices
 
     @pl.when(k == 0)
     def _():
-        copies = weight_copies(pieces, expand_all, shrink_all, sems)
+        copies = weight_copies(pieces, weights, sems)
         for copy in copies:
             copy.start()
-        small = vectors_ref[:, :128]
+        small, wide = vectors_ref[:, :128], vectors_ref[:, 128:]
         for i in range(3):
             gains[i : i + 1, :] = spread(small, (2 + i) * share, share, width)
-        wide = spread(vectors_ref[:, 128:], 0, hidden_share, 4 * step)
         for i in range(4):
-            bias_row[i, 0:1, :] = wide[:, i * step : (i + 1) * step]
+            bias_row[i, 0:1, :] = spread(wide, i * share, share, width)
         for rows in tiles:
             normal, rate = norm_parts(residual_ref[rows, :])
             normal_ref[rows, :] = normal
@@ -441,11 +446,10 @@
         for copy in copies:
             copy.wait()
 
-    blocks = step // 16
-    expand = expand_all[pl.ds(k * blocks, blocks)].reshape(step, width)
-    shrink = shrink_all[k].reshape(width, step)
+    expand = weights[k, 0].reshape(width, width)
+    shrink = weights[k, 1].reshape(width, width)
     bias = bias_row[k][0:1, :]
-    bias_grad = jnp.zeros((1, step), F32)
+    bias_grad = jnp.zeros((1, width), F32)
     acts, hids = [], []
     for rows in tiles:
         hidden = nt(second[rows, :], expand) + bias
@@ -459,16 +463,14 @@
         acts.append(activated)
         hids.append(hidden_grad)
     bias_grads[k, 0:1, :] = bias_grad
-    shrink_grad[k] = low(tn(cotangent_ref[...], jnp.concatenate(acts, axis=0))).reshape(
-        width // 16, 16, step
-    )
-    expand_grad[pl.ds(k * blocks, blocks)] = low(
-        tn(jnp.concatenate(hids, axis=0), second[...])
-    ).reshape(blocks, 16, width)
-
-    @pl.when(k == steps - 1)
+    grads[k, 1] = low(tn(cotangent_ref[...], jnp.concatenate(acts, axis=0))).reshape(
+        width // 16, 16, width
+    )
+    grads[k, 0] = low(tn(jnp.concatenate(hids, axis=0), second[...])).reshape(width // 16, 16, width)
+
+    @pl.when(k == 3)
     def _():
-        copies = grad_copies(expand_grad, shrink_grad, grads, sems)
+        copies = grad_copies(grads, outs, sems)
         for copy in copies:
             copy.start()
         gain = gains[0:1, :]
@@ -491,16 +493,18 @@
             + collect(shift_grad, devices, 3 * share, share)
             + collect(outer, devices, 4 * share, share)
         )
-        wide = jnp.concatenate([bias_grads[i][0:1, :] for i in range(4)], axis=1)
-        sums_ref[:, 128:] = collect(wide, devices, 0, hidden_share)
+        sums_ref[:, 128:] = functools.reduce(
+            lambda a, b: a + b,
+            [collect(bias_grads[i][0:1, :], devices, i * share, share) for i in range(4)],
+        )
         for copy in copies:
             copy.wait()
 
 
-def feed_forward(residual, vectors, cotangent, pieces, grad_shapes, hidden):
+def feed_forward(residual, vectors, cotangent, pieces, grad_shapes):
     length, width = residual.shape
-    step = hidden // 4
     shape = jax.ShapeDtypeStruct
+    weights = (4, 2, width // 16, 16, width)
     return pl.pallas_call(
         functools.partial(ffn_kernel, len(pieces)),
         grid=(4,),
@@ -511,35 +515,69 @@
             shape(vectors.shape, F32),
         ]
         + [shape(s, BF16) for s in grad_shapes],
-        in_specs=[fixed((length, width)), fixed(vectors.shape), fixed((length, width))]
-        + anywhere(pieces),
+        in_specs=[fixed((length, width)), fixed(vectors.shape), fixed((length, width))] + anywhere(pieces),
         out_specs=[fixed((length, width))] * 3 + [fixed(vectors.shape)] + anywhere(grad_shapes),
         scratch_shapes=[
-            pltpu.VMEM((hidden // 16, 16, width), BF16),
-            pltpu.VMEM((4, width // 16, 16, step), BF16),
-            pltpu.VMEM((hidden // 16, 16, width), BF16),
-            pltpu.VMEM((4, width // 16, 16, step), BF16),
+            pltpu.VMEM(weights, BF16),
+            pltpu.VMEM(weights, BF16),
             pltpu.VMEM((length, width), BF16),
             pltpu.VMEM((length, width), F32),
             pltpu.VMEM((length, 1), F32),
             pltpu.VMEM((length, width), F32),
             pltpu.VMEM((length, width), F32),
             pltpu.VMEM((8, width), F32),
-            pltpu.VMEM((4, 8, step), F32),
-            pltpu.VMEM((4, 8, step), F32),
-            pltpu.SemaphoreType.DMA((max(2, 2 * vectors.shape[0]),)),
+            pltpu.VMEM((4, 8, width), F32),
+            pltpu.VMEM((4, 8, width), F32),
+            pltpu.SemaphoreType.DMA((64,)),
         ],
         compiler_params=params(),
-        cost_estimate=cost(27),
+        cost_estimate=cost(26),
         name="feed_forward",
     )(residual, vectors, cotangent, *pieces)
 
 
-def pair_grads(branch_ref, normed_ref, weight_in, weight_out, kept, heads_ref, outs, grad, backs, made):
-    grad[...] = low(nt(branch_ref[...], weight_out))
-    attend_backward(grad, kept, backs)
+def heads_kernel(branch_ref, weight_ref, heads_ref, grad_ref, output_grad_ref):
+    grad_ref[...] = low(nt(branch_ref[...], weight_ref[...]))
+    output_grad_ref[...] = low(tn(branch_ref[...], heads_ref[...]))
+
+
+def heads_back(branch, weights, heads):
+    slots, length, pair = heads.shape
+    width = branch.shape[1]
+    shape = jax.ShapeDtypeStruct
+    outs = [shape((slots, length, pair), BF16), shape((slots, width, pair), BF16)]
+    last = width // pair
+    return pl.pallas_call(
+        heads_kernel,
+        grid=(slots,),
+        out_shape=outs,
+        in_specs=[
+            fixed((length, width)),
+            pl.BlockSpec((None, pair, width), lambda a: (a, last, 0)),
+        ]
+        + by_slot([heads]),
+        out_specs=by_slot(outs),
+        compiler_params=params(),
+        cost_estimate=cost(4),
+        name="heads_back",
+    )(branch, weights, heads)
+
+
+def later_slots(shapes, first):
+    return [
+        pl.BlockSpec((None,) + s.shape[1:], lambda a, rank=len(s.shape): (a + first,) + (0,) * (rank - 1))
+        for s in shapes
+    ]
+
+
+def anywhere(members):
+    return [pl.BlockSpec(memory_space=pl.ANY)] * len(members)
+
+
+def pair_grads(grad_ref, output_grad_ref, normed_ref, kept, outs, backs, made):
+    attend_backward(grad_ref, kept, backs)
     made[:, : 4 * PAIR] = low(tn(normed_ref[...], backs[...]))
-    made[:, 4 * PAIR :] = low(tn(branch_ref[...], heads_ref[...]))
+    made[:, 4 * PAIR :] = output_grad_ref[...]
     if len(outs) == 1:
         outs[0][...] = made[...]
         return
@@ -551,16 +589,13 @@
             out[chip] = made[pl.ds(start, rows), :]
 
 
-def back_rest_kernel(count, waits, parts_out, branch_ref, normed_ref, own_ref, *refs):
-    pieces, refs = refs[:count], refs[count + waits :]
-    kept, heads_ref, refs = refs[:9], refs[9], refs[10:]
+def back_rest_kernel(waits, parts_out, normed_ref, *refs):
+    refs = refs[waits:]
+    weight, grad_ref, output_grad_ref, kept, refs = refs[0], refs[1], refs[2], refs[3:12], refs[12:]
     sum_ref, outs = refs[0], refs[1 : 1 + parts_out]
-    weight, grad, backs, made = refs[1 + parts_out :]
+    backs, made = refs[1 + parts_out :]
     width = normed_ref.shape[1]
-    fill(weight, own_ref, pieces, pl.program_id(0) + 1)
-    pair_grads(
-        branch_ref, normed_ref, None, weight[width:, :], kept, heads_ref, outs, grad, backs, made
-    )
+    pair_grads(grad_ref, output_grad_ref, normed_ref, kept, outs, backs, made)
 
     @pl.when(pl.program_id(0) == 0)
     def _():
@@ -569,108 +604,74 @@
     sum_ref[...] += nt(backs[...], weight[:width, :])
 
 
-def back_scratch(length, width):
-    return [
-        pltpu.VMEM((length, PAIR), BF16),
-        pltpu.VMEM((length, 4 * PAIR), BF16),
-        pltpu.VMEM((width, 5 * PAIR), BF16),
-    ]
-
-
-def later_slots(shapes, first):
-    return [
-        pl.BlockSpec((None,) + s.shape[1:], lambda a, rank=len(s.shape): (a + first,) + (0,) * (rank - 1))
-        for s in shapes
-    ]
-
-
-def anywhere(members):
-    return [pl.BlockSpec(memory_space=pl.ANY)] * len(members)
-
-
-def backward_rest(branch, normed, own, pieces, waits, kept, grad_shapes):
-    length, width = branch.shape
-    slots = kept[0].shape[0] - 1
+def backward_rest(normed, waits, members, grad_shapes):
+    length, width = normed.shape
+    slots = members[0].shape[0] - 1
     shape = jax.ShapeDtypeStruct
-    grads = [shape((slots,) + s, BF16) for s in grad_shapes]
+    grads = [shape(s[:-2] + (slots,) + s[-2:], BF16) for s in grad_shapes]
+    if len(grads) == 2:
+        grad_specs = [
+            pl.BlockSpec((g.shape[0], None) + g.shape[2:], lambda a: (0, a, 0, 0)) for g in grads
+        ]
+    else:
+        grad_specs = by_slot(grads)
     return pl.pallas_call(
-        functools.partial(back_rest_kernel, len(pieces), len(waits), len(grads)),
+        functools.partial(back_rest_kernel, len(waits), len(grads)),
         grid=(slots,),
         out_shape=[shape((length, width), F32)] + grads,
-        in_specs=[fixed(o.shape) for o in (branch, normed, own, *pieces)]
-        + anywhere(waits)
-        + later_slots(kept, 1),
-        out_specs=[fixed((length, width))] + by_slot(grads),
-        scratch_shapes=[pltpu.VMEM(own.shape, BF16)] + back_scratch(length, width),
+        in_specs=[fixed(normed.shape)] + anywhere(waits) + later_slots(members, 1),
+        out_specs=[fixed((length, width))] + grad_specs,
+        scratch_shapes=[pltpu.VMEM((length, 4 * PAIR), BF16), pltpu.VMEM((width, 5 * PAIR), BF16)],
         compiler_params=params(),
-        cost_estimate=cost(30),
+        cost_estimate=cost(28),
         name="attend_back_rest",
-    )(branch, normed, own, *pieces, *waits, *kept)
-
-
-def back_first_kernel(waits, parts_out, branch_ref, normed_ref, weight_ref, *refs):
+    )(normed, *waits, *members)
+
+
+def back_first_kernel(waits, parts_out, normed_ref, tokens_ref, vectors_ref, total_ref, residual_grad_ref, before_ref, *refs):
     refs = refs[waits:]
-    kept, heads_ref, refs = refs[:9], refs[9], refs[10:]
-    backs, outs = refs[0], refs[1 : 1 + parts_out]
-    grad, made = refs[1 + parts_out :]
-    width = normed_ref.shape[1]
-    pair_grads(
-        branch_ref, normed_ref, None, weight_ref[width:, :], kept, heads_ref, outs, grad, backs, made
-    )
-
-
-def backward_first(branch, normed, weight, waits, kept):
-    length, width = branch.shape
-    shape = jax.ShapeDtypeStruct
-    outs = [shape((length, 4 * PAIR), BF16), shape((width, 5 * PAIR), BF16)]
-    scratch = back_scratch(length, width)
-    return pl.pallas_call(
-        functools.partial(back_first_kernel, len(waits), 1),
-        grid=(1,),
-        out_shape=outs,
-        in_specs=[fixed(o.shape) for o in (branch, normed, weight)]
-        + anywhere(waits)
-        + later_slots(kept, 0),
-        out_specs=[fixed(o.shape) for o in outs],
-        scratch_shapes=[scratch[0], scratch[2]],
-        compiler_params=params(),
-        cost_estimate=cost(11),
-        name="attend_back_first",
-    )(branch, normed, weight, *waits, *kept)
-
-
-def last_kernel(tokens_ref, vectors_ref, backs_ref, weight_ref, total_ref, grad_ref, before_ref, out_ref, sums_ref):
-    length, width = tokens_ref.shape
+    weight, grad_ref, output_grad_ref, kept, refs = refs[0], refs[1], refs[2], refs[3:12], refs[12:]
+    input_grad_ref, sums_ref, outs = refs[0], refs[1], refs[2 : 2 + parts_out]
+    backs, made = refs[2 + parts_out :]
+    length, width = normed_ref.shape
     devices = vectors_ref.shape[0]
     share = width // devices
+    pair_grads(grad_ref, output_grad_ref, normed_ref, kept, outs, backs, made)
     gain = spread(vectors_ref[:, :128], 0, share, width)
     gain_grad = jnp.zeros((1, width), F32)
     shift_grad = jnp.zeros((1, width), F32)
     for rows in [slice(r, r + 256) for r in range(0, length, 256)]:
-        grad = total_ref[rows, :] + nt(backs_ref[rows, :], weight_ref[:width, :])
+        grad = total_ref[rows, :] + nt(backs[rows, :], weight[:width, :])
         normal, rate = norm_parts(tokens_ref[rows, :].astype(F32))
         gain_grad = gain_grad + jnp.sum(grad * normal, axis=0, keepdims=True)
         shift_grad = shift_grad + jnp.sum(grad, axis=0, keepdims=True)
-        out_ref[rows, :] = low(grad_ref[rows, :] + norm_back(grad, normal, rate, gain))
-    sums_ref[:, :128] = (
+        input_grad_ref[rows, :] = low(residual_grad_ref[rows, :] + norm_back(grad, normal, rate, gain))
+    sums_ref[...] = jnp.zeros_like(sums_ref)
+    sums_ref[:, 0, :] = (
         before_ref[:, :128]
         + collect(gain_grad, devices, 0, share)
         + collect(shift_grad, devices, share, share)
     )
-    sums_ref[:, 128:] = before_ref[:, 128:]
-
-
-def finish(tokens, vectors, backs, weight, total, grad, before):
+    sums_ref[:, 1, :] = before_ref[:, 128:]
+
+
+def backward_first(normed, tokens, vectors, total, residual_grad, before, waits, members, grad_shapes):
+    length, width = normed.shape
     shape = jax.ShapeDtypeStruct
+    operands = (normed, tokens, vectors, total, residual_grad, before)
+    outs = [shape((length, width), BF16), shape((before.shape[0], 8, 128), F32)]
+    outs += [shape(s, BF16) for s in grad_shapes]
     return pl.pallas_call(
-        last_kernel,
-        out_shape=[shape(tokens.shape, BF16), shape(before.shape, F32)],
-        in_specs=vmem(7),
-        out_specs=vmem(2),
+        functools.partial(back_first_kernel, len(waits), len(grad_shapes)),
+        grid=(1,),
+        out_shape=outs,
+        in_specs=[fixed(o.shape) for o in operands] + anywhere(waits) + later_slots(members, 0),
+        out_specs=[fixed(o.shape) for o in outs],
+        scratch_shapes=[pltpu.VMEM((length, 4 * PAIR), BF16), pltpu.VMEM((width, 5 * PAIR), BF16)],
         compiler_params=params(),
-        cost_estimate=cost(5),
-        name="norm_back",
-    )(tokens, vectors, backs, weight, total, grad, before)
+        cost_estimate=cost(14),
+        name="attend_back_first",
+    )(*operands, *waits, *members)
 
 
 def flip(count, bit):
@@ -685,10 +686,13 @@
     return functools.reduce(lambda a, b: a + b, [m.astype(F32) for m in members])
 
 
-def across(shares, chips, seqs):
-    held = [shares] + [lax.ppermute(shares, "seq", flip(seqs, 2 * r)) for r in range(1, chips)]
-    mates = [lax.ppermute(h, "seq", flip(seqs, 1)) for h in held]
-    return [member for both in zip(held, mates) for member in both]
+def across(part_a, part_b, join, seqs):
+    def send(v, bit):
+        return lax.ppermute(v, "seq", flip(seqs, bit))
+
+    a_x, b_y = send(part_a, 2), send(part_b, 4)
+    held = [part_a, part_b, a_x, b_y, send(join(part_a, a_x), 4), send(join(part_b, b_y), 2)]
+    return held + [send(h, 1) for h in held]
 
 
 def join_cores(keep, send, chips, seqs):
@@ -725,9 +729,8 @@
     width = inputs.shape[1]
     share = width // devices
     hidden_share = expand_weight.shape[1]
-    hidden = hidden_share * devices
     z = lax.axis_index("head")
-    direct = share % 16 == 0 and hidden_share == 4 * share and (width + PAIR) % (16 * seqs) == 0
+    direct = seqs == 8 and slots == 4 and share == 16 and hidden_share == 4 * share
 
     own = jnp.concatenate(
         [
@@ -736,94 +739,78 @@
         ],
         axis=0,
     )
-    small = jnp.concatenate([attn_gain, attn_shift, ffn_gain, ffn_shift, shrink_bias])
-    row = jnp.concatenate(
-        [
-            small,
-            jnp.zeros((128 - small.shape[0],), BF16),
-            expand_bias,
-            jnp.zeros((128 - expand_bias.shape[0],), BF16),
-        ]
-    )
-    expand_t = expand_weight.T
-    shrink_t = shrink_weight.T
+    places = [(attn_gain, 0), (attn_shift, 1), (ffn_gain, 2), (ffn_shift, 3), (shrink_bias, 4)]
+    row = jnp.pad(expand_bias, (128, 128 - hidden_share))
+    for member, i in places:
+        row = row + jnp.pad(member, (i * share, 256 - (i + 1) * share))
     vectors = None
+    expand_t = expand_weight.T.reshape(4, share, width)
+    shrink_t = shrink_weight.reshape(devices, 4, share, share).transpose(1, 3, 0, 2).reshape(4, share, width)
     if direct:
         rows = own.shape[0] // seqs
         piece = lax.dynamic_slice_in_dim(own, lax.axis_index("seq") * rows, rows, axis=0)
         block = jnp.pad(row[None, :], ((0, 15), (0, width - 256)))
         piece = jnp.concatenate([piece, block], axis=0)
         came = [lax.ppermute(piece, "head", turn(slots, a)) for a in range(1, slots)]
-        pieces = across(jnp.concatenate(came + [block], axis=0), chips, seqs)
-        load = jnp.concatenate(
-            [expand_t.reshape(4, 16, width)]
-            + [shrink_t[None, :, k * width : (k + 1) * width] for k in range(4)],
-            axis=0,
+        part_a = jnp.concatenate([came[0][:rows], came[1][:rows]], axis=0)
+        part_b = jnp.concatenate([came[2][:rows]] + [c[rows:] for c in came] + [block], axis=0)
+        pieces = across(part_a, part_b, lambda *m: jnp.concatenate(m, axis=0), seqs)
+        load = jnp.stack([expand_t, shrink_t], axis=1)
+        came = [load] + [lax.ppermute(load, "head", turn(slots, a)) for a in range(1, slots)]
+        ffn_pieces = across(
+            jnp.stack([c[:2] for c in came]), jnp.stack([c[2:] for c in came]), lambda *m: jnp.stack(m), seqs
         )
-        near = jnp.stack([load] + [lax.ppermute(load, "head", turn(slots, a)) for a in range(1, slots)])
-        ffn_pieces = across(near, chips, seqs)
         pair_shapes = [(chips, width // seqs, 5 * PAIR)] * 2
-        ffn_shapes = [(chips, slots, 8, 16, width)] * 2
+        ffn_shapes = [(chips, slots, 4, 2, 16, width)] * 2
     else:
         every = lax.all_gather(own, "head", axis=0, tiled=False)
         pieces = [jnp.concatenate([every[(z + slots - a) % slots] for a in range(1, slots)], axis=0)]
         vectors = lax.all_to_all(
             jnp.broadcast_to(row[None, :], (devices, 256)), ("seq", "head"), 0, 0, tiled=True
         )
-        ffn_pieces = [
-            lax.all_gather(expand_t, ("seq", "head"), axis=0, tiled=True).reshape(hidden // 16, 16, width),
-            lax.all_gather(shrink_t, ("seq", "head"), axis=0, tiled=True)
-            .reshape(width // 16, 16, 4, hidden // 4)
-            .transpose(2, 0, 1, 3),
-        ]
+        both = lax.all_gather(jnp.stack([expand_t, shrink_t], axis=1), ("seq", "head"), axis=2, tiled=True)
+        ffn_pieces = [both.reshape(4, 2, width // 16, 16, width)]
         pair_shapes = [(width, 5 * PAIR)]
-        ffn_shapes = [(hidden // 16, 16, width), (4, width // 16, 16, hidden // 4)]
-
-    normed, residual, vectors, kept = forward(inputs, own, pieces, vectors, devices, slots)
+        ffn_shapes = [ffn_pieces[0].shape]
+
+    normed, residual, vectors, weights, kept = forward(inputs, own, pieces, vectors, devices, slots)
+    kept, heads = kept[:-1], kept[-1]
     result, residual_grad, branch, sums, *ffn_grads = feed_forward(
-        residual, vectors, cotangent, ffn_pieces, ffn_shapes, hidden
-    )
+        residual, vectors, cotangent, ffn_pieces, ffn_shapes
+    )
+    heads_grad, output_grad = heads_back(branch, weights, heads)
+    members = [weights, heads_grad, output_grad, *kept]
     waits, later = [], []
     if direct:
         ffn_held, waits = join_cores(*ffn_grads, chips, seqs)
-    total, *rest_grads = backward_rest(branch, normed, own, pieces, waits, kept, pair_shapes)
+    total, *rest_grads = backward_rest(normed, waits, members, pair_shapes)
     if direct:
-        ffn_mine = join_chips(ffn_held, waits, seqs)
-        ffn_sends = [low(ffn_mine[a]) for a in range(1, slots)]
-        rest_held, rest_sends = join_cores(*[jnp.swapaxes(g, 0, 1) for g in rest_grads], chips, seqs)
-        later = ffn_sends + rest_sends
-    backs, first_grad = backward_first(branch, normed, own, later, kept)
-    input_grad, sums = finish(inputs, vectors, backs, own, total, residual_grad, sums)
+        ffn_mine = low(join_chips(ffn_held, waits, seqs))
+        rest_held, rest_sends = join_cores(*rest_grads, chips, seqs)
+        later = [ffn_mine] + rest_sends
+    input_grad, sums, *first_grads = backward_first(
+        normed, inputs, vectors, total, residual_grad, sums, later, members, pair_shapes
+    )
 
     if direct:
-        first_all = lax.all_to_all(first_grad, "seq", 0, 0, tiled=True)
-        ffn_came = [lax.ppermute(m, "head", turn(slots, a + 1)) for a, m in enumerate(ffn_sends)]
-        ffn_sum = add(ffn_mine[0], *ffn_came)
-        expand_grad = ffn_sum[:4].reshape(hidden_share, width)
-        shrink_grad = jnp.concatenate([ffn_sum[4 + k] for k in range(4)], axis=1)
+        ffn_sum = add(*lax.all_to_all(ffn_mine, "head", 0, 0, tiled=True))
         rest = join_chips(rest_held, rest_sends, seqs)
         rest_came = [
             lax.ppermute(low(rest[a - 1]), "head", turn(slots, slots - a)) for a in range(1, slots)
         ]
-        first_all = first_all.reshape((seqs,) + rest.shape[1:])
-        pair_sum = add(*[first_all[i] for i in range(seqs)], *rest_came)
+        pair_sum = add(join_chips(*join_cores(*first_grads, chips, seqs), seqs), *rest_came)
     else:
-        expand_grad = lax.psum_scatter(
-            ffn_grads[0].reshape(hidden, width).astype(F32), ("seq", "head"), scatter_dimension=0, tiled=True
+        ffn_sum = lax.psum_scatter(
+            ffn_grads[0].astype(F32).reshape(4, 2, width, width), ("seq", "head"), scatter_dimension=2, tiled=True
         )
-        shrink_grad = lax.psum_scatter(
-            ffn_grads[1].transpose(1, 2, 0, 3).reshape(width, hidden).astype(F32),
-            ("seq", "head"),
-            scatter_dimension=0,
-            tiled=True,
-        )
-        every = jnp.concatenate([first_grad[None], rest_grads[0]], axis=0).astype(F32)
+        every = jnp.concatenate([first_grads[0][None], rest_grads[0]], axis=0).astype(F32)
         every = jnp.stack([every[(z + slots - p) % slots] for p in range(slots)])
         pair_sum = lax.psum_scatter(every, "head", scatter_dimension=0, tiled=False)
         pair_sum = lax.psum_scatter(pair_sum, "seq", scatter_dimension=0, tiled=True)
 
     sums = jnp.sum(lax.all_to_all(sums, ("seq", "head"), 0, 0, tiled=True), axis=0)
-    vector = [sums[i * share : (i + 1) * share] for i in range(5)]
+    vector = [sums[0, i * share : (i + 1) * share] for i in range(5)]
+    shrink_grad = ffn_sum[:, 1].reshape(4, share, devices, share).transpose(2, 0, 3, 1)
     return (
         result,
         input_grad,
@@ -836,9 +823,9 @@
         pair_sum[:, 4 * PAIR :].T,
         vector[2],
         vector[3],
-        expand_grad.T,
-        sums[128 : 128 + hidden_share],
-        shrink_grad.T,
+        ffn_sum[:, 0].reshape(hidden_share, width).T,
+        sums[1, :hidden_share],
+        shrink_grad.reshape(devices * hidden_share, share),
         vector[4],
     )
 

time: 216 us -> 227 us (1.051)
  waiting for transfers between devices: 61.8 us -> 79.1 us
  local copies, waits for them, and re-layouts: 15.9 us -> 9.73 us
  starting transfers between devices: 40.1 us -> 44.9 us
  Pallas kernels: 88.5 us -> 85.1 us
    ppermute x6 -> x9, waiting for transfers between devices: 0.02 us -> 26.9 us  [join_chips(): lax.ppermute(m, 'seq', flip(seqs, 2 * r + 2))]
    ppermute x3, waiting for transfers between devices: 0.52 us -> 16.4 us  [body(): lax.ppermute(piece, 'head', turn(slots, a))]
    ppermute x17 -> x20, waiting for transfers between devices: 36.6 us -> 23.6 us  [send(): return lax.ppermute(v, 'seq', flip(seqs, bit))]
    ppermute x3, waiting for transfers between devices: 7.73 us -> 0.01 us  [body(): lax.ppermute(load, 'head', turn(slots, a))]
    all_to_all x1, waiting for transfers between devices: 0.01 us -> 7.2 us  [body(): ffn_sum = add(*lax.all_to_all(ffn_mine, 'head', 0, 0, tiled=True))]
    ppermute x3, waiting for transfers between devices: 6.64 us -> 0.01 us  [body(): lax.ppermute(low(rest[a - 1]), 'head', turn(slots, slots - a))]
    concatenate x2 -> x1, local copies, waits for them, and re-layouts: 4.82 us -> 0.01 us  [body(): pieces = across(part_a, part_b, lambda *m: jnp.concatenate(m, axis=0), seqs)]
    ppermute x2 -> x3, waiting for transfers between devices: 4.25 us -> 0.01 us  [join_cores(): other = lax.ppermute(send, 'seq', flip(seqs, 1))]
  transfers between devices with their start and end apart: 36 -> 43, of which waited for: 13 -> 17; matrix products, arithmetic and copies ran while one was open for 6% -> 4% of each run, Pallas kernels for 29% -> 9%
where the time goes in v3:
time: 227 us; the launch traced here: 226 us
  Pallas kernels  85.1 us (37%)
  waiting for transfers between devices  79.1 us (35%)
  starting transfers between devices  44.9 us (20%)
  local copies, waits for them, and re-layouts  9.73 us (4%)
  other arithmetic  5.93 us (3%)
    ppermute x9, waiting for transfers between devices, join_chips(): lax.ppermute(m, 'seq', flip(seqs, 2 * r + 2))  26.9 us
    pallas_call x1, Pallas kernels, feed_forward(): pl.pallas_call(functools.partial(ffn_kernel, len(pieces)), grid=(4,), out...  26 us
    pallas_call x1, Pallas kernels, backward_rest(): pl.pallas_call(functools.partial(back_rest_kernel, len(waits), len(grads)...  25.1 us
    ppermute x20, waiting for transfers between devices, send(): return lax.ppermute(v, 'seq', flip(seqs, bit))  23.6 us
    ppermute x3, waiting for transfers between devices, body(): lax.ppermute(piece, 'head', turn(slots, a))  16.4 us
    pallas_call x1, Pallas kernels, forward(): pl.pallas_call(functools.partial(forward_kernel, len(pieces), slots), gri...  15.6 us
    pallas_call x1, Pallas kernels, backward_first(): pl.pallas_call(functools.partial(back_first_kernel, len(waits), len(grad_...  12.7 us
    ppermute x20, starting transfers between devices, send(): return lax.ppermute(v, 'seq', flip(seqs, bit))  11.4 us
  transfers between devices with their start and end apart: 43, of which 17 were waited for; matrix products, arithmetic and copies ran while one was open for 4% of the time, Pallas kernels for 9%

profile of v3, /device:TPU:0, one launch (start us, length us, event | category | flops | bytes accessed | tf_op | source)
XLA Modules:
  0.0 226.2 jit_solution(9976646802059413905)
XLA Ops:
  0.8 1.4 reshape.91
  2.2 0.8 stack_reshape.7
  3.0 4.1 %collective-permute-start.14 = (bf16[4,2,16,512]{3,2,1,0:T(8,128)(2,1)S(1)}, bf16[4,2,16,512]{3,2,1,0:T(8,128)(2,1)S(1)}, u32[]{:S(2)}, u32[]{:S(2)}) collective-permute-start(bf16[4,2,16,512]{3,2,1,0:T(8,128)(2,1)S(1)} %pad_maximum_fusion.6), channel_id=1, source_target_pairs={{0,2},{1,3},{2,0},{3,1},{4,6},{5,7},{6,4},{7,5},{8,10},{9,11},{10,... | collective-permute-start | bytes 393224 | tf_op jit(solution)/shard_map/ppermute | solution.py:759
  7.1 1.6 collective-permute-start.13
  8.7 2.2 collective-permute-start.15
  11.4 0.6 collective-permute-start
  11.9 13.5 %collective-permute-done.1 = bf16[96,512]{1,0:T(8,128)(2,1)S(1)} collective-permute-done((bf16[96,512]{1,0:T(8,128)(2,1)S(1)}, bf16[96,512]{1,0:T(8,128)(2,1)S(1)}, u32[]{:S(2)}, u32[]{:S(2)}) %collective-permute-start.1) | collective-permute-done | bytes 98336 | tf_op jit(solution)/shard_map/ppermute | solution.py:754
  25.4 1.5 collective-permute-start.2
  27.1 3.0 %collective-permute-done.2 = bf16[96,512]{1,0:T(8,128)(2,1)S(1)} collective-permute-done((bf16[96,512]{1,0:T(8,128)(2,1)S(1)}, bf16[96,512]{1,0:T(8,128)(2,1)S(1)}, u32[]{:S(2)}, u32[]{:S(2)}) %collective-permute-start.2) | collective-permute-done | bytes 98336 | tf_op jit(solution)/shard_map/ppermute | solution.py:754
  30.0 1.5 collective-permute-start.3
  31.8 1.6 collective-permute-start.4
  33.5 0.6 collective-permute-start.17
  34.1 4.4 %collective-permute-done.4.refs_3_ = bf16[144,512]{1,0:T(8,128)(2,1)S(1)} collective-permute-done((bf16[144,512]{1,0:T(8,128)(2,1)S(1)}, bf16[144,512]{1,0:T(8,128)(2,1)S(1)}, u32[]{:S(2)}, u32[]{:S(2)}) %collective-permute-start.4) | collective-permute-done | bytes 147488 | tf_op jit(solution)/shard_map/ppermute | solution.py:691
  38.5 0.5 collective-permute-start.16
  39.1 4.6 %collective-permute-done.17.refs_3_ = bf16[4,2,2,16,512]{4,3,2,1,0:T(8,128)(2,1)S(1)} collective-permute-done((bf16[4,2,2,16,512]{4,3,2,1,0:T(8,128)(2,1)S(1)}, bf16[4,2,2,16,512]{4,3,2,1,0:T(8,128)(2,1)S(1)}, u32[]{:S(2)}, u32[]{:S(2)}) %collective-permute-start.17) | collective-permute-done | bytes 262176 | tf_op jit(solution)/shard_map/ppermute | solution.py:691
  43.7 1.5 collective-permute-start.5
  45.3 0.7 collective-permute-done.16.refs_2_
  46.0 0.5 collective-permute-start.6
  46.6 1.7 collective-permute-start.18
  48.2 1.5 collective-permute-start.19
  49.7 4.6 %collective-permute-done.5.refs_4_ = bf16[320,512]{1,0:T(8,128)(2,1)S(1)} collective-permute-done((bf16[320,512]{1,0:T(8,128)(2,1)S(1)}, bf16[320,512]{1,0:T(8,128)(2,1)S(1)}, u32[]{:S(2)}, u32[]{:S(2)}) %collective-permute-start.5) | collective-permute-done | bytes 327712 | tf_op jit(solution)/shard_map/ppermute | solution.py:691
  54.3 0.5 collective-permute-start.10
  54.8 1.1 collective-permute-done.6.refs_5_
  56.5 1.3 collective-permute-done.9.refs_8_
  57.9 0.4 collective-permute-start.23
  58.3 6.0 %collective-permute-done.18.refs_4_ = bf16[2,4,2,2,16,512]{5,4,3,2,1,0:T(8,128)(2,1)S(1)} collective-permute-done((bf16[2,4,2,2,16,512]{5,4,3,2,1,0:T(8,128)(2,1)S(1)}, bf16[2,4,2,2,16,512]{5,4,3,2,1,0:T(8,128)(2,1)S(1)}, u32[]{:S(2)}, u32[]{:S(2)}) %collective-permute-start.18) | collective-permute-done | bytes 524320 | tf_op jit(solution)/shard_map/ppermute | solution.py:691
  64.3 0.7 collective-permute-done.19.refs_5_
  65.0 0.5 collective-permute-start.25
  65.8 15.6 %attend_forward.1 = (bf16[1024,512]{1,0:T(8,128)(2,1)}, f32[1024,512]{1,0:T(8,128)}, bf16[32,256]{1,0:T(8,128)(2,1)}, bf16[4,640,512]{2,1,0:T(8,128)(2,1)}, bf16...) custom-call(bf16[1024,512]{1,0:T(8,128)(2,1)} %tokens_ref.3, ...), custom_call_target="tpu_custom_call" | custom-call | flops 16000000000 | bytes 16000000 | tf_op jit(solution)/shard_map/attend_forward/pallas_call | solution.py:350
  81.6 0.6 copy-done.37
  82.8 26.0 %feed_forward.1 = (bf16[1024,512]{1,0:T(8,128)(2,1)}, f32[1024,512]{1,0:T(8,128)}, bf16[1024,512]{1,0:T(8,128)(2,1)}, f32[32,256]{1,0:T(8,128)}, bf16[4,4,4,2,16...) custom-call(f32[1024,512]{1,0:T(8,128)} %get-tuple-element.44.residual_ref, ...), custom_call_target="tpu_custom_call" | custom-call | flops 25999998976 | bytes 26000000 | tf_op jit(solution)/shard_map/feed_forward/pallas_call | solution.py:508
  108.8 0.5 collective-permute-start.26
  109.4 5.7 %heads_back.1 = (bf16[4,1024,128]{2,1,0:T(8,128)(2,1)}, bf16[4,512,128]{2,1,0:T(8,128)(2,1)}) custom-call(bf16[1024,512]{1,0:T(8,128)(2,1)} %get-tuple-element.51.branch_ref, bf16[4,640,512]{2,1,0:T(8,128)(2,1)} %get-tuple-element.50.weight_ref.refs_3_.refs_4_, bf16[4,1024,128]{2,1,0:T(8,128)(2,1)} %get-tuple-element.52.heads_ref), custom_call_target="tpu_custom_call" | custom-call | flops 4000000000 | bytes 4000000 | tf_op jit(solution)/shard_map/heads_back/pallas_call | solution.py:550
  115.1 1.7 fusion.5
  116.7 25.1 %attend_back_rest.1 = (f32[1024,512]{1,0:T(8,128)}, bf16[4,3,64,640]{3,2,1,0:T(8,128)(2,1)}, bf16[4,3,64,640]{3,2,1,0:T(8,128)(2,1)}) custom-call(bf16[1024,512]{1,0:T(8,128)(2,1)} %get-tuple-element.47.normed_ref, bf16[4,4,2,16,512]{4,3,2,1,0:T(8,128)(2,1)} %get-tuple-element.75.refs_0_, bf16[4,4,2,16,512]{4,3,2,1,0:T(8,128)(2,1)} %get-tuple-element.74.refs_1_, ...), custom_call_target="tpu_custom_call" | custom-call | flops 28000000000 | bytes 28000000 | tf_op jit(solution)/shard_map/attend_back_rest/pallas_call | solution.py:618
  141.9 1.3 collective-permute-start.29
  143.2 0.8 collective-permute-start.28
  144.0 1.5 collective-permute-start.27
  145.5 12.2 %collective-permute-done.29 = bf16[4,4,2,16,512]{4,3,2,1,0:T(8,128)(2,1)S(1)} collective-permute-done((bf16[4,4,2,16,512]{4,3,2,1,0:T(8,128)(2,1)S(1)}, bf16[4,4,2,16,512]{4,3,2,1,0:T(8,128)(2,1)S(1)}, u32[]{:S(2)}, u32[]{:S(2)}) %collective-permute-start.29) | collective-permute-done | bytes 524320 | tf_op jit(solution)/shard_map/ppermute | solution.py:705
  157.6 10.6 %collective-permute-done.28 = bf16[4,4,2,16,512]{4,3,2,1,0:T(8,128)(2,1)S(1)} collective-permute-done((bf16[4,4,2,16,512]{4,3,2,1,0:T(8,128)(2,1)S(1)}, bf16[4,4,2,16,512]{4,3,2,1,0:T(8,128)(2,1)S(1)}, u32[]{:S(2)}, u32[]{:S(2)}) %collective-permute-start.28) | collective-permute-done | bytes 524320 | tf_op jit(solution)/shard_map/ppermute | solution.py:705
  168.2 1.3 fusion.2.refs_0_
  169.5 1.0 fusion.11
  170.5 12.7 %attend_back_first.1 = (bf16[1024,512]{1,0:T(8,128)(2,1)}, f32[32,8,128]{2,1,0:T(8,128)}, bf16[4,64,640]{2,1,0:T(8,128)(2,1)}, bf16[4,64,640]{2,1,0:T(8,128)(2,1)}) custom-call(bf16[1024,512]{1,0:T(8,128)(2,1)} %get-tuple-element.47.normed_ref, bf16[1024,512]{1,0:T(8,128)(2,1)} %tokens_ref.3, bf16[32,256]{1,0:T(8,128)(2,1)} %get-tuple-element.45.vectors_ref, ...), custom_call_target="tpu_custom_call" | custom-call | flops 14000000000 | bytes 14000000 | tf_op jit(solution)/shard_map/attend_back_first/pallas_call | solution.py:664
  183.2 4.3 %all-to-all-start = ((f32[32,8,128]{2,1,0:T(8,128)}), f32[32,8,128]{2,1,0:T(8,128)S(1)}, u32[]{:S(2)}, u32[]{:S(2)}) async-start(f32[32,8,128]{2,1,0:T(8,128)} %get-tuple-element.70), calls=%async_computation | async-start | bytes 262144 | tf_op jit(solution)/shard_map/all_to_all | solution.py:811
  187.5 2.7 %collective-permute-start.37 = (bf16[3,64,640]{2,1,0:T(8,128)(2,1)}, bf16[3,64,640]{2,1,0:T(8,128)(2,1)}, u32[]{:S(2)}, u32[]{:S(2)}) collective-permute-start(bf16[3,64,640]{2,1,0:T(8,128)(2,1)} %get-tuple-element.76.refs_3_), channel_id=1, source_target_pairs={{0,24},{4,28},{8,16},{12,20},{16,8},{20,12},{24,0},{28,4},{1,25},{... | collective-permute-start | bytes 737288 | tf_op jit(solution)/shard_map/ppermute | solution.py:705
  190.2 0.6 collective-permute-start.36
  191.1 4.9 %all-to-all-done = f32[32,8,128]{2,1,0:T(8,128)S(1)} async-done(((f32[32,8,128]{2,1,0:T(8,128)}), f32[32,8,128]{2,1,0:T(8,128)S(1)}, u32[]{:S(2)}, u32[]{:S(2)}) %all-to-all-start) | async-done | bytes 131104 | tf_op jit(solution)/shard_map/all_to_all | solution.py:811
  195.9 3.5 %all-to-all-start.1 = ((bf16[4,4,2,16,512]{4,3,2,1,0:T(8,128)(2,1)}), bf16[4,4,2,16,512]{4,3,2,1,0:T(8,128)(2,1)S(1)}, u32[]{:S(2)}, u32[]{:S(2)}) async-start(bf16[4,4,2,16,512]{4,3,2,1,0:T(8,128)(2,1)} %fusion.2.refs_0_), calls=%async_computation.1 | async-start | bytes 1048576 | tf_op jit(solution)/shard_map/all_to_all | solution.py:796
  199.4 3.8 %collective-permute-done.36 = bf16[3,64,640]{2,1,0:T(8,128)(2,1)} collective-permute-done((bf16[3,64,640]{2,1,0:T(8,128)(2,1)}, bf16[3,64,640]{2,1,0:T(8,128)(2,1)}, u32[]{:S(2)}, u32[]{:S(2)}) %collective-permute-start.36) | collective-permute-done | bytes 245792 | tf_op jit(solution)/shard_map/ppermute | solution.py:705
  203.2 1.3 fusion.8
  204.6 0.7 slice_bitcast_fusion.2
  205.3 3.3 %collective-permute-start.38 = (bf16[64,640]{1,0:T(8,128)(2,1)S(1)}, bf16[64,640]{1,0:T(8,128)(2,1)S(1)}, u32[]{:S(2)}, u32[]{:S(2)}) collective-permute-start(bf16[64,640]{1,0:T(8,128)(2,1)S(1)} %get-tuple-element.88), channel_id=1, source_target_pairs={{0,3},{1,0},{2,1},{3,2},{4,7},{5,4},{6,5},{7,6},{8,11},{9,8},{10,9... | collective-permute-start | bytes 245768 | tf_op jit(solution)/shard_map/ppermute | solution.py:799
  208.6 1.1 collective-permute-start.39
  209.8 0.6 slice_bitcast_fusion.10
  210.4 0.5 slice_bitcast_fusion.11
  210.9 7.2 %all-to-all-done.1 = bf16[4,4,2,16,512]{4,3,2,1,0:T(8,128)(2,1)S(1)} async-done(((bf16[4,4,2,16,512]{4,3,2,1,0:T(8,128)(2,1)}), bf16[4,4,2,16,512]{4,3,2,1,0:T(8,128)(2,1)S(1)}, u32[]{:S(2)}, u32[]{:S(2)}) %all-to-all-start.1) | async-done | bytes 524320 | tf_op jit(solution)/shard_map/all_to_all | solution.py:796
  218.3 1.0 collective-permute-start.32
  219.3 1.6 collective-permute-start.34
  220.9 0.9 collective-permute-start.33
  221.8 0.7 fusion.26
  222.5 0.4 reshape_squeeze.7
  222.9 0.7 copy.34
  223.6 1.6 reshape.92
  225.6 0.7 slice_bitcast_fusion.9
  (159 shorter events, 3.5 us)
Async XLA Ops:
  3.0 28.6 %collective-permute-start.14 = (bf16[4,2,16,512]{3,2,1,0:T(8,128)(2,1)S(1)}, bf16[4,2,16,512]{3,2,1,0:T(8,128)(2,1)S(1)}, u32[]{:S(2)}, u32[]{:S(2)}) collective-permute-start(bf16[4,2,16,512]{3,2,1,0:T(8,128)(2,1)S(1)} %pad_maximum_fusion.6), channel_id=1, source_target_pairs={{0,2},{1,3},{2,0},{3,1},{4,6},{5,7},{6,4},{7,5},{8,10},{9,11},{10,... | collective-permute-start | bytes 393224 | tf_op jit(solution)/shard_map/ppermute | solution.py:759
  7.1 24.6 %collective-permute-start.13 = (bf16[4,2,16,512]{3,2,1,0:T(8,128)(2,1)S(1)}, bf16[4,2,16,512]{3,2,1,0:T(8,128)(2,1)S(1)}, u32[]{:S(2)}, u32[]{:S(2)}) collective-permute-start(bf16[4,2,16,512]{3,2,1,0:T(8,128)(2,1)S(1)} %pad_maximum_fusion.6), channel_id=1, source_target_pairs={{0,1},{1,2},{2,3},{3,0},{4,5},{5,6},{6,7},{7,4},{8,9},{9,10},{10,1... | collective-permute-start | bytes 393224 | tf_op jit(solution)/shard_map/ppermute | solution.py:759
  8.7 24.7 %collective-permute-start.15 = (bf16[4,2,16,512]{3,2,1,0:T(8,128)(2,1)S(1)}, bf16[4,2,16,512]{3,2,1,0:T(8,128)(2,1)S(1)}, u32[]{:S(2)}, u32[]{:S(2)}) collective-permute-start(bf16[4,2,16,512]{3,2,1,0:T(8,128)(2,1)S(1)} %pad_maximum_fusion.6), channel_id=1, source_target_pairs={{0,3},{1,0},{2,1},{3,2},{4,7},{5,4},{6,5},{7,6},{8,11},{9,8},{10,9... | collective-permute-start | bytes 393224 | tf_op jit(solution)/shard_map/ppermute | solution.py:759
  11.2 27.8 %copy-start.2 = (bf16[640,512]{1,0:T(8,128)(2,1)}, bf16[640,512]{1,0:T(8,128)(2,1)S(1)}, u32[]{:S(2)}) copy-start(bf16[640,512]{1,0:T(8,128)(2,1)S(1)} %pad_maximum_fusion.own_ref) | copy-start | bytes 1966084
  11.3 14.2 %collective-permute-start.1 = (bf16[96,512]{1,0:T(8,128)(2,1)S(1)}, bf16[96,512]{1,0:T(8,128)(2,1)S(1)}, u32[]{:S(2)}, u32[]{:S(2)}) collective-permute-start(bf16[96,512]{1,0:T(8,128)(2,1)S(1)} %pad_maximum_fusion.8), channel_id=1, source_target_pairs={{0,2},{1,3},{2,0},{3,1},{4,6},{5,7},{6,4},{7,5},{8,10},{9,11},{10,... | collective-permute-start | bytes 294920 | tf_op jit(solution)/shard_map/ppermute | solution.py:754
  11.4 15.6 %collective-permute-start = (bf16[96,512]{1,0:T(8,128)(2,1)S(1)}, bf16[96,512]{1,0:T(8,128)(2,1)S(1)}, u32[]{:S(2)}, u32[]{:S(2)}) collective-permute-start(bf16[96,512]{1,0:T(8,128)(2,1)S(1)} %pad_maximum_fusion.8), channel_id=1, source_target_pairs={{0,1},{1,2},{2,3},{3,0},{4,5},{5,6},{6,7},{7,4},{8,9},{9,10},{10,1... | collective-permute-start | bytes 294920 | tf_op jit(solution)/shard_map/ppermute | solution.py:754
  25.4 4.6 %collective-permute-start.2 = (bf16[96,512]{1,0:T(8,128)(2,1)S(1)}, bf16[96,512]{1,0:T(8,128)(2,1)S(1)}, u32[]{:S(2)}, u32[]{:S(2)}) collective-permute-start(bf16[96,512]{1,0:T(8,128)(2,1)S(1)} %pad_maximum_fusion.8), channel_id=1, source_target_pairs={{0,3},{1,0},{2,1},{3,2},{4,7},{5,4},{6,5},{7,6},{8,11},{9,8},{10,9... | collective-permute-start | bytes 294920 | tf_op jit(solution)/shard_map/ppermute | solution.py:754
  27.0 18.3 %copy-start.14 = (bf16[160,512]{1,0:T(8,128)(2,1)}, bf16[160,512]{1,0:T(8,128)(2,1)S(1)}, u32[]{:S(2)}) copy-start(bf16[160,512]{1,0:T(8,128)(2,1)S(1)} %pad_maximum_fusion.7.refs_0_) | copy-start | bytes 491524
  27.0 21.2 %collective-permute-start.7 = (bf16[160,512]{1,0:T(8,128)(2,1)S(1)}, bf16[160,512]{1,0:T(8,128)(2,1)S(1)}, u32[]{:S(2)}, u32[]{:S(2)}) collective-permute-start(bf16[160,512]{1,0:T(8,128)(2,1)S(1)} %pad_maximum_fusion.7.refs_0_), channel_id=1, source_target_pairs={{0,4},{4,0},{8,12},{12,8},{16,20},{20,16},{24,28},{28,24},{1,5},{5... | collective-permute-start | bytes 491528 | tf_op jit(solution)/shard_map/ppermute | solution.py:691
  30.0 9.0 %collective-permute-start.3 = (bf16[160,512]{1,0:T(8,128)(2,1)S(1)}, bf16[160,512]{1,0:T(8,128)(2,1)S(1)}, u32[]{:S(2)}, u32[]{:S(2)}) collective-permute-start(bf16[160,512]{1,0:T(8,128)(2,1)S(1)} %pad_maximum_fusion.7.refs_0_), channel_id=1, source_target_pairs={{0,8},{4,12},{8,0},{12,4},{16,24},{20,28},{24,16},{28,20},{1,9},{5... | collective-permute-start | bytes 491528 | tf_op jit(solution)/shard_map/ppermute | solution.py:691
  31.7 13.6 %copy-start.21 = (bf16[144,512]{1,0:T(8,128)(2,1)}, bf16[144,512]{1,0:T(8,128)(2,1)S(1)}, u32[]{:S(2)}) copy-start(bf16[144,512]{1,0:T(8,128)(2,1)S(1)} %get-tuple-element.118.refs_1_) | copy-start | bytes 442372
  31.7 14.9 %collective-permute-start.8 = (bf16[144,512]{1,0:T(8,128)(2,1)S(1)}, bf16[144,512]{1,0:T(8,128)(2,1)S(1)}, u32[]{:S(2)}, u32[]{:S(2)}) collective-permute-start(bf16[144,512]{1,0:T(8,128)(2,1)S(1)} %get-tuple-element.118.refs_1_), channel_id=1, source_target_pairs={{0,4},{4,0},{8,12},{12,8},{16,20},{20,16},{24,28},{28,24},{1,5},{5... | collective-permute-start | bytes 442376 | tf_op jit(solution)/shard_map/ppermute | solution.py:691
  31.8 6.7 %collective-permute-start.4 = (bf16[144,512]{1,0:T(8,128)(2,1)S(1)}, bf16[144,512]{1,0:T(8,128)(2,1)S(1)}, u32[]{:S(2)}, u32[]{:S(2)}) collective-permute-start(bf16[144,512]{1,0:T(8,128)(2,1)S(1)} %get-tuple-element.118.refs_1_), channel_id=1, source_target_pairs={{0,16},{4,20},{8,24},{12,28},{16,0},{20,4},{24,8},{28,12},{1,17},{... | collective-permute-start | bytes 442376 | tf_op jit(solution)/shard_map/ppermute | solution.py:691
  33.5 47.9 %copy-start.7 = (bf16[4,2,2,16,512]{4,3,2,1,0:T(8,128)(2,1)}, bf16[4,2,2,16,512]{4,3,2,1,0:T(8,128)(2,1)S(1)}, u32[]{:S(2)}) copy-start(bf16[4,2,2,16,512]{4,3,2,1,0:T(8,128)(2,1)S(1)} %get-tuple-element.85.refs_1_) | copy-start | bytes 786436
  33.5 10.2 %collective-permute-start.17 = (bf16[4,2,2,16,512]{4,3,2,1,0:T(8,128)(2,1)S(1)}, bf16[4,2,2,16,512]{4,3,2,1,0:T(8,128)(2,1)S(1)}, u32[]{:S(2)}, u32[]{:S(2)}) collective-permute-start(bf16[4,2,2,16,512]{4,3,2,1,0:T(8,128)(2,1)S(1)} %get-tuple-element.85.refs_1_), channel_id=1, source_target_pairs={{0,16},{4,20},{8,24},{12,28},{16,0},{20,4},{24,8},{28,12},{1,17},{... | collective-permute-start | bytes 786440 | tf_op jit(solution)/shard_map/ppermute | solution.py:691
  34.1 47.3 %copy-start.8 = (bf16[4,2,2,16,512]{4,3,2,1,0:T(8,128)(2,1)}, bf16[4,2,2,16,512]{4,3,2,1,0:T(8,128)(2,1)S(1)}, u32[]{:S(2)}) copy-start(bf16[4,2,2,16,512]{4,3,2,1,0:T(8,128)(2,1)S(1)} %get-tuple-element.87.refs_0_) | copy-start | bytes 786436
  38.5 27.0 %copy-start.15 = (bf16[144,512]{1,0:T(8,128)(2,1)}, bf16[144,512]{1,0:T(8,128)(2,1)S(1)}, u32[]{:S(2)}) copy-start(bf16[144,512]{1,0:T(8,128)(2,1)S(1)} %collective-permute-done.4.refs_3_) | copy-start | bytes 442372
  38.5 7.5 %collective-permute-start.16 = (bf16[4,2,2,16,512]{4,3,2,1,0:T(8,128)(2,1)S(1)}, bf16[4,2,2,16,512]{4,3,2,1,0:T(8,128)(2,1)S(1)}, u32[]{:S(2)}, u32[]{:S(2)}) collective-permute-start(bf16[4,2,2,16,512]{4,3,2,1,0:T(8,128)(2,1)S(1)} %get-tuple-element.87.refs_0_), channel_id=1, source_target_pairs={{0,8},{4,12},{8,0},{12,4},{16,24},{20,28},{24,16},{28,20},{1,9},{5... | collective-permute-start | bytes 786440 | tf_op jit(solution)/shard_map/ppermute | solution.py:691
  39.0 26.5 %copy-start.13 = (bf16[160,512]{1,0:T(8,128)(2,1)}, bf16[160,512]{1,0:T(8,128)(2,1)S(1)}, u32[]{:S(2)}) copy-start(bf16[160,512]{1,0:T(8,128)(2,1)S(1)} %collective-permute-done.3.refs_2_) | copy-start | bytes 491524
  39.0 15.3 %collective-permute-start.21 = (bf16[4,2,2,16,512]{4,3,2,1,0:T(8,128)(2,1)S(1)}, bf16[4,2,2,16,512]{4,3,2,1,0:T(8,128)(2,1)S(1)}, u32[]{:S(2)}, u32[]{:S(2)}) collective-permute-start(bf16[4,2,2,16,512]{4,3,2,1,0:T(8,128)(2,1)S(1)} %get-tuple-element.85.refs_1_), channel_id=1, source_target_pairs={{0,4},{4,0},{8,12},{12,8},{16,20},{20,16},{24,28},{28,24},{1,5},{5... | collective-permute-start | bytes 786440 | tf_op jit(solution)/shard_map/ppermute | solution.py:691
  43.7 37.7 %copy-start.9 = (bf16[4,2,2,16,512]{4,3,2,1,0:T(8,128)(2,1)}, bf16[4,2,2,16,512]{4,3,2,1,0:T(8,128)(2,1)S(1)}, u32[]{:S(2)}) copy-start(bf16[4,2,2,16,512]{4,3,2,1,0:T(8,128)(2,1)S(1)} %collective-permute-done.17.refs_3_) | copy-start | bytes 786436
  43.7 10.6 %collective-permute-start.5 = (bf16[320,512]{1,0:T(8,128)(2,1)S(1)}, bf16[320,512]{1,0:T(8,128)(2,1)S(1)}, u32[]{:S(2)}, u32[]{:S(2)}) collective-permute-start(bf16[320,512]{1,0:T(8,128)(2,1)S(1)} %pad_maximum_fusion.3), channel_id=1, source_target_pairs={{0,16},{4,20},{8,24},{12,28},{16,0},{20,4},{24,8},{28,12},{1,17},{... | collective-permute-start | bytes 983048 | tf_op jit(solution)/shard_map/ppermute | solution.py:691
  46.0 35.4 %copy-start.10 = (bf16[4,2,2,16,512]{4,3,2,1,0:T(8,128)(2,1)}, bf16[4,2,2,16,512]{4,3,2,1,0:T(8,128)(2,1)S(1)}, u32[]{:S(2)}) copy-start(bf16[4,2,2,16,512]{4,3,2,1,0:T(8,128)(2,1)S(1)} %collective-permute-done.16.refs_2_) | copy-start | bytes 786436
  46.0 9.9 %collective-permute-start.6 = (bf16[288,512]{1,0:T(8,128)(2,1)S(1)}, bf16[288,512]{1,0:T(8,128)(2,1)S(1)}, u32[]{:S(2)}, u32[]{:S(2)}) collective-permute-start(bf16[288,512]{1,0:T(8,128)(2,1)S(1)} %constant_dynamic-update-slice_fusion.4), channel_id=1, source_target_pairs={{0,8},{4,12},{8,0},{12,4},{16,24},{20,28},{24,16},{28,20},{1,9},{5... | collective-permute-start | bytes 884744 | tf_op jit(solution)/shard_map/ppermute | solution.py:691
  46.6 18.9 %copy-start.42 = (bf16[144,512]{1,0:T(8,128)(2,1)}, bf16[144,512]{1,0:T(8,128)(2,1)S(1)}, u32[]{:S(2)}) copy-start(bf16[144,512]{1,0:T(8,128)(2,1)S(1)} %collective-permute-done.8.refs_7_) | copy-start | bytes 442372
  46.6 17.7 %collective-permute-start.18 = (bf16[2,4,2,2,16,512]{5,4,3,2,1,0:T(8,128)(2,1)S(1)}, bf16[2,4,2,2,16,512]{5,4,3,2,1,0:T(8,128)(2,1)S(1)}, u32[]{:S(2)}, u32[]{:S(2)}) collective-permute-start(bf16[2,4,2,2,16,512]{5,4,3,2,1,0:T(8,128)(2,1)S(1)} %pad_maximum_fusion.1), channel_id=1, source_target_pairs={{0,16},{4,20},{8,24},{12,28},{16,0},{20,4},{24,8},{28,12},{1,17},{... | collective-permute-start | bytes 1572872 | tf_op jit(solution)/shard_map/ppermute | solution.py:691
  48.2 17.3 %copy-start.40 = (bf16[160,512]{1,0:T(8,128)(2,1)}, bf16[160,512]{1,0:T(8,128)(2,1)S(1)}, u32[]{:S(2)}) copy-start(bf16[160,512]{1,0:T(8,128)(2,1)S(1)} %collective-permute-done.7.refs_6_) | copy-start | bytes 491524
  48.2 16.7 %collective-permute-start.19 = (bf16[2,4,2,2,16,512]{5,4,3,2,1,0:T(8,128)(2,1)S(1)}, bf16[2,4,2,2,16,512]{5,4,3,2,1,0:T(8,128)(2,1)S(1)}, u32[]{:S(2)}, u32[]{:S(2)}) collective-permute-start(bf16[2,4,2,2,16,512]{5,4,3,2,1,0:T(8,128)(2,1)S(1)} %pad_maximum_fusion.2), channel_id=1, source_target_pairs={{0,8},{4,12},{8,0},{12,4},{16,24},{20,28},{24,16},{28,20},{1,9},{5... | collective-permute-start | bytes 1572872 | tf_op jit(solution)/shard_map/ppermute | solution.py:691
  54.3 11.2 %copy-start.32 = (bf16[320,512]{1,0:T(8,128)(2,1)}, bf16[320,512]{1,0:T(8,128)(2,1)S(1)}, u32[]{:S(2)}) copy-start(bf16[320,512]{1,0:T(8,128)(2,1)S(1)} %collective-permute-done.5.refs_4_) | copy-start | bytes 983044
  54.3 10.6 %collective-permute-start.11 = (bf16[320,512]{1,0:T(8,128)(2,1)S(1)}, bf16[320,512]{1,0:T(8,128)(2,1)S(1)}, u32[]{:S(2)}, u32[]{:S(2)}) collective-permute-start(bf16[320,512]{1,0:T(8,128)(2,1)S(1)} %collective-permute-done.5.refs_4_), channel_id=1, source_target_pairs={{0,4},{4,0},{8,12},{12,8},{16,20},{20,16},{24,28},{28,24},{1,5},{5... | collective-permute-start | bytes 983048 | tf_op jit(solution)/shard_map/ppermute | solution.py:691
  54.3 27.1 %copy-start.36 = (bf16[4,2,2,16,512]{4,3,2,1,0:T(8,128)(2,1)}, bf16[4,2,2,16,512]{4,3,2,1,0:T(8,128)(2,1)S(1)}, u32[]{:S(2)}) copy-start(bf16[4,2,2,16,512]{4,3,2,1,0:T(8,128)(2,1)S(1)} %collective-permute-done.21.refs_7_) | copy-start | bytes 786436
  54.3 1.8 collective-permute-start.10
  56.0 2.0 collective-permute-start.12
  56.2 1.6 collective-permute-start.9
  57.8 23.7 %collective-permute-start.20 = (bf16[4,2,2,16,512]{4,3,2,1,0:T(8,128)(2,1)S(1)}, bf16[4,2,2,16,512]{4,3,2,1,0:T(8,128)(2,1)S(1)}, u32[]{:S(2)}, u32[]{:S(2)}) collective-permute-start(bf16[4,2,2,16,512]{4,3,2,1,0:T(8,128)(2,1)S(1)} %get-tuple-element.87.refs_0_), channel_id=1, source_target_pairs={{0,4},{4,0},{8,12},{12,8},{16,20},{20,16},{24,28},{28,24},{1,5},{5... | collective-permute-start | bytes 786440 | tf_op jit(solution)/shard_map/ppermute | solution.py:691
  57.9 23.6 %collective-permute-start.23 = (bf16[4,2,2,16,512]{4,3,2,1,0:T(8,128)(2,1)S(1)}, bf16[4,2,2,16,512]{4,3,2,1,0:T(8,128)(2,1)S(1)}, u32[]{:S(2)}, u32[]{:S(2)}) collective-permute-start(bf16[4,2,2,16,512]{4,3,2,1,0:T(8,128)(2,1)S(1)} %collective-permute-done.17.refs_3_), channel_id=1, source_target_pairs={{0,4},{4,0},{8,12},{12,8},{16,20},{20,16},{24,28},{28,24},{1,5},{5... | collective-permute-start | bytes 786440 | tf_op jit(solution)/shard_map/ppermute | solution.py:691
  64.3 17.2 %copy-start.28 = (bf16[2,4,2,2,16,512]{5,4,3,2,1,0:T(8,128)(2,1)}, bf16[2,4,2,2,16,512]{5,4,3,2,1,0:T(8,128)(2,1)S(1)}, u32[]{:S(2)}) copy-start(bf16[2,4,2,2,16,512]{5,4,3,2,1,0:T(8,128)(2,1)S(1)} %collective-permute-done.18.refs_4_) | copy-start | bytes 1572868
  64.3 17.2 %collective-permute-start.22 = (bf16[4,2,2,16,512]{4,3,2,1,0:T(8,128)(2,1)S(1)}, bf16[4,2,2,16,512]{4,3,2,1,0:T(8,128)(2,1)S(1)}, u32[]{:S(2)}, u32[]{:S(2)}) collective-permute-start(bf16[4,2,2,16,512]{4,3,2,1,0:T(8,128)(2,1)S(1)} %collective-permute-done.16.refs_2_), channel_id=1, source_target_pairs={{0,4},{4,0},{8,12},{12,8},{16,20},{20,16},{24,28},{28,24},{1,5},{5... | collective-permute-start | bytes 786440 | tf_op jit(solution)/shard_map/ppermute | solution.py:691
  65.0 16.5 %copy-start.29 = (bf16[2,4,2,2,16,512]{5,4,3,2,1,0:T(8,128)(2,1)}, bf16[2,4,2,2,16,512]{5,4,3,2,1,0:T(8,128)(2,1)S(1)}, u32[]{:S(2)}) copy-start(bf16[2,4,2,2,16,512]{5,4,3,2,1,0:T(8,128)(2,1)S(1)} %collective-permute-done.19.refs_5_) | copy-start | bytes 1572868
  65.0 16.6 %collective-permute-start.24 = (bf16[2,4,2,2,16,512]{5,4,3,2,1,0:T(8,128)(2,1)S(1)}, bf16[2,4,2,2,16,512]{5,4,3,2,1,0:T(8,128)(2,1)S(1)}, u32[]{:S(2)}, u32[]{:S(2)}) collective-permute-start(bf16[2,4,2,2,16,512]{5,4,3,2,1,0:T(8,128)(2,1)S(1)} %collective-permute-done.18.refs_4_), channel_id=1, source_target_pairs={{0,4},{4,0},{8,12},{12,8},{16,20},{20,16},{24,28},{28,24},{1,5},{5... | collective-permute-start | bytes 1572872 | tf_op jit(solution)/shard_map/ppermute | solution.py:691
  65.0 16.6 %collective-permute-start.25 = (bf16[2,4,2,2,16,512]{5,4,3,2,1,0:T(8,128)(2,1)S(1)}, bf16[2,4,2,2,16,512]{5,4,3,2,1,0:T(8,128)(2,1)S(1)}, u32[]{:S(2)}, u32[]{:S(2)}) collective-permute-start(bf16[2,4,2,2,16,512]{5,4,3,2,1,0:T(8,128)(2,1)S(1)} %collective-permute-done.19.refs_5_), channel_id=1, source_target_pairs={{0,4},{4,0},{8,12},{12,8},{16,20},{20,16},{24,28},{28,24},{1,5},{5... | collective-permute-start | bytes 1572872 | tf_op jit(solution)/shard_map/ppermute | solution.py:691
  108.8 6.2 %collective-permute-start.26 = (bf16[4,4,4,2,16,512]{5,4,3,2,1,0:T(8,128)(2,1)}, bf16[4,4,4,2,16,512]{5,4,3,2,1,0:T(8,128)(2,1)S(1)}, u32[]{:S(2)}, u32[]{:S(2)}) collective-permute-start(bf16[4,4,4,2,16,512]{5,4,3,2,1,0:T(8,128)(2,1)} %get-tuple-element.49), channel_id=1, source_target_pairs={{0,4},{4,0},{8,12},{12,8},{16,20},{20,16},{24,28},{28,24},{1,5},{5... | collective-permute-start | bytes 6291464 | tf_op jit(solution)/shard_map/ppermute | solution.py:699
  116.7 25.2 %copy-start.5 = (bf16[4,4,2,16,512]{4,3,2,1,0:T(8,128)(2,1)S(1)}, bf16[4,4,2,16,512]{4,3,2,1,0:T(8,128)(2,1)}, u32[]{:S(2)}) copy-start(bf16[4,4,2,16,512]{4,3,2,1,0:T(8,128)(2,1)} %get-tuple-element.73.refs_2_) | copy-start | bytes 1572868
  116.7 26.5 %copy-start.4 = (bf16[4,4,2,16,512]{4,3,2,1,0:T(8,128)(2,1)S(1)}, bf16[4,4,2,16,512]{4,3,2,1,0:T(8,128)(2,1)}, u32[]{:S(2)}) copy-start(bf16[4,4,2,16,512]{4,3,2,1,0:T(8,128)(2,1)} %get-tuple-element.74.refs_1_) | copy-start | bytes 1572868
  116.7 27.2 %copy-start.3 = (bf16[4,4,2,16,512]{4,3,2,1,0:T(8,128)(2,1)S(1)}, bf16[4,4,2,16,512]{4,3,2,1,0:T(8,128)(2,1)}, u32[]{:S(2)}) copy-start(bf16[4,4,2,16,512]{4,3,2,1,0:T(8,128)(2,1)} %get-tuple-element.75.refs_0_) | copy-start | bytes 1572868
  141.8 27.7 %copy-start.1 = (bf16[4,3,64,640]{3,2,1,0:T(8,128)(2,1)S(1)}, bf16[4,3,64,640]{3,2,1,0:T(8,128)(2,1)}, u32[]{:S(2)}) copy-start(bf16[4,3,64,640]{3,2,1,0:T(8,128)(2,1)} %get-tuple-element.67) | copy-start | bytes 2949124
  141.8 27.7 %collective-permute-start.30 = (bf16[4,3,64,640]{3,2,1,0:T(8,128)(2,1)}, bf16[4,3,64,640]{3,2,1,0:T(8,128)(2,1)S(1)}, u32[]{:S(2)}, u32[]{:S(2)}) collective-permute-start(bf16[4,3,64,640]{3,2,1,0:T(8,128)(2,1)} %get-tuple-element.68), channel_id=1, source_target_pairs={{0,4},{4,0},{8,12},{12,8},{16,20},{20,16},{24,28},{28,24},{1,5},{5... | collective-permute-start | bytes 2949128 | tf_op jit(solution)/shard_map/ppermute | solution.py:699
  141.9 15.7 %collective-permute-start.29 = (bf16[4,4,2,16,512]{4,3,2,1,0:T(8,128)(2,1)S(1)}, bf16[4,4,2,16,512]{4,3,2,1,0:T(8,128)(2,1)S(1)}, u32[]{:S(2)}, u32[]{:S(2)}) collective-permute-start(bf16[4,4,2,16,512]{4,3,2,1,0:T(8,128)(2,1)S(1)} %copy-done.5), channel_id=1, source_target_pairs={{0,24},{4,28},{8,16},{12,20},{16,8},{20,12},{24,0},{28,4},{1,25},{... | collective-permute-start | bytes 1572872 | tf_op jit(solution)/shard_map/ppermute | solution.py:705
  143.2 25.1 %collective-permute-start.28 = (bf16[4,4,2,16,512]{4,3,2,1,0:T(8,128)(2,1)S(1)}, bf16[4,4,2,16,512]{4,3,2,1,0:T(8,128)(2,1)S(1)}, u32[]{:S(2)}, u32[]{:S(2)}) collective-permute-start(bf16[4,4,2,16,512]{4,3,2,1,0:T(8,128)(2,1)S(1)} %copy-done.4), channel_id=1, source_target_pairs={{0,16},{4,20},{8,24},{12,28},{16,0},{20,4},{24,8},{28,12},{1,17},{... | collective-permute-start | bytes 1572872 | tf_op jit(solution)/shard_map/ppermute | solution.py:705
  144.0 24.3 %collective-permute-start.27 = (bf16[4,4,2,16,512]{4,3,2,1,0:T(8,128)(2,1)S(1)}, bf16[4,4,2,16,512]{4,3,2,1,0:T(8,128)(2,1)S(1)}, u32[]{:S(2)}, u32[]{:S(2)}) collective-permute-start(bf16[4,4,2,16,512]{4,3,2,1,0:T(8,128)(2,1)S(1)} %copy-done.3), channel_id=1, source_target_pairs={{0,8},{4,12},{8,0},{12,4},{16,24},{20,28},{24,16},{28,20},{1,9},{5... | collective-permute-start | bytes 1572872 | tf_op jit(solution)/shard_map/ppermute | solution.py:705
  170.5 20.3 %copy-start.12 = (bf16[3,64,640]{2,1,0:T(8,128)(2,1)S(1)}, bf16[3,64,640]{2,1,0:T(8,128)(2,1)}, u32[]{:S(2)}) copy-start(bf16[3,64,640]{2,1,0:T(8,128)(2,1)} %get-tuple-element.78.refs_1_) | copy-start | bytes 737284
  183.2 35.0 %copy-start.6 = (bf16[4,64,640]{2,1,0:T(8,128)(2,1)S(1)}, bf16[4,64,640]{2,1,0:T(8,128)(2,1)}, u32[]{:S(2)}) copy-start(bf16[4,64,640]{2,1,0:T(8,128)(2,1)} %get-tuple-element.71) | copy-start | bytes 983044
  183.2 12.7 %all-to-all-start = ((f32[32,8,128]{2,1,0:T(8,128)}), f32[32,8,128]{2,1,0:T(8,128)S(1)}, u32[]{:S(2)}, u32[]{:S(2)}) async-start(f32[32,8,128]{2,1,0:T(8,128)} %get-tuple-element.70), calls=%async_computation | async-start | bytes 262144 | tf_op jit(solution)/shard_map/all_to_all | solution.py:811
  187.5 11.9 %collective-permute-start.37 = (bf16[3,64,640]{2,1,0:T(8,128)(2,1)}, bf16[3,64,640]{2,1,0:T(8,128)(2,1)}, u32[]{:S(2)}, u32[]{:S(2)}) collective-permute-start(bf16[3,64,640]{2,1,0:T(8,128)(2,1)} %get-tuple-element.76.refs_3_), channel_id=1, source_target_pairs={{0,24},{4,28},{8,16},{12,20},{16,8},{20,12},{24,0},{28,4},{1,25},{... | collective-permute-start | bytes 737288 | tf_op jit(solution)/shard_map/ppermute | solution.py:705
  190.2 13.0 %collective-permute-start.36 = (bf16[3,64,640]{2,1,0:T(8,128)(2,1)}, bf16[3,64,640]{2,1,0:T(8,128)(2,1)}, u32[]{:S(2)}, u32[]{:S(2)}) collective-permute-start(bf16[3,64,640]{2,1,0:T(8,128)(2,1)} %get-tuple-element.77.refs_2_), channel_id=1, source_target_pairs={{0,16},{4,20},{8,24},{12,28},{16,0},{20,4},{24,8},{28,12},{1,17},{... | collective-permute-start | bytes 737288 | tf_op jit(solution)/shard_map/ppermute | solution.py:705
  190.8 12.5 %collective-permute-start.35 = (bf16[3,64,640]{2,1,0:T(8,128)(2,1)S(1)}, bf16[3,64,640]{2,1,0:T(8,128)(2,1)}, u32[]{:S(2)}, u32[]{:S(2)}) collective-permute-start(bf16[3,64,640]{2,1,0:T(8,128)(2,1)S(1)} %copy-done.12), channel_id=1, source_target_pairs={{0,8},{4,12},{8,0},{12,4},{16,24},{20,28},{24,16},{28,20},{1,9},{5... | collective-permute-start | bytes 737288 | tf_op jit(solution)/shard_map/ppermute | solution.py:705
  191.0 27.1 %collective-permute-start.31 = (bf16[4,64,640]{2,1,0:T(8,128)(2,1)}, bf16[4,64,640]{2,1,0:T(8,128)(2,1)S(1)}, u32[]{:S(2)}, u32[]{:S(2)}) collective-permute-start(bf16[4,64,640]{2,1,0:T(8,128)(2,1)} %get-tuple-element.72), channel_id=1, source_target_pairs={{0,4},{4,0},{8,12},{12,8},{16,20},{20,16},{24,28},{28,24},{1,5},{5... | collective-permute-start | bytes 983048 | tf_op jit(solution)/shard_map/ppermute | solution.py:699
  195.9 22.2 %all-to-all-start.1 = ((bf16[4,4,2,16,512]{4,3,2,1,0:T(8,128)(2,1)}), bf16[4,4,2,16,512]{4,3,2,1,0:T(8,128)(2,1)S(1)}, u32[]{:S(2)}, u32[]{:S(2)}) async-start(bf16[4,4,2,16,512]{4,3,2,1,0:T(8,128)(2,1)} %fusion.2.refs_0_), calls=%async_computation.1 | async-start | bytes 1048576 | tf_op jit(solution)/shard_map/all_to_all | solution.py:796
  205.3 15.6 %collective-permute-start.38 = (bf16[64,640]{1,0:T(8,128)(2,1)S(1)}, bf16[64,640]{1,0:T(8,128)(2,1)S(1)}, u32[]{:S(2)}, u32[]{:S(2)}) collective-permute-start(bf16[64,640]{1,0:T(8,128)(2,1)S(1)} %get-tuple-element.88), channel_id=1, source_target_pairs={{0,3},{1,0},{2,1},{3,2},{4,7},{5,4},{6,5},{7,6},{8,11},{9,8},{10,9... | collective-permute-start | bytes 245768 | tf_op jit(solution)/shard_map/ppermute | solution.py:799
  208.6 16.6 %collective-permute-start.40 = (bf16[64,640]{1,0:T(8,128)(2,1)}, bf16[64,640]{1,0:T(8,128)(2,1)S(1)}, u32[]{:S(2)}, u32[]{:S(2)}) collective-permute-start(bf16[64,640]{1,0:T(8,128)(2,1)} %get-tuple-element.89), channel_id=1, source_target_pairs={{0,1},{1,2},{2,3},{3,0},{4,5},{5,6},{6,7},{7,4},{8,9},{9,10},{10,1... | collective-permute-start | bytes 245768 | tf_op jit(solution)/shard_map/ppermute | solution.py:799
  208.6 16.6 %collective-permute-start.39 = (bf16[64,640]{1,0:T(8,128)(2,1)}, bf16[64,640]{1,0:T(8,128)(2,1)S(1)}, u32[]{:S(2)}, u32[]{:S(2)}) collective-permute-start(bf16[64,640]{1,0:T(8,128)(2,1)} %get-tuple-element.90), channel_id=1, source_target_pairs={{0,2},{1,3},{2,0},{3,1},{4,6},{5,7},{6,4},{7,5},{8,10},{9,11},{10,... | collective-permute-start | bytes 245768 | tf_op jit(solution)/shard_map/ppermute | solution.py:799
  218.3 6.9 %collective-permute-start.32 = (bf16[64,640]{1,0:T(8,128)(2,1)S(1)}, bf16[64,640]{1,0:T(8,128)(2,1)S(1)}, u32[]{:S(2)}, u32[]{:S(2)}) collective-permute-start(bf16[64,640]{1,0:T(8,128)(2,1)S(1)} %get-tuple-element.79), channel_id=1, source_target_pairs={{0,8},{4,12},{8,0},{12,4},{16,24},{20,28},{24,16},{28,20},{1,9},{5... | collective-permute-start | bytes 245768 | tf_op jit(solution)/shard_map/ppermute | solution.py:705
  219.3 5.9 %collective-permute-start.34 = (bf16[64,640]{1,0:T(8,128)(2,1)S(1)}, bf16[64,640]{1,0:T(8,128)(2,1)S(1)}, u32[]{:S(2)}, u32[]{:S(2)}) collective-permute-start(bf16[64,640]{1,0:T(8,128)(2,1)S(1)} %get-tuple-element.80), channel_id=1, source_target_pairs={{0,24},{4,28},{8,16},{12,20},{16,8},{20,12},{24,0},{28,4},{1,25},{... | collective-permute-start | bytes 245768 | tf_op jit(solution)/shard_map/ppermute | solution.py:705
  220.9 4.6 %collective-permute-start.33 = (bf16[64,640]{1,0:T(8,128)(2,1)S(1)}, bf16[64,640]{1,0:T(8,128)(2,1)S(1)}, u32[]{:S(2)}, u32[]{:S(2)}) collective-permute-start(bf16[64,640]{1,0:T(8,128)(2,1)S(1)} %get-tuple-element.81), channel_id=1, source_target_pairs={{0,16},{4,20},{8,24},{12,28},{16,0},{20,4},{24,8},{28,12},{1,17},{... | collective-permute-start | bytes 245768 | tf_op jit(solution)/shard_map/ppermute | solution.py:705
  (23 other events, 161.3 us)

commit v4 on v3

v4 whole, which is shorter than its diff:
```python
import functools

import jax
import jax.numpy as jnp
from jax import lax
from jax.experimental import pallas as pl
from jax.experimental.pallas import tpu as pltpu
from jax.sharding import PartitionSpec as P

EPSILON = 1e-5
CHUNK = 128
PAIR = 128
F32 = jnp.float32
BF16 = jnp.bfloat16
LIMIT = 56 * 1024 * 1024


def nn(a, b):
    return lax.dot_general(a, b, (((1,), (0,)), ((), ())), preferred_element_type=F32)


def nt(a, b):
    return lax.dot_general(a, b, (((1,), (1,)), ((), ())), preferred_element_type=F32)


def tn(a, b):
    return lax.dot_general(a, b, (((0,), (0,)), ((), ())), preferred_element_type=F32)


def low(v):
    return v.astype(BF16)


def iota(shape, axis):
    return lax.broadcasted_iota(jnp.int32, shape, axis)


def first_half(shape):
    return iota(shape, 1) < PAIR // 2


def stacked(block):
    left = first_half(block.shape)
    zero = jnp.zeros_like(block)
    return jnp.concatenate([jnp.where(left, block, zero), jnp.where(left, zero, block)], axis=0)


def parts(v):
    high = low(v)
    return jnp.concatenate([high, low(v - high.astype(F32))], axis=1)


def whole(v):
    return v[:, :PAIR] + v[:, PAIR:]


def head_block(shape=(PAIR, PAIR)):
    return (iota(shape, 0) < PAIR // 2) == (iota(shape, 1) < PAIR // 2)


def causal_pair():
    return iota((CHUNK, 2 * CHUNK), 0) >= (iota((CHUNK, 2 * CHUNK), 1) & (CHUNK - 1))


def causal_pair_t():
    return iota((CHUNK, 2 * CHUNK), 0) <= (iota((CHUNK, 2 * CHUNK), 1) & (CHUNK - 1))


def ones_where(mask):
    return low(jnp.where(mask, 1.0, 0.0))


def norm_parts(tokens):
    average = jnp.mean(tokens, axis=-1, keepdims=True)
    centred = tokens - average
    rate = lax.rsqrt(jnp.mean(centred * centred, axis=-1, keepdims=True) + EPSILON)
    return centred * rate, rate


def norm_back(grad, normal, rate, gain):
    w = grad * gain
    return rate * (
        w
        - jnp.mean(w, axis=-1, keepdims=True)
        - normal * jnp.mean(w * normal, axis=-1, keepdims=True)
    )


def chunks(length):
    return [slice(c * CHUNK, (c + 1) * CHUNK) for c in range(length // CHUNK)]


def attend_forward(normed, weight, keep):
    q_ref, k_ref, v_ref, powers_ref, inverse_ref, score_ref, prob_ref, key_state, value_state, heads_ref = keep
    cuts = chunks(normed.shape[0])
    tri = ones_where(iota((CHUNK, CHUNK), 0) >= iota((CHUNK, CHUNK), 1))
    same = head_block()
    both = jnp.concatenate([ones_where(same)] * 2, axis=0)
    causal = causal_pair()
    left = first_half((CHUNK, PAIR))
    carried = jnp.zeros((1, PAIR), F32)
    key_sum = jnp.zeros((PAIR, PAIR), F32)
    value_sum = jnp.zeros((PAIR, PAIR), F32)

    def masked(product):
        return low(jnp.where(causal, product, 0.0))

    def lift(score):
        top_a = jnp.max(jnp.where(left, score, -jnp.inf), axis=-1, keepdims=True)
        top_b = jnp.max(jnp.where(left, -jnp.inf, score), axis=-1, keepdims=True)
        return jnp.exp(score - jnp.where(left, top_a, top_b))

    for first in range(0, len(cuts), 8):
        group = list(range(first, min(first + 8, len(cuts))))
        each = range(len(group))
        rows = slice(group[0] * CHUNK, (group[-1] + 1) * CHUNK)
        made = nn(normed[rows, :], weight)
        cut = [made[i * CHUNK : (i + 1) * CHUNK, :] for i in each]
        q = [low(low(m[:, :PAIR]).astype(F32) * 0.125) for m in cut]
        k = [low(m[:, PAIR : 2 * PAIR]) for m in cut]
        v = [low(m[:, 2 * PAIR : 3 * PAIR]) for m in cut]
        powers = [jnp.exp(m[:, 3 * PAIR :]) for m in cut]
        powers_low = [low(p) for p in powers]
        local = [whole(nn(tri, parts(p))) for p in powers]
        scored = [masked(nt(q[i], stacked(k[i]))) for i in each]
        inverse = []
        for i in each:
            running = local[i] + carried
            carried = running[CHUNK - 1 :, :]
            inverse.append(1.0 / running)
        powers_two = [stacked(m) for m in powers_low]
        for i, c in enumerate(group):
            key_state[c, :, :] = low(jnp.where(same, key_sum, 0.0))
            value_state[c, :, :] = low(jnp.where(same, value_sum, 0.0))
            if c + 1 < len(cuts):
                key_sum = key_sum + tn(k[i], powers_low[i])
                value_sum = value_sum + tn(powers_low[i], v[i])
        score = [
            (nn(scored[i], powers_two[i]) + nn(q[i], key_state[c, :, :])) * inverse[i]
            for i, c in enumerate(group)
        ]
        lifted = [lift(m) for m in score]
        prob = [lifted[i] / nn(parts(lifted[i]), both) for i in each]
        reading = [low(prob[i] * inverse[i]) for i in each]
        mixing = [masked(nt(reading[i], powers_two[i])) for i in each]
        for i, c in enumerate(group):
            q_ref[cuts[c], :] = q[i]
            k_ref[cuts[c], :] = k[i]
            v_ref[cuts[c], :] = v[i]
            powers_ref[cuts[c], :] = powers[i]
            inverse_ref[cuts[c], :] = inverse[i]
            score_ref[cuts[c], :] = score[i]
            prob_ref[cuts[c], :] = prob[i]
        for i, c in enumerate(group):
            heads_ref[cuts[c], :] = low(
                nn(mixing[i], stacked(v[i])) + nn(reading[i], value_state[c, :, :])
            )


def attend_backward(heads_grad, kept, backs):
    q_ref, k_ref, v_ref, powers_ref, inverse_ref, score_ref, prob_ref, key_state, value_state = kept
    cuts = chunks(heads_grad.shape[0])
    same = head_block()
    both = jnp.concatenate([ones_where(same)] * 2, axis=0)
    causal = causal_pair()
    causal_t = causal_pair_t()
    tri_t = ones_where(iota((CHUNK, CHUNK), 0) <= iota((CHUNK, CHUNK), 1))
    after_sum = jnp.zeros((1, PAIR), F32)
    read_sum = jnp.zeros((PAIR, PAIR), F32)
    score_sum = jnp.zeros((PAIR, PAIR), F32)

    def masked(product, mask):
        return low(jnp.where(mask, product, 0.0))

    for first in reversed(range(0, len(cuts), 4)):
        group = list(reversed(range(first, min(first + 4, len(cuts)))))
        load = lambda ref: [ref[cuts[c], :] for c in group]
        q, k, v, grad = load(q_ref), load(k_ref), load(v_ref), load(heads_grad)
        inverse, prob, powers = load(inverse_ref), load(prob_ref), load(powers_ref)
        each = range(len(group))
        powers_low = [low(p) for p in powers]
        reading = [low(prob[i] * inverse[i]) for i in each]
        powers_two, values_two = [stacked(m) for m in powers_low], [stacked(m) for m in v]
        grad_two, reading_two = [stacked(m) for m in grad], [stacked(m) for m in reading]
        mixing_grad = [masked(nt(grad[i], values_two[i]), causal) for i in each]
        reading_grad = [
            nn(mixing_grad[i], powers_two[i]) + nt(grad[i], value_state[group[i], :, :]) for i in each
        ]
        mixing_grad_t = [masked(nt(v[i], grad_two[i]), causal_t) for i in each]
        mixing_t = [masked(nt(powers_low[i], reading_two[i]), causal_t) for i in each]
        read_states = []
        for i in each:
            read_states.append(low(jnp.where(same, read_sum, 0.0)))
            if group[i]:
                read_sum = read_sum + tn(reading[i], grad[i])
        prob_grad = [reading_grad[i] * inverse[i] for i in each]
        weighed = [prob[i] * prob_grad[i] for i in each]
        slots_grad = [weighed[i] - prob[i] * nn(parts(weighed[i]), both) for i in each]
        summed_grad = [low(slots_grad[i] * inverse[i]) for i in each]
        running_grad = [
            -inverse[i] * (weighed[i] + slots_grad[i] * score_ref[cuts[group[i]], :]) for i in each
        ]
        powers_grad = [
            nn(mixing_grad_t[i], reading_two[i]) + nt(v[i], read_states[i]) for i in each
        ]
        for i in each:
            backs[cuts[group[i]], 2 * PAIR : 3 * PAIR] = low(
                nn(mixing_t[i], grad_two[i]) + nn(powers_low[i], read_states[i])
            )
        queries_two, keys_two = [stacked(m) for m in q], [stacked(m) for m in k]
        scored_t = [masked(nt(k[i], queries_two[i]), causal_t) for i in each]
        summed_two = [stacked(m) for m in summed_grad]
        score_states = []
        for i in each:
            score_states.append(low(jnp.where(same, score_sum, 0.0)))
            if group[i]:
                score_sum = score_sum + tn(q[i], summed_grad[i])
        scored_grad = [masked(nt(summed_grad[i], powers_two[i]), causal) for i in each]
        scored_grad_t = [masked(nt(powers_low[i], summed_two[i]), causal_t) for i in each]
        later = [whole(nn(tri_t, parts(running_grad[i]))) for i in each]
        powers_grad = [
            powers_grad[i] + nn(scored_t[i], summed_two[i]) + nn(k[i], score_states[i]) for i in each
        ]
        for i in each:
            rows = cuts[group[i]]
            backs[rows, :PAIR] = low(
                0.125 * (nn(scored_grad[i], keys_two[i]) + nt(summed_grad[i], key_state[group[i], :, :]))
            )
            backs[rows, PAIR : 2 * PAIR] = low(
                nn(scored_grad_t[i], queries_two[i]) + nt(powers_low[i], score_states[i])
            )
            total = later[i] + after_sum
            after_sum = total[:1, :]
            backs[rows, 3 * PAIR :] = low((powers_grad[i] + total) * powers[i])


def kept_shapes(length, lead=()):
    n = length // CHUNK
    shape = jax.ShapeDtypeStruct
    return (
        [shape(lead + (length, PAIR), BF16)] * 3
        + [shape(lead + (length, PAIR), F32)] * 4
        + [shape(lead + (n, PAIR, PAIR), BF16)] * 2
    )


def fixed(shape):
    return pl.BlockSpec(shape, lambda a: (0,) * len(shape))


def one_slot(members, slot):
    return [
        pl.BlockSpec((None,) + s.shape[1:], lambda a, rank=len(s.shape): (slot,) + (0,) * (rank - 1))
        for s in members
    ]


def by_step(members, first=0):
    return [
        pl.BlockSpec((None,) + s.shape[1:], lambda a, rank=len(s.shape): (a + first,) + (0,) * (rank - 1))
        for s in members
    ]


def anywhere(members):
    return [pl.BlockSpec(memory_space=pl.ANY)] * len(members)


def mark_spec():
    return pl.BlockSpec(memory_space=pltpu.SMEM)


MARK = jax.ShapeDtypeStruct((1,), F32)


def cost(micros):
    return pl.CostEstimate(flops=int(micros * 1e9), bytes_accessed=int(micros * 1e6), transcendentals=0)


def params():
    return pltpu.CompilerParams(vmem_limit_bytes=LIMIT)


def select(width, offset, share, total):
    return ones_where(
        iota((width, total), 0) == offset + (iota((width, total), 1) & (share - 1))
    )


def owned(devices, share, total):
    return iota((devices, total), 0) == lax.shift_right_logical(
        iota((devices, total), 1), share.bit_length() - 1
    )


def spread(rows, offset, share, total):
    each = nn(rows, select(rows.shape[1], offset, share, total))
    return jnp.sum(jnp.where(owned(rows.shape[0], share, total), each, 0.0), axis=0, keepdims=True)


def collect(rows, devices, share):
    total = rows[0].shape[1]
    mine = owned(devices, share, total)
    out = jnp.zeros((devices, 128), F32)
    for i, row in enumerate(rows):
        rest = jnp.where(mine, row, 0.0)
        high = low(rest)
        pair = jnp.concatenate([high, low(rest - high.astype(F32))], axis=0)
        made = nt(pair, select(128, i * share, share, total))
        out = out + made[:devices] + made[devices:]
    return out


def own_device(core, chip, slots):
    return (lax.axis_index("seq") ^ (2 * chip + core)) * slots


def fill(weight, own_ref, pieces, slot):
    @pl.when(slot == 0)
    def _():
        weight[...] = own_ref[...]

    @pl.when(slot > 0)
    def _():
        rows = weight.shape[0] // len(pieces)
        mine = lax.axis_index("seq") if len(pieces) > 1 else 0
        start = pl.multiple_of((slot - 1) * rows, 16)
        for r, piece in enumerate(pieces):
            weight[pl.ds(pl.multiple_of((mine ^ r) * rows, rows), rows), :] = piece[pl.ds(start, rows), :]


def gather_vectors(pieces, rows, slots, vectors):
    for r, piece in enumerate(pieces):
        block = piece[(slots - 1) * rows :, :256].astype(F32)
        for a in range(slots):
            z = lax.rem(lax.axis_index("head") + slots - a, slots)
            source = own_device(r % 2, r // 2, slots) + z
            for i in range(2):
                part = block[a : a + 1, 128 * i : 128 * (i + 1)]
                vectors[pl.ds(source, 1), i : i + 1, :] = part[None]


def forward_kernel(count, slots, tokens_ref, own_ref, *refs):
    pieces, refs = refs[:count], refs[count:]
    if count == 1:
        given, refs = refs[0], refs[1:]
    normed_ref, rows_ref, residual_ref, second_ref, mark, heads_ref, weight = refs[:7]
    keep, staged, vectors = refs[7:-2], refs[-2], refs[-1]
    slot = pl.program_id(0)
    length, width = tokens_ref.shape
    share = width // vectors.shape[0]
    tiles = [slice(r, r + 256) for r in range(0, length, 256)]

    @pl.when(slot == 0)
    def _():
        if count == 1:
            vectors[...] = given[:, :8, :].astype(F32)
        else:
            gather_vectors(pieces, weight.shape[0] // count, slots, vectors)
        for i in range(9):
            part = low(vectors[:, 0 if i < 5 else 1, :])
            rows_ref[i : i + 1, :] = spread(part, (i if i < 5 else i - 5) * share, share, width)
        gain, shift = rows_ref[0:1, :], rows_ref[1:2, :]
        for rows in tiles:
            tokens = tokens_ref[rows, :].astype(F32)
            normal, _ = norm_parts(tokens)
            normed_ref[rows, :] = low(normal * gain + shift)
            residual_ref[rows, :] = tokens
        mark[0] = 1.0

    fill(weight, own_ref, pieces, slot)
    attend_forward(normed_ref, weight[:width, :], list(keep) + [staged])
    heads_ref[...] = staged[...]
    residual_ref[...] += nn(staged[...], weight[width:, :])

    @pl.when(slot == slots - 1)
    def _():
        gain, shift = rows_ref[2:3, :], rows_ref[3:4, :]
        for rows in tiles:
            normal, _ = norm_parts(residual_ref[rows, :])
            second_ref[rows, :] = low(normal * gain + shift)


def forward(tokens, own, pieces, vectors, devices, slots):
    length, width = tokens.shape
    shape = jax.ShapeDtypeStruct
    operands = [tokens, own, *pieces, *vectors]
    outs = [
        shape((length, width), BF16),
        shape((16, width), F32),
        shape((length, width), F32),
        shape((length, width), BF16),
    ]
    stacked_outs = [shape((slots, length, PAIR), BF16), shape((slots, width + PAIR, 4 * PAIR), BF16)]
    stacked_outs += kept_shapes(length, (slots,))
    made = pl.pallas_call(
        functools.partial(forward_kernel, len(pieces), slots),
        grid=(slots,),
        out_shape=outs + [MARK] + stacked_outs,
        in_specs=[fixed(o.shape) for o in operands],
        out_specs=[fixed(o.shape) for o in outs] + [mark_spec()] + by_step(stacked_outs),
        scratch_shapes=[pltpu.VMEM((length, PAIR), BF16), pltpu.VMEM((devices, 8, 128), F32)],
        compiler_params=params(),
        cost_estimate=cost(17),
        name="attend_forward",
    )(*operands)
    return made[:5], made[5:]


GELU_A = 0.7978845608028654
GELU_B = 0.044715


def gelu_both(u):
    square = u * u
    bend = jnp.tanh(GELU_A * (u + GELU_B * (square * u)))
    half = 0.5 * (1.0 + bend)
    slope = half + 0.5 * u * (1.0 - bend * bend) * (GELU_A * (1.0 + 3.0 * GELU_B * square))
    return u * half, slope


def weight_copies(block, pieces, weights, sems):
    if len(pieces) == 1:
        return [pltpu.make_async_copy(pieces[0].at[block], weights.at[block], sems.at[block, 0])]
    copies = []
    for r, piece in enumerate(pieces):
        slots = piece.shape[0]
        copies.append(
            pltpu.make_async_copy(
                piece.at[:, pl.ds(2 * block, 2)],
                weights.at[block, pl.ds(own_device(r % 2, r // 2, slots), slots)],
                sems.at[block, len(copies)],
            )
        )
    return copies


def grad_copies(block, grads, outs, sems):
    if len(outs) == 1:
        return [pltpu.make_async_copy(grads.at[block], outs[0].at[block], sems.at[block, 0])]
    copies = []
    for core, out in enumerate(outs):
        chips, slots = out.shape[:2]
        for chip in range(chips):
            target = (2 * chip + ((lax.axis_index("seq") & 1) ^ core)) * slots
            copies.append(
                pltpu.make_async_copy(
                    grads.at[block, pl.ds(target, slots)],
                    out.at[chip, :, block],
                    sems.at[block, len(copies)],
                )
            )
    return copies


def ffn_kernel(count, second_ref, rows_ref, cotangent_ref, residual_hbm, *refs):
    pieces = refs[:count]
    result_ref, grad_ref, branch_ref, sums_ref = refs[count : count + 4]
    outs = refs[count + 4 : -8]
    weights, grads, residual, total, back, in_sems, out_sems, residual_sem = refs[-8:]
    k = pl.program_id(0)
    length, width = second_ref.shape
    tiles = [slice(r, r + 256) for r in range(0, length, 256)]
    fetch = pltpu.make_async_copy(residual_hbm, residual, residual_sem)

    @pl.when(k == 0)
    def _():
        for block in range(4):
            for copy in weight_copies(block, pieces, weights, in_sems):
                copy.start()
        fetch.start()
        total[...] = jnp.zeros_like(total)
        back[...] = jnp.zeros_like(back)

    for block in range(4):

        @pl.when(k == block)
        def _(block=block):
            for copy in weight_copies(block, pieces, weights, in_sems):
                copy.wait()

    expand = weights[k, :, 0].reshape(width, width)
    shrink = weights[k, :, 1].reshape(width, width)
    bias = rows_ref[pl.ds(5 + k, 1), :]
    bias_grad = jnp.zeros((1, width), F32)
    acts, hids = [], []
    for rows in tiles:
        hidden = nt(second_ref[rows, :], expand) + bias
        pull = nn(cotangent_ref[rows, :], shrink)
        value, slope = gelu_both(hidden)
        activated = low(value)
        hidden_grad = low(pull * slope)
        bias_grad = bias_grad + jnp.sum(hidden_grad.astype(F32), axis=0, keepdims=True)
        total[rows, :] += nt(activated, shrink)
        back[rows, :] += nn(hidden_grad, expand)
        acts.append(activated)
        hids.append(hidden_grad)
    sums_ref[pl.ds(5 + k, 1), :] = bias_grad
    grads[k, :, 1] = low(tn(cotangent_ref[...], jnp.concatenate(acts, axis=0))).reshape(
        width // 16, 16, width
    )
    grads[k, :, 0] = low(tn(jnp.concatenate(hids, axis=0), second_ref[...])).reshape(width // 16, 16, width)
    for block in range(4):

        @pl.when(k == block)
        def _(block=block):
            for copy in grad_copies(block, grads, outs, out_sems):
                copy.start()

    @pl.when(k == 3)
    def _():
        fetch.wait()
        gain, bias = rows_ref[2:3, :], rows_ref[4:5, :]
        gain_grad = jnp.zeros((1, width), F32)
        shift_grad = jnp.zeros((1, width), F32)
        outer = jnp.zeros((1, width), F32)
        for rows in tiles:
            base = residual[rows, :]
            result_ref[rows, :] = low(base + total[rows, :] + bias)
            grad = back[rows, :]
            normal, rate = norm_parts(base)
            upstream = cotangent_ref[rows, :].astype(F32)
            gain_grad = gain_grad + jnp.sum(grad * normal, axis=0, keepdims=True)
            shift_grad = shift_grad + jnp.sum(grad, axis=0, keepdims=True)
            outer = outer + jnp.sum(upstream, axis=0, keepdims=True)
            full = upstream + norm_back(grad, normal, rate, gain)
            grad_ref[rows, :] = full
            branch_ref[rows, :] = low(full)
        sums_ref[0:2, :] = jnp.zeros((2, width), F32)
        sums_ref[2:3, :] = gain_grad
        sums_ref[3:4, :] = shift_grad
        sums_ref[4:5, :] = outer
        for block in range(4):
            for copy in grad_copies(block, grads, outs, out_sems):
                copy.wait()


def feed_forward(second, rows, cotangent, residual, pieces, grad_shapes):
    length, width = second.shape
    shape = jax.ShapeDtypeStruct
    weights = (4, width // 16, 2, 16, width)
    outs = [
        shape((length, width), BF16),
        shape((length, width), F32),
        shape((length, width), BF16),
        shape((16, width), F32),
    ]
    return pl.pallas_call(
        functools.partial(ffn_kernel, len(pieces)),
        grid=(4,),
        out_shape=outs + [shape(s, BF16) for s in grad_shapes],
        in_specs=[fixed(o.shape) for o in (second, rows, cotangent)] + anywhere([residual, *pieces]),
        out_specs=[fixed(o.shape) for o in outs] + anywhere(grad_shapes),
        scratch_shapes=[
            pltpu.VMEM(weights, BF16),
            pltpu.VMEM(weights, BF16),
            pltpu.VMEM((length, width), F32),
            pltpu.VMEM((length, width), F32),
            pltpu.VMEM((length, width), F32),
            pltpu.SemaphoreType.DMA((4, 8)),
            pltpu.SemaphoreType.DMA((4, 8)),
            pltpu.SemaphoreType.DMA,
        ],
        compiler_params=params(),
        cost_estimate=cost(22),
        name="feed_forward",
    )(second, rows, cotangent, residual, *pieces)


def heads_kernel(branch_ref, weight_ref, heads_ref, grad_ref, output_grad_ref, mark):
    slots = heads_ref.shape[0]
    weight = weight_ref[...].reshape(slots * PAIR, weight_ref.shape[2])
    grad = low(nt(branch_ref[...], weight))
    output_grad = low(tn(branch_ref[...], jnp.concatenate([heads_ref[a] for a in range(slots)], axis=1)))
    for a in range(slots):
        grad_ref[a] = grad[:, a * PAIR : (a + 1) * PAIR]
        output_grad_ref[a] = output_grad[:, a * PAIR : (a + 1) * PAIR]
    mark[0] = 1.0


def heads_back(branch, weights, heads):
    slots = heads.shape[0]
    length, width = branch.shape
    shape = jax.ShapeDtypeStruct
    outs = [shape((slots, length, PAIR), BF16), shape((slots, width, PAIR), BF16)]
    return pl.pallas_call(
        heads_kernel,
        grid=(1,),
        out_shape=outs + [MARK],
        in_specs=[
            fixed((length, width)),
            pl.BlockSpec((slots, PAIR, width), lambda a: (0, width // PAIR, 0)),
        ]
        + [fixed(heads.shape)],
        out_specs=[fixed(o.shape) for o in outs] + [mark_spec()],
        compiler_params=params(),
        cost_estimate=cost(4),
        name="heads_back",
    )(branch, weights, heads)


def pair_grads(grad_ref, output_grad_ref, normed_ref, kept, outs, backs, made):
    attend_backward(grad_ref, kept, backs)
    made[:, : 4 * PAIR] = low(tn(normed_ref[...], backs[...]))
    made[:, 4 * PAIR :] = output_grad_ref[...]
    if len(outs) == 1:
        outs[0][...] = made[...]
        return
    seq = lax.axis_index("seq")
    rows = outs[1].shape[0]
    for chip in range(outs[0].shape[0]):
        for core, out in enumerate((outs[0].at[chip], outs[1 + chip])):
            start = pl.multiple_of((seq ^ (2 * chip + core)) * rows, rows)
            out[...] = made[pl.ds(start, rows), :]


def back_kernel(waits, parts_out, normed_ref, rows_ref, before_ref, tokens_hbm, residual_grad_hbm, *refs):
    refs = refs[waits:]
    weight, grad_ref, output_grad_ref, kept, refs = refs[0], refs[1], refs[2], refs[3:12], refs[12:]
    input_grad_ref, sums_ref, outs, mark = refs[0], refs[1], refs[2 : 2 + parts_out], refs[2 + parts_out]
    backs, made, total, tokens, residual_grad, sems = refs[3 + parts_out :]
    length, width = normed_ref.shape
    devices = sums_ref.shape[0]
    share = width // devices
    step, steps = pl.program_id(0), pl.num_programs(0)
    copies = [
        pltpu.make_async_copy(tokens_hbm, tokens, sems.at[0]),
        pltpu.make_async_copy(residual_grad_hbm, residual_grad, sems.at[1]),
    ]

    @pl.when(step == 0)
    def _():
        for copy in copies:
            copy.start()
        total[...] = jnp.zeros_like(total)
        mark[0] = 1.0

    pair_grads(grad_ref, output_grad_ref, normed_ref, kept, outs, backs, made)
    total[...] += nt(backs[...], weight[:width, :])

    @pl.when(step == steps - 1)
    def _():
        for copy in copies:
            copy.wait()
        gain = rows_ref[0:1, :]
        gain_grad = jnp.zeros((1, width), F32)
        shift_grad = jnp.zeros((1, width), F32)
        for rows in [slice(r, r + 256) for r in range(0, length, 256)]:
            grad = total[rows, :]
            normal, rate = norm_parts(tokens[rows, :].astype(F32))
            gain_grad = gain_grad + jnp.sum(grad * normal, axis=0, keepdims=True)
            shift_grad = shift_grad + jnp.sum(grad, axis=0, keepdims=True)
            input_grad_ref[rows, :] = low(residual_grad[rows, :] + norm_back(grad, normal, rate, gain))
        sums_ref[...] = jnp.zeros_like(sums_ref)
        small = [gain_grad, shift_grad] + [before_ref[i : i + 1, :] for i in range(2, 5)]
        sums_ref[:, 0, :] = collect(small, devices, share)
        sums_ref[:, 1, :] = collect([before_ref[i : i + 1, :] for i in range(5, 9)], devices, share)


def backward(normed, rows, before, tokens, residual_grad, devices, waits, members, grad_shapes):
    length, width = normed.shape
    slots = members[0].shape[0]
    shape = jax.ShapeDtypeStruct
    outs = [shape((length, width), BF16), shape((devices, 8, 128), F32)]
    grads = [shape(s[:-2] + (slots,) + s[-2:], BF16) for s in grad_shapes]
    grad_specs = [
        by_step([g])[0]
        if len(g.shape) == 3
        else pl.BlockSpec((g.shape[0], None) + g.shape[2:], lambda a: (0, a, 0, 0))
        for g in grads
    ]
    large = [tokens, residual_grad]
    return pl.pallas_call(
        functools.partial(back_kernel, len(waits), len(grad_shapes)),
        grid=(slots,),
        out_shape=outs + grads + [MARK],
        in_specs=[fixed(o.shape) for o in (normed, rows, before)] + anywhere(large + waits) + by_step(members),
        out_specs=[fixed(o.shape) for o in outs] + grad_specs + [mark_spec()],
        scratch_shapes=[
            pltpu.VMEM((length, 4 * PAIR), BF16),
            pltpu.VMEM((width, 5 * PAIR), BF16),
            pltpu.VMEM((length, width), F32),
        ]
        + [pltpu.VMEM((length, width), m.dtype) for m in large]
        + [pltpu.SemaphoreType.DMA((2,))],
        compiler_params=params(),
        cost_estimate=cost(27),
        name="attend_back",
    )(normed, rows, before, *large, *waits, *members)


def after(value, *others):
    return pl.pallas_call(
        lambda *refs: None,
        out_shape=jax.ShapeDtypeStruct(value.shape, value.dtype),
        in_specs=anywhere((value,) + others),
        out_specs=anywhere([value])[0],
        input_output_aliases={0: 0},
        name="after",
    )(value, *others)


def join_kernel(chips, slots, ffn_ref, *refs):
    keep_ref, others, sums_ref, refs = refs[0], refs[1 : 1 + chips], refs[1 + chips], refs[2 + chips :]
    ffn_outs, outs, sums_out = refs[:slots], refs[slots : slots + chips], refs[slots + chips]
    z = lax.axis_index("head")
    for a, out in enumerate(ffn_outs):
        place = lax.rem(z + a, slots)
        out[...] = low(functools.reduce(lambda x, y: x + y, [ffn_ref[c, pl.ds(place, 1)][0].astype(F32) for c in range(chips)]))
    for chip, out in enumerate(outs):
        out[...] = low(keep_ref[chip].astype(F32) + others[chip][...].astype(F32))
    sums_out[...] = sums_ref[...]


def join(ffn, keep, others, sums):
    shape = jax.ShapeDtypeStruct
    chips, slots = ffn.shape[:2]
    operands = [ffn, keep, *others, sums]
    outs = [shape(ffn.shape[2:], BF16)] * slots + [shape(keep.shape[1:], BF16)] * chips
    outs += [shape(sums.shape, F32)]
    made = pl.pallas_call(
        functools.partial(join_kernel, chips, slots),
        grid=(1,),
        out_shape=outs,
        in_specs=[fixed(o.shape) for o in operands],
        out_specs=[fixed(o.shape) for o in outs],
        compiler_params=params(),
        cost_estimate=cost(3),
        name="join",
    )(*operands)
    return made[:slots], made[slots : slots + chips], made[-1]


def sum_plane_kernel(slots, *refs):
    pairs, mine_ref, sends = refs[: -slots - 1], refs[-slots - 1], refs[-slots:-1]
    for a in range(slots):
        mine = functools.reduce(lambda x, y: x + y, [p[a].astype(F32) for p in pairs])
        if a == 0:
            mine_ref[...] = mine
        else:
            sends[a - 1][...] = low(mine)
    refs[-1][0] = 1.0


def sum_plane(pairs, waits):
    shape = jax.ShapeDtypeStruct
    slots = pairs[0].shape[0]
    outs = [shape(pairs[0].shape[1:], F32)] + [shape(pairs[0].shape[1:], BF16)] * (slots - 1)

    def kernel(*refs):
        sum_plane_kernel(slots, *refs[: len(pairs)], *refs[len(pairs) + len(waits) :])

    return pl.pallas_call(
        kernel,
        grid=(1,),
        out_shape=outs + [MARK],
        in_specs=[fixed(p.shape) for p in pairs] + anywhere(waits),
        out_specs=[fixed(o.shape) for o in outs] + [mark_spec()],
        compiler_params=params(),
        cost_estimate=cost(2),
        name="sum_plane",
    )(*pairs, *waits)


def settle_kernel(slots, *refs):
    ffn, sums_ref, expand_ref, shrink_ref, vector_ref = refs[:slots], *refs[slots + 1 :]
    blocks, _, share, width = ffn[0].shape
    total = functools.reduce(lambda x, y: x + y, [f[...].astype(F32) for f in ffn])
    expand_ref[...] = total[:, 0].reshape(blocks * share, width).T
    for i in range(blocks):
        shrink_ref[:, i] = total[i, 1].T.reshape(width // share, share, share)
    vector_ref[...] = jnp.sum(sums_ref[...], axis=0)


def settle(ffn, sums, wait):
    shape = jax.ShapeDtypeStruct
    slots = len(ffn)
    blocks, _, share, width = ffn[0].shape
    outs = [
        shape((width, blocks * share), F32),
        shape((width // share, blocks, share, share), F32),
        shape(sums.shape[1:], F32),
    ]

    def kernel(*refs):
        settle_kernel(slots, *refs[:slots], None, *refs[slots : slots + 1], *refs[slots + 2 :])

    return pl.pallas_call(
        kernel,
        grid=(1,),
        out_shape=outs,
        in_specs=[fixed(o.shape) for o in (*ffn, sums)] + anywhere([wait]),
        out_specs=[fixed(o.shape) for o in outs],
        compiler_params=params(),
        cost_estimate=cost(3),
        name="settle",
    )(*ffn, sums, wait)


def flip(count, bit):
    return [(i, i ^ bit) for i in range(count)]


def turn(count, by):
    return [(i, (i + by) % count) for i in range(count)]


def add(*members):
    return functools.reduce(lambda a, b: a + b, [m.astype(F32) for m in members])


def to_mate(shares, seqs):
    return lax.ppermute(shares, "seq", flip(seqs, 1))


def over_chips(shares, chips, seqs):
    return [shares] + [lax.ppermute(shares, "seq", flip(seqs, 2 * r)) for r in range(1, chips)]


def over_cores(held, seqs):
    return [member for h in held for member in (h, to_mate(h, seqs))]


def to_chips(shares, seqs):
    plane = [list(range(core, seqs, 2)) for core in range(2)]
    return lax.all_to_all(shares, "seq", 0, 0, axis_index_groups=plane, tiled=True)


def from_chips(sends, seqs):
    return [lax.ppermute(m, "seq", flip(seqs, 2 * r + 2)) for r, m in enumerate(sends)]


def body(
    inputs,
    attn_gain,
    attn_shift,
    query_weight,
    key_weight,
    value_weight,
    control_weight,
    output_weight,
    ffn_gain,
    ffn_shift,
    expand_weight,
    expand_bias,
    shrink_weight,
    shrink_bias,
    cotangent,
):
    seqs, slots = lax.axis_size("seq"), lax.axis_size("head")
    devices = seqs * slots
    chips = seqs // 2
    width = inputs.shape[1]
    share = width // devices
    hidden_share = expand_weight.shape[1]
    z = lax.axis_index("head")
    direct = seqs == 8 and slots == 4 and share == 16 and hidden_share == 4 * share

    own = jnp.concatenate(
        [
            jnp.concatenate([query_weight, key_weight, value_weight, control_weight], axis=1),
            output_weight,
        ],
        axis=0,
    )
    places = [(attn_gain, 0), (attn_shift, 1), (ffn_gain, 2), (ffn_shift, 3), (shrink_bias, 4)]
    row = functools.reduce(
        lambda a, b: a + b,
        [jnp.pad(m, (i * share, width - (i + 1) * share)) for m, i in places]
        + [jnp.pad(expand_bias, (128, width - 128 - hidden_share))],
    )
    block = jnp.pad(row[None, :], ((0, 15), (0, 0)))
    expand_t = expand_weight.T.reshape(4, share, width)
    shrink_t = shrink_weight.reshape(devices, 4, share, share).transpose(1, 3, 0, 2).reshape(4, share, width)
    load = jnp.stack([expand_t, shrink_t], axis=1)
    if direct:
        rows = own.shape[0] // seqs
        piece = lax.dynamic_slice_in_dim(own, lax.axis_index("seq") * rows, rows, axis=0)
        piece = jnp.concatenate([piece, block], axis=0)
        came = [lax.ppermute(piece, "head", turn(slots, a)) for a in range(1, slots)]
        for a in range(1, slots):
            block = block + jnp.pad(came[a - 1][rows : rows + 1], ((a, 15 - a), (0, 0)))
        near = jnp.concatenate([c[:rows] for c in came] + [block], axis=0)
        pieces, vectors = over_cores(over_chips(near, chips, seqs), seqs), []
        load = jnp.broadcast_to(load.reshape(1, 8, share, width), (slots, 8, share, width))
        load = lax.all_to_all(after(load, near), "head", 0, 0, tiled=True)
        held = over_chips(load, chips, seqs)
        pair_shapes = [(chips, width // seqs, 5 * PAIR)] + [(width // seqs, 5 * PAIR)] * chips
        ffn_shapes = [(chips, slots, 4, 2, 16, width)] * 2
    else:
        every = lax.all_gather(own, "head", axis=0, tiled=False)
        pieces = [jnp.concatenate([every[(z + slots - a) % slots] for a in range(1, slots)], axis=0)]
        block = jnp.concatenate([block[:1, :128], block[:1, 128:256], block[2:, :128]], axis=0)
        vectors = [lax.all_gather(block, ("seq", "head"), axis=0, tiled=False)]
        both = lax.all_gather(load, ("seq", "head"), axis=2, tiled=True)
        ffn_pieces = [both.reshape(4, 2, width // 16, 16, width).transpose(0, 2, 1, 3, 4)]
        pair_shapes = [(width, 5 * PAIR)]
        ffn_shapes = [ffn_pieces[0].shape]

    (normed, rows, residual, second, _), (heads, weights, *members) = forward(
        inputs, own, pieces, vectors, devices, slots
    )
    if direct:
        ffn_pieces = over_cores(held[:-1] + [after(held[-1], second)], seqs)
    result, residual_grad, branch, sums, *ffn_grads = feed_forward(
        second, rows, cotangent, residual, ffn_pieces, ffn_shapes
    )
    heads_grad, output_grad, mark = heads_back(branch, weights, heads)
    members = [weights, heads_grad, output_grad, *members]
    waits = []
    if direct:
        ffn_mine = low(add(ffn_grads[0], to_mate(ffn_grads[1], seqs)) * mark[0])
        waits = [ffn_mine]
    input_grad, sums, *pair_grads, _ = backward(
        normed, rows, sums, inputs, residual_grad, devices, waits, members, pair_shapes
    )

    if direct:
        keep, *sends = pair_grads
        ffn, pairs, sums = join(
            to_chips(ffn_mine, seqs), keep, [to_mate(s, seqs) for s in sends], sums
        )
        ffn = [ffn[0]] + [lax.ppermute(ffn[a], "head", turn(slots, a)) for a in range(1, slots)]
        pairs = [pairs[0]] + from_chips(pairs[1:], seqs)
        sums = lax.all_to_all(sums, ("seq", "head"), 0, 0, tiled=True)
        mine, *sends, wait = sum_plane(pairs, ffn[1:] + [sums])
        expand_grad, shrink_grad, sums = settle(ffn, sums, wait)
        came = [lax.ppermute(m, "head", turn(slots, slots - 1 - a)) for a, m in enumerate(sends)]
        pair_sum = add(mine, *came)
    else:
        ffn_sum = lax.psum_scatter(
            ffn_grads[0].astype(F32).transpose(0, 2, 1, 3, 4).reshape(4, 2, width, width), ("seq", "head"), scatter_dimension=2, tiled=True
        )
        every = pair_grads[0].astype(F32)
        every = jnp.stack([every[(z + slots - p) % slots] for p in range(slots)])
        pair_sum = lax.psum_scatter(every, "head", scatter_dimension=0, tiled=False)
        pair_sum = lax.psum_scatter(pair_sum, "seq", scatter_dimension=0, tiled=True)

        sums = jnp.sum(lax.all_to_all(sums, ("seq", "head"), 0, 0, tiled=True), axis=0)
        expand_grad = ffn_sum[:, 0].reshape(hidden_share, width).T
        shrink_grad = ffn_sum[:, 1].reshape(4, share, devices, share).transpose(2, 0, 3, 1)

    vector = [sums[0, i * share : (i + 1) * share] for i in range(5)]
    return (
        result,
        input_grad,
        vector[0],
        vector[1],
        pair_sum[:, :PAIR],
        pair_sum[:, PAIR : 2 * PAIR],
        pair_sum[:, 2 * PAIR : 3 * PAIR],
        pair_sum[:, 3 * PAIR : 4 * PAIR],
        pair_sum[:, 4 * PAIR :].T,
        vector[2],
        vector[3],
        expand_grad,
        sums[1, :hidden_share],
        shrink_grad.reshape(devices * hidden_share, share),
        vector[4],
    )


def solution(mesh):
    placed = (
        P(("seq", "head"), None),
        P(("seq", "head")),
        P(("seq", "head")),
        P(None, "head"),
        P(None, "head"),
        P(None, "head"),
        P(None, "head"),
        P("head", None),
        P(("seq", "head")),
        P(("seq", "head")),
        P(None, ("seq", "head")),
        P(("seq", "head")),
        P(None, ("seq", "head")),
        P(("seq", "head")),
        P(("seq", "head"), None),
    )
    return jax.shard_map(
        body,
        mesh=mesh,
        in_specs=placed,
        out_specs=(
            P(("seq", "head"), None),
            P(("seq", "head"), None),
            P(("seq", "head")),
            P(("seq", "head")),
            P("seq", "head"),
            P("seq", "head"),
            P("seq", "head"),
            P("seq", "head"),
            P("head", "seq"),
            P(("seq", "head")),
            P(("seq", "head")),
            P(None, ("seq", "head")),
            P(("seq", "head")),
            P(None, ("seq", "head")),
            P(("seq", "head")),
        ),
        check_vma=False,
    )
```

time: 227 us -> 177 us (0.78)
  waiting for transfers between devices: 79.1 us -> 35.2 us
  Pallas kernels: 85.1 us -> 78.4 us
  local copies, waits for them, and re-layouts: 9.73 us -> 14.4 us
  starting transfers between devices: 44.9 us -> 41.4 us
    ppermute x38 -> x28, waiting for transfers between devices: 50.5 us -> 29.6 us  [the longest x6 16.5 us: over_chips(): lax.ppermute(shares, 'seq', flip(seqs, 2 * r))]
    all_to_all x2 -> x3, waiting for transfers between devices: 12.1 us -> 0.01 us  [the longest x1 0.01 us: body(): load = lax.all_to_all(after(load, near), 'head', 0, 0, tiled=True)]
    ppermute x38 -> x28, starting transfers between devices: 35.1 us -> 23.1 us  [the longest x6 7 us: over_chips(): lax.ppermute(shares, 'seq', flip(seqs, 2 * r))]
    ppermute x3, waiting for transfers between devices: 16.4 us -> 5.58 us  [body(): lax.ppermute(piece, 'head', turn(slots, a))]
    pallas_call x3 -> x7, Pallas kernels: 43.5 us -> 36.8 us  [the longest x1 23.7 us: backward(): pl.pallas_call(functools.partial(back_kernel, len(waits), len(grad_shapes...]
    unnamed x93 -> x58, local copies, waits for them, and re-layouts: 1.63 us -> 8.03 us
    all_to_all x2 -> x3, starting transfers between devices: 7.73 us -> 12.2 us  [the longest x1 5.03 us: body(): sums = lax.all_to_all(sums, ('seq', 'head'), 0, 0, tiled=True)]
    ppermute x3, starting transfers between devices: 2.16 us -> 6.11 us  [body(): lax.ppermute(piece, 'head', turn(slots, a))]
  transfers between devices with their start and end apart: 43 -> 34, of which waited for: 17 -> 15; matrix products, arithmetic and copies ran while one was open for 4% -> 5% of each run, Pallas kernels for 9% -> 27%
where the time goes in v4:
time: 177 us; the launch traced here: 176 us
  Pallas kernels  78.4 us (44%)
  starting transfers between devices  41.4 us (23%)
  waiting for transfers between devices  35.2 us (20%)
  local copies, waits for them, and re-layouts  14.4 us (8%)
  other arithmetic  6.02 us (3%)
    pallas_call x1, Pallas kernels, feed_forward(): pl.pallas_call(functools.partial(ffn_kernel, len(pieces)), grid=(4,), out...  24.8 us
    pallas_call x1, Pallas kernels, backward(): pl.pallas_call(functools.partial(back_kernel, len(waits), len(grad_shapes...  23.7 us
    pallas_call x1, Pallas kernels, forward(): pl.pallas_call(functools.partial(forward_kernel, len(pieces), slots), gri...  16.8 us
    ppermute x6, waiting for transfers between devices, over_chips(): lax.ppermute(shares, 'seq', flip(seqs, 2 * r))  16.5 us
    ppermute x3, waiting for transfers between devices, body(): lax.ppermute(ffn[a], 'head', turn(slots, a))  8.47 us
    unnamed x58, local copies, waits for them, and re-layouts  8.03 us
    ppermute x6, starting transfers between devices, over_chips(): lax.ppermute(shares, 'seq', flip(seqs, 2 * r))  7 us
    ppermute x3, starting transfers between devices, body(): lax.ppermute(piece, 'head', turn(slots, a))  6.11 us
  transfers between devices with their start and end apart: 34, of which 15 were waited for; matrix products, arithmetic and copies ran while one was open for 5% of the time, Pallas kernels for 27%

profile of v4, /device:TPU:0, one launch (start us, length us, event | category | flops | bytes accessed | tf_op | source)
XLA Modules:
  0.0 176.4 jit_solution(1710752284939749178)
XLA Ops:
  0.7 0.8 pad_add_fusion.1
  1.5 1.2 pad_maximum_fusion.own_ref
  2.8 5.1 %collective-permute-start.2 = (bf16[96,512]{1,0:T(8,128)(2,1)S(1)}, bf16[96,512]{1,0:T(8,128)(2,1)S(1)}, u32[]{:S(2)}, u32[]{:S(2)}) collective-permute-start(bf16[96,512]{1,0:T(8,128)(2,1)S(1)} %pad_maximum_fusion.3), channel_id=1, source_target_pairs={{0,3},{1,0},{2,1},{3,2},{4,7},{5,4},{6,5},{7,6},{8,11},{9,8},{10,9... | collective-permute-start | bytes 294920 | tf_op jit(solution)/shard_map/ppermute | solution.py:880
  7.9 1.0 collective-permute-start
  8.9 1.2 reshape.38
  10.3 0.8 stack_reshape.7
  11.1 5.5 %collective-permute-done.1 = bf16[96,512]{1,0:T(8,128)(2,1)S(1)} collective-permute-done((bf16[96,512]{1,0:T(8,128)(2,1)S(1)}, bf16[96,512]{1,0:T(8,128)(2,1)S(1)}, u32[]{:S(2)}, u32[]{:S(2)}) %collective-permute-start.1) | collective-permute-done | bytes 98336 | tf_op jit(solution)/shard_map/ppermute | solution.py:880
  16.8 0.7 pad_maximum_fusion.1.refs_0_.refs_1_
  17.5 0.9 broadcast_in_dim.12.refs_0_
  18.3 3.5 %all-to-all-start = ((bf16[4,8,16,512]{3,2,1,0:T(8,128)(2,1)}), bf16[4,8,16,512]{3,2,1,0:T(8,128)(2,1)S(1)}, u32[]{:S(2)}, u32[]{:S(2)}) async-start(bf16[4,8,16,512]{3,2,1,0:T(8,128)(2,1)} %after.2), calls=%async_computation | async-start | bytes 1048576 | tf_op jit(solution)/shard_map/all_to_all | solution.py:886
  21.9 2.5 %collective-permute-start.8 = (bf16[256,512]{1,0:T(8,128)(2,1)S(1)}, bf16[256,512]{1,0:T(8,128)(2,1)S(1)}, u32[]{:S(2)}, u32[]{:S(2)}) collective-permute-start(bf16[256,512]{1,0:T(8,128)(2,1)S(1)} %copy-done.2), channel_id=1, source_target_pairs={{0,24},{4,28},{8,16},{12,20},{16,8},{20,12},{24,0},{28,4},{1,25},{... | collective-permute-start | bytes 786440 | tf_op jit(solution)/shard_map/ppermute | solution.py:817
  24.3 0.5 collective-permute-start.6
  24.8 0.5 collective-permute-start.4
  25.4 6.7 %collective-permute-done.8.refs_6_ = bf16[256,512]{1,0:T(8,128)(2,1)S(1)} collective-permute-done((bf16[256,512]{1,0:T(8,128)(2,1)S(1)}, bf16[256,512]{1,0:T(8,128)(2,1)S(1)}, u32[]{:S(2)}, u32[]{:S(2)}) %collective-permute-start.8) | collective-permute-done | bytes 262176 | tf_op jit(solution)/shard_map/ppermute | solution.py:817
  32.1 4.1 %collective-permute-done.6.refs_4_ = bf16[256,512]{1,0:T(8,128)(2,1)S(1)} collective-permute-done((bf16[256,512]{1,0:T(8,128)(2,1)S(1)}, bf16[256,512]{1,0:T(8,128)(2,1)S(1)}, u32[]{:S(2)}, u32[]{:S(2)}) %collective-permute-start.6) | collective-permute-done | bytes 262176 | tf_op jit(solution)/shard_map/ppermute | solution.py:817
  36.2 0.4 collective-permute-start.5
  36.7 2.0 %collective-permute-start.15 = (bf16[4,8,16,512]{3,2,1,0:T(8,128)(2,1)S(1)}, bf16[4,8,16,512]{3,2,1,0:T(8,128)(2,1)S(1)}, u32[]{:S(2)}, u32[]{:S(2)}) collective-permute-start(bf16[4,8,16,512]{3,2,1,0:T(8,128)(2,1)S(1)} %all-to-all-done.refs_0_), channel_id=1, source_target_pairs={{0,24},{4,28},{8,16},{12,20},{16,8},{20,12},{24,0},{28,4},{1,25},{... | collective-permute-start | bytes 1572872 | tf_op jit(solution)/shard_map/ppermute | solution.py:817
  38.7 0.9 collective-permute-start.13
  39.6 0.5 collective-permute-start.11
  40.2 16.8 %attend_forward.1 = (bf16[1024,512]{1,0:T(8,128)(2,1)}, f32[16,512]{1,0:T(8,128)}, f32[1024,512]{1,0:T(8,128)}, bf16[1024,512]{1,0:T(8,128)(2,1)}, f32[1]{0:T(12...) custom-call(bf16[1024,512]{1,0:T(8,128)(2,1)} %tokens_hbm.1, ...), custom_call_target="tpu_custom_call" | custom-call | flops 16999999488 | bytes 17000000 | tf_op jit(solution)/shard_map/attend_forward/pallas_call | solution.py:396
  57.1 5.6 %collective-permute-done.13.refs_4_ = bf16[4,8,16,512]{3,2,1,0:T(8,128)(2,1)S(1)} collective-permute-done((bf16[4,8,16,512]{3,2,1,0:T(8,128)(2,1)S(1)}, bf16[4,8,16,512]{3,2,1,0:T(8,128)(2,1)S(1)}, u32[]{:S(2)}, u32[]{:S(2)}) %collective-permute-start.13) | collective-permute-done | bytes 524320 | tf_op jit(solution)/shard_map/ppermute | solution.py:817
  62.8 0.4 collective-permute-start.12
  63.3 0.8 copy-done.5
  64.1 0.2 collective-permute-start.16
  64.2 0.4 collective-permute-done.14.refs_5_
  64.6 0.9 collective-permute-done.12.refs_3_
  65.5 0.8 collective-permute-done.16.refs_7_
  66.4 0.8 copy-done.13
  67.1 24.8 %feed_forward.1 = (bf16[1024,512]{1,0:T(8,128)(2,1)}, f32[1024,512]{1,0:T(8,128)}, bf16[1024,512]{1,0:T(8,128)(2,1)}, f32[16,512]{1,0:T(8,128)}, bf16[4,4,4,2,16...) custom-call(bf16[1024,512]{1,0:T(8,128)(2,1)} %get-tuple-element.63.refs_1_.second_ref, ...), custom_call_target="tpu_custom_call" | custom-call | flops 22000001024 | bytes 22000000 | tf_op jit(solution)/shard_map/feed_forward/pallas_call | solution.py:548
  91.9 0.2 collective-permute-start.17
  92.1 4.0 %heads_back.1 = (bf16[4,1024,128]{2,1,0:T(8,128)(2,1)}, bf16[4,512,128]{2,1,0:T(8,128)(2,1)}, f32[1]{0:T(128)}) custom-call(bf16[1024,512]{1,0:T(8,128)(2,1)} %get-tuple-element.72.branch_ref, bf16[4,640,512]{2,1,0:T(8,128)(2,1)} %get-tuple-element.73.weight_ref.refs_1_, bf16[4,1024,128]{2,1,0:T(8,128)(2,1)} %get-tuple-element.74.heads_ref), custom_call_target="tpu_custom_call" | custom-call | flops 4000000000 | bytes 4000000 | tf_op jit(solution)/shard_map/heads_back/pallas_call | solution.py:586
  96.1 0.3 collective-permute-done.17
  96.4 3.1 %multiply_convert_fusion.refs_0_ = bf16[4,4,4,2,16,512]{5,4,3,2,1,0:T(8,128)(2,1)} fusion(bf16[4,4,4,2,16,512]{5,4,3,2,1,0:T(8,128)(2,1)S(1)} %collective-permute-done.17, bf16[4,4,4,2,16,512]{5,4,3,2,1,0:T(8,128)(2,1)S(1)} %copy-done, f32[]{:T(128)} %bitcast.4), kind=kLoop, calls=%fused_computation | loop fusion | flops 5242880 | bytes 6291460 | tf_op jit(solution)/shard_map/convert_element_type | solution.py:31
  99.5 3.6 %all-to-all-start.1 = ((bf16[4,4,4,2,16,512]{5,4,3,2,1,0:T(8,128)(2,1)}), bf16[4,4,4,2,16,512]{5,4,3,2,1,0:T(8,128)(2,1)S(1)}, u32[]{:S(2)}, u32[]{:S(2)}) async-start(bf16[4,4,4,2,16,512]{5,4,3,2,1,0:T(8,128)(2,1)} %multiply_convert_fusion.refs_0_), calls=%async_computation.1 | async-start | bytes 4194304 | tf_op jit(solution)/shard_map/all_to_all | solution.py:826
  103.1 23.7 %attend_back.1 = (bf16[1024,512]{1,0:T(8,128)(2,1)}, f32[32,8,128]{2,1,0:T(8,128)}, bf16[4,4,64,640]{3,2,1,0:T(8,128)(2,1)}, bf16[4,64,640]{2,1,0:T(8,128)(2,1)}...) custom-call(bf16[1024,512]{1,0:T(8,128)(2,1)} %get-tuple-element.67.normed_, ...), custom_call_target="tpu_custom_call" | custom-call | flops 27000000512 | bytes 27000000 | tf_op jit(solution)/shard_map/attend_back/pallas_call | solution.py:673
  126.8 0.2 collective-permute-start.18
  127.0 0.4 collective-permute-start.19
  127.5 0.4 collective-permute-start.21
  127.9 0.8 collective-permute-done.18.refs_1_
  128.7 0.5 collective-permute-done.19.refs_2_
  129.2 0.5 collective-permute-done.20.refs_3_
  129.7 0.5 collective-permute-done.21.refs_4_
  130.1 0.2 copy-done.19
  130.4 0.5 copy-done.20
  130.8 0.7 copy-done.1
  131.6 3.8 %join.1 = (bf16[4,2,16,512]{3,2,1,0:T(8,128)(2,1)}, bf16[4,2,16,512]{3,2,1,0:T(8,128)(2,1)}, bf16[4,2,16,512]{3,2,1,0:T(8,128)(2,1)}, bf16[4,2,16,512]{3,2,1,0:T...) custom-call(bf16[4,4,4,2,16,512]{5,4,3,2,1,0:T(8,128)(2,1)} %copy-do, ...), custom_call_target="tpu_custom_call" | custom-call | flops 3000000000 | bytes 3000000 | tf_op jit(solution)/shard_map/join/pallas_call | solution.py:721
  135.4 2.0 %collective-permute-start.25 = (bf16[4,64,640]{2,1,0:T(8,128)(2,1)}, bf16[4,64,640]{2,1,0:T(8,128)(2,1)S(1)}, u32[]{:S(2)}, u32[]{:S(2)}) collective-permute-start(bf16[4,64,640]{2,1,0:T(8,128)(2,1)} %get-tuple-element.100), channel_id=1, source_target_pairs={{0,8},{4,12},{8,0},{12,4},{16,24},{20,28},{24,16},{28,20},{1,9},{5... | collective-permute-start | bytes 983048 | tf_op jit(solution)/shard_map/ppermute | solution.py:830
  137.3 1.5 collective-permute-start.26
  138.9 1.6 collective-permute-start.22
  140.5 5.0 %all-to-all-start.2 = ((f32[32,8,128]{2,1,0:T(8,128)}), f32[32,8,128]{2,1,0:T(8,128)S(1)}, u32[]{:S(2)}, u32[]{:S(2)}) async-start(f32[32,8,128]{2,1,0:T(8,128)} %get-tuple-element.98), calls=%async_computation.2 | async-start | bytes 262144 | tf_op jit(solution)/shard_map/all_to_all | solution.py:925
  145.5 2.7 %collective-permute-start.23 = (bf16[4,2,16,512]{3,2,1,0:T(8,128)(2,1)}, bf16[4,2,16,512]{3,2,1,0:T(8,128)(2,1)S(1)}, u32[]{:S(2)}, u32[]{:S(2)}) collective-permute-start(bf16[4,2,16,512]{3,2,1,0:T(8,128)(2,1)} %get-tuple-element.96), channel_id=1, source_target_pairs={{0,2},{1,3},{2,0},{3,1},{4,6},{5,7},{6,4},{7,5},{8,10},{9,11},{10,... | collective-permute-start | bytes 393224 | tf_op jit(solution)/shard_map/ppermute | solution.py:923
  148.3 1.5 collective-permute-start.24
  149.8 8.5 %collective-permute-done.23.refs_5_.refs_2_ = bf16[4,2,16,512]{3,2,1,0:T(8,128)(2,1)S(1)} collective-permute-done((bf16[4,2,16,512]{3,2,1,0:T(8,128)(2,1)}, bf16[4,2,16,512]{3,2,1,0:T(8,128)(2,1)S(1)}, u32[]{:S(2)}, u32[]{:S(2)}) %collective-permute-start.23) | collective-permute-done | bytes 131104 | tf_op jit(solution)/shard_map/ppermute | solution.py:923
  158.3 0.6 copy-done.26
  159.0 0.1 copy-done.14
  159.4 2.1 %sum_plane.1 = (f32[64,640]{1,0:T(8,128)}, bf16[64,640]{1,0:T(8,128)(2,1)}, bf16[64,640]{1,0:T(8,128)(2,1)}, bf16[64,640]{1,0:T(8,128)(2,1)}, f32[1]{0:T(128)}) custom-call(bf16[4,64,640]{2,1,0:T(8,128)(2,1)} %get-tuple-element.99.refs_0_, bf16[4,64,640]{2,1,0:T(8,128)(2,1)} %copy-done.14, bf16[4,64,640]{2,1,0:T(8,128)(2,1)} %copy-done.15, ...), custom_call_target="tpu_custom_call" | custom-call | flops 2000000000 | bytes 2000000 | tf_op jit(solution)/shard_map/sum_plane/pallas_call | solution.py:753
  161.5 3.7 %collective-permute-start.28 = (bf16[64,640]{1,0:T(8,128)(2,1)}, bf16[64,640]{1,0:T(8,128)(2,1)S(1)}, u32[]{:S(2)}, u32[]{:S(2)}) collective-permute-start(bf16[64,640]{1,0:T(8,128)(2,1)} %get-tuple-element.106), channel_id=1, source_target_pairs={{0,3},{1,0},{2,1},{3,2},{4,7},{5,4},{6,5},{7,6},{8,11},{9,8},{10,9... | collective-permute-start | bytes 245768 | tf_op jit(solution)/shard_map/ppermute | solution.py:928
  165.2 0.6 collective-permute-start.29
  165.8 3.3 %settle.1 = (f32[512,64]{1,0:T(8,128)}, f32[32,4,16,16]{3,2,1,0:T(8,128)}, f32[8,128]{1,0:T(8,128)}) custom-call(bf16[4,2,16,512]{3,2,1,0:T(8,128)(2,1)} %get-tuple-element.94.refs_0_, bf16[4,2,16,512]{3,2,1,0:T(8,128)(2,1)} %copy-done.25, bf16[4,2,16,512]{3,2,1,0:T(8,128)(2,1)} %copy-done.26, bf16[4,2,16,512]{3,2,1,0:T(8,128)(2,1)} %copy-done.27, ...), custom_call_target="tpu_custom_call" | custom-call | flops 3000000000 | bytes 3000000 | tf_op jit(solution)/shard_map/settle/pallas_call | solution.py:788
  169.1 1.5 slice_bitcast_fusion.1
  170.6 1.2 slice_bitcast_fusion.2
  171.8 1.7 copy.40
  173.5 2.2 %copy.41 = f32[2048,16]{0,1:T(8,128)} copy(f32[2048,16]{1,0:T(8,128)} %bitcast.26) | data formatting | bytes 262144
  175.7 0.7 slice_bitcast_fusion
  (96 shorter events, 1.2 us)
Async XLA Ops:
  0.6 10.4 %copy-start.8 = (bf16[512,64]{0,1:T(8,128)(2,1)S(1)}, bf16[512,64]{0,1:T(8,128)(2,1)}, u32[]{:S(2)}) copy-start(bf16[512,64]{0,1:T(8,128)(2,1)} %param.25) | copy-start | bytes 196612
  2.8 15.6 %copy-start.3 = (bf16[640,512]{1,0:T(8,128)(2,1)}, bf16[640,512]{1,0:T(8,128)(2,1)S(1)}, u32[]{:S(2)}) copy-start(bf16[640,512]{1,0:T(8,128)(2,1)S(1)} %pad_maximum_fusion.own_ref) | copy-start | bytes 1966084
  2.8 8.3 %collective-permute-start.2 = (bf16[96,512]{1,0:T(8,128)(2,1)S(1)}, bf16[96,512]{1,0:T(8,128)(2,1)S(1)}, u32[]{:S(2)}, u32[]{:S(2)}) collective-permute-start(bf16[96,512]{1,0:T(8,128)(2,1)S(1)} %pad_maximum_fusion.3), channel_id=1, source_target_pairs={{0,3},{1,0},{2,1},{3,2},{4,7},{5,4},{6,5},{7,6},{8,11},{9,8},{10,9... | collective-permute-start | bytes 294920 | tf_op jit(solution)/shard_map/ppermute | solution.py:880
  7.9 8.7 %collective-permute-start.1 = (bf16[96,512]{1,0:T(8,128)(2,1)S(1)}, bf16[96,512]{1,0:T(8,128)(2,1)S(1)}, u32[]{:S(2)}, u32[]{:S(2)}) collective-permute-start(bf16[96,512]{1,0:T(8,128)(2,1)S(1)} %pad_maximum_fusion.3), channel_id=1, source_target_pairs={{0,2},{1,3},{2,0},{3,1},{4,6},{5,7},{6,4},{7,5},{8,10},{9,11},{10,... | collective-permute-start | bytes 294920 | tf_op jit(solution)/shard_map/ppermute | solution.py:880
  7.9 8.8 %collective-permute-start = (bf16[96,512]{1,0:T(8,128)(2,1)S(1)}, bf16[96,512]{1,0:T(8,128)(2,1)S(1)}, u32[]{:S(2)}, u32[]{:S(2)}) collective-permute-start(bf16[96,512]{1,0:T(8,128)(2,1)S(1)} %pad_maximum_fusion.3), channel_id=1, source_target_pairs={{0,1},{1,2},{2,3},{3,0},{4,5},{5,6},{6,7},{7,4},{8,9},{9,10},{10,1... | collective-permute-start | bytes 294920 | tf_op jit(solution)/shard_map/ppermute | solution.py:880
  17.5 4.4 %copy-start.2 = (bf16[256,512]{1,0:T(8,128)(2,1)S(1)}, bf16[256,512]{1,0:T(8,128)(2,1)}, u32[]{:S(2)}) copy-start(bf16[256,512]{1,0:T(8,128)(2,1)} %pad_maximum_fusion.1.refs_0_.refs_1_) | copy-start | bytes 786436
  18.3 18.3 %all-to-all-start = ((bf16[4,8,16,512]{3,2,1,0:T(8,128)(2,1)}), bf16[4,8,16,512]{3,2,1,0:T(8,128)(2,1)S(1)}, u32[]{:S(2)}, u32[]{:S(2)}) async-start(bf16[4,8,16,512]{3,2,1,0:T(8,128)(2,1)} %after.2), calls=%async_computation | async-start | bytes 1048576 | tf_op jit(solution)/shard_map/all_to_all | solution.py:886
  21.9 10.2 %collective-permute-start.8 = (bf16[256,512]{1,0:T(8,128)(2,1)S(1)}, bf16[256,512]{1,0:T(8,128)(2,1)S(1)}, u32[]{:S(2)}, u32[]{:S(2)}) collective-permute-start(bf16[256,512]{1,0:T(8,128)(2,1)S(1)} %copy-done.2), channel_id=1, source_target_pairs={{0,24},{4,28},{8,16},{12,20},{16,8},{20,12},{24,0},{28,4},{1,25},{... | collective-permute-start | bytes 786440 | tf_op jit(solution)/shard_map/ppermute | solution.py:817
  24.3 11.8 %collective-permute-start.6 = (bf16[256,512]{1,0:T(8,128)(2,1)S(1)}, bf16[256,512]{1,0:T(8,128)(2,1)S(1)}, u32[]{:S(2)}, u32[]{:S(2)}) collective-permute-start(bf16[256,512]{1,0:T(8,128)(2,1)S(1)} %copy-done.2), channel_id=1, source_target_pairs={{0,16},{4,20},{8,24},{12,28},{16,0},{20,4},{24,8},{28,12},{1,17},{... | collective-permute-start | bytes 786440 | tf_op jit(solution)/shard_map/ppermute | solution.py:817
  24.8 11.4 %collective-permute-start.4 = (bf16[256,512]{1,0:T(8,128)(2,1)S(1)}, bf16[256,512]{1,0:T(8,128)(2,1)S(1)}, u32[]{:S(2)}, u32[]{:S(2)}) collective-permute-start(bf16[256,512]{1,0:T(8,128)(2,1)S(1)} %copy-done.2), channel_id=1, source_target_pairs={{0,8},{4,12},{8,0},{12,4},{16,24},{20,28},{24,16},{28,20},{1,9},{5... | collective-permute-start | bytes 786440 | tf_op jit(solution)/shard_map/ppermute | solution.py:817
  25.4 13.3 %collective-permute-start.3 = (bf16[256,512]{1,0:T(8,128)(2,1)S(1)}, bf16[256,512]{1,0:T(8,128)(2,1)S(1)}, u32[]{:S(2)}, u32[]{:S(2)}) collective-permute-start(bf16[256,512]{1,0:T(8,128)(2,1)S(1)} %copy-done.2), channel_id=1, source_target_pairs={{0,4},{4,0},{8,12},{12,8},{16,20},{20,16},{24,28},{28,24},{1,5},{5... | collective-permute-start | bytes 786440 | tf_op jit(solution)/shard_map/ppermute | solution.py:813
  32.1 8.1 %copy-start.21 = (bf16[256,512]{1,0:T(8,128)(2,1)}, bf16[256,512]{1,0:T(8,128)(2,1)S(1)}, u32[]{:S(2)}) copy-start(bf16[256,512]{1,0:T(8,128)(2,1)S(1)} %collective-permute-done.8.refs_6_) | copy-start | bytes 786436
  32.1 7.6 %collective-permute-start.9 = (bf16[256,512]{1,0:T(8,128)(2,1)S(1)}, bf16[256,512]{1,0:T(8,128)(2,1)}, u32[]{:S(2)}, u32[]{:S(2)}) collective-permute-start(bf16[256,512]{1,0:T(8,128)(2,1)S(1)} %collective-permute-done.8.refs_6_), channel_id=1, source_target_pairs={{0,4},{4,0},{8,12},{12,8},{16,20},{20,16},{24,28},{28,24},{1,5},{5... | collective-permute-start | bytes 786440 | tf_op jit(solution)/shard_map/ppermute | solution.py:813
  36.1 4.0 %copy-start.22 = (bf16[256,512]{1,0:T(8,128)(2,1)}, bf16[256,512]{1,0:T(8,128)(2,1)S(1)}, u32[]{:S(2)}) copy-start(bf16[256,512]{1,0:T(8,128)(2,1)S(1)} %collective-permute-done.6.refs_4_) | copy-start | bytes 786436
  36.1 4.0 %collective-permute-start.7 = (bf16[256,512]{1,0:T(8,128)(2,1)S(1)}, bf16[256,512]{1,0:T(8,128)(2,1)}, u32[]{:S(2)}, u32[]{:S(2)}) collective-permute-start(bf16[256,512]{1,0:T(8,128)(2,1)S(1)} %collective-permute-done.6.refs_4_), channel_id=1, source_target_pairs={{0,4},{4,0},{8,12},{12,8},{16,20},{20,16},{24,28},{28,24},{1,5},{5... | collective-permute-start | bytes 786440 | tf_op jit(solution)/shard_map/ppermute | solution.py:813
  36.2 3.9 %copy-start.23 = (bf16[256,512]{1,0:T(8,128)(2,1)}, bf16[256,512]{1,0:T(8,128)(2,1)S(1)}, u32[]{:S(2)}) copy-start(bf16[256,512]{1,0:T(8,128)(2,1)S(1)} %collective-permute-done.4.refs_2_) | copy-start | bytes 786436
  36.2 3.9 %collective-permute-start.5 = (bf16[256,512]{1,0:T(8,128)(2,1)S(1)}, bf16[256,512]{1,0:T(8,128)(2,1)}, u32[]{:S(2)}, u32[]{:S(2)}) collective-permute-start(bf16[256,512]{1,0:T(8,128)(2,1)S(1)} %collective-permute-done.4.refs_2_), channel_id=1, source_target_pairs={{0,4},{4,0},{8,12},{12,8},{16,20},{20,16},{24,28},{28,24},{1,5},{5... | collective-permute-start | bytes 786440 | tf_op jit(solution)/shard_map/ppermute | solution.py:813
  36.7 20.4 %copy-start.4 = (bf16[4,8,16,512]{3,2,1,0:T(8,128)(2,1)}, bf16[4,8,16,512]{3,2,1,0:T(8,128)(2,1)S(1)}, u32[]{:S(2)}) copy-start(bf16[4,8,16,512]{3,2,1,0:T(8,128)(2,1)S(1)} %all-to-all-done.refs_0_) | copy-start | bytes 1572868
  36.7 26.6 %collective-permute-start.15 = (bf16[4,8,16,512]{3,2,1,0:T(8,128)(2,1)S(1)}, bf16[4,8,16,512]{3,2,1,0:T(8,128)(2,1)S(1)}, u32[]{:S(2)}, u32[]{:S(2)}) collective-permute-start(bf16[4,8,16,512]{3,2,1,0:T(8,128)(2,1)S(1)} %all-to-all-done.refs_0_), channel_id=1, source_target_pairs={{0,24},{4,28},{8,16},{12,20},{16,8},{20,12},{24,0},{28,4},{1,25},{... | collective-permute-start | bytes 1572872 | tf_op jit(solution)/shard_map/ppermute | solution.py:817
  38.7 1.5 copy-start.24
  38.7 24.0 %collective-permute-start.13 = (bf16[4,8,16,512]{3,2,1,0:T(8,128)(2,1)S(1)}, bf16[4,8,16,512]{3,2,1,0:T(8,128)(2,1)S(1)}, u32[]{:S(2)}, u32[]{:S(2)}) collective-permute-start(bf16[4,8,16,512]{3,2,1,0:T(8,128)(2,1)S(1)} %all-to-all-done.refs_0_), channel_id=1, source_target_pairs={{0,16},{4,20},{8,24},{12,28},{16,0},{20,4},{24,8},{28,12},{1,17},{... | collective-permute-start | bytes 1572872 | tf_op jit(solution)/shard_map/ppermute | solution.py:817
  39.6 23.2 %collective-permute-start.11 = (bf16[4,8,16,512]{3,2,1,0:T(8,128)(2,1)S(1)}, bf16[4,8,16,512]{3,2,1,0:T(8,128)(2,1)S(1)}, u32[]{:S(2)}, u32[]{:S(2)}) collective-permute-start(bf16[4,8,16,512]{3,2,1,0:T(8,128)(2,1)S(1)} %all-to-all-done.refs_0_), channel_id=1, source_target_pairs={{0,8},{4,12},{8,0},{12,4},{16,24},{20,28},{24,16},{28,20},{1,9},{5... | collective-permute-start | bytes 1572872 | tf_op jit(solution)/shard_map/ppermute | solution.py:817
  57.0 7.2 %collective-permute-start.10 = (bf16[4,8,16,512]{3,2,1,0:T(8,128)(2,1)S(1)}, bf16[4,8,16,512]{3,2,1,0:T(8,128)(2,1)S(1)}, u32[]{:S(2)}, u32[]{:S(2)}) collective-permute-start(bf16[4,8,16,512]{3,2,1,0:T(8,128)(2,1)S(1)} %all-to-all-done.refs_0_), channel_id=1, source_target_pairs={{0,4},{4,0},{8,12},{12,8},{16,20},{20,16},{24,28},{28,24},{1,5},{5... | collective-permute-start | bytes 1572872 | tf_op jit(solution)/shard_map/ppermute | solution.py:813
  62.7 3.6 %copy-start.9 = (bf16[4,8,16,512]{3,2,1,0:T(8,128)(2,1)}, bf16[4,8,16,512]{3,2,1,0:T(8,128)(2,1)S(1)}, u32[]{:S(2)}) copy-start(bf16[4,8,16,512]{3,2,1,0:T(8,128)(2,1)S(1)} %collective-permute-done.13.refs_4_) | copy-start | bytes 1572868
  62.7 1.9 %collective-permute-start.14 = (bf16[4,8,16,512]{3,2,1,0:T(8,128)(2,1)S(1)}, bf16[4,8,16,512]{3,2,1,0:T(8,128)(2,1)S(1)}, u32[]{:S(2)}, u32[]{:S(2)}) collective-permute-start(bf16[4,8,16,512]{3,2,1,0:T(8,128)(2,1)S(1)} %collective-permute-done.13.refs_4_), channel_id=1, source_target_pairs={{0,4},{4,0},{8,12},{12,8},{16,20},{20,16},{24,28},{28,24},{1,5},{5... | collective-permute-start | bytes 1572872 | tf_op jit(solution)/shard_map/ppermute | solution.py:813
  62.8 3.5 %copy-start.10 = (bf16[4,8,16,512]{3,2,1,0:T(8,128)(2,1)}, bf16[4,8,16,512]{3,2,1,0:T(8,128)(2,1)S(1)}, u32[]{:S(2)}) copy-start(bf16[4,8,16,512]{3,2,1,0:T(8,128)(2,1)S(1)} %collective-permute-done.11.refs_2_) | copy-start | bytes 1572868
  62.8 2.7 %collective-permute-start.12 = (bf16[4,8,16,512]{3,2,1,0:T(8,128)(2,1)S(1)}, bf16[4,8,16,512]{3,2,1,0:T(8,128)(2,1)}, u32[]{:S(2)}, u32[]{:S(2)}) collective-permute-start(bf16[4,8,16,512]{3,2,1,0:T(8,128)(2,1)S(1)} %collective-permute-done.11.refs_2_), channel_id=1, source_target_pairs={{0,4},{4,0},{8,12},{12,8},{16,20},{20,16},{24,28},{28,24},{1,5},{5... | collective-permute-start | bytes 1572872 | tf_op jit(solution)/shard_map/ppermute | solution.py:813
  63.2 0.8 copy-start.5
  64.1 2.3 %collective-permute-start.16 = (bf16[4,8,16,512]{3,2,1,0:T(8,128)(2,1)}, bf16[4,8,16,512]{3,2,1,0:T(8,128)(2,1)S(1)}, u32[]{:S(2)}, u32[]{:S(2)}) collective-permute-start(bf16[4,8,16,512]{3,2,1,0:T(8,128)(2,1)} %after.3.refs_6_), channel_id=1, source_target_pairs={{0,4},{4,0},{8,12},{12,8},{16,20},{20,16},{24,28},{28,24},{1,5},{5... | collective-permute-start | bytes 1572872 | tf_op jit(solution)/shard_map/ppermute | solution.py:813
  64.2 2.1 %copy-start.11 = (bf16[4,8,16,512]{3,2,1,0:T(8,128)(2,1)}, bf16[4,8,16,512]{3,2,1,0:T(8,128)(2,1)S(1)}, u32[]{:S(2)}) copy-start(bf16[4,8,16,512]{3,2,1,0:T(8,128)(2,1)S(1)} %collective-permute-done.10.refs_1_) | copy-start | bytes 1572868
  64.6 1.7 copy-start.12
  66.3 0.8 copy-start.13
  91.9 4.4 %collective-permute-start.17 = (bf16[4,4,4,2,16,512]{5,4,3,2,1,0:T(8,128)(2,1)}, bf16[4,4,4,2,16,512]{5,4,3,2,1,0:T(8,128)(2,1)S(1)}, u32[]{:S(2)}, u32[]{:S(2)}) collective-permute-start(bf16[4,4,4,2,16,512]{5,4,3,2,1,0:T(8,128)(2,1)} %get-tuple-element.71), channel_id=1, source_target_pairs={{0,4},{4,0},{8,12},{12,8},{16,20},{20,16},{24,28},{28,24},{1,5},{5... | collective-permute-start | bytes 6291464 | tf_op jit(solution)/shard_map/ppermute | solution.py:813
  92.1 4.2 %copy-start = (bf16[4,4,4,2,16,512]{5,4,3,2,1,0:T(8,128)(2,1)S(1)}, bf16[4,4,4,2,16,512]{5,4,3,2,1,0:T(8,128)(2,1)}, u32[]{:S(2)}) copy-start(bf16[4,4,4,2,16,512]{5,4,3,2,1,0:T(8,128)(2,1)} %get-tuple-element.70) | copy-start | bytes 6291460
  99.5 30.6 %all-to-all-start.1 = ((bf16[4,4,4,2,16,512]{5,4,3,2,1,0:T(8,128)(2,1)}), bf16[4,4,4,2,16,512]{5,4,3,2,1,0:T(8,128)(2,1)S(1)}, u32[]{:S(2)}, u32[]{:S(2)}) async-start(bf16[4,4,4,2,16,512]{5,4,3,2,1,0:T(8,128)(2,1)} %multiply_convert_fusion.refs_0_), calls=%async_computation.1 | async-start | bytes 4194304 | tf_op jit(solution)/shard_map/all_to_all | solution.py:826
  126.8 1.9 %collective-permute-start.18 = (bf16[4,64,640]{2,1,0:T(8,128)(2,1)}, bf16[4,64,640]{2,1,0:T(8,128)(2,1)S(1)}, u32[]{:S(2)}, u32[]{:S(2)}) collective-permute-start(bf16[4,64,640]{2,1,0:T(8,128)(2,1)} %get-tuple-element.89), channel_id=1, source_target_pairs={{0,4},{4,0},{8,12},{12,8},{16,20},{20,16},{24,28},{28,24},{1,5},{5... | collective-permute-start | bytes 983048 | tf_op jit(solution)/shard_map/ppermute | solution.py:813
  127.0 2.2 %collective-permute-start.19 = (bf16[4,64,640]{2,1,0:T(8,128)(2,1)}, bf16[4,64,640]{2,1,0:T(8,128)(2,1)S(1)}, u32[]{:S(2)}, u32[]{:S(2)}) collective-permute-start(bf16[4,64,640]{2,1,0:T(8,128)(2,1)} %get-tuple-element.90), channel_id=1, source_target_pairs={{0,4},{4,0},{8,12},{12,8},{16,20},{20,16},{24,28},{28,24},{1,5},{5... | collective-permute-start | bytes 983048 | tf_op jit(solution)/shard_map/ppermute | solution.py:813
  127.4 2.3 %collective-permute-start.20 = (bf16[4,64,640]{2,1,0:T(8,128)(2,1)}, bf16[4,64,640]{2,1,0:T(8,128)(2,1)S(1)}, u32[]{:S(2)}, u32[]{:S(2)}) collective-permute-start(bf16[4,64,640]{2,1,0:T(8,128)(2,1)} %get-tuple-element.91), channel_id=1, source_target_pairs={{0,4},{4,0},{8,12},{12,8},{16,20},{20,16},{24,28},{28,24},{1,5},{5... | collective-permute-start | bytes 983048 | tf_op jit(solution)/shard_map/ppermute | solution.py:813
  127.5 2.6 %collective-permute-start.21 = (bf16[4,64,640]{2,1,0:T(8,128)(2,1)}, bf16[4,64,640]{2,1,0:T(8,128)(2,1)S(1)}, u32[]{:S(2)}, u32[]{:S(2)}) collective-permute-start(bf16[4,64,640]{2,1,0:T(8,128)(2,1)} %get-tuple-element.92), channel_id=1, source_target_pairs={{0,4},{4,0},{8,12},{12,8},{16,20},{20,16},{24,28},{28,24},{1,5},{5... | collective-permute-start | bytes 983048 | tf_op jit(solution)/shard_map/ppermute | solution.py:813
  128.7 1.4 copy-start.17
  129.2 1.0 copy-start.18
  129.7 0.7 copy-start.19
  130.1 0.7 copy-start.20
  130.1 1.4 copy-start.1
  135.4 22.9 %collective-permute-start.25 = (bf16[4,64,640]{2,1,0:T(8,128)(2,1)}, bf16[4,64,640]{2,1,0:T(8,128)(2,1)S(1)}, u32[]{:S(2)}, u32[]{:S(2)}) collective-permute-start(bf16[4,64,640]{2,1,0:T(8,128)(2,1)} %get-tuple-element.100), channel_id=1, source_target_pairs={{0,8},{4,12},{8,0},{12,4},{16,24},{20,28},{24,16},{28,20},{1,9},{5... | collective-permute-start | bytes 983048 | tf_op jit(solution)/shard_map/ppermute | solution.py:830
  137.3 20.9 %collective-permute-start.26 = (bf16[4,64,640]{2,1,0:T(8,128)(2,1)}, bf16[4,64,640]{2,1,0:T(8,128)(2,1)S(1)}, u32[]{:S(2)}, u32[]{:S(2)}) collective-permute-start(bf16[4,64,640]{2,1,0:T(8,128)(2,1)} %get-tuple-element.101), channel_id=1, source_target_pairs={{0,16},{4,20},{8,24},{12,28},{16,0},{20,4},{24,8},{28,12},{1,17},{... | collective-permute-start | bytes 983048 | tf_op jit(solution)/shard_map/ppermute | solution.py:830
  138.8 19.5 %collective-permute-start.27 = (bf16[4,64,640]{2,1,0:T(8,128)(2,1)}, bf16[4,64,640]{2,1,0:T(8,128)(2,1)S(1)}, u32[]{:S(2)}, u32[]{:S(2)}) collective-permute-start(bf16[4,64,640]{2,1,0:T(8,128)(2,1)} %get-tuple-element.102), channel_id=1, source_target_pairs={{0,24},{4,28},{8,16},{12,20},{16,8},{20,12},{24,0},{28,4},{1,25},{... | collective-permute-start | bytes 983048 | tf_op jit(solution)/shard_map/ppermute | solution.py:830
  138.9 9.4 %collective-permute-start.22 = (bf16[4,2,16,512]{3,2,1,0:T(8,128)(2,1)}, bf16[4,2,16,512]{3,2,1,0:T(8,128)(2,1)S(1)}, u32[]{:S(2)}, u32[]{:S(2)}) collective-permute-start(bf16[4,2,16,512]{3,2,1,0:T(8,128)(2,1)} %get-tuple-element.95), channel_id=1, source_target_pairs={{0,1},{1,2},{2,3},{3,0},{4,5},{5,6},{6,7},{7,4},{8,9},{9,10},{10,1... | collective-permute-start | bytes 393224 | tf_op jit(solution)/shard_map/ppermute | solution.py:923
  140.5 17.7 %all-to-all-start.2 = ((f32[32,8,128]{2,1,0:T(8,128)}), f32[32,8,128]{2,1,0:T(8,128)S(1)}, u32[]{:S(2)}, u32[]{:S(2)}) async-start(f32[32,8,128]{2,1,0:T(8,128)} %get-tuple-element.98), calls=%async_computation.2 | async-start | bytes 262144 | tf_op jit(solution)/shard_map/all_to_all | solution.py:925
  145.5 12.7 %collective-permute-start.23 = (bf16[4,2,16,512]{3,2,1,0:T(8,128)(2,1)}, bf16[4,2,16,512]{3,2,1,0:T(8,128)(2,1)S(1)}, u32[]{:S(2)}, u32[]{:S(2)}) collective-permute-start(bf16[4,2,16,512]{3,2,1,0:T(8,128)(2,1)} %get-tuple-element.96), channel_id=1, source_target_pairs={{0,2},{1,3},{2,0},{3,1},{4,6},{5,7},{6,4},{7,5},{8,10},{9,11},{10,... | collective-permute-start | bytes 393224 | tf_op jit(solution)/shard_map/ppermute | solution.py:923
  148.3 10.0 %copy-start.25 = (bf16[4,2,16,512]{3,2,1,0:T(8,128)(2,1)}, bf16[4,2,16,512]{3,2,1,0:T(8,128)(2,1)S(1)}, u32[]{:S(2)}) copy-start(bf16[4,2,16,512]{3,2,1,0:T(8,128)(2,1)S(1)} %collective-permute-done.22.refs_4_.refs_1_) | copy-start | bytes 393220
  148.3 9.9 %collective-permute-start.24 = (bf16[4,2,16,512]{3,2,1,0:T(8,128)(2,1)}, bf16[4,2,16,512]{3,2,1,0:T(8,128)(2,1)S(1)}, u32[]{:S(2)}, u32[]{:S(2)}) collective-permute-start(bf16[4,2,16,512]{3,2,1,0:T(8,128)(2,1)} %get-tuple-element.97), channel_id=1, source_target_pairs={{0,3},{1,0},{2,1},{3,2},{4,7},{5,4},{6,5},{7,6},{8,11},{9,8},{10,9... | collective-permute-start | bytes 393224 | tf_op jit(solution)/shard_map/ppermute | solution.py:923
  158.2 0.7 copy-start.26
  158.2 0.7 copy-start.27
  158.2 0.8 copy-start.7
  158.2 0.9 copy-start.14
  158.3 1.0 copy-start.15
  158.3 1.1 copy-start.16
  161.5 14.2 %collective-permute-start.28 = (bf16[64,640]{1,0:T(8,128)(2,1)}, bf16[64,640]{1,0:T(8,128)(2,1)S(1)}, u32[]{:S(2)}, u32[]{:S(2)}) collective-permute-start(bf16[64,640]{1,0:T(8,128)(2,1)} %get-tuple-element.106), channel_id=1, source_target_pairs={{0,3},{1,0},{2,1},{3,2},{4,7},{5,4},{6,5},{7,6},{8,11},{9,8},{10,9... | collective-permute-start | bytes 245768 | tf_op jit(solution)/shard_map/ppermute | solution.py:928
  165.2 10.5 %collective-permute-start.29 = (bf16[64,640]{1,0:T(8,128)(2,1)}, bf16[64,640]{1,0:T(8,128)(2,1)S(1)}, u32[]{:S(2)}, u32[]{:S(2)}) collective-permute-start(bf16[64,640]{1,0:T(8,128)(2,1)} %get-tuple-element.107), channel_id=1, source_target_pairs={{0,2},{1,3},{2,0},{3,1},{4,6},{5,7},{6,4},{7,5},{8,10},{9,11},{10,... | collective-permute-start | bytes 245768 | tf_op jit(solution)/shard_map/ppermute | solution.py:928
  165.8 9.9 %collective-permute-start.30 = (bf16[64,640]{1,0:T(8,128)(2,1)}, bf16[64,640]{1,0:T(8,128)(2,1)S(1)}, u32[]{:S(2)}, u32[]{:S(2)}) collective-permute-start(bf16[64,640]{1,0:T(8,128)(2,1)} %get-tuple-element.108), channel_id=1, source_target_pairs={{0,1},{1,2},{2,3},{3,0},{4,5},{5,6},{6,7},{7,4},{8,9},{9,10},{10,1... | collective-permute-start | bytes 245768 | tf_op jit(solution)/shard_map/ppermute | solution.py:928
  165.8 9.9 %copy-start.6 = (f32[64,640]{1,0:T(8,128)S(1)}, f32[64,640]{1,0:T(8,128)}, u32[]{:S(2)}) copy-start(f32[64,640]{1,0:T(8,128)} %get-tuple-element.105) | copy-start | bytes 491524

commit v5 on v4

--- a/solution.py
+++ b/solution.py
@@ -12,7 +12,6 @@
 PAIR = 128
 F32 = jnp.float32
 BF16 = jnp.bfloat16
-LIMIT = 56 * 1024 * 1024
 
 
 def nn(a, b):
@@ -236,7 +235,7 @@
 
 def kept_shapes(length, lead=()):
     n = length // CHUNK
-    shape = jax.ShapeDtypeStruct
+    shape = pltpu.HBM
     return (
         [shape(lead + (length, PAIR), BF16)] * 3
         + [shape(lead + (length, PAIR), F32)] * 4
@@ -277,8 +276,8 @@
     return pl.CostEstimate(flops=int(micros * 1e9), bytes_accessed=int(micros * 1e6), transcendentals=0)
 
 
-def params():
-    return pltpu.CompilerParams(vmem_limit_bytes=LIMIT)
+def params(megabytes=56):
+    return pltpu.CompilerParams(vmem_limit_bytes=megabytes * 1024 * 1024)
 
 
 def select(width, offset, share, total):
@@ -391,7 +390,7 @@
         shape((length, width), F32),
         shape((length, width), BF16),
     ]
-    stacked_outs = [shape((slots, length, PAIR), BF16), shape((slots, width + PAIR, 4 * PAIR), BF16)]
+    stacked_outs = [shape((slots, length, PAIR), BF16), pltpu.HBM((slots, width + PAIR, 4 * PAIR), BF16)]
     stacked_outs += kept_shapes(length, (slots,))
     made = pl.pallas_call(
         functools.partial(forward_kernel, len(pieces), slots),
@@ -400,7 +399,7 @@
         in_specs=[fixed(o.shape) for o in operands],
         out_specs=[fixed(o.shape) for o in outs] + [mark_spec()] + by_step(stacked_outs),
         scratch_shapes=[pltpu.VMEM((length, PAIR), BF16), pltpu.VMEM((devices, 8, 128), F32)],
-        compiler_params=params(),
+        compiler_params=params(44),
         cost_estimate=cost(17),
         name="attend_forward",
     )(*operands)
@@ -455,13 +454,20 @@
 
 def ffn_kernel(count, second_ref, rows_ref, cotangent_ref, residual_hbm, *refs):
     pieces = refs[:count]
-    result_ref, grad_ref, branch_ref, sums_ref = refs[count : count + 4]
-    outs = refs[count + 4 : -8]
-    weights, grads, residual, total, back, in_sems, out_sems, residual_sem = refs[-8:]
+    result_hbm, branch_hbm, sums_ref = refs[count : count + 3]
+    outs = refs[count + 3 : -11]
+    (weights, grads, residual, total, back, result, branch, in_sems, out_sems, residual_sem, tile_sems) = refs[-11:]
     k = pl.program_id(0)
     length, width = second_ref.shape
     tiles = [slice(r, r + 256) for r in range(0, length, 256)]
     fetch = pltpu.make_async_copy(residual_hbm, residual, residual_sem)
+
+    def leave(rows):
+        tile = rows.start // 256
+        return [
+            pltpu.make_async_copy(source.at[rows, :], target.at[rows, :], tile_sems.at[i, tile])
+            for i, (source, target) in enumerate([(result, result_hbm), (branch, branch_hbm)])
+        ]
 
     @pl.when(k == 0)
     def _():
@@ -516,20 +522,23 @@
         outer = jnp.zeros((1, width), F32)
         for rows in tiles:
             base = residual[rows, :]
-            result_ref[rows, :] = low(base + total[rows, :] + bias)
+            result[rows, :] = low(base + total[rows, :] + bias)
             grad = back[rows, :]
             normal, rate = norm_parts(base)
             upstream = cotangent_ref[rows, :].astype(F32)
             gain_grad = gain_grad + jnp.sum(grad * normal, axis=0, keepdims=True)
             shift_grad = shift_grad + jnp.sum(grad, axis=0, keepdims=True)
             outer = outer + jnp.sum(upstream, axis=0, keepdims=True)
-            full = upstream + norm_back(grad, normal, rate, gain)
-            grad_ref[rows, :] = full
-            branch_ref[rows, :] = low(full)
+            branch[rows, :] = low(upstream + norm_back(grad, normal, rate, gain))
+            for copy in leave(rows):
+                copy.start()
         sums_ref[0:2, :] = jnp.zeros((2, width), F32)
         sums_ref[2:3, :] = gain_grad
         sums_ref[3:4, :] = shift_grad
         sums_ref[4:5, :] = outer
+        for rows in tiles:
+            for copy in leave(rows):
+                copy.wait()
         for block in range(4):
             for copy in grad_copies(block, grads, outs, out_sems):
                 copy.wait()
@@ -541,7 +550,6 @@
     weights = (4, width // 16, 2, 16, width)
     outs = [
         shape((length, width), BF16),
-        shape((length, width), F32),
         shape((length, width), BF16),
         shape((16, width), F32),
     ]
@@ -550,18 +558,21 @@
         grid=(4,),
         out_shape=outs + [shape(s, BF16) for s in grad_shapes],
         in_specs=[fixed(o.shape) for o in (second, rows, cotangent)] + anywhere([residual, *pieces]),
-        out_specs=[fixed(o.shape) for o in outs] + anywhere(grad_shapes),
+        out_specs=anywhere(outs[:2]) + [fixed(outs[2].shape)] + anywhere(grad_shapes),
         scratch_shapes=[
             pltpu.VMEM(weights, BF16),
             pltpu.VMEM(weights, BF16),
             pltpu.VMEM((length, width), F32),
             pltpu.VMEM((length, width), F32),
             pltpu.VMEM((length, width), F32),
+            pltpu.VMEM((length, width), BF16),
+            pltpu.VMEM((length, width), BF16),
             pltpu.SemaphoreType.DMA((4, 8)),
             pltpu.SemaphoreType.DMA((4, 8)),
             pltpu.SemaphoreType.DMA,
+            pltpu.SemaphoreType.DMA((2, length // 256)),
         ],
-        compiler_params=params(),
+        compiler_params=params(44),
         cost_estimate=cost(22),
         name="feed_forward",
     )(second, rows, cotangent, residual, *pieces)
@@ -593,36 +604,47 @@
         ]
         + [fixed(heads.shape)],
         out_specs=[fixed(o.shape) for o in outs] + [mark_spec()],
-        compiler_params=params(),
+        compiler_params=params(16),
         cost_estimate=cost(4),
         name="heads_back",
     )(branch, weights, heads)
 
 
-def pair_grads(grad_ref, output_grad_ref, normed_ref, kept, outs, backs, made):
+def pair_grads(grad_ref, output_grad_ref, normed_ref, kept, backs, made):
     attend_backward(grad_ref, kept, backs)
     made[:, : 4 * PAIR] = low(tn(normed_ref[...], backs[...]))
     made[:, 4 * PAIR :] = output_grad_ref[...]
+
+
+def leave_copies(slot, made, outs, sems):
     if len(outs) == 1:
-        outs[0][...] = made[...]
-        return
+        return [pltpu.make_async_copy(made, outs[0].at[slot], sems.at[0])]
     seq = lax.axis_index("seq")
-    rows = outs[1].shape[0]
-    for chip in range(outs[0].shape[0]):
+    chips = outs[0].shape[0]
+    rows = made.shape[0] // (2 * chips)
+    copies = []
+    for chip in range(chips):
         for core, out in enumerate((outs[0].at[chip], outs[1 + chip])):
             start = pl.multiple_of((seq ^ (2 * chip + core)) * rows, rows)
-            out[...] = made[pl.ds(start, rows), :]
-
-
-def back_kernel(waits, parts_out, normed_ref, rows_ref, before_ref, tokens_hbm, residual_grad_hbm, *refs):
+            copies.append(
+                pltpu.make_async_copy(
+                    made.at[pl.ds(start, rows), :],
+                    out.at[pl.ds(pl.multiple_of(slot * rows, rows), rows), :],
+                    sems.at[len(copies)],
+                )
+            )
+    return copies
+
+
+def back_kernel(waits, parts_out, slots, normed_ref, rows_ref, before_ref, tokens_hbm, residual_grad_hbm, *refs):
     refs = refs[waits:]
     weight, grad_ref, output_grad_ref, kept, refs = refs[0], refs[1], refs[2], refs[3:12], refs[12:]
     input_grad_ref, sums_ref, outs, mark = refs[0], refs[1], refs[2 : 2 + parts_out], refs[2 + parts_out]
-    backs, made, total, tokens, residual_grad, sems = refs[3 + parts_out :]
+    backs, made, total, tokens, residual_grad, vector_blocks, sems, out_sems = refs[3 + parts_out :]
     length, width = normed_ref.shape
     devices = sums_ref.shape[0]
     share = width // devices
-    step, steps = pl.program_id(0), pl.num_programs(0)
+    step, steps = pl.program_id(0), slots
     copies = [
         pltpu.make_async_copy(tokens_hbm, tokens, sems.at[0]),
         pltpu.make_async_copy(residual_grad_hbm, residual_grad, sems.at[1]),
@@ -635,7 +657,16 @@
         total[...] = jnp.zeros_like(total)
         mark[0] = 1.0
 
-    pair_grads(grad_ref, output_grad_ref, normed_ref, kept, outs, backs, made)
+    parity = lax.rem(step, 2)
+
+    @pl.when(step >= 2)
+    def _():
+        for copy in leave_copies(step - 2, made.at[parity], outs, out_sems.at[parity]):
+            copy.wait()
+
+    pair_grads(grad_ref, output_grad_ref, normed_ref, kept, backs, made.at[parity])
+    for copy in leave_copies(step, made.at[parity], outs, out_sems.at[parity]):
+        copy.start()
     total[...] += nt(backs[...], weight[:width, :])
 
     @pl.when(step == steps - 1)
@@ -650,39 +681,60 @@
             normal, rate = norm_parts(tokens[rows, :].astype(F32))
             gain_grad = gain_grad + jnp.sum(grad * normal, axis=0, keepdims=True)
             shift_grad = shift_grad + jnp.sum(grad, axis=0, keepdims=True)
-            input_grad_ref[rows, :] = low(residual_grad[rows, :] + norm_back(grad, normal, rate, gain))
-        sums_ref[...] = jnp.zeros_like(sums_ref)
+            input_grad_ref[rows, :] = low(residual_grad[rows, :].astype(F32) + norm_back(grad, normal, rate, gain))
         small = [gain_grad, shift_grad] + [before_ref[i : i + 1, :] for i in range(2, 5)]
-        sums_ref[:, 0, :] = collect(small, devices, share)
-        sums_ref[:, 1, :] = collect([before_ref[i : i + 1, :] for i in range(5, 9)], devices, share)
+        sums_ref[:, :128] = collect(small, devices, share)
+        sums_ref[:, 128:] = collect([before_ref[i : i + 1, :] for i in range(5, 9)], devices, share)
+        leaving = []
+        if parts_out > 1:
+            z, chips = lax.axis_index("head"), outs[0].shape[0]
+            for chip in range(chips):
+                for core, out in enumerate((outs[0].at[chip], outs[1 + chip])):
+                    n = len(leaving)
+                    rows = [
+                        sums_ref[pl.ds(own_device(core, chip, steps) + lax.rem(z + steps - a, steps), 1), :]
+                        for a in range(steps)
+                    ]
+                    block = jnp.concatenate(rows + [jnp.zeros((16 - steps, 256), F32)], axis=0)
+                    vector_blocks[n] = vector_rows(block, made.shape[2])
+                    leaving.append(
+                        pltpu.make_async_copy(
+                            vector_blocks.at[n], out.at[pl.ds(out.shape[0] - 16, 16), :], sems.at[2 + n]
+                        )
+                    )
+        for copy in leaving:
+            copy.start()
+        for last in (steps - 2, steps - 1):
+            for copy in leave_copies(last, made.at[last % 2], outs, out_sems.at[last % 2]):
+                copy.wait()
+        for copy in leaving:
+            copy.wait()
 
 
 def backward(normed, rows, before, tokens, residual_grad, devices, waits, members, grad_shapes):
     length, width = normed.shape
     slots = members[0].shape[0]
     shape = jax.ShapeDtypeStruct
-    outs = [shape((length, width), BF16), shape((devices, 8, 128), F32)]
-    grads = [shape(s[:-2] + (slots,) + s[-2:], BF16) for s in grad_shapes]
-    grad_specs = [
-        by_step([g])[0]
-        if len(g.shape) == 3
-        else pl.BlockSpec((g.shape[0], None) + g.shape[2:], lambda a: (0, a, 0, 0))
-        for g in grads
-    ]
+    outs = [shape((length, width), BF16), shape((devices, 256), F32)]
+    grads = [shape(s, BF16) for s in grad_shapes]
     large = [tokens, residual_grad]
     return pl.pallas_call(
-        functools.partial(back_kernel, len(waits), len(grad_shapes)),
+        functools.partial(back_kernel, len(waits), len(grad_shapes), slots),
         grid=(slots,),
         out_shape=outs + grads + [MARK],
         in_specs=[fixed(o.shape) for o in (normed, rows, before)] + anywhere(large + waits) + by_step(members),
-        out_specs=[fixed(o.shape) for o in outs] + grad_specs + [mark_spec()],
+        out_specs=[fixed(o.shape) for o in outs] + anywhere(grads) + [mark_spec()],
         scratch_shapes=[
             pltpu.VMEM((length, 4 * PAIR), BF16),
-            pltpu.VMEM((width, 5 * PAIR), BF16),
+            pltpu.VMEM((2, width, 5 * PAIR), BF16),
             pltpu.VMEM((length, width), F32),
         ]
         + [pltpu.VMEM((length, width), m.dtype) for m in large]
-        + [pltpu.SemaphoreType.DMA((2,))],
+        + [
+            pltpu.VMEM((8, 16, 5 * PAIR), BF16),
+            pltpu.SemaphoreType.DMA((10,)),
+            pltpu.SemaphoreType.DMA((2, 8)),
+        ],
         compiler_params=params(),
         cost_estimate=cost(27),
         name="attend_back",
@@ -700,24 +752,34 @@
     )(value, *others)
 
 
-def join_kernel(chips, slots, ffn_ref, *refs):
-    keep_ref, others, sums_ref, refs = refs[0], refs[1 : 1 + chips], refs[1 + chips], refs[2 + chips :]
-    ffn_outs, outs, sums_out = refs[:slots], refs[slots : slots + chips], refs[slots + chips]
+def vector_values(block):
+    return block[:, :256].astype(F32) + block[:, 256:512].astype(F32)
+
+
+def vector_rows(values, width):
+    high = low(values)
+    rest = jnp.zeros((values.shape[0], width - 512), BF16)
+    return jnp.concatenate([high, low(values - high.astype(F32)), rest], axis=1)
+
+
+def join_kernel(chips, slots, ffn_ref, keep_ref, *refs):
+    others, ffn_outs, outs = refs[:chips], refs[chips : chips + slots], refs[chips + slots :]
     z = lax.axis_index("head")
     for a, out in enumerate(ffn_outs):
         place = lax.rem(z + a, slots)
-        out[...] = low(functools.reduce(lambda x, y: x + y, [ffn_ref[c, pl.ds(place, 1)][0].astype(F32) for c in range(chips)]))
+        out[...] = low(add(*[ffn_ref[c, pl.ds(place, 1)][0] for c in range(chips)]))
+    body = keep_ref.shape[1] - 16
     for chip, out in enumerate(outs):
-        out[...] = low(keep_ref[chip].astype(F32) + others[chip][...].astype(F32))
-    sums_out[...] = sums_ref[...]
-
-
-def join(ffn, keep, others, sums):
+        out[:body, :] = low(add(keep_ref[chip, :body, :], others[chip][:body, :]))
+        values = vector_values(keep_ref[chip, body:, :]) + vector_values(others[chip][body:, :])
+        out[body:, :] = vector_rows(values, out.shape[1])
+
+
+def join(ffn, keep, others):
     shape = jax.ShapeDtypeStruct
     chips, slots = ffn.shape[:2]
-    operands = [ffn, keep, *others, sums]
+    operands = [ffn, keep, *others]
     outs = [shape(ffn.shape[2:], BF16)] * slots + [shape(keep.shape[1:], BF16)] * chips
-    outs += [shape(sums.shape, F32)]
     made = pl.pallas_call(
         functools.partial(join_kernel, chips, slots),
         grid=(1,),
@@ -728,27 +790,32 @@
         cost_estimate=cost(3),
         name="join",
     )(*operands)
-    return made[:slots], made[slots : slots + chips], made[-1]
-
-
-def sum_plane_kernel(slots, *refs):
-    pairs, mine_ref, sends = refs[: -slots - 1], refs[-slots - 1], refs[-slots:-1]
+    return made[:slots], made[slots:]
+
+
+def sum_plane_kernel(slots, pairs, mine_ref, vector_ref, sends, mark):
+    rows = mine_ref.shape[0]
+    values = functools.reduce(lambda x, y: x + y, [vector_values(p[slots * rows :, :]) for p in pairs])
+    vector_ref[...] = values[:8, :]
     for a in range(slots):
-        mine = functools.reduce(lambda x, y: x + y, [p[a].astype(F32) for p in pairs])
+        mine = add(*[p[a * rows : (a + 1) * rows, :] for p in pairs])
         if a == 0:
             mine_ref[...] = mine
         else:
-            sends[a - 1][...] = low(mine)
-    refs[-1][0] = 1.0
-
-
-def sum_plane(pairs, waits):
+            sends[a - 1][:rows, :] = low(mine)
+            sends[a - 1][rows:, :] = vector_rows(jnp.broadcast_to(values[a : a + 1, :], (16, 256)), mine.shape[1])
+    mark[0] = 1.0
+
+
+def sum_plane(pairs, slots, waits):
     shape = jax.ShapeDtypeStruct
-    slots = pairs[0].shape[0]
-    outs = [shape(pairs[0].shape[1:], F32)] + [shape(pairs[0].shape[1:], BF16)] * (slots - 1)
+    rows, columns = (pairs[0].shape[0] - 16) // slots, pairs[0].shape[1]
+    outs = [shape((rows, columns), F32), shape((8, 256), F32)]
+    outs += [shape((rows + 16, columns), BF16)] * (slots - 1)
 
     def kernel(*refs):
-        sum_plane_kernel(slots, *refs[: len(pairs)], *refs[len(pairs) + len(waits) :])
+        made = refs[len(pairs) + len(waits) :]
+        sum_plane_kernel(slots, refs[: len(pairs)], made[0], made[1], made[2:-1], made[-1])
 
     return pl.pallas_call(
         kernel,
@@ -756,45 +823,39 @@
         out_shape=outs + [MARK],
         in_specs=[fixed(p.shape) for p in pairs] + anywhere(waits),
         out_specs=[fixed(o.shape) for o in outs] + [mark_spec()],
-        compiler_params=params(),
+        compiler_params=params(12),
         cost_estimate=cost(2),
         name="sum_plane",
     )(*pairs, *waits)
 
 
-def settle_kernel(slots, *refs):
-    ffn, sums_ref, expand_ref, shrink_ref, vector_ref = refs[:slots], *refs[slots + 1 :]
+def settle_kernel(ffn, expand_ref, shrink_ref):
     blocks, _, share, width = ffn[0].shape
-    total = functools.reduce(lambda x, y: x + y, [f[...].astype(F32) for f in ffn])
+    total = add(*[f[...] for f in ffn])
     expand_ref[...] = total[:, 0].reshape(blocks * share, width).T
     for i in range(blocks):
         shrink_ref[:, i] = total[i, 1].T.reshape(width // share, share, share)
-    vector_ref[...] = jnp.sum(sums_ref[...], axis=0)
-
-
-def settle(ffn, sums, wait):
+
+
+def settle(ffn, wait):
     shape = jax.ShapeDtypeStruct
     slots = len(ffn)
     blocks, _, share, width = ffn[0].shape
-    outs = [
-        shape((width, blocks * share), F32),
-        shape((width // share, blocks, share, share), F32),
-        shape(sums.shape[1:], F32),
-    ]
+    outs = [shape((width, blocks * share), F32), shape((width // share, blocks, share, share), F32)]
 
     def kernel(*refs):
-        settle_kernel(slots, *refs[:slots], None, *refs[slots : slots + 1], *refs[slots + 2 :])
+        settle_kernel(refs[:slots], *refs[slots + 1 :])
 
     return pl.pallas_call(
         kernel,
         grid=(1,),
         out_shape=outs,
-        in_specs=[fixed(o.shape) for o in (*ffn, sums)] + anywhere([wait]),
+        in_specs=[fixed(f.shape) for f in ffn] + anywhere([wait]),
         out_specs=[fixed(o.shape) for o in outs],
-        compiler_params=params(),
+        compiler_params=params(12),
         cost_estimate=cost(3),
         name="settle",
-    )(*ffn, sums, wait)
+    )(*ffn, wait)
 
 
 def flip(count, bit):
@@ -885,7 +946,8 @@
         load = jnp.broadcast_to(load.reshape(1, 8, share, width), (slots, 8, share, width))
         load = lax.all_to_all(after(load, near), "head", 0, 0, tiled=True)
         held = over_chips(load, chips, seqs)
-        pair_shapes = [(chips, width // seqs, 5 * PAIR)] + [(width // seqs, 5 * PAIR)] * chips
+        tall = (slots * width // seqs + 16, 5 * PAIR)
+        pair_shapes = [(chips,) + tall] + [tall] * chips
         ffn_shapes = [(chips, slots, 4, 2, 16, width)] * 2
     else:
         every = lax.all_gather(own, "head", axis=0, tiled=False)
@@ -894,7 +956,7 @@
         vectors = [lax.all_gather(block, ("seq", "head"), axis=0, tiled=False)]
         both = lax.all_gather(load, ("seq", "head"), axis=2, tiled=True)
         ffn_pieces = [both.reshape(4, 2, width // 16, 16, width).transpose(0, 2, 1, 3, 4)]
-        pair_shapes = [(width, 5 * PAIR)]
+        pair_shapes = [(slots, width, 5 * PAIR)]
         ffn_shapes = [ffn_pieces[0].shape]
 
     (normed, rows, residual, second, _), (heads, weights, *members) = forward(
@@ -902,7 +964,7 @@
     )
     if direct:
         ffn_pieces = over_cores(held[:-1] + [after(held[-1], second)], seqs)
-    result, residual_grad, branch, sums, *ffn_grads = feed_forward(
+    result, branch, sums, *ffn_grads = feed_forward(
         second, rows, cotangent, residual, ffn_pieces, ffn_shapes
     )
     heads_grad, output_grad, mark = heads_back(branch, weights, heads)
@@ -912,21 +974,22 @@
         ffn_mine = low(add(ffn_grads[0], to_mate(ffn_grads[1], seqs)) * mark[0])
         waits = [ffn_mine]
     input_grad, sums, *pair_grads, _ = backward(
-        normed, rows, sums, inputs, residual_grad, devices, waits, members, pair_shapes
+        normed, rows, sums, inputs, branch, devices, waits, members, pair_shapes
     )
 
     if direct:
         keep, *sends = pair_grads
-        ffn, pairs, sums = join(
-            to_chips(ffn_mine, seqs), keep, [to_mate(s, seqs) for s in sends], sums
-        )
+        ffn, pairs = join(to_chips(ffn_mine, seqs), keep, [to_mate(m, seqs) for m in sends])
         ffn = [ffn[0]] + [lax.ppermute(ffn[a], "head", turn(slots, a)) for a in range(1, slots)]
         pairs = [pairs[0]] + from_chips(pairs[1:], seqs)
-        sums = lax.all_to_all(sums, ("seq", "head"), 0, 0, tiled=True)
-        mine, *sends, wait = sum_plane(pairs, ffn[1:] + [sums])
-        expand_grad, shrink_grad, sums = settle(ffn, sums, wait)
+        mine, sums, *sends, wait = sum_plane(pairs, slots, ffn[1:])
+        expand_grad, shrink_grad = settle(ffn, wait)
         came = [lax.ppermute(m, "head", turn(slots, slots - 1 - a)) for a, m in enumerate(sends)]
-        pair_sum = add(mine, *came)
+        rows = mine.shape[0]
+        pair_sum = add(mine, *[c[:rows] for c in came])
+        sums = sums[0] + functools.reduce(
+            lambda a, b: a + b, [c[rows, :256].astype(F32) + c[rows, 256:512].astype(F32) for c in came]
+        )
     else:
         ffn_sum = lax.psum_scatter(
             ffn_grads[0].astype(F32).transpose(0, 2, 1, 3, 4).reshape(4, 2, width, width), ("seq", "head"), scatter_dimension=2, tiled=True
@@ -936,11 +999,13 @@
         pair_sum = lax.psum_scatter(every, "head", scatter_dimension=0, tiled=False)
         pair_sum = lax.psum_scatter(pair_sum, "seq", scatter_dimension=0, tiled=True)
 
-        sums = jnp.sum(lax.all_to_all(sums, ("seq", "head"), 0, 0, tiled=True), axis=0)
+        sums = jnp.sum(
+            lax.all_to_all(sums.reshape(devices, 1, 256), ("seq", "head"), 0, 0, tiled=True), axis=(0, 1)
+        )
         expand_grad = ffn_sum[:, 0].reshape(hidden_share, width).T
         shrink_grad = ffn_sum[:, 1].reshape(4, share, devices, share).transpose(2, 0, 3, 1)
 
-    vector = [sums[0, i * share : (i + 1) * share] for i in range(5)]
+    vector = [sums[i * share : (i + 1) * share] for i in range(5)]
     return (
         result,
         input_grad,
@@ -954,7 +1019,7 @@
         vector[2],
         vector[3],
         expand_grad,
-        sums[1, :hidden_share],
+        sums[128 : 128 + hidden_share],
         shrink_grad.reshape(devices * hidden_share, share),
         vector[4],
     )

time: 177 us -> 171 us (0.966)
  Pallas kernels: 78.4 us -> 68 us
  starting transfers between devices: 41.4 us -> 35.5 us
  local copies, waits for them, and re-layouts: 14.4 us -> 19.9 us
  waiting for transfers between devices: 35.2 us -> 40.4 us
    unnamed x58 -> x54, local copies, waits for them, and re-layouts: 8.03 us -> 15.1 us
    all_to_all x1 -> x0, starting transfers between devices: 5.03 us -> none  [body(): sums = lax.all_to_all(sums, ('seq', 'head'), 0, 0, tiled=True)]
    ppermute x3, waiting for transfers between devices: 0.01 us -> 4.96 us  [body(): lax.ppermute(m, 'head', turn(slots, slots - 1 - a))]
    ppermute x6, waiting for transfers between devices: 16.5 us -> 12.9 us  [over_chips(): lax.ppermute(shares, 'seq', flip(seqs, 2 * r))]
    squeeze x2 -> x0, local copies, waits for them, and re-layouts: 2.67 us -> none  [the longest x1 1.47 us: body(): vector = [sums[0, i * share:(i + 1) * share] for i in range(5)]]
    pallas_call x1, Pallas kernels: 3.95 us -> 1.29 us  [heads_back(): pl.pallas_call(heads_kernel, grid=(1,), out_shape=outs + [MARK], in_specs...]
    pallas_call x1, Pallas kernels: 16.8 us -> 14.4 us  [forward(): pl.pallas_call(functools.partial(forward_kernel, len(pieces), slots), gri...]
    pallas_call x1, Pallas kernels: 24.8 us -> 22.5 us  [feed_forward(): pl.pallas_call(functools.partial(ffn_kernel, len(pieces)), grid=(4,), out...]
  transfers between devices with their start and end apart: 34 -> 33, of which waited for: 15 -> 19; matrix products, arithmetic and copies ran while one was open for 5% -> 2% of each run, Pallas kernels for 27% -> 24%
where the time goes in v5:
time: 171 us
  Pallas kernels  68 us (40%)
  waiting for transfers between devices  40.4 us (24%)
  starting transfers between devices  35.5 us (21%)
  local copies, waits for them, and re-layouts  19.9 us (12%)
  other arithmetic  6.08 us (4%)
    pallas_call x1, Pallas kernels, backward(): pl.pallas_call(functools.partial(back_kernel, len(waits), len(grad_shapes...  24.3 us
    pallas_call x1, Pallas kernels, feed_forward(): pl.pallas_call(functools.partial(ffn_kernel, len(pieces)), grid=(4,), out...  22.5 us
    unnamed x54, local copies, waits for them, and re-layouts  15.1 us
    pallas_call x1, Pallas kernels, forward(): pl.pallas_call(functools.partial(forward_kernel, len(pieces), slots), gri...  14.4 us
    ppermute x6, waiting for transfers between devices, over_chips(): lax.ppermute(shares, 'seq', flip(seqs, 2 * r))  12.9 us
    ppermute x3, waiting for transfers between devices, body(): lax.ppermute(ffn[a], 'head', turn(slots, a))  9.88 us
    ppermute x6, starting transfers between devices, over_chips(): lax.ppermute(shares, 'seq', flip(seqs, 2 * r))  7 us
    ppermute x3, starting transfers between devices, body(): lax.ppermute(piece, 'head', turn(slots, a))  6.11 us
  transfers between devices with their start and end apart: 33, of which 19 were waited for; matrix products, arithmetic and copies ran while one was open for 2% of the time, Pallas kernels for 24%

profile of v5, /device:TPU:0, one launch (start us, length us, event | category | flops | bytes accessed | tf_op | source)
XLA Modules:
  0.0 170.7 jit_solution(17374283553175909471)
XLA Ops:
  0.7 0.8 pad_add_fusion.1
  1.5 1.2 pad_maximum_fusion.own_ref
  2.8 5.1 %collective-permute-start.2 = (bf16[96,512]{1,0:T(8,128)(2,1)S(1)}, bf16[96,512]{1,0:T(8,128)(2,1)S(1)}, u32[]{:S(2)}, u32[]{:S(2)}) collective-permute-start(bf16[96,512]{1,0:T(8,128)(2,1)S(1)} %pad_maximum_fusion.3), channel_id=1, source_target_pairs={{0,3},{1,0},{2,1},{3,2},{4,7},{5,4},{6,5},{7,6},{8,11},{9,8},{10,9... | collective-permute-start | bytes 294920 | tf_op jit(solution)/shard_map/ppermute | solution.py:941
  7.9 1.0 collective-permute-start
  8.9 1.2 reshape.49
  10.3 0.8 stack_reshape.7
  11.1 5.5 %collective-permute-done.1 = bf16[96,512]{1,0:T(8,128)(2,1)S(1)} collective-permute-done((bf16[96,512]{1,0:T(8,128)(2,1)S(1)}, bf16[96,512]{1,0:T(8,128)(2,1)S(1)}, u32[]{:S(2)}, u32[]{:S(2)}) %collective-permute-start.1) | collective-permute-done | bytes 98336 | tf_op jit(solution)/shard_map/ppermute | solution.py:941
  16.7 0.7 pad_maximum_fusion.1.refs_0_.refs_1_
  17.5 0.9 broadcast_in_dim.12.refs_0_
  18.3 3.5 %all-to-all-start = ((bf16[4,8,16,512]{3,2,1,0:T(8,128)(2,1)}), bf16[4,8,16,512]{3,2,1,0:T(8,128)(2,1)S(1)}, u32[]{:S(2)}, u32[]{:S(2)}) async-start(bf16[4,8,16,512]{3,2,1,0:T(8,128)(2,1)} %after.2), calls=%async_computation | async-start | bytes 1048576 | tf_op jit(solution)/shard_map/all_to_all | solution.py:947
  21.9 2.5 %collective-permute-start.8 = (bf16[256,512]{1,0:T(8,128)(2,1)S(1)}, bf16[256,512]{1,0:T(8,128)(2,1)S(1)}, u32[]{:S(2)}, u32[]{:S(2)}) collective-permute-start(bf16[256,512]{1,0:T(8,128)(2,1)S(1)} %copy-done), channel_id=1, source_target_pairs={{0,24},{4,28},{8,16},{12,20},{16,8},{20,12},{24,0},{28,4},{1,25},{... | collective-permute-start | bytes 786440 | tf_op jit(solution)/shard_map/ppermute | solution.py:878
  24.3 0.5 collective-permute-start.6
  24.8 0.5 collective-permute-start.4
  25.4 6.7 %collective-permute-done.8.refs_6_ = bf16[256,512]{1,0:T(8,128)(2,1)S(1)} collective-permute-done((bf16[256,512]{1,0:T(8,128)(2,1)S(1)}, bf16[256,512]{1,0:T(8,128)(2,1)S(1)}, u32[]{:S(2)}, u32[]{:S(2)}) %collective-permute-start.8) | collective-permute-done | bytes 262176 | tf_op jit(solution)/shard_map/ppermute | solution.py:878
  32.1 4.1 %collective-permute-done.6.refs_4_ = bf16[256,512]{1,0:T(8,128)(2,1)S(1)} collective-permute-done((bf16[256,512]{1,0:T(8,128)(2,1)S(1)}, bf16[256,512]{1,0:T(8,128)(2,1)S(1)}, u32[]{:S(2)}, u32[]{:S(2)}) %collective-permute-start.6) | collective-permute-done | bytes 262176 | tf_op jit(solution)/shard_map/ppermute | solution.py:878
  36.7 2.0 %collective-permute-start.15 = (bf16[4,8,16,512]{3,2,1,0:T(8,128)(2,1)S(1)}, bf16[4,8,16,512]{3,2,1,0:T(8,128)(2,1)S(1)}, u32[]{:S(2)}, u32[]{:S(2)}) collective-permute-start(bf16[4,8,16,512]{3,2,1,0:T(8,128)(2,1)S(1)} %all-to-all-done.refs_0_), channel_id=1, source_target_pairs={{0,24},{4,28},{8,16},{12,20},{16,8},{20,12},{24,0},{28,4},{1,25},{... | collective-permute-start | bytes 1572872 | tf_op jit(solution)/shard_map/ppermute | solution.py:878
  38.7 0.9 collective-permute-start.13
  39.6 0.5 collective-permute-start.11
  40.2 1.2 copy-done.6
  41.4 14.4 %attend_forward.1 = (bf16[1024,512]{1,0:T(8,128)(2,1)S(1)}, f32[16,512]{1,0:T(8,128)S(1)}, f32[1024,512]{1,0:T(8,128)S(1)}, bf16[1024,512]{1,0:T(8,128)(2,1)S(1)...) custom-call(bf16[1024,512]{1,0:T(8,128)(2,1)S(1)} %copy-done.6, ...), custom_call_target="tpu_custom_call" | custom-call | flops 16999999488 | bytes 17000000 | tf_op jit(solution)/shard_map/attend_forward/pallas_call | solution.py:395
  55.8 1.0 copy-done.1
  56.8 1.0 copy-done.9
  57.7 1.3 copy-done.15
  59.0 1.0 copy-done.16
  60.1 0.6 copy-done.17
  60.7 2.0 %collective-permute-done.13.refs_4_ = bf16[4,8,16,512]{3,2,1,0:T(8,128)(2,1)S(1)} collective-permute-done((bf16[4,8,16,512]{3,2,1,0:T(8,128)(2,1)S(1)}, bf16[4,8,16,512]{3,2,1,0:T(8,128)(2,1)S(1)}, u32[]{:S(2)}, u32[]{:S(2)}) %collective-permute-start.13) | collective-permute-done | bytes 524320 | tf_op jit(solution)/shard_map/ppermute | solution.py:878
  63.2 0.8 copy-done.3
  64.2 0.6 collective-permute-done.14.refs_5_
  64.8 1.0 collective-permute-done.12.refs_3_
  65.7 0.6 collective-permute-done.16.refs_7_
  66.3 1.0 copy-done.4
  67.4 1.2 copy-done.5
  68.6 22.5 %feed_forward.1 = (bf16[1024,512]{1,0:T(8,128)(2,1)}, bf16[1024,512]{1,0:T(8,128)(2,1)S(1)}, f32[16,512]{1,0:T(8,128)S(1)}, bf16[4,4,4,2,16,512]{5,4,3,2,1,0:T(8,128)(2,1)S(1)}, bf16[4,4,4,2,16,512]{5,4,3,2,1,0:T(8,128)(2,1)}) custom-call(bf16[1024,512]{1,0:T(8,128)(2,1)S(1)} %copy-done.2, f32[16,512]{1,0:T(8,128)S(1)} %copy-done.18, ...), custom_call_target="tpu_custom_call" | custom-call | flops 22000001024 | bytes 22000000 | tf_op jit(solution)/shard_map/feed_forward/pallas_call | solution.py:556
  91.3 1.3 heads_back.1
  92.7 0.9 copy-done.12
  93.6 0.8 copy-done.13
  94.4 1.1 collective-permute-done.17
  95.6 3.2 %multiply_convert_fusion.refs_0_ = bf16[4,4,4,2,16,512]{5,4,3,2,1,0:T(8,128)(2,1)} fusion(bf16[4,4,4,2,16,512]{5,4,3,2,1,0:T(8,128)(2,1)S(1)} %collective-permute-done.17, bf16[4,4,4,2,16,512]{5,4,3,2,1,0:T(8,128)(2,1)S(1)} %get-tuple-element.67, f32[]{:T(128)} %bitcast.4), kind=kLoop, calls=%fused_computation | loop fusion | flops 5242880 | bytes 6291460 | tf_op jit(solution)/shard_map/convert_element_type | solution.py:30
  98.8 3.6 %all-to-all-start.1 = ((bf16[4,4,4,2,16,512]{5,4,3,2,1,0:T(8,128)(2,1)}), bf16[4,4,4,2,16,512]{5,4,3,2,1,0:T(8,128)(2,1)S(1)}, u32[]{:S(2)}, u32[]{:S(2)}) async-start(bf16[4,4,4,2,16,512]{5,4,3,2,1,0:T(8,128)(2,1)} %multiply_convert_fusion.refs_0_), calls=%async_computation.1 | async-start | bytes 4194304 | tf_op jit(solution)/shard_map/all_to_all | solution.py:887
  102.4 24.3 %attend_back.1 = (bf16[1024,512]{1,0:T(8,128)(2,1)}, f32[32,256]{1,0:T(8,128)}, bf16[4,272,640]{2,1,0:T(8,128)(2,1)}, bf16[272,640]{1,0:T(8,128)(2,1)}, bf16[272...) custom-call(bf16[1024,512]{1,0:T(8,128)(2,1)} %copy-done.16, ...), custom_call_target="tpu_custom_call" | custom-call | flops 27000000512 | bytes 27000000 | tf_op jit(solution)/shard_map/attend_back/pallas_call | solution.py:721
  127.8 0.8 collective-permute-done.18.refs_0_
  128.7 0.5 collective-permute-done.19.refs_1_
  130.9 0.7 copy-done.20
  131.6 3.8 %join.1 = (bf16[4,2,16,512]{3,2,1,0:T(8,128)(2,1)}, bf16[4,2,16,512]{3,2,1,0:T(8,128)(2,1)}, bf16[4,2,16,512]{3,2,1,0:T(8,128)(2,1)}, bf16[4,2,16,512]{3,2,1,0:T...) custom-call(bf16[4,4,4,2,16,512]{5,4,3,2,1,0:T(8,128)(2,1)} %copy-do, ...), custom_call_target="tpu_custom_call" | custom-call | flops 3000000000 | bytes 3000000 | tf_op jit(solution)/shard_map/join/pallas_call | solution.py:783
  135.4 1.9 %collective-permute-start.22 = (bf16[272,640]{1,0:T(8,128)(2,1)}, bf16[272,640]{1,0:T(8,128)(2,1)S(1)}, u32[]{:S(2)}, u32[]{:S(2)}) collective-permute-start(bf16[272,640]{1,0:T(8,128)(2,1)} %get-tuple-element.90), channel_id=1, source_target_pairs={{0,8},{4,12},{8,0},{12,4},{16,24},{20,28},{24,16},{28,20},{1,9},{5... | collective-permute-start | bytes 1044488 | tf_op jit(solution)/shard_map/ppermute | solution.py:891
  137.4 1.5 collective-permute-start.23
  138.9 1.6 collective-permute-start.25
  140.6 2.4 %collective-permute-start.26 = (bf16[4,2,16,512]{3,2,1,0:T(8,128)(2,1)}, bf16[4,2,16,512]{3,2,1,0:T(8,128)(2,1)S(1)}, u32[]{:S(2)}, u32[]{:S(2)}) collective-permute-start(bf16[4,2,16,512]{3,2,1,0:T(8,128)(2,1)} %get-tuple-element.94), channel_id=1, source_target_pairs={{0,2},{1,3},{2,0},{3,1},{4,6},{5,7},{6,4},{7,5},{8,10},{9,11},{10,... | collective-permute-start | bytes 393224 | tf_op jit(solution)/shard_map/ppermute | solution.py:983
  142.9 4.6 %collective-permute-done.25.refs_4_.refs_1_ = bf16[4,2,16,512]{3,2,1,0:T(8,128)(2,1)S(1)} collective-permute-done((bf16[4,2,16,512]{3,2,1,0:T(8,128)(2,1)}, bf16[4,2,16,512]{3,2,1,0:T(8,128)(2,1)S(1)}, u32[]{:S(2)}, u32[]{:S(2)}) %collective-permute-start.25) | collective-permute-done | bytes 131104 | tf_op jit(solution)/shard_map/ppermute | solution.py:983
  147.5 0.8 collective-permute-start.27
  148.3 3.3 %collective-permute-done.26.refs_5_.refs_2_ = bf16[4,2,16,512]{3,2,1,0:T(8,128)(2,1)S(1)} collective-permute-done((bf16[4,2,16,512]{3,2,1,0:T(8,128)(2,1)}, bf16[4,2,16,512]{3,2,1,0:T(8,128)(2,1)S(1)}, u32[]{:S(2)}, u32[]{:S(2)}) %collective-permute-start.26) | collective-permute-done | bytes 131104 | tf_op jit(solution)/shard_map/ppermute | solution.py:983
  151.6 2.0 %collective-permute-done.27.refs_6_.refs_3_ = bf16[4,2,16,512]{3,2,1,0:T(8,128)(2,1)S(1)} collective-permute-done((bf16[4,2,16,512]{3,2,1,0:T(8,128)(2,1)}, bf16[4,2,16,512]{3,2,1,0:T(8,128)(2,1)S(1)}, u32[]{:S(2)}, u32[]{:S(2)}) %collective-permute-start.27) | collective-permute-done | bytes 131104 | tf_op jit(solution)/shard_map/ppermute | solution.py:983
  153.6 1.4 collective-permute-done.23.refs_2_
  155.0 1.0 copy-done.8
  156.0 0.6 sum_plane.1
  156.5 3.5 %collective-permute-start.28 = (bf16[80,640]{1,0:T(8,128)(2,1)S(1)}, bf16[80,640]{1,0:T(8,128)(2,1)S(1)}, u32[]{:S(2)}, u32[]{:S(2)}) collective-permute-start(bf16[80,640]{1,0:T(8,128)(2,1)S(1)} %get-tuple-element.97), channel_id=1, source_target_pairs={{0,3},{1,0},{2,1},{3,2},{4,7},{5,4},{6,5},{7,6},{8,11},{9,8},{10,9... | collective-permute-start | bytes 307208 | tf_op jit(solution)/shard_map/ppermute | solution.py:987
  160.0 1.1 collective-permute-start.30
  161.2 1.0 settle.1
  162.2 0.8 copy.40
  163.0 1.0 copy.41
  163.9 5.0 %collective-permute-done.29 = bf16[80,640]{1,0:T(8,128)(2,1)S(1)} collective-permute-done((bf16[80,640]{1,0:T(8,128)(2,1)S(1)}, bf16[80,640]{1,0:T(8,128)(2,1)S(1)}, u32[]{:S(2)}, u32[]{:S(2)}) %collective-permute-start.29) | collective-permute-done | bytes 102432 | tf_op jit(solution)/shard_map/ppermute | solution.py:987
  168.9 0.5 slice_bitcast_fusion.2
  169.4 0.6 slice_bitcast_fusion.1
  170.1 0.7 slice_bitcast_fusion
  (91 shorter events, 4.7 us)
Async XLA Ops:
  0.6 10.4 %copy-start.21 = (bf16[512,64]{0,1:T(8,128)(2,1)S(1)}, bf16[512,64]{0,1:T(8,128)(2,1)}, u32[]{:S(2)}) copy-start(bf16[512,64]{0,1:T(8,128)(2,1)} %param.25) | copy-start | bytes 196612
  2.8 8.3 %collective-permute-start.2 = (bf16[96,512]{1,0:T(8,128)(2,1)S(1)}, bf16[96,512]{1,0:T(8,128)(2,1)S(1)}, u32[]{:S(2)}, u32[]{:S(2)}) collective-permute-start(bf16[96,512]{1,0:T(8,128)(2,1)S(1)} %pad_maximum_fusion.3), channel_id=1, source_target_pairs={{0,3},{1,0},{2,1},{3,2},{4,7},{5,4},{6,5},{7,6},{8,11},{9,8},{10,9... | collective-permute-start | bytes 294920 | tf_op jit(solution)/shard_map/ppermute | solution.py:941
  7.9 8.7 %collective-permute-start.1 = (bf16[96,512]{1,0:T(8,128)(2,1)S(1)}, bf16[96,512]{1,0:T(8,128)(2,1)S(1)}, u32[]{:S(2)}, u32[]{:S(2)}) collective-permute-start(bf16[96,512]{1,0:T(8,128)(2,1)S(1)} %pad_maximum_fusion.3), channel_id=1, source_target_pairs={{0,2},{1,3},{2,0},{3,1},{4,6},{5,7},{6,4},{7,5},{8,10},{9,11},{10,... | collective-permute-start | bytes 294920 | tf_op jit(solution)/shard_map/ppermute | solution.py:941
  7.9 8.8 %collective-permute-start = (bf16[96,512]{1,0:T(8,128)(2,1)S(1)}, bf16[96,512]{1,0:T(8,128)(2,1)S(1)}, u32[]{:S(2)}, u32[]{:S(2)}) collective-permute-start(bf16[96,512]{1,0:T(8,128)(2,1)S(1)} %pad_maximum_fusion.3), channel_id=1, source_target_pairs={{0,1},{1,2},{2,3},{3,0},{4,5},{5,6},{6,7},{7,4},{8,9},{9,10},{10,1... | collective-permute-start | bytes 294920 | tf_op jit(solution)/shard_map/ppermute | solution.py:941
  17.5 4.4 %copy-start = (bf16[256,512]{1,0:T(8,128)(2,1)S(1)}, bf16[256,512]{1,0:T(8,128)(2,1)}, u32[]{:S(2)}) copy-start(bf16[256,512]{1,0:T(8,128)(2,1)} %pad_maximum_fusion.1.refs_0_.refs_1_) | copy-start | bytes 786436
  18.3 18.3 %all-to-all-start = ((bf16[4,8,16,512]{3,2,1,0:T(8,128)(2,1)}), bf16[4,8,16,512]{3,2,1,0:T(8,128)(2,1)S(1)}, u32[]{:S(2)}, u32[]{:S(2)}) async-start(bf16[4,8,16,512]{3,2,1,0:T(8,128)(2,1)} %after.2), calls=%async_computation | async-start | bytes 1048576 | tf_op jit(solution)/shard_map/all_to_all | solution.py:947
  21.9 10.2 %collective-permute-start.8 = (bf16[256,512]{1,0:T(8,128)(2,1)S(1)}, bf16[256,512]{1,0:T(8,128)(2,1)S(1)}, u32[]{:S(2)}, u32[]{:S(2)}) collective-permute-start(bf16[256,512]{1,0:T(8,128)(2,1)S(1)} %copy-done), channel_id=1, source_target_pairs={{0,24},{4,28},{8,16},{12,20},{16,8},{20,12},{24,0},{28,4},{1,25},{... | collective-permute-start | bytes 786440 | tf_op jit(solution)/shard_map/ppermute | solution.py:878
  24.3 11.8 %collective-permute-start.6 = (bf16[256,512]{1,0:T(8,128)(2,1)S(1)}, bf16[256,512]{1,0:T(8,128)(2,1)S(1)}, u32[]{:S(2)}, u32[]{:S(2)}) collective-permute-start(bf16[256,512]{1,0:T(8,128)(2,1)S(1)} %copy-done), channel_id=1, source_target_pairs={{0,16},{4,20},{8,24},{12,28},{16,0},{20,4},{24,8},{28,12},{1,17},{... | collective-permute-start | bytes 786440 | tf_op jit(solution)/shard_map/ppermute | solution.py:878
  24.8 11.4 %collective-permute-start.4 = (bf16[256,512]{1,0:T(8,128)(2,1)S(1)}, bf16[256,512]{1,0:T(8,128)(2,1)S(1)}, u32[]{:S(2)}, u32[]{:S(2)}) collective-permute-start(bf16[256,512]{1,0:T(8,128)(2,1)S(1)} %copy-done), channel_id=1, source_target_pairs={{0,8},{4,12},{8,0},{12,4},{16,24},{20,28},{24,16},{28,20},{1,9},{5... | collective-permute-start | bytes 786440 | tf_op jit(solution)/shard_map/ppermute | solution.py:878
  25.4 13.3 %collective-permute-start.3 = (bf16[256,512]{1,0:T(8,128)(2,1)S(1)}, bf16[256,512]{1,0:T(8,128)(2,1)S(1)}, u32[]{:S(2)}, u32[]{:S(2)}) collective-permute-start(bf16[256,512]{1,0:T(8,128)(2,1)S(1)} %copy-done), channel_id=1, source_target_pairs={{0,4},{4,0},{8,12},{12,8},{16,20},{20,16},{24,28},{28,24},{1,5},{5... | collective-permute-start | bytes 786440 | tf_op jit(solution)/shard_map/ppermute | solution.py:874
  32.1 7.6 %collective-permute-start.9 = (bf16[256,512]{1,0:T(8,128)(2,1)S(1)}, bf16[256,512]{1,0:T(8,128)(2,1)}, u32[]{:S(2)}, u32[]{:S(2)}) collective-permute-start(bf16[256,512]{1,0:T(8,128)(2,1)S(1)} %collective-permute-done.8.refs_6_), channel_id=1, source_target_pairs={{0,4},{4,0},{8,12},{12,8},{16,20},{20,16},{24,28},{28,24},{1,5},{5... | collective-permute-start | bytes 786440 | tf_op jit(solution)/shard_map/ppermute | solution.py:874
  36.1 4.0 %collective-permute-start.7 = (bf16[256,512]{1,0:T(8,128)(2,1)S(1)}, bf16[256,512]{1,0:T(8,128)(2,1)}, u32[]{:S(2)}, u32[]{:S(2)}) collective-permute-start(bf16[256,512]{1,0:T(8,128)(2,1)S(1)} %collective-permute-done.6.refs_4_), channel_id=1, source_target_pairs={{0,4},{4,0},{8,12},{12,8},{16,20},{20,16},{24,28},{28,24},{1,5},{5... | collective-permute-start | bytes 786440 | tf_op jit(solution)/shard_map/ppermute | solution.py:874
  36.2 3.9 %collective-permute-start.5 = (bf16[256,512]{1,0:T(8,128)(2,1)S(1)}, bf16[256,512]{1,0:T(8,128)(2,1)}, u32[]{:S(2)}, u32[]{:S(2)}) collective-permute-start(bf16[256,512]{1,0:T(8,128)(2,1)S(1)} %collective-permute-done.4.refs_2_), channel_id=1, source_target_pairs={{0,4},{4,0},{8,12},{12,8},{16,20},{20,16},{24,28},{28,24},{1,5},{5... | collective-permute-start | bytes 786440 | tf_op jit(solution)/shard_map/ppermute | solution.py:874
  36.7 26.6 %collective-permute-start.15 = (bf16[4,8,16,512]{3,2,1,0:T(8,128)(2,1)S(1)}, bf16[4,8,16,512]{3,2,1,0:T(8,128)(2,1)S(1)}, u32[]{:S(2)}, u32[]{:S(2)}) collective-permute-start(bf16[4,8,16,512]{3,2,1,0:T(8,128)(2,1)S(1)} %all-to-all-done.refs_0_), channel_id=1, source_target_pairs={{0,24},{4,28},{8,16},{12,20},{16,8},{20,12},{24,0},{28,4},{1,25},{... | collective-permute-start | bytes 1572872 | tf_op jit(solution)/shard_map/ppermute | solution.py:878
  38.7 24.0 %collective-permute-start.13 = (bf16[4,8,16,512]{3,2,1,0:T(8,128)(2,1)S(1)}, bf16[4,8,16,512]{3,2,1,0:T(8,128)(2,1)S(1)}, u32[]{:S(2)}, u32[]{:S(2)}) collective-permute-start(bf16[4,8,16,512]{3,2,1,0:T(8,128)(2,1)S(1)} %all-to-all-done.refs_0_), channel_id=1, source_target_pairs={{0,16},{4,20},{8,24},{12,28},{16,0},{20,4},{24,8},{28,12},{1,17},{... | collective-permute-start | bytes 1572872 | tf_op jit(solution)/shard_map/ppermute | solution.py:878
  39.6 23.3 %collective-permute-start.11 = (bf16[4,8,16,512]{3,2,1,0:T(8,128)(2,1)S(1)}, bf16[4,8,16,512]{3,2,1,0:T(8,128)(2,1)}, u32[]{:S(2)}, u32[]{:S(2)}) collective-permute-start(bf16[4,8,16,512]{3,2,1,0:T(8,128)(2,1)S(1)} %all-to-all-done.refs_0_), channel_id=1, source_target_pairs={{0,8},{4,12},{8,0},{12,4},{16,24},{20,28},{24,16},{28,20},{1,9},{5... | collective-permute-start | bytes 1572872 | tf_op jit(solution)/shard_map/ppermute | solution.py:878
  40.2 1.2 copy-start.6
  55.8 1.0 copy-start.1
  56.8 1.0 copy-start.9
  57.7 1.3 copy-start.15
  59.0 1.0 copy-start.16
  60.1 0.6 copy-start.17
  60.7 3.5 %collective-permute-start.10 = (bf16[4,8,16,512]{3,2,1,0:T(8,128)(2,1)S(1)}, bf16[4,8,16,512]{3,2,1,0:T(8,128)(2,1)S(1)}, u32[]{:S(2)}, u32[]{:S(2)}) collective-permute-start(bf16[4,8,16,512]{3,2,1,0:T(8,128)(2,1)S(1)} %all-to-all-done.refs_0_), channel_id=1, source_target_pairs={{0,4},{4,0},{8,12},{12,8},{16,20},{20,16},{24,28},{28,24},{1,5},{5... | collective-permute-start | bytes 1572872 | tf_op jit(solution)/shard_map/ppermute | solution.py:874
  60.7 5.7 %copy-start.2 = (bf16[1024,512]{1,0:T(8,128)(2,1)S(1)}, bf16[1024,512]{1,0:T(8,128)(2,1)}, u32[]{:S(2)}) copy-start(bf16[1024,512]{1,0:T(8,128)(2,1)} %copy-done.1) | copy-start | bytes 3145732
  60.7 5.7 %copy-start.18 = (f32[16,512]{1,0:T(8,128)S(1)}, f32[16,512]{1,0:T(8,128)}, u32[]{:S(2)}) copy-start(f32[16,512]{1,0:T(8,128)} %copy-done.17) | copy-start | bytes 98308
  62.7 2.0 %collective-permute-start.14 = (bf16[4,8,16,512]{3,2,1,0:T(8,128)(2,1)S(1)}, bf16[4,8,16,512]{3,2,1,0:T(8,128)(2,1)}, u32[]{:S(2)}, u32[]{:S(2)}) collective-permute-start(bf16[4,8,16,512]{3,2,1,0:T(8,128)(2,1)S(1)} %collective-permute-done.13.refs_4_), channel_id=1, source_target_pairs={{0,4},{4,0},{8,12},{12,8},{16,20},{20,16},{24,28},{28,24},{1,5},{5... | collective-permute-start | bytes 1572872 | tf_op jit(solution)/shard_map/ppermute | solution.py:874
  62.9 2.8 %collective-permute-start.12 = (bf16[4,8,16,512]{3,2,1,0:T(8,128)(2,1)}, bf16[4,8,16,512]{3,2,1,0:T(8,128)(2,1)}, u32[]{:S(2)}, u32[]{:S(2)}) collective-permute-start(bf16[4,8,16,512]{3,2,1,0:T(8,128)(2,1)} %collective-permute-done.11.refs_2_), channel_id=1, source_target_pairs={{0,4},{4,0},{8,12},{12,8},{16,20},{20,16},{24,28},{28,24},{1,5},{5... | collective-permute-start | bytes 1572872 | tf_op jit(solution)/shard_map/ppermute | solution.py:874
  63.2 0.8 copy-start.3
  64.0 2.3 %collective-permute-start.16 = (bf16[4,8,16,512]{3,2,1,0:T(8,128)(2,1)}, bf16[4,8,16,512]{3,2,1,0:T(8,128)(2,1)S(1)}, u32[]{:S(2)}, u32[]{:S(2)}) collective-permute-start(bf16[4,8,16,512]{3,2,1,0:T(8,128)(2,1)} %after.3.refs_6_), channel_id=1, source_target_pairs={{0,4},{4,0},{8,12},{12,8},{16,20},{20,16},{24,28},{28,24},{1,5},{5... | collective-permute-start | bytes 1572872 | tf_op jit(solution)/shard_map/ppermute | solution.py:874
  66.3 1.0 copy-start.4
  67.4 1.2 copy-start.5
  68.6 22.7 %copy-start.7 = (bf16[4,640,512]{2,1,0:T(8,128)(2,1)S(1)}, bf16[4,640,512]{2,1,0:T(8,128)(2,1)}, u32[]{:S(2)}) copy-start(bf16[4,640,512]{2,1,0:T(8,128)(2,1)} %get-tuple-element.69.weight_ref.refs_1_) | copy-start | bytes 7864324
  68.6 22.7 %copy-start.10 = (bf16[4,1024,128]{2,1,0:T(8,128)(2,1)S(1)}, bf16[4,1024,128]{2,1,0:T(8,128)(2,1)}, u32[]{:S(2)}) copy-start(bf16[4,1024,128]{2,1,0:T(8,128)(2,1)} %copy-done.9) | copy-start | bytes 3145732
  91.1 1.5 copy-start.11
  91.1 1.5 copy-start.19
  91.1 4.4 %collective-permute-start.17 = (bf16[4,4,4,2,16,512]{5,4,3,2,1,0:T(8,128)(2,1)}, bf16[4,4,4,2,16,512]{5,4,3,2,1,0:T(8,128)(2,1)S(1)}, u32[]{:S(2)}, u32[]{:S(2)}) collective-permute-start(bf16[4,4,4,2,16,512]{5,4,3,2,1,0:T(8,128)(2,1)} %get-tuple-element.68), channel_id=1, source_target_pairs={{0,4},{4,0},{8,12},{12,8},{16,20},{20,16},{24,28},{28,24},{1,5},{5... | collective-permute-start | bytes 6291464 | tf_op jit(solution)/shard_map/ppermute | solution.py:874
  92.7 1.0 copy-start.12
  93.6 0.8 copy-start.13
  98.8 31.4 %all-to-all-start.1 = ((bf16[4,4,4,2,16,512]{5,4,3,2,1,0:T(8,128)(2,1)}), bf16[4,4,4,2,16,512]{5,4,3,2,1,0:T(8,128)(2,1)S(1)}, u32[]{:S(2)}, u32[]{:S(2)}) async-start(bf16[4,4,4,2,16,512]{5,4,3,2,1,0:T(8,128)(2,1)} %multiply_convert_fusion.refs_0_), calls=%async_computation.1 | async-start | bytes 4194304 | tf_op jit(solution)/shard_map/all_to_all | solution.py:887
  126.7 1.9 %collective-permute-start.18 = (bf16[272,640]{1,0:T(8,128)(2,1)}, bf16[272,640]{1,0:T(8,128)(2,1)S(1)}, u32[]{:S(2)}, u32[]{:S(2)}) collective-permute-start(bf16[272,640]{1,0:T(8,128)(2,1)} %get-tuple-element.85), channel_id=1, source_target_pairs={{0,4},{4,0},{8,12},{12,8},{16,20},{20,16},{24,28},{28,24},{1,5},{5... | collective-permute-start | bytes 1044488 | tf_op jit(solution)/shard_map/ppermute | solution.py:874
  126.9 2.2 %collective-permute-start.19 = (bf16[272,640]{1,0:T(8,128)(2,1)}, bf16[272,640]{1,0:T(8,128)(2,1)S(1)}, u32[]{:S(2)}, u32[]{:S(2)}) collective-permute-start(bf16[272,640]{1,0:T(8,128)(2,1)} %get-tuple-element.86), channel_id=1, source_target_pairs={{0,4},{4,0},{8,12},{12,8},{16,20},{20,16},{24,28},{28,24},{1,5},{5... | collective-permute-start | bytes 1044488 | tf_op jit(solution)/shard_map/ppermute | solution.py:874
  127.3 2.4 %collective-permute-start.20 = (bf16[272,640]{1,0:T(8,128)(2,1)}, bf16[272,640]{1,0:T(8,128)(2,1)S(1)}, u32[]{:S(2)}, u32[]{:S(2)}) collective-permute-start(bf16[272,640]{1,0:T(8,128)(2,1)} %get-tuple-element.87), channel_id=1, source_target_pairs={{0,4},{4,0},{8,12},{12,8},{16,20},{20,16},{24,28},{28,24},{1,5},{5... | collective-permute-start | bytes 1044488 | tf_op jit(solution)/shard_map/ppermute | solution.py:874
  127.4 2.7 %collective-permute-start.21 = (bf16[272,640]{1,0:T(8,128)(2,1)}, bf16[272,640]{1,0:T(8,128)(2,1)S(1)}, u32[]{:S(2)}, u32[]{:S(2)}) collective-permute-start(bf16[272,640]{1,0:T(8,128)(2,1)} %get-tuple-element.88), channel_id=1, source_target_pairs={{0,4},{4,0},{8,12},{12,8},{16,20},{20,16},{24,28},{28,24},{1,5},{5... | collective-permute-start | bytes 1044488 | tf_op jit(solution)/shard_map/ppermute | solution.py:874
  128.7 1.5 copy-start.22
  129.2 1.0 copy-start.23
  129.6 0.7 copy-start.24
  130.1 0.7 copy-start.25
  130.2 1.5 copy-start.20
  135.4 18.1 %collective-permute-start.22 = (bf16[272,640]{1,0:T(8,128)(2,1)}, bf16[272,640]{1,0:T(8,128)(2,1)S(1)}, u32[]{:S(2)}, u32[]{:S(2)}) collective-permute-start(bf16[272,640]{1,0:T(8,128)(2,1)} %get-tuple-element.90), channel_id=1, source_target_pairs={{0,8},{4,12},{8,0},{12,4},{16,24},{20,28},{24,16},{28,20},{1,9},{5... | collective-permute-start | bytes 1044488 | tf_op jit(solution)/shard_map/ppermute | solution.py:891
  137.4 17.6 %collective-permute-start.23 = (bf16[272,640]{1,0:T(8,128)(2,1)}, bf16[272,640]{1,0:T(8,128)(2,1)S(1)}, u32[]{:S(2)}, u32[]{:S(2)}) collective-permute-start(bf16[272,640]{1,0:T(8,128)(2,1)} %get-tuple-element.91), channel_id=1, source_target_pairs={{0,16},{4,20},{8,24},{12,28},{16,0},{20,4},{24,8},{28,12},{1,17},{... | collective-permute-start | bytes 1044488 | tf_op jit(solution)/shard_map/ppermute | solution.py:891
  138.9 16.1 %collective-permute-start.24 = (bf16[272,640]{1,0:T(8,128)(2,1)}, bf16[272,640]{1,0:T(8,128)(2,1)S(1)}, u32[]{:S(2)}, u32[]{:S(2)}) collective-permute-start(bf16[272,640]{1,0:T(8,128)(2,1)} %get-tuple-element.92), channel_id=1, source_target_pairs={{0,24},{4,28},{8,16},{12,20},{16,8},{20,12},{24,0},{28,4},{1,25},{... | collective-permute-start | bytes 1044488 | tf_op jit(solution)/shard_map/ppermute | solution.py:891
  138.9 8.6 %collective-permute-start.25 = (bf16[4,2,16,512]{3,2,1,0:T(8,128)(2,1)}, bf16[4,2,16,512]{3,2,1,0:T(8,128)(2,1)S(1)}, u32[]{:S(2)}, u32[]{:S(2)}) collective-permute-start(bf16[4,2,16,512]{3,2,1,0:T(8,128)(2,1)} %get-tuple-element.93), channel_id=1, source_target_pairs={{0,1},{1,2},{2,3},{3,0},{4,5},{5,6},{6,7},{7,4},{8,9},{9,10},{10,1... | collective-permute-start | bytes 393224 | tf_op jit(solution)/shard_map/ppermute | solution.py:983
  140.6 11.0 %collective-permute-start.26 = (bf16[4,2,16,512]{3,2,1,0:T(8,128)(2,1)}, bf16[4,2,16,512]{3,2,1,0:T(8,128)(2,1)S(1)}, u32[]{:S(2)}, u32[]{:S(2)}) collective-permute-start(bf16[4,2,16,512]{3,2,1,0:T(8,128)(2,1)} %get-tuple-element.94), channel_id=1, source_target_pairs={{0,2},{1,3},{2,0},{3,1},{4,6},{5,7},{6,4},{7,5},{8,10},{9,11},{10,... | collective-permute-start | bytes 393224 | tf_op jit(solution)/shard_map/ppermute | solution.py:983
  147.5 6.1 %collective-permute-start.27 = (bf16[4,2,16,512]{3,2,1,0:T(8,128)(2,1)}, bf16[4,2,16,512]{3,2,1,0:T(8,128)(2,1)S(1)}, u32[]{:S(2)}, u32[]{:S(2)}) collective-permute-start(bf16[4,2,16,512]{3,2,1,0:T(8,128)(2,1)} %get-tuple-element.95), channel_id=1, source_target_pairs={{0,3},{1,0},{2,1},{3,2},{4,7},{5,4},{6,5},{7,6},{8,11},{9,8},{10,9... | collective-permute-start | bytes 393224 | tf_op jit(solution)/shard_map/ppermute | solution.py:983
  155.0 1.0 copy-start.8
  156.0 5.2 %copy-start.14 = (bf16[4,2,16,512]{3,2,1,0:T(8,128)(2,1)S(1)}, bf16[4,2,16,512]{3,2,1,0:T(8,128)(2,1)}, u32[]{:S(2)}) copy-start(bf16[4,2,16,512]{3,2,1,0:T(8,128)(2,1)} %get-tuple-element.101.refs_0_) | copy-start | bytes 393220
  156.5 7.4 %collective-permute-start.28 = (bf16[80,640]{1,0:T(8,128)(2,1)S(1)}, bf16[80,640]{1,0:T(8,128)(2,1)S(1)}, u32[]{:S(2)}, u32[]{:S(2)}) collective-permute-start(bf16[80,640]{1,0:T(8,128)(2,1)S(1)} %get-tuple-element.97), channel_id=1, source_target_pairs={{0,3},{1,0},{2,1},{3,2},{4,7},{5,4},{6,5},{7,6},{8,11},{9,8},{10,9... | collective-permute-start | bytes 307208 | tf_op jit(solution)/shard_map/ppermute | solution.py:987
  160.0 8.9 %collective-permute-start.29 = (bf16[80,640]{1,0:T(8,128)(2,1)S(1)}, bf16[80,640]{1,0:T(8,128)(2,1)S(1)}, u32[]{:S(2)}, u32[]{:S(2)}) collective-permute-start(bf16[80,640]{1,0:T(8,128)(2,1)S(1)} %get-tuple-element.98), channel_id=1, source_target_pairs={{0,2},{1,3},{2,0},{3,1},{4,6},{5,7},{6,4},{7,5},{8,10},{9,11},{10,... | collective-permute-start | bytes 307208 | tf_op jit(solution)/shard_map/ppermute | solution.py:987
  160.0 8.9 %collective-permute-start.30 = (bf16[80,640]{1,0:T(8,128)(2,1)S(1)}, bf16[80,640]{1,0:T(8,128)(2,1)S(1)}, u32[]{:S(2)}, u32[]{:S(2)}) collective-permute-start(bf16[80,640]{1,0:T(8,128)(2,1)S(1)} %get-tuple-element.99), channel_id=1, source_target_pairs={{0,1},{1,2},{2,3},{3,0},{4,5},{5,6},{6,7},{7,4},{8,9},{9,10},{10,1... | collective-permute-start | bytes 307208 | tf_op jit(solution)/shard_map/ppermute | solution.py:987

commit v6 on v5

--- a/solution.py
+++ b/solution.py
@@ -452,15 +452,20 @@
     return copies
 
 
-def ffn_kernel(count, second_ref, rows_ref, cotangent_ref, residual_hbm, *refs):
+def ffn_kernel(count, second_ref, rows_ref, cotangent_hbm, residual_hbm, *refs):
     pieces = refs[:count]
     result_hbm, branch_hbm, sums_ref = refs[count : count + 3]
-    outs = refs[count + 3 : -11]
-    (weights, grads, residual, total, back, result, branch, in_sems, out_sems, residual_sem, tile_sems) = refs[-11:]
+    outs = refs[count + 3 : -13]
+    (weights, grads, residual, cotangent_ref, total, back, result, branch, in_sems, out_sems, residual_sem, tile_sems, cotangent_sems) = refs[-13:]
     k = pl.program_id(0)
     length, width = second_ref.shape
     tiles = [slice(r, r + 256) for r in range(0, length, 256)]
     fetch = pltpu.make_async_copy(residual_hbm, residual, residual_sem)
+
+    def arrive(rows):
+        return pltpu.make_async_copy(
+            cotangent_hbm.at[rows, :], cotangent_ref.at[rows, :], cotangent_sems.at[rows.start // 256]
+        )
 
     def leave(rows):
         tile = rows.start // 256
@@ -471,7 +476,11 @@
 
     @pl.when(k == 0)
     def _():
-        for block in range(4):
+        for copy in weight_copies(0, pieces, weights, in_sems):
+            copy.start()
+        for rows in tiles:
+            arrive(rows).start()
+        for block in range(1, 4):
             for copy in weight_copies(block, pieces, weights, in_sems):
                 copy.start()
         fetch.start()
@@ -484,6 +493,9 @@
         def _(block=block):
             for copy in weight_copies(block, pieces, weights, in_sems):
                 copy.wait()
+            if block == 0:
+                for rows in tiles:
+                    arrive(rows).wait()
 
     expand = weights[k, :, 0].reshape(width, width)
     shrink = weights[k, :, 1].reshape(width, width)
@@ -557,12 +569,14 @@
         functools.partial(ffn_kernel, len(pieces)),
         grid=(4,),
         out_shape=outs + [shape(s, BF16) for s in grad_shapes],
-        in_specs=[fixed(o.shape) for o in (second, rows, cotangent)] + anywhere([residual, *pieces]),
+        in_specs=[fixed(o.shape) for o in (second, rows)]
+        + [pl.BlockSpec(memory_space=pltpu.HBM)] * (2 + len(pieces)),
         out_specs=anywhere(outs[:2]) + [fixed(outs[2].shape)] + anywhere(grad_shapes),
         scratch_shapes=[
             pltpu.VMEM(weights, BF16),
             pltpu.VMEM(weights, BF16),
             pltpu.VMEM((length, width), F32),
+            pltpu.VMEM((length, width), BF16),
             pltpu.VMEM((length, width), F32),
             pltpu.VMEM((length, width), F32),
             pltpu.VMEM((length, width), BF16),
@@ -571,6 +585,7 @@
             pltpu.SemaphoreType.DMA((4, 8)),
             pltpu.SemaphoreType.DMA,
             pltpu.SemaphoreType.DMA((2, length // 256)),
+            pltpu.SemaphoreType.DMA((length // 256,)),
         ],
         compiler_params=params(44),
         cost_estimate=cost(22),
@@ -786,7 +801,7 @@
         out_shape=outs,
         in_specs=[fixed(o.shape) for o in operands],
         out_specs=[fixed(o.shape) for o in outs],
-        compiler_params=params(),
+        compiler_params=params(44),
         cost_estimate=cost(3),
         name="join",
     )(*operands)
@@ -959,19 +974,19 @@
         pair_shapes = [(slots, width, 5 * PAIR)]
         ffn_shapes = [ffn_pieces[0].shape]
 
-    (normed, rows, residual, second, _), (heads, weights, *members) = forward(
+    (normed, rows, residual, second, mark), (heads, weights, *members) = forward(
         inputs, own, pieces, vectors, devices, slots
     )
     if direct:
-        ffn_pieces = over_cores(held[:-1] + [after(held[-1], second)], seqs)
+        ffn_pieces = over_cores(held[:-1] + [low(held[-1].astype(F32) * mark[0])], seqs)
     result, branch, sums, *ffn_grads = feed_forward(
         second, rows, cotangent, residual, ffn_pieces, ffn_shapes
     )
-    heads_grad, output_grad, mark = heads_back(branch, weights, heads)
+    heads_grad, output_grad, _ = heads_back(branch, weights, heads)
     members = [weights, heads_grad, output_grad, *members]
     waits = []
     if direct:
-        ffn_mine = low(add(ffn_grads[0], to_mate(ffn_grads[1], seqs)) * mark[0])
+        ffn_mine = low(add(ffn_grads[0], to_mate(ffn_grads[1], seqs)))
         waits = [ffn_mine]
     input_grad, sums, *pair_grads, _ = backward(
         normed, rows, sums, inputs, branch, devices, waits, members, pair_shapes

time: 171 us -> 164 us (0.959)
  local copies, waits for them, and re-layouts: 19.9 us -> 12.1 us
  waiting for transfers between devices: 40.4 us -> 43.4 us
  Pallas kernels: 68 us -> 65.6 us
    unnamed x54 -> x28, local copies, waits for them, and re-layouts: 15.1 us -> 7.31 us
    ppermute x6, waiting for transfers between devices: 12.9 us -> 16.4 us  [over_chips(): lax.ppermute(shares, 'seq', flip(seqs, 2 * r))]
    pallas_call x1, Pallas kernels: 3.84 us -> 0.61 us  [join(): pl.pallas_call(functools.partial(join_kernel, chips, slots), grid=(1,), o...]
  transfers between devices with their start and end apart: 33 -> 33, of which waited for: 19 -> 19; matrix products, arithmetic and copies ran while one was open for 2% -> 3% of each run, Pallas kernels for 24% -> 25%
where the time goes in v6:
time: 164 us
  Pallas kernels  65.6 us (40%)
  waiting for transfers between devices  43.4 us (26%)
  starting transfers between devices  35.5 us (22%)
  local copies, waits for them, and re-layouts  12.1 us (7%)
  other arithmetic  5.95 us (4%)
    pallas_call x1, Pallas kernels, backward(): pl.pallas_call(functools.partial(back_kernel, len(waits), len(grad_shapes...  24.3 us
    pallas_call x1, Pallas kernels, feed_forward(): pl.pallas_call(functools.partial(ffn_kernel, len(pieces)), grid=(4,), out...  23 us
    ppermute x6, waiting for transfers between devices, over_chips(): lax.ppermute(shares, 'seq', flip(seqs, 2 * r))  16.4 us
    pallas_call x1, Pallas kernels, forward(): pl.pallas_call(functools.partial(forward_kernel, len(pieces), slots), gri...  14.8 us
    ppermute x3, waiting for transfers between devices, body(): lax.ppermute(ffn[a], 'head', turn(slots, a))  9.42 us
    unnamed x28, local copies, waits for them, and re-layouts  7.31 us
    ppermute x6, starting transfers between devices, over_chips(): lax.ppermute(shares, 'seq', flip(seqs, 2 * r))  7.03 us
    ppermute x3, starting transfers between devices, body(): lax.ppermute(piece, 'head', turn(slots, a))  6.11 us
  transfers between devices with their start and end apart: 33, of which 19 were waited for; matrix products, arithmetic and copies ran while one was open for 3% of the time, Pallas kernels for 25%

profile of v6, /device:TPU:0, one launch (start us, length us, event | category | flops | bytes accessed | tf_op | source)
XLA Modules:
  0.0 163.6 jit_solution(13994404165756125055)
XLA Ops:
  0.7 0.8 pad_add_fusion.1
  1.5 1.2 pad_maximum_fusion.own_ref
  2.8 5.1 %collective-permute-start.2 = (bf16[96,512]{1,0:T(8,128)(2,1)S(1)}, bf16[96,512]{1,0:T(8,128)(2,1)S(1)}, u32[]{:S(2)}, u32[]{:S(2)}) collective-permute-start(bf16[96,512]{1,0:T(8,128)(2,1)S(1)} %pad_maximum_fusion.3), channel_id=1, source_target_pairs={{0,3},{1,0},{2,1},{3,2},{4,7},{5,4},{6,5},{7,6},{8,11},{9,8},{10,9... | collective-permute-start | bytes 294920 | tf_op jit(solution)/shard_map/ppermute | solution.py:956
  7.9 1.0 collective-permute-start
  8.9 1.2 reshape.49
  10.3 0.8 stack_reshape.7
  11.1 5.5 %collective-permute-done.1 = bf16[96,512]{1,0:T(8,128)(2,1)S(1)} collective-permute-done((bf16[96,512]{1,0:T(8,128)(2,1)S(1)}, bf16[96,512]{1,0:T(8,128)(2,1)S(1)}, u32[]{:S(2)}, u32[]{:S(2)}) %collective-permute-start.1) | collective-permute-done | bytes 98336 | tf_op jit(solution)/shard_map/ppermute | solution.py:956
  16.7 0.7 pad_maximum_fusion.1.refs_0_.refs_1_
  17.5 0.9 broadcast_in_dim.12.refs_0_
  18.3 3.5 %all-to-all-start = ((bf16[4,8,16,512]{3,2,1,0:T(8,128)(2,1)}), bf16[4,8,16,512]{3,2,1,0:T(8,128)(2,1)S(1)}, u32[]{:S(2)}, u32[]{:S(2)}) async-start(bf16[4,8,16,512]{3,2,1,0:T(8,128)(2,1)} %after.1), calls=%async_computation | async-start | bytes 1048576 | tf_op jit(solution)/shard_map/all_to_all | solution.py:962
  21.9 2.5 %collective-permute-start.8 = (bf16[256,512]{1,0:T(8,128)(2,1)S(1)}, bf16[256,512]{1,0:T(8,128)(2,1)}, u32[]{:S(2)}, u32[]{:S(2)}) collective-permute-start(bf16[256,512]{1,0:T(8,128)(2,1)S(1)} %copy-done), channel_id=1, source_target_pairs={{0,24},{4,28},{8,16},{12,20},{16,8},{20,12},{24,0},{28,4},{1,25},{... | collective-permute-start | bytes 786440 | tf_op jit(solution)/shard_map/ppermute | solution.py:893
  24.4 0.5 collective-permute-start.6
  24.9 0.5 collective-permute-start.4
  25.4 6.8 %collective-permute-done.8.refs_6_ = bf16[256,512]{1,0:T(8,128)(2,1)} collective-permute-done((bf16[256,512]{1,0:T(8,128)(2,1)S(1)}, bf16[256,512]{1,0:T(8,128)(2,1)}, u32[]{:S(2)}, u32[]{:S(2)}) %collective-permute-start.8) | collective-permute-done | bytes 262176 | tf_op jit(solution)/shard_map/ppermute | solution.py:893
  32.2 4.1 %collective-permute-done.6.refs_4_ = bf16[256,512]{1,0:T(8,128)(2,1)} collective-permute-done((bf16[256,512]{1,0:T(8,128)(2,1)S(1)}, bf16[256,512]{1,0:T(8,128)(2,1)}, u32[]{:S(2)}, u32[]{:S(2)}) %collective-permute-start.6) | collective-permute-done | bytes 262176 | tf_op jit(solution)/shard_map/ppermute | solution.py:893
  36.4 0.4 collective-permute-start.5
  36.8 1.9 %collective-permute-start.15 = (bf16[4,8,16,512]{3,2,1,0:T(8,128)(2,1)S(1)}, bf16[4,8,16,512]{3,2,1,0:T(8,128)(2,1)S(1)}, u32[]{:S(2)}, u32[]{:S(2)}) collective-permute-start(bf16[4,8,16,512]{3,2,1,0:T(8,128)(2,1)S(1)} %all-to-all-done.refs_0_), channel_id=1, source_target_pairs={{0,24},{4,28},{8,16},{12,20},{16,8},{20,12},{24,0},{28,4},{1,25},{... | collective-permute-start | bytes 1572872 | tf_op jit(solution)/shard_map/ppermute | solution.py:893
  38.7 1.0 collective-permute-start.13
  39.7 0.5 collective-permute-start.11
  40.3 14.8 %attend_forward.1 = (bf16[1024,512]{1,0:T(8,128)(2,1)S(1)}, f32[16,512]{1,0:T(8,128)S(1)}, f32[1024,512]{1,0:T(8,128)S(1)}, bf16[1024,512]{1,0:T(8,128)(2,1)S(1)...) custom-call(bf16[1024,512]{1,0:T(8,128)(2,1)S(1)} %copy-done.2, ...), custom_call_target="tpu_custom_call" | custom-call | flops 16999999488 | bytes 17000000 | tf_op jit(solution)/shard_map/attend_forward/pallas_call | solution.py:395
  55.1 1.4 copy-done.8
  56.4 1.0 copy-done.9
  57.4 5.4 %collective-permute-done.13.refs_4_ = bf16[4,8,16,512]{3,2,1,0:T(8,128)(2,1)S(1)} collective-permute-done((bf16[4,8,16,512]{3,2,1,0:T(8,128)(2,1)S(1)}, bf16[4,8,16,512]{3,2,1,0:T(8,128)(2,1)S(1)}, u32[]{:S(2)}, u32[]{:S(2)}) %collective-permute-start.13) | collective-permute-done | bytes 524320 | tf_op jit(solution)/shard_map/ppermute | solution.py:893
  62.9 0.4 collective-permute-start.12
  63.4 0.8 multiply_convert_fusion.refs_6_
  64.2 0.5 collective-permute-done.14.refs_5_
  64.7 0.7 collective-permute-done.12.refs_3_
  65.5 0.7 collective-permute-done.16.refs_7_
  66.2 23.0 %feed_forward.1 = (bf16[1024,512]{1,0:T(8,128)(2,1)}, bf16[1024,512]{1,0:T(8,128)(2,1)S(1)}, f32[16,512]{1,0:T(8,128)S(1)}, bf16[4,4,4,2,16,512]{5,4,3,2,1,0:T(8,128)(2,1)S(1)}, bf16[4,4,4,2,16,512]{5,4,3,2,1,0:T(8,128)(2,1)}) custom-call(bf16[1024,512]{1,0:T(8,128)(2,1)S(1)} %get-tuple-element.60.second_ref, f32[16,512]{1,0:T(8,128)S(1)} %get-tuple-element.61.rows_ref, ...), custom_call_target="tpu_custom_call" | custom-call | flops 22000001024 | bytes 22000000 | tf_op jit(solution)/shard_map/feed_forward/pallas_call | solution.py:568
  89.3 0.2 collective-permute-start.17
  89.5 1.3 heads_back.1
  90.9 1.0 copy-done.6
  91.9 0.8 copy-done.7
  92.7 1.1 collective-permute-done.17
  93.7 2.3 %add_convert_fusion.refs_0_ = bf16[4,4,4,2,16,512]{5,4,3,2,1,0:T(8,128)(2,1)} fusion(bf16[4,4,4,2,16,512]{5,4,3,2,1,0:T(8,128)(2,1)S(1)} %collective-permute-done.17, bf16[4,4,4,2,16,512]{5,4,3,2,1,0:T(8,128)(2,1)S(1)} %get-tuple-element.68), kind=kLoop, calls=%fused_computation | loop fusion | flops 4194304 | bytes 6291456 | tf_op jit(solution)/shard_map/convert_element_type | solution.py:30
  96.0 3.6 %all-to-all-start.1 = ((bf16[4,4,4,2,16,512]{5,4,3,2,1,0:T(8,128)(2,1)}), bf16[4,4,4,2,16,512]{5,4,3,2,1,0:T(8,128)(2,1)S(1)}, u32[]{:S(2)}, u32[]{:S(2)}) async-start(bf16[4,4,4,2,16,512]{5,4,3,2,1,0:T(8,128)(2,1)} %add_convert_fusion.refs_0_), calls=%async_computation.1 | async-start | bytes 4194304 | tf_op jit(solution)/shard_map/all_to_all | solution.py:902
  99.7 24.3 %attend_back.1 = (bf16[1024,512]{1,0:T(8,128)(2,1)}, f32[32,256]{1,0:T(8,128)}, bf16[4,272,640]{2,1,0:T(8,128)(2,1)}, bf16[272,640]{1,0:T(8,128)(2,1)}, bf16[272...) custom-call(bf16[1024,512]{1,0:T(8,128)(2,1)} %copy-done.9, ...), custom_call_target="tpu_custom_call" | custom-call | flops 27000000512 | bytes 27000000 | tf_op jit(solution)/shard_map/attend_back/pallas_call | solution.py:736
  124.2 0.4 collective-permute-start.19
  124.7 0.4 collective-permute-start.21
  125.1 0.8 collective-permute-done.18.refs_0_
  125.9 0.5 collective-permute-done.19.refs_1_
  126.4 0.5 collective-permute-done.20.refs_2_
  126.9 0.5 collective-permute-done.21.refs_3_
  127.4 1.3 copy-done.3
  128.8 0.6 join.1
  129.4 2.0 %collective-permute-start.22 = (bf16[272,640]{1,0:T(8,128)(2,1)S(1)}, bf16[272,640]{1,0:T(8,128)(2,1)S(1)}, u32[]{:S(2)}, u32[]{:S(2)}) collective-permute-start(bf16[272,640]{1,0:T(8,128)(2,1)S(1)} %get-tuple-element.90), channel_id=1, source_target_pairs={{0,8},{4,12},{8,0},{12,4},{16,24},{20,28},{24,16},{28,20},{1,9},{5... | collective-permute-start | bytes 1044488 | tf_op jit(solution)/shard_map/ppermute | solution.py:906
  131.4 1.5 collective-permute-start.23
  132.9 1.6 %collective-permute-start.25 = (bf16[4,2,16,512]{3,2,1,0:T(8,128)(2,1)S(1)}, bf16[4,2,16,512]{3,2,1,0:T(8,128)(2,1)S(1)}, u32[]{:S(2)}, u32[]{:S(2)}) collective-permute-start(bf16[4,2,16,512]{3,2,1,0:T(8,128)(2,1)S(1)} %get-tuple-element.93), channel_id=1, source_target_pairs={{0,1},{1,2},{2,3},{3,0},{4,5},{5,6},{6,7},{7,4},{8,9},{9,10},{10,1... | collective-permute-start | bytes 393224 | tf_op jit(solution)/shard_map/ppermute | solution.py:998
  134.6 2.4 %collective-permute-start.26 = (bf16[4,2,16,512]{3,2,1,0:T(8,128)(2,1)S(1)}, bf16[4,2,16,512]{3,2,1,0:T(8,128)(2,1)S(1)}, u32[]{:S(2)}, u32[]{:S(2)}) collective-permute-start(bf16[4,2,16,512]{3,2,1,0:T(8,128)(2,1)S(1)} %get-tuple-element.94), channel_id=1, source_target_pairs={{0,2},{1,3},{2,0},{3,1},{4,6},{5,7},{6,4},{7,5},{8,10},{9,11},{10,... | collective-permute-start | bytes 393224 | tf_op jit(solution)/shard_map/ppermute | solution.py:998
  136.9 4.4 %collective-permute-done.25.refs_4_.refs_1_ = bf16[4,2,16,512]{3,2,1,0:T(8,128)(2,1)S(1)} collective-permute-done((bf16[4,2,16,512]{3,2,1,0:T(8,128)(2,1)S(1)}, bf16[4,2,16,512]{3,2,1,0:T(8,128)(2,1)S(1)}, u32[]{:S(2)}, u32[]{:S(2)}) %collective-permute-start.25) | collective-permute-done | bytes 131104 | tf_op jit(solution)/shard_map/ppermute | solution.py:998
  141.3 0.7 collective-permute-start.27
  142.1 3.4 %collective-permute-done.26.refs_5_.refs_2_ = bf16[4,2,16,512]{3,2,1,0:T(8,128)(2,1)S(1)} collective-permute-done((bf16[4,2,16,512]{3,2,1,0:T(8,128)(2,1)S(1)}, bf16[4,2,16,512]{3,2,1,0:T(8,128)(2,1)S(1)}, u32[]{:S(2)}, u32[]{:S(2)}) %collective-permute-start.26) | collective-permute-done | bytes 131104 | tf_op jit(solution)/shard_map/ppermute | solution.py:998
  145.4 1.7 %collective-permute-done.27.refs_6_.refs_3_ = bf16[4,2,16,512]{3,2,1,0:T(8,128)(2,1)S(1)} collective-permute-done((bf16[4,2,16,512]{3,2,1,0:T(8,128)(2,1)S(1)}, bf16[4,2,16,512]{3,2,1,0:T(8,128)(2,1)S(1)}, u32[]{:S(2)}, u32[]{:S(2)}) %collective-permute-start.27) | collective-permute-done | bytes 131104 | tf_op jit(solution)/shard_map/ppermute | solution.py:998
  147.1 1.7 %collective-permute-done.23.refs_2_ = bf16[272,640]{1,0:T(8,128)(2,1)S(1)} collective-permute-done((bf16[272,640]{1,0:T(8,128)(2,1)S(1)}, bf16[272,640]{1,0:T(8,128)(2,1)S(1)}, u32[]{:S(2)}, u32[]{:S(2)}) %collective-permute-start.23) | collective-permute-done | bytes 348192 | tf_op jit(solution)/shard_map/ppermute | solution.py:906
  148.8 0.6 sum_plane.1
  149.3 3.5 %collective-permute-start.28 = (bf16[80,640]{1,0:T(8,128)(2,1)S(1)}, bf16[80,640]{1,0:T(8,128)(2,1)S(1)}, u32[]{:S(2)}, u32[]{:S(2)}) collective-permute-start(bf16[80,640]{1,0:T(8,128)(2,1)S(1)} %get-tuple-element.97), channel_id=1, source_target_pairs={{0,3},{1,0},{2,1},{3,2},{4,7},{5,4},{6,5},{7,6},{8,11},{9,8},{10,9... | collective-permute-start | bytes 307208 | tf_op jit(solution)/shard_map/ppermute | solution.py:1002
  152.8 1.1 collective-permute-start.30
  154.0 1.0 settle.1
  155.0 0.8 copy.39
  155.8 1.0 copy.40
  156.8 5.0 %collective-permute-done.29 = bf16[80,640]{1,0:T(8,128)(2,1)S(1)} collective-permute-done((bf16[80,640]{1,0:T(8,128)(2,1)S(1)}, bf16[80,640]{1,0:T(8,128)(2,1)S(1)}, u32[]{:S(2)}, u32[]{:S(2)}) %collective-permute-start.29) | collective-permute-done | bytes 102432 | tf_op jit(solution)/shard_map/ppermute | solution.py:1002
  161.7 0.5 slice_bitcast_fusion.2
  162.2 0.6 slice_bitcast_fusion.1
  162.9 0.7 slice_bitcast_fusion
  (65 shorter events, 1.1 us)
Async XLA Ops:
  0.6 10.4 %copy-start.12 = (bf16[512,64]{0,1:T(8,128)(2,1)S(1)}, bf16[512,64]{0,1:T(8,128)(2,1)}, u32[]{:S(2)}) copy-start(bf16[512,64]{0,1:T(8,128)(2,1)} %param.25) | copy-start | bytes 196612
  2.8 8.3 %collective-permute-start.2 = (bf16[96,512]{1,0:T(8,128)(2,1)S(1)}, bf16[96,512]{1,0:T(8,128)(2,1)S(1)}, u32[]{:S(2)}, u32[]{:S(2)}) collective-permute-start(bf16[96,512]{1,0:T(8,128)(2,1)S(1)} %pad_maximum_fusion.3), channel_id=1, source_target_pairs={{0,3},{1,0},{2,1},{3,2},{4,7},{5,4},{6,5},{7,6},{8,11},{9,8},{10,9... | collective-permute-start | bytes 294920 | tf_op jit(solution)/shard_map/ppermute | solution.py:956
  7.9 8.7 %collective-permute-start.1 = (bf16[96,512]{1,0:T(8,128)(2,1)S(1)}, bf16[96,512]{1,0:T(8,128)(2,1)S(1)}, u32[]{:S(2)}, u32[]{:S(2)}) collective-permute-start(bf16[96,512]{1,0:T(8,128)(2,1)S(1)} %pad_maximum_fusion.3), channel_id=1, source_target_pairs={{0,2},{1,3},{2,0},{3,1},{4,6},{5,7},{6,4},{7,5},{8,10},{9,11},{10,... | collective-permute-start | bytes 294920 | tf_op jit(solution)/shard_map/ppermute | solution.py:956
  7.9 8.8 %collective-permute-start = (bf16[96,512]{1,0:T(8,128)(2,1)S(1)}, bf16[96,512]{1,0:T(8,128)(2,1)S(1)}, u32[]{:S(2)}, u32[]{:S(2)}) collective-permute-start(bf16[96,512]{1,0:T(8,128)(2,1)S(1)} %pad_maximum_fusion.3), channel_id=1, source_target_pairs={{0,1},{1,2},{2,3},{3,0},{4,5},{5,6},{6,7},{7,4},{8,9},{9,10},{10,1... | collective-permute-start | bytes 294920 | tf_op jit(solution)/shard_map/ppermute | solution.py:956
  11.1 29.2 %copy-start.2 = (bf16[1024,512]{1,0:T(8,128)(2,1)S(1)}, bf16[1024,512]{1,0:T(8,128)(2,1)}, u32[]{:S(2)}) copy-start(bf16[1024,512]{1,0:T(8,128)(2,1)} %tokens_hbm.1) | copy-start | bytes 3145732
  17.5 4.4 %copy-start = (bf16[256,512]{1,0:T(8,128)(2,1)S(1)}, bf16[256,512]{1,0:T(8,128)(2,1)}, u32[]{:S(2)}) copy-start(bf16[256,512]{1,0:T(8,128)(2,1)} %pad_maximum_fusion.1.refs_0_.refs_1_) | copy-start | bytes 786436
  18.3 18.4 %all-to-all-start = ((bf16[4,8,16,512]{3,2,1,0:T(8,128)(2,1)}), bf16[4,8,16,512]{3,2,1,0:T(8,128)(2,1)S(1)}, u32[]{:S(2)}, u32[]{:S(2)}) async-start(bf16[4,8,16,512]{3,2,1,0:T(8,128)(2,1)} %after.1), calls=%async_computation | async-start | bytes 1048576 | tf_op jit(solution)/shard_map/all_to_all | solution.py:962
  21.9 44.4 %copy-start.1 = (bf16[1024,512]{1,0:T(8,128)(2,1)S(1)}, bf16[1024,512]{1,0:T(8,128)(2,1)}, u32[]{:S(2)}) copy-start(bf16[1024,512]{1,0:T(8,128)(2,1)} %cotangent_hbm.1) | copy-start | bytes 3145732
  21.9 10.3 %collective-permute-start.8 = (bf16[256,512]{1,0:T(8,128)(2,1)S(1)}, bf16[256,512]{1,0:T(8,128)(2,1)}, u32[]{:S(2)}, u32[]{:S(2)}) collective-permute-start(bf16[256,512]{1,0:T(8,128)(2,1)S(1)} %copy-done), channel_id=1, source_target_pairs={{0,24},{4,28},{8,16},{12,20},{16,8},{20,12},{24,0},{28,4},{1,25},{... | collective-permute-start | bytes 786440 | tf_op jit(solution)/shard_map/ppermute | solution.py:893
  24.4 11.9 %collective-permute-start.6 = (bf16[256,512]{1,0:T(8,128)(2,1)S(1)}, bf16[256,512]{1,0:T(8,128)(2,1)}, u32[]{:S(2)}, u32[]{:S(2)}) collective-permute-start(bf16[256,512]{1,0:T(8,128)(2,1)S(1)} %copy-done), channel_id=1, source_target_pairs={{0,16},{4,20},{8,24},{12,28},{16,0},{20,4},{24,8},{28,12},{1,17},{... | collective-permute-start | bytes 786440 | tf_op jit(solution)/shard_map/ppermute | solution.py:893
  24.9 11.5 %collective-permute-start.4 = (bf16[256,512]{1,0:T(8,128)(2,1)S(1)}, bf16[256,512]{1,0:T(8,128)(2,1)}, u32[]{:S(2)}, u32[]{:S(2)}) collective-permute-start(bf16[256,512]{1,0:T(8,128)(2,1)S(1)} %copy-done), channel_id=1, source_target_pairs={{0,8},{4,12},{8,0},{12,4},{16,24},{20,28},{24,16},{28,20},{1,9},{5... | collective-permute-start | bytes 786440 | tf_op jit(solution)/shard_map/ppermute | solution.py:893
  25.4 13.3 %collective-permute-start.3 = (bf16[256,512]{1,0:T(8,128)(2,1)S(1)}, bf16[256,512]{1,0:T(8,128)(2,1)}, u32[]{:S(2)}, u32[]{:S(2)}) collective-permute-start(bf16[256,512]{1,0:T(8,128)(2,1)S(1)} %copy-done), channel_id=1, source_target_pairs={{0,4},{4,0},{8,12},{12,8},{16,20},{20,16},{24,28},{28,24},{1,5},{5... | collective-permute-start | bytes 786440 | tf_op jit(solution)/shard_map/ppermute | solution.py:889
  32.2 7.5 %collective-permute-start.9 = (bf16[256,512]{1,0:T(8,128)(2,1)}, bf16[256,512]{1,0:T(8,128)(2,1)}, u32[]{:S(2)}, u32[]{:S(2)}) collective-permute-start(bf16[256,512]{1,0:T(8,128)(2,1)} %collective-permute-done.8.refs_6_), channel_id=1, source_target_pairs={{0,4},{4,0},{8,12},{12,8},{16,20},{20,16},{24,28},{28,24},{1,5},{5... | collective-permute-start | bytes 786440 | tf_op jit(solution)/shard_map/ppermute | solution.py:889
  36.3 4.0 %collective-permute-start.7 = (bf16[256,512]{1,0:T(8,128)(2,1)}, bf16[256,512]{1,0:T(8,128)(2,1)}, u32[]{:S(2)}, u32[]{:S(2)}) collective-permute-start(bf16[256,512]{1,0:T(8,128)(2,1)} %collective-permute-done.6.refs_4_), channel_id=1, source_target_pairs={{0,4},{4,0},{8,12},{12,8},{16,20},{20,16},{24,28},{28,24},{1,5},{5... | collective-permute-start | bytes 786440 | tf_op jit(solution)/shard_map/ppermute | solution.py:889
  36.4 3.9 %collective-permute-start.5 = (bf16[256,512]{1,0:T(8,128)(2,1)}, bf16[256,512]{1,0:T(8,128)(2,1)}, u32[]{:S(2)}, u32[]{:S(2)}) collective-permute-start(bf16[256,512]{1,0:T(8,128)(2,1)} %collective-permute-done.4.refs_2_), channel_id=1, source_target_pairs={{0,4},{4,0},{8,12},{12,8},{16,20},{20,16},{24,28},{28,24},{1,5},{5... | collective-permute-start | bytes 786440 | tf_op jit(solution)/shard_map/ppermute | solution.py:889
  36.8 26.6 %collective-permute-start.15 = (bf16[4,8,16,512]{3,2,1,0:T(8,128)(2,1)S(1)}, bf16[4,8,16,512]{3,2,1,0:T(8,128)(2,1)S(1)}, u32[]{:S(2)}, u32[]{:S(2)}) collective-permute-start(bf16[4,8,16,512]{3,2,1,0:T(8,128)(2,1)S(1)} %all-to-all-done.refs_0_), channel_id=1, source_target_pairs={{0,24},{4,28},{8,16},{12,20},{16,8},{20,12},{24,0},{28,4},{1,25},{... | collective-permute-start | bytes 1572872 | tf_op jit(solution)/shard_map/ppermute | solution.py:893
  38.7 24.1 %collective-permute-start.13 = (bf16[4,8,16,512]{3,2,1,0:T(8,128)(2,1)S(1)}, bf16[4,8,16,512]{3,2,1,0:T(8,128)(2,1)S(1)}, u32[]{:S(2)}, u32[]{:S(2)}) collective-permute-start(bf16[4,8,16,512]{3,2,1,0:T(8,128)(2,1)S(1)} %all-to-all-done.refs_0_), channel_id=1, source_target_pairs={{0,16},{4,20},{8,24},{12,28},{16,0},{20,4},{24,8},{28,12},{1,17},{... | collective-permute-start | bytes 1572872 | tf_op jit(solution)/shard_map/ppermute | solution.py:893
  39.7 23.2 %collective-permute-start.11 = (bf16[4,8,16,512]{3,2,1,0:T(8,128)(2,1)S(1)}, bf16[4,8,16,512]{3,2,1,0:T(8,128)(2,1)S(1)}, u32[]{:S(2)}, u32[]{:S(2)}) collective-permute-start(bf16[4,8,16,512]{3,2,1,0:T(8,128)(2,1)S(1)} %all-to-all-done.refs_0_), channel_id=1, source_target_pairs={{0,8},{4,12},{8,0},{12,4},{16,24},{20,28},{24,16},{28,20},{1,9},{5... | collective-permute-start | bytes 1572872 | tf_op jit(solution)/shard_map/ppermute | solution.py:893
  55.0 1.4 copy-start.8
  56.4 1.0 copy-start.9
  57.4 31.8 %copy-start.10 = (f32[16,512]{1,0:T(8,128)}, f32[16,512]{1,0:T(8,128)S(1)}, u32[]{:S(2)}) copy-start(f32[16,512]{1,0:T(8,128)S(1)} %get-tuple-element.61.rows_ref) | copy-start | bytes 98308
  57.4 6.8 %collective-permute-start.10 = (bf16[4,8,16,512]{3,2,1,0:T(8,128)(2,1)S(1)}, bf16[4,8,16,512]{3,2,1,0:T(8,128)(2,1)S(1)}, u32[]{:S(2)}, u32[]{:S(2)}) collective-permute-start(bf16[4,8,16,512]{3,2,1,0:T(8,128)(2,1)S(1)} %all-to-all-done.refs_0_), channel_id=1, source_target_pairs={{0,4},{4,0},{8,12},{12,8},{16,20},{20,16},{24,28},{28,24},{1,5},{5... | collective-permute-start | bytes 1572872 | tf_op jit(solution)/shard_map/ppermute | solution.py:889
  62.8 1.9 %collective-permute-start.14 = (bf16[4,8,16,512]{3,2,1,0:T(8,128)(2,1)S(1)}, bf16[4,8,16,512]{3,2,1,0:T(8,128)(2,1)S(1)}, u32[]{:S(2)}, u32[]{:S(2)}) collective-permute-start(bf16[4,8,16,512]{3,2,1,0:T(8,128)(2,1)S(1)} %collective-permute-done.13.refs_4_), channel_id=1, source_target_pairs={{0,4},{4,0},{8,12},{12,8},{16,20},{20,16},{24,28},{28,24},{1,5},{5... | collective-permute-start | bytes 1572872 | tf_op jit(solution)/shard_map/ppermute | solution.py:889
  62.9 2.6 %collective-permute-start.12 = (bf16[4,8,16,512]{3,2,1,0:T(8,128)(2,1)S(1)}, bf16[4,8,16,512]{3,2,1,0:T(8,128)(2,1)S(1)}, u32[]{:S(2)}, u32[]{:S(2)}) collective-permute-start(bf16[4,8,16,512]{3,2,1,0:T(8,128)(2,1)S(1)} %collective-permute-done.11.refs_2_), channel_id=1, source_target_pairs={{0,4},{4,0},{8,12},{12,8},{16,20},{20,16},{24,28},{28,24},{1,5},{5... | collective-permute-start | bytes 1572872 | tf_op jit(solution)/shard_map/ppermute | solution.py:889
  64.1 2.1 %collective-permute-start.16 = (bf16[4,8,16,512]{3,2,1,0:T(8,128)(2,1)S(1)}, bf16[4,8,16,512]{3,2,1,0:T(8,128)(2,1)S(1)}, u32[]{:S(2)}, u32[]{:S(2)}) collective-permute-start(bf16[4,8,16,512]{3,2,1,0:T(8,128)(2,1)S(1)} %multiply_convert_fusion.refs_6_), channel_id=1, source_target_pairs={{0,4},{4,0},{8,12},{12,8},{16,20},{20,16},{24,28},{28,24},{1,5},{5... | collective-permute-start | bytes 1572872 | tf_op jit(solution)/shard_map/ppermute | solution.py:889
  66.2 23.3 %copy-start.4 = (bf16[4,640,512]{2,1,0:T(8,128)(2,1)S(1)}, bf16[4,640,512]{2,1,0:T(8,128)(2,1)}, u32[]{:S(2)}) copy-start(bf16[4,640,512]{2,1,0:T(8,128)(2,1)} %get-tuple-element.70.weight_ref.refs_1_) | copy-start | bytes 7864324
  89.3 1.5 copy-start.5
  89.3 1.5 copy-start.11
  89.3 4.4 %collective-permute-start.17 = (bf16[4,4,4,2,16,512]{5,4,3,2,1,0:T(8,128)(2,1)}, bf16[4,4,4,2,16,512]{5,4,3,2,1,0:T(8,128)(2,1)S(1)}, u32[]{:S(2)}, u32[]{:S(2)}) collective-permute-start(bf16[4,4,4,2,16,512]{5,4,3,2,1,0:T(8,128)(2,1)} %get-tuple-element.69), channel_id=1, source_target_pairs={{0,4},{4,0},{8,12},{12,8},{16,20},{20,16},{24,28},{28,24},{1,5},{5... | collective-permute-start | bytes 6291464 | tf_op jit(solution)/shard_map/ppermute | solution.py:889
  90.8 1.0 copy-start.6
  91.9 0.8 copy-start.7
  96.0 31.4 %all-to-all-start.1 = ((bf16[4,4,4,2,16,512]{5,4,3,2,1,0:T(8,128)(2,1)}), bf16[4,4,4,2,16,512]{5,4,3,2,1,0:T(8,128)(2,1)S(1)}, u32[]{:S(2)}, u32[]{:S(2)}) async-start(bf16[4,4,4,2,16,512]{5,4,3,2,1,0:T(8,128)(2,1)} %add_convert_fusion.refs_0_), calls=%async_computation.1 | async-start | bytes 4194304 | tf_op jit(solution)/shard_map/all_to_all | solution.py:902
  124.0 1.9 %collective-permute-start.18 = (bf16[272,640]{1,0:T(8,128)(2,1)}, bf16[272,640]{1,0:T(8,128)(2,1)S(1)}, u32[]{:S(2)}, u32[]{:S(2)}) collective-permute-start(bf16[272,640]{1,0:T(8,128)(2,1)} %get-tuple-element.85), channel_id=1, source_target_pairs={{0,4},{4,0},{8,12},{12,8},{16,20},{20,16},{24,28},{28,24},{1,5},{5... | collective-permute-start | bytes 1044488 | tf_op jit(solution)/shard_map/ppermute | solution.py:889
  124.2 2.2 %collective-permute-start.19 = (bf16[272,640]{1,0:T(8,128)(2,1)}, bf16[272,640]{1,0:T(8,128)(2,1)S(1)}, u32[]{:S(2)}, u32[]{:S(2)}) collective-permute-start(bf16[272,640]{1,0:T(8,128)(2,1)} %get-tuple-element.86), channel_id=1, source_target_pairs={{0,4},{4,0},{8,12},{12,8},{16,20},{20,16},{24,28},{28,24},{1,5},{5... | collective-permute-start | bytes 1044488 | tf_op jit(solution)/shard_map/ppermute | solution.py:889
  124.6 2.4 %collective-permute-start.20 = (bf16[272,640]{1,0:T(8,128)(2,1)}, bf16[272,640]{1,0:T(8,128)(2,1)S(1)}, u32[]{:S(2)}, u32[]{:S(2)}) collective-permute-start(bf16[272,640]{1,0:T(8,128)(2,1)} %get-tuple-element.87), channel_id=1, source_target_pairs={{0,4},{4,0},{8,12},{12,8},{16,20},{20,16},{24,28},{28,24},{1,5},{5... | collective-permute-start | bytes 1044488 | tf_op jit(solution)/shard_map/ppermute | solution.py:889
  124.7 2.7 %collective-permute-start.21 = (bf16[272,640]{1,0:T(8,128)(2,1)}, bf16[272,640]{1,0:T(8,128)(2,1)S(1)}, u32[]{:S(2)}, u32[]{:S(2)}) collective-permute-start(bf16[272,640]{1,0:T(8,128)(2,1)} %get-tuple-element.88), channel_id=1, source_target_pairs={{0,4},{4,0},{8,12},{12,8},{16,20},{20,16},{24,28},{28,24},{1,5},{5... | collective-permute-start | bytes 1044488 | tf_op jit(solution)/shard_map/ppermute | solution.py:889
  127.4 1.3 copy-start.3
  129.4 17.7 %collective-permute-start.22 = (bf16[272,640]{1,0:T(8,128)(2,1)S(1)}, bf16[272,640]{1,0:T(8,128)(2,1)S(1)}, u32[]{:S(2)}, u32[]{:S(2)}) collective-permute-start(bf16[272,640]{1,0:T(8,128)(2,1)S(1)} %get-tuple-element.90), channel_id=1, source_target_pairs={{0,8},{4,12},{8,0},{12,4},{16,24},{20,28},{24,16},{28,20},{1,9},{5... | collective-permute-start | bytes 1044488 | tf_op jit(solution)/shard_map/ppermute | solution.py:906
  131.4 17.4 %collective-permute-start.23 = (bf16[272,640]{1,0:T(8,128)(2,1)S(1)}, bf16[272,640]{1,0:T(8,128)(2,1)S(1)}, u32[]{:S(2)}, u32[]{:S(2)}) collective-permute-start(bf16[272,640]{1,0:T(8,128)(2,1)S(1)} %get-tuple-element.91), channel_id=1, source_target_pairs={{0,16},{4,20},{8,24},{12,28},{16,0},{20,4},{24,8},{28,12},{1,17},{... | collective-permute-start | bytes 1044488 | tf_op jit(solution)/shard_map/ppermute | solution.py:906
  132.9 15.9 %collective-permute-start.24 = (bf16[272,640]{1,0:T(8,128)(2,1)S(1)}, bf16[272,640]{1,0:T(8,128)(2,1)S(1)}, u32[]{:S(2)}, u32[]{:S(2)}) collective-permute-start(bf16[272,640]{1,0:T(8,128)(2,1)S(1)} %get-tuple-element.92), channel_id=1, source_target_pairs={{0,24},{4,28},{8,16},{12,20},{16,8},{20,12},{24,0},{28,4},{1,25},{... | collective-permute-start | bytes 1044488 | tf_op jit(solution)/shard_map/ppermute | solution.py:906
  132.9 8.4 %collective-permute-start.25 = (bf16[4,2,16,512]{3,2,1,0:T(8,128)(2,1)S(1)}, bf16[4,2,16,512]{3,2,1,0:T(8,128)(2,1)S(1)}, u32[]{:S(2)}, u32[]{:S(2)}) collective-permute-start(bf16[4,2,16,512]{3,2,1,0:T(8,128)(2,1)S(1)} %get-tuple-element.93), channel_id=1, source_target_pairs={{0,1},{1,2},{2,3},{3,0},{4,5},{5,6},{6,7},{7,4},{8,9},{9,10},{10,1... | collective-permute-start | bytes 393224 | tf_op jit(solution)/shard_map/ppermute | solution.py:998
  134.6 10.9 %collective-permute-start.26 = (bf16[4,2,16,512]{3,2,1,0:T(8,128)(2,1)S(1)}, bf16[4,2,16,512]{3,2,1,0:T(8,128)(2,1)S(1)}, u32[]{:S(2)}, u32[]{:S(2)}) collective-permute-start(bf16[4,2,16,512]{3,2,1,0:T(8,128)(2,1)S(1)} %get-tuple-element.94), channel_id=1, source_target_pairs={{0,2},{1,3},{2,0},{3,1},{4,6},{5,7},{6,4},{7,5},{8,10},{9,11},{10,... | collective-permute-start | bytes 393224 | tf_op jit(solution)/shard_map/ppermute | solution.py:998
  141.3 5.8 %collective-permute-start.27 = (bf16[4,2,16,512]{3,2,1,0:T(8,128)(2,1)S(1)}, bf16[4,2,16,512]{3,2,1,0:T(8,128)(2,1)S(1)}, u32[]{:S(2)}, u32[]{:S(2)}) collective-permute-start(bf16[4,2,16,512]{3,2,1,0:T(8,128)(2,1)S(1)} %get-tuple-element.95), channel_id=1, source_target_pairs={{0,3},{1,0},{2,1},{3,2},{4,7},{5,4},{6,5},{7,6},{8,11},{9,8},{10,9... | collective-permute-start | bytes 393224 | tf_op jit(solution)/shard_map/ppermute | solution.py:998
  149.3 7.4 %collective-permute-start.28 = (bf16[80,640]{1,0:T(8,128)(2,1)S(1)}, bf16[80,640]{1,0:T(8,128)(2,1)S(1)}, u32[]{:S(2)}, u32[]{:S(2)}) collective-permute-start(bf16[80,640]{1,0:T(8,128)(2,1)S(1)} %get-tuple-element.97), channel_id=1, source_target_pairs={{0,3},{1,0},{2,1},{3,2},{4,7},{5,4},{6,5},{7,6},{8,11},{9,8},{10,9... | collective-permute-start | bytes 307208 | tf_op jit(solution)/shard_map/ppermute | solution.py:1002
  152.8 8.9 %collective-permute-start.29 = (bf16[80,640]{1,0:T(8,128)(2,1)S(1)}, bf16[80,640]{1,0:T(8,128)(2,1)S(1)}, u32[]{:S(2)}, u32[]{:S(2)}) collective-permute-start(bf16[80,640]{1,0:T(8,128)(2,1)S(1)} %get-tuple-element.98), channel_id=1, source_target_pairs={{0,2},{1,3},{2,0},{3,1},{4,6},{5,7},{6,4},{7,5},{8,10},{9,11},{10,... | collective-permute-start | bytes 307208 | tf_op jit(solution)/shard_map/ppermute | solution.py:1002
  152.8 8.9 %collective-permute-start.30 = (bf16[80,640]{1,0:T(8,128)(2,1)S(1)}, bf16[80,640]{1,0:T(8,128)(2,1)S(1)}, u32[]{:S(2)}, u32[]{:S(2)}) collective-permute-start(bf16[80,640]{1,0:T(8,128)(2,1)S(1)} %get-tuple-element.99), channel_id=1, source_target_pairs={{0,1},{1,2},{2,3},{3,0},{4,5},{5,6},{6,7},{7,4},{8,9},{9,10},{10,1... | collective-permute-start | bytes 307208 | tf_op jit(solution)/shard_map/ppermute | solution.py:1002

commit v7 on v6

--- a/solution.py
+++ b/solution.py
@@ -323,7 +323,7 @@
     def _():
         rows = weight.shape[0] // len(pieces)
         mine = lax.axis_index("seq") if len(pieces) > 1 else 0
-        start = pl.multiple_of((slot - 1) * rows, 16)
+        start = pl.multiple_of((3 - slot if len(pieces) > 1 else slot - 1) * rows, 16)
         for r, piece in enumerate(pieces):
             weight[pl.ds(pl.multiple_of((mine ^ r) * rows, rows), rows), :] = piece[pl.ds(start, rows), :]
 
@@ -412,10 +412,9 @@
 
 def gelu_both(u):
     square = u * u
-    bend = jnp.tanh(GELU_A * (u + GELU_B * (square * u)))
-    half = 0.5 * (1.0 + bend)
-    slope = half + 0.5 * u * (1.0 - bend * bend) * (GELU_A * (1.0 + 3.0 * GELU_B * square))
-    return u * half, slope
+    half = 0.5 + 0.5 * jnp.tanh(u * (GELU_A + GELU_A * GELU_B * square))
+    value = u * half
+    return value, half + value * (1.0 - half) * (2.0 * GELU_A + 6.0 * GELU_A * GELU_B * square)
 
 
 def weight_copies(block, pieces, weights, sems):
@@ -767,6 +766,40 @@
     )(value, *others)
 
 
+def near_kernel(slots, block_ref, load_ref, *refs):
+    came, (near_ref, loads_ref) = refs[: slots - 1], refs[slots - 1 :]
+    rows = came[0].shape[0] - 16
+    for a, piece in enumerate(came):
+        near_ref[a * rows : (a + 1) * rows, :] = piece[:rows, :]
+    lines = [block_ref[...].astype(F32)[0:1, :]]
+    lines += [piece[rows:, :].astype(F32)[0:1, :] for piece in reversed(came)]
+    lines += [jnp.zeros((16 - slots, block_ref.shape[1]), F32)]
+    near_ref[(slots - 1) * rows :, :] = low(jnp.concatenate(lines, axis=0))
+    for z in range(slots):
+        loads_ref[z] = load_ref[...]
+
+
+def join_near(block, load, came):
+    shape = jax.ShapeDtypeStruct
+    slots = len(came) + 1
+    rows = came[0].shape[0] - 16
+    operands = [block, load, *came]
+    outs = [
+        shape(((slots - 1) * rows + 16, block.shape[1]), BF16),
+        shape((slots,) + load.shape, BF16),
+    ]
+    return pl.pallas_call(
+        functools.partial(near_kernel, slots),
+        grid=(1,),
+        out_shape=outs,
+        in_specs=[fixed(o.shape) for o in operands],
+        out_specs=[fixed(o.shape) for o in outs],
+        compiler_params=params(12),
+        cost_estimate=cost(1),
+        name="join_near",
+    )(*operands)
+
+
 def vector_values(block):
     return block[:, :256].astype(F32) + block[:, 256:512].astype(F32)
 
@@ -871,6 +904,35 @@
         cost_estimate=cost(3),
         name="settle",
     )(*ffn, wait)
+
+
+def finish_kernel(share, hidden_share, mine_ref, sums_ref, *refs):
+    came, parts, vectors = refs[:3], refs[3:8], refs[8:]
+    rows = mine_ref.shape[0]
+    total = add(mine_ref[...], *[c[:rows, :] for c in came])
+    for i, part in enumerate(parts):
+        part[...] = total[:, i * PAIR : (i + 1) * PAIR]
+    values = add(sums_ref[0:1, :], *[vector_values(c[rows:, :])[0:1, :] for c in came])
+    for i, vector in enumerate(vectors[:-1]):
+        vector[...] = values[0, i * share : (i + 1) * share]
+    vectors[-1][...] = values[0, 128 : 128 + hidden_share]
+
+
+def finish(mine, sums, came, share, hidden_share):
+    shape = jax.ShapeDtypeStruct
+    operands = [mine, sums, *came]
+    outs = [shape((mine.shape[0], PAIR), F32)] * 5 + [shape((share,), F32)] * 5 + [shape((hidden_share,), F32)]
+    made = pl.pallas_call(
+        functools.partial(finish_kernel, share, hidden_share),
+        grid=(1,),
+        out_shape=outs,
+        in_specs=[fixed(o.shape) for o in operands],
+        out_specs=[fixed(o.shape) for o in outs],
+        compiler_params=params(12),
+        cost_estimate=cost(1),
+        name="finish",
+    )(*operands)
+    return made[:5], made[5:]
 
 
 def flip(count, bit):
@@ -954,12 +1016,9 @@
         piece = lax.dynamic_slice_in_dim(own, lax.axis_index("seq") * rows, rows, axis=0)
         piece = jnp.concatenate([piece, block], axis=0)
         came = [lax.ppermute(piece, "head", turn(slots, a)) for a in range(1, slots)]
-        for a in range(1, slots):
-            block = block + jnp.pad(came[a - 1][rows : rows + 1], ((a, 15 - a), (0, 0)))
-        near = jnp.concatenate([c[:rows] for c in came] + [block], axis=0)
+        near, loads = join_near(block, load.reshape(8, share, width), came[::-1])
         pieces, vectors = over_cores(over_chips(near, chips, seqs), seqs), []
-        load = jnp.broadcast_to(load.reshape(1, 8, share, width), (slots, 8, share, width))
-        load = lax.all_to_all(after(load, near), "head", 0, 0, tiled=True)
+        load = lax.all_to_all(loads, "head", 0, 0, tiled=True)
         held = over_chips(load, chips, seqs)
         tall = (slots * width // seqs + 16, 5 * PAIR)
         pair_shapes = [(chips,) + tall] + [tall] * chips
@@ -1000,11 +1059,7 @@
         mine, sums, *sends, wait = sum_plane(pairs, slots, ffn[1:])
         expand_grad, shrink_grad = settle(ffn, wait)
         came = [lax.ppermute(m, "head", turn(slots, slots - 1 - a)) for a, m in enumerate(sends)]
-        rows = mine.shape[0]
-        pair_sum = add(mine, *[c[:rows] for c in came])
-        sums = sums[0] + functools.reduce(
-            lambda a, b: a + b, [c[rows, :256].astype(F32) + c[rows, 256:512].astype(F32) for c in came]
-        )
+        parts, vector = finish(mine, sums, came[::-1], share, hidden_share)
     else:
         ffn_sum = lax.psum_scatter(
             ffn_grads[0].astype(F32).transpose(0, 2, 1, 3, 4).reshape(4, 2, width, width), ("seq", "head"), scatter_dimension=2, tiled=True
@@ -1020,21 +1075,20 @@
         expand_grad = ffn_sum[:, 0].reshape(hidden_share, width).T
         shrink_grad = ffn_sum[:, 1].reshape(4, share, devices, share).transpose(2, 0, 3, 1)
 
-    vector = [sums[i * share : (i + 1) * share] for i in range(5)]
+        parts = [pair_sum[:, i * PAIR : (i + 1) * PAIR] for i in range(5)]
+        vector = [sums[i * share : (i + 1) * share] for i in range(5)] + [sums[128 : 128 + hidden_share]]
+
     return (
         result,
         input_grad,
         vector[0],
         vector[1],
-        pair_sum[:, :PAIR],
-        pair_sum[:, PAIR : 2 * PAIR],
-        pair_sum[:, 2 * PAIR : 3 * PAIR],
-        pair_sum[:, 3 * PAIR : 4 * PAIR],
-        pair_sum[:, 4 * PAIR :].T,
+        *parts[:4],
+        parts[4].T,
         vector[2],
         vector[3],
         expand_grad,
-        sums[128 : 128 + hidden_share],
+        vector[5],
         shrink_grad.reshape(devices * hidden_share, share),
         vector[4],
     )

time: 164 us -> 159 us (0.970)
  waiting for transfers between devices: 43.4 us -> 37.1 us
  starting transfers between devices: 35.5 us -> 39.1 us
  local copies, waits for them, and re-layouts: 12.1 us -> 9.35 us
    ppermute x3, waiting for transfers between devices: 4.97 us -> 2.19 us  [body(): lax.ppermute(m, 'head', turn(slots, slots - 1 - a))]
    ppermute x3, waiting for transfers between devices: 5.57 us -> 3.12 us  [body(): lax.ppermute(piece, 'head', turn(slots, a))]
    unnamed x28 -> x26, local copies, waits for them, and re-layouts: 7.31 us -> 7.23 us
  transfers between devices with their start and end apart: 33 -> 33, of which waited for: 19 -> 19; matrix products, arithmetic and copies ran while one was open for 3% -> 3% of each run, Pallas kernels for 25% -> 26%
where the time goes in v7:
time: 159 us; the launch traced here: 158 us
  Pallas kernels  66.6 us (42%)
  starting transfers between devices  39.1 us (25%)
  waiting for transfers between devices  37.1 us (23%)
  local copies, waits for them, and re-layouts  9.35 us (6%)
  other arithmetic  5.14 us (3%)
    pallas_call x1, Pallas kernels, backward(): pl.pallas_call(functools.partial(back_kernel, len(waits), len(grad_shapes...  24.3 us
    pallas_call x1, Pallas kernels, feed_forward(): pl.pallas_call(functools.partial(ffn_kernel, len(pieces)), grid=(4,), out...  22.5 us
    ppermute x6, waiting for transfers between devices, over_chips(): lax.ppermute(shares, 'seq', flip(seqs, 2 * r))  15.6 us
    pallas_call x1, Pallas kernels, forward(): pl.pallas_call(functools.partial(forward_kernel, len(pieces), slots), gri...  14.8 us
    ppermute x3, waiting for transfers between devices, body(): lax.ppermute(ffn[a], 'head', turn(slots, a))  9.14 us
    unnamed x26, local copies, waits for them, and re-layouts  7.23 us
    ppermute x3, starting transfers between devices, body(): lax.ppermute(piece, 'head', turn(slots, a))  7.01 us
    ppermute x6, starting transfers between devices, over_chips(): lax.ppermute(shares, 'seq', flip(seqs, 2 * r))  6.98 us
  transfers between devices with their start and end apart: 33, of which 19 were waited for; matrix products, arithmetic and copies ran while one was open for 3% of the time, Pallas kernels for 26%

profile of v7, /device:TPU:0, one launch (start us, length us, event | category | flops | bytes accessed | tf_op | source)
XLA Modules:
  0.0 158.2 jit_solution(9782975362156561188)
XLA Ops:
  0.7 0.8 pad_add_fusion
  1.5 1.2 pad_maximum_fusion.own_ref
  2.8 3.1 %collective-permute-start.2 = (bf16[96,512]{1,0:T(8,128)(2,1)S(1)}, bf16[96,512]{1,0:T(8,128)(2,1)S(1)}, u32[]{:S(2)}, u32[]{:S(2)}) collective-permute-start(bf16[96,512]{1,0:T(8,128)(2,1)S(1)} %pad_maximum_fusion.2), channel_id=1, source_target_pairs={{0,1},{1,2},{2,3},{3,0},{4,5},{5,6},{6,7},{7,4},{8,9},{9,10},{10,1... | collective-permute-start | bytes 294920 | tf_op jit(solution)/shard_map/ppermute | solution.py:1018
  5.9 2.6 %collective-permute-start.1 = (bf16[96,512]{1,0:T(8,128)(2,1)S(1)}, bf16[96,512]{1,0:T(8,128)(2,1)S(1)}, u32[]{:S(2)}, u32[]{:S(2)}) collective-permute-start(bf16[96,512]{1,0:T(8,128)(2,1)S(1)} %pad_maximum_fusion.2), channel_id=1, source_target_pairs={{0,2},{1,3},{2,0},{3,1},{4,6},{5,7},{6,4},{7,5},{8,10},{9,11},{10,... | collective-permute-start | bytes 294920 | tf_op jit(solution)/shard_map/ppermute | solution.py:1018
  8.5 1.3 collective-permute-start
  9.8 1.2 reshape.39
  11.2 0.8 stack_reshape.7
  12.0 3.1 %collective-permute-done.1.refs_1_ = bf16[96,512]{1,0:T(8,128)(2,1)S(1)} collective-permute-done((bf16[96,512]{1,0:T(8,128)(2,1)S(1)}, bf16[96,512]{1,0:T(8,128)(2,1)S(1)}, u32[]{:S(2)}, u32[]{:S(2)}) %collective-permute-start.1) | collective-permute-done | bytes 98336 | tf_op jit(solution)/shard_map/ppermute | solution.py:1018
  15.1 0.8 join_near.1
  15.9 4.9 %all-to-all-start = ((bf16[4,8,16,512]{3,2,1,0:T(8,128)(2,1)}), bf16[4,8,16,512]{3,2,1,0:T(8,128)(2,1)S(1)}, u32[]{:S(2)}, u32[]{:S(2)}) async-start(bf16[4,8,16,512]{3,2,1,0:T(8,128)(2,1)} %get-tuple-element.77), calls=%async_computation | async-start | bytes 1048576 | tf_op jit(solution)/shard_map/all_to_all | solution.py:1021
  20.8 2.4 %collective-permute-start.8 = (bf16[256,512]{1,0:T(8,128)(2,1)S(1)}, bf16[256,512]{1,0:T(8,128)(2,1)}, u32[]{:S(2)}, u32[]{:S(2)}) collective-permute-start(bf16[256,512]{1,0:T(8,128)(2,1)S(1)} %get-tuple-element.73.refs_0_), channel_id=1, source_target_pairs={{0,24},{4,28},{8,16},{12,20},{16,8},{20,12},{24,0},{28,4},{1,25},{... | collective-permute-start | bytes 786440 | tf_op jit(solution)/shard_map/ppermute | solution.py:955
  23.3 0.5 collective-permute-start.6
  23.8 0.5 collective-permute-start.4
  24.3 6.8 %collective-permute-done.8.refs_6_ = bf16[256,512]{1,0:T(8,128)(2,1)} collective-permute-done((bf16[256,512]{1,0:T(8,128)(2,1)S(1)}, bf16[256,512]{1,0:T(8,128)(2,1)}, u32[]{:S(2)}, u32[]{:S(2)}) %collective-permute-start.8) | collective-permute-done | bytes 262176 | tf_op jit(solution)/shard_map/ppermute | solution.py:955
  31.1 3.2 %collective-permute-done.6.refs_4_ = bf16[256,512]{1,0:T(8,128)(2,1)} collective-permute-done((bf16[256,512]{1,0:T(8,128)(2,1)S(1)}, bf16[256,512]{1,0:T(8,128)(2,1)}, u32[]{:S(2)}, u32[]{:S(2)}) %collective-permute-start.6) | collective-permute-done | bytes 262176 | tf_op jit(solution)/shard_map/ppermute | solution.py:955
  34.4 0.4 collective-permute-start.5
  34.8 2.0 %collective-permute-start.15 = (bf16[4,8,16,512]{3,2,1,0:T(8,128)(2,1)S(1)}, bf16[4,8,16,512]{3,2,1,0:T(8,128)(2,1)S(1)}, u32[]{:S(2)}, u32[]{:S(2)}) collective-permute-start(bf16[4,8,16,512]{3,2,1,0:T(8,128)(2,1)S(1)} %all-to-all-done.refs_0_), channel_id=1, source_target_pairs={{0,24},{4,28},{8,16},{12,20},{16,8},{20,12},{24,0},{28,4},{1,25},{... | collective-permute-start | bytes 1572872 | tf_op jit(solution)/shard_map/ppermute | solution.py:955
  36.9 0.9 collective-permute-start.13
  37.8 0.5 collective-permute-start.11
  38.3 14.8 %attend_forward.1 = (bf16[1024,512]{1,0:T(8,128)(2,1)S(1)}, f32[16,512]{1,0:T(8,128)S(1)}, f32[1024,512]{1,0:T(8,128)S(1)}, bf16[1024,512]{1,0:T(8,128)(2,1)S(1)...) custom-call(bf16[1024,512]{1,0:T(8,128)(2,1)S(1)} %copy-done.1, ...), custom_call_target="tpu_custom_call" | custom-call | flops 16999999488 | bytes 17000000 | tf_op jit(solution)/shard_map/attend_forward/pallas_call | solution.py:395
  53.1 1.4 copy-done.7
  54.5 1.0 copy-done.8
  55.5 5.4 %collective-permute-done.13.refs_4_ = bf16[4,8,16,512]{3,2,1,0:T(8,128)(2,1)S(1)} collective-permute-done((bf16[4,8,16,512]{3,2,1,0:T(8,128)(2,1)S(1)}, bf16[4,8,16,512]{3,2,1,0:T(8,128)(2,1)S(1)}, u32[]{:S(2)}, u32[]{:S(2)}) %collective-permute-start.13) | collective-permute-done | bytes 524320 | tf_op jit(solution)/shard_map/ppermute | solution.py:955
  61.0 0.4 collective-permute-start.12
  61.4 0.8 multiply_convert_fusion.refs_6_
  62.3 0.5 collective-permute-done.14.refs_5_
  62.8 0.7 collective-permute-done.12.refs_3_
  63.6 0.7 collective-permute-done.16.refs_7_
  64.3 22.5 %feed_forward.1 = (bf16[1024,512]{1,0:T(8,128)(2,1)}, bf16[1024,512]{1,0:T(8,128)(2,1)S(1)}, f32[16,512]{1,0:T(8,128)S(1)}, bf16[4,4,4,2,16,512]{5,4,3,2,1,0:T(8,128)(2,1)S(1)}, bf16[4,4,4,2,16,512]{5,4,3,2,1,0:T(8,128)(2,1)}) custom-call(bf16[1024,512]{1,0:T(8,128)(2,1)S(1)} %get-tuple-element.74.second_ref, f32[16,512]{1,0:T(8,128)S(1)} %get-tuple-element.75.rows_ref, ...), custom_call_target="tpu_custom_call" | custom-call | flops 22000001024 | bytes 22000000 | tf_op jit(solution)/shard_map/feed_forward/pallas_call | solution.py:567
  86.8 0.2 collective-permute-start.17
  87.0 1.3 heads_back.1
  88.4 1.0 copy-done.5
  89.3 0.8 copy-done.6
  90.1 1.1 collective-permute-done.17
  91.3 2.3 %add_convert_fusion.refs_0_ = bf16[4,4,4,2,16,512]{5,4,3,2,1,0:T(8,128)(2,1)} fusion(bf16[4,4,4,2,16,512]{5,4,3,2,1,0:T(8,128)(2,1)S(1)} %collective-permute-done.17, bf16[4,4,4,2,16,512]{5,4,3,2,1,0:T(8,128)(2,1)S(1)} %get-tuple-element.83), kind=kLoop, calls=%fused_computation | loop fusion | flops 4194304 | bytes 6291456 | tf_op jit(solution)/shard_map/convert_element_type | solution.py:30
  93.6 3.6 %all-to-all-start.1 = ((bf16[4,4,4,2,16,512]{5,4,3,2,1,0:T(8,128)(2,1)}), bf16[4,4,4,2,16,512]{5,4,3,2,1,0:T(8,128)(2,1)S(1)}, u32[]{:S(2)}, u32[]{:S(2)}) async-start(bf16[4,4,4,2,16,512]{5,4,3,2,1,0:T(8,128)(2,1)} %add_convert_fusion.refs_0_), calls=%async_computation.1 | async-start | bytes 4194304 | tf_op jit(solution)/shard_map/all_to_all | solution.py:964
  97.2 24.3 %attend_back.1 = (bf16[1024,512]{1,0:T(8,128)(2,1)}, f32[32,256]{1,0:T(8,128)}, bf16[4,272,640]{2,1,0:T(8,128)(2,1)}, bf16[272,640]{1,0:T(8,128)(2,1)}, bf16[272...) custom-call(bf16[1024,512]{1,0:T(8,128)(2,1)} %copy-done.8, ...), custom_call_target="tpu_custom_call" | custom-call | flops 27000000512 | bytes 27000000 | tf_op jit(solution)/shard_map/attend_back/pallas_call | solution.py:735
  121.5 0.2 collective-permute-start.18
  121.7 0.4 collective-permute-start.19
  122.2 0.4 collective-permute-start.21
  122.6 0.8 collective-permute-done.18.refs_0_
  123.4 0.5 collective-permute-done.19.refs_1_
  123.9 0.5 collective-permute-done.20.refs_2_
  124.4 0.5 collective-permute-done.21.refs_3_
  124.9 1.3 copy-done.2
  126.3 0.6 join.1
  126.9 2.0 %collective-permute-start.22 = (bf16[272,640]{1,0:T(8,128)(2,1)S(1)}, bf16[272,640]{1,0:T(8,128)(2,1)S(1)}, u32[]{:S(2)}, u32[]{:S(2)}) collective-permute-start(bf16[272,640]{1,0:T(8,128)(2,1)S(1)} %get-tuple-element.105), channel_id=1, source_target_pairs={{0,8},{4,12},{8,0},{12,4},{16,24},{20,28},{24,16},{28,20},{1,9},{5... | collective-permute-start | bytes 1044488 | tf_op jit(solution)/shard_map/ppermute | solution.py:968
  128.9 1.5 collective-permute-start.23
  130.5 2.6 %collective-permute-start.25 = (bf16[4,2,16,512]{3,2,1,0:T(8,128)(2,1)S(1)}, bf16[4,2,16,512]{3,2,1,0:T(8,128)(2,1)S(1)}, u32[]{:S(2)}, u32[]{:S(2)}) collective-permute-start(bf16[4,2,16,512]{3,2,1,0:T(8,128)(2,1)S(1)} %get-tuple-element.108), channel_id=1, source_target_pairs={{0,1},{1,2},{2,3},{3,0},{4,5},{5,6},{6,7},{7,4},{8,9},{9,10},{10,1... | collective-permute-start | bytes 393224 | tf_op jit(solution)/shard_map/ppermute | solution.py:1057
  133.0 1.5 collective-permute-start.26
  134.6 4.1 %collective-permute-done.25.refs_4_.refs_1_ = bf16[4,2,16,512]{3,2,1,0:T(8,128)(2,1)S(1)} collective-permute-done((bf16[4,2,16,512]{3,2,1,0:T(8,128)(2,1)S(1)}, bf16[4,2,16,512]{3,2,1,0:T(8,128)(2,1)S(1)}, u32[]{:S(2)}, u32[]{:S(2)}) %collective-permute-start.25) | collective-permute-done | bytes 131104 | tf_op jit(solution)/shard_map/ppermute | solution.py:1057
  138.7 1.1 collective-permute-start.27
  139.7 3.2 %collective-permute-done.26.refs_5_.refs_2_ = bf16[4,2,16,512]{3,2,1,0:T(8,128)(2,1)S(1)} collective-permute-done((bf16[4,2,16,512]{3,2,1,0:T(8,128)(2,1)S(1)}, bf16[4,2,16,512]{3,2,1,0:T(8,128)(2,1)S(1)}, u32[]{:S(2)}, u32[]{:S(2)}) %collective-permute-start.26) | collective-permute-done | bytes 131104 | tf_op jit(solution)/shard_map/ppermute | solution.py:1057
  142.9 1.8 %collective-permute-done.27.refs_6_.refs_3_ = bf16[4,2,16,512]{3,2,1,0:T(8,128)(2,1)S(1)} collective-permute-done((bf16[4,2,16,512]{3,2,1,0:T(8,128)(2,1)S(1)}, bf16[4,2,16,512]{3,2,1,0:T(8,128)(2,1)S(1)}, u32[]{:S(2)}, u32[]{:S(2)}) %collective-permute-start.27) | collective-permute-done | bytes 131104 | tf_op jit(solution)/shard_map/ppermute | solution.py:1057
  144.8 1.5 collective-permute-done.23.refs_2_
  146.3 0.6 sum_plane.1
  146.9 2.6 %collective-permute-start.28 = (bf16[80,640]{1,0:T(8,128)(2,1)S(1)}, bf16[80,640]{1,0:T(8,128)(2,1)S(1)}, u32[]{:S(2)}, u32[]{:S(2)}) collective-permute-start(bf16[80,640]{1,0:T(8,128)(2,1)S(1)} %get-tuple-element.113), channel_id=1, source_target_pairs={{0,1},{1,2},{2,3},{3,0},{4,5},{5,6},{6,7},{7,4},{8,9},{9,10},{10,1... | collective-permute-start | bytes 307208 | tf_op jit(solution)/shard_map/ppermute | solution.py:1061
  149.5 1.5 collective-permute-start.29
  151.0 1.5 collective-permute-start.30
  152.5 1.0 settle.1
  153.5 0.8 copy.36
  154.3 1.0 copy.37
  155.3 2.2 %collective-permute-done.29.refs_1_ = bf16[80,640]{1,0:T(8,128)(2,1)S(1)} collective-permute-done((bf16[80,640]{1,0:T(8,128)(2,1)S(1)}, bf16[80,640]{1,0:T(8,128)(2,1)S(1)}, u32[]{:S(2)}, u32[]{:S(2)}) %collective-permute-start.29) | collective-permute-done | bytes 102432 | tf_op jit(solution)/shard_map/ppermute | solution.py:1061
  157.5 0.7 finish.1
  (50 shorter events, 0.8 us)
Async XLA Ops:
  0.6 11.3 %copy-start.11 = (bf16[512,64]{0,1:T(8,128)(2,1)S(1)}, bf16[512,64]{0,1:T(8,128)(2,1)}, u32[]{:S(2)}) copy-start(bf16[512,64]{0,1:T(8,128)(2,1)} %param.25) | copy-start | bytes 196612
  2.8 9.2 %collective-permute-start.2 = (bf16[96,512]{1,0:T(8,128)(2,1)S(1)}, bf16[96,512]{1,0:T(8,128)(2,1)S(1)}, u32[]{:S(2)}, u32[]{:S(2)}) collective-permute-start(bf16[96,512]{1,0:T(8,128)(2,1)S(1)} %pad_maximum_fusion.2), channel_id=1, source_target_pairs={{0,1},{1,2},{2,3},{3,0},{4,5},{5,6},{6,7},{7,4},{8,9},{9,10},{10,1... | collective-permute-start | bytes 294920 | tf_op jit(solution)/shard_map/ppermute | solution.py:1018
  5.9 9.2 %collective-permute-start.1 = (bf16[96,512]{1,0:T(8,128)(2,1)S(1)}, bf16[96,512]{1,0:T(8,128)(2,1)S(1)}, u32[]{:S(2)}, u32[]{:S(2)}) collective-permute-start(bf16[96,512]{1,0:T(8,128)(2,1)S(1)} %pad_maximum_fusion.2), channel_id=1, source_target_pairs={{0,2},{1,3},{2,0},{3,1},{4,6},{5,7},{6,4},{7,5},{8,10},{9,11},{10,... | collective-permute-start | bytes 294920 | tf_op jit(solution)/shard_map/ppermute | solution.py:1018
  8.5 6.6 %collective-permute-start = (bf16[96,512]{1,0:T(8,128)(2,1)S(1)}, bf16[96,512]{1,0:T(8,128)(2,1)S(1)}, u32[]{:S(2)}, u32[]{:S(2)}) collective-permute-start(bf16[96,512]{1,0:T(8,128)(2,1)S(1)} %pad_maximum_fusion.2), channel_id=1, source_target_pairs={{0,3},{1,0},{2,1},{3,2},{4,7},{5,4},{6,5},{7,6},{8,11},{9,8},{10,9... | collective-permute-start | bytes 294920 | tf_op jit(solution)/shard_map/ppermute | solution.py:1018
  15.1 23.2 %copy-start.1 = (bf16[1024,512]{1,0:T(8,128)(2,1)S(1)}, bf16[1024,512]{1,0:T(8,128)(2,1)}, u32[]{:S(2)}) copy-start(bf16[1024,512]{1,0:T(8,128)(2,1)} %tokens_hbm.1) | copy-start | bytes 3145732
  15.9 18.9 %all-to-all-start = ((bf16[4,8,16,512]{3,2,1,0:T(8,128)(2,1)}), bf16[4,8,16,512]{3,2,1,0:T(8,128)(2,1)S(1)}, u32[]{:S(2)}, u32[]{:S(2)}) async-start(bf16[4,8,16,512]{3,2,1,0:T(8,128)(2,1)} %get-tuple-element.77), calls=%async_computation | async-start | bytes 1048576 | tf_op jit(solution)/shard_map/all_to_all | solution.py:1021
  20.8 43.5 %copy-start = (bf16[1024,512]{1,0:T(8,128)(2,1)S(1)}, bf16[1024,512]{1,0:T(8,128)(2,1)}, u32[]{:S(2)}) copy-start(bf16[1024,512]{1,0:T(8,128)(2,1)} %cotangent_hbm.1) | copy-start | bytes 3145732
  20.8 10.3 %collective-permute-start.8 = (bf16[256,512]{1,0:T(8,128)(2,1)S(1)}, bf16[256,512]{1,0:T(8,128)(2,1)}, u32[]{:S(2)}, u32[]{:S(2)}) collective-permute-start(bf16[256,512]{1,0:T(8,128)(2,1)S(1)} %get-tuple-element.73.refs_0_), channel_id=1, source_target_pairs={{0,24},{4,28},{8,16},{12,20},{16,8},{20,12},{24,0},{28,4},{1,25},{... | collective-permute-start | bytes 786440 | tf_op jit(solution)/shard_map/ppermute | solution.py:955
  23.3 11.1 %collective-permute-start.6 = (bf16[256,512]{1,0:T(8,128)(2,1)S(1)}, bf16[256,512]{1,0:T(8,128)(2,1)}, u32[]{:S(2)}, u32[]{:S(2)}) collective-permute-start(bf16[256,512]{1,0:T(8,128)(2,1)S(1)} %get-tuple-element.73.refs_0_), channel_id=1, source_target_pairs={{0,16},{4,20},{8,24},{12,28},{16,0},{20,4},{24,8},{28,12},{1,17},{... | collective-permute-start | bytes 786440 | tf_op jit(solution)/shard_map/ppermute | solution.py:955
  23.8 10.7 %collective-permute-start.4 = (bf16[256,512]{1,0:T(8,128)(2,1)S(1)}, bf16[256,512]{1,0:T(8,128)(2,1)}, u32[]{:S(2)}, u32[]{:S(2)}) collective-permute-start(bf16[256,512]{1,0:T(8,128)(2,1)S(1)} %get-tuple-element.73.refs_0_), channel_id=1, source_target_pairs={{0,8},{4,12},{8,0},{12,4},{16,24},{20,28},{24,16},{28,20},{1,9},{5... | collective-permute-start | bytes 786440 | tf_op jit(solution)/shard_map/ppermute | solution.py:955
  24.3 12.6 %collective-permute-start.3 = (bf16[256,512]{1,0:T(8,128)(2,1)S(1)}, bf16[256,512]{1,0:T(8,128)(2,1)}, u32[]{:S(2)}, u32[]{:S(2)}) collective-permute-start(bf16[256,512]{1,0:T(8,128)(2,1)S(1)} %get-tuple-element.73.refs_0_), channel_id=1, source_target_pairs={{0,4},{4,0},{8,12},{12,8},{16,20},{20,16},{24,28},{28,24},{1,5},{5... | collective-permute-start | bytes 786440 | tf_op jit(solution)/shard_map/ppermute | solution.py:951
  31.1 6.7 %collective-permute-start.9 = (bf16[256,512]{1,0:T(8,128)(2,1)}, bf16[256,512]{1,0:T(8,128)(2,1)}, u32[]{:S(2)}, u32[]{:S(2)}) collective-permute-start(bf16[256,512]{1,0:T(8,128)(2,1)} %collective-permute-done.8.refs_6_), channel_id=1, source_target_pairs={{0,4},{4,0},{8,12},{12,8},{16,20},{20,16},{24,28},{28,24},{1,5},{5... | collective-permute-start | bytes 786440 | tf_op jit(solution)/shard_map/ppermute | solution.py:951
  34.3 4.0 %collective-permute-start.7 = (bf16[256,512]{1,0:T(8,128)(2,1)}, bf16[256,512]{1,0:T(8,128)(2,1)}, u32[]{:S(2)}, u32[]{:S(2)}) collective-permute-start(bf16[256,512]{1,0:T(8,128)(2,1)} %collective-permute-done.6.refs_4_), channel_id=1, source_target_pairs={{0,4},{4,0},{8,12},{12,8},{16,20},{20,16},{24,28},{28,24},{1,5},{5... | collective-permute-start | bytes 786440 | tf_op jit(solution)/shard_map/ppermute | solution.py:951
  34.4 3.9 %collective-permute-start.5 = (bf16[256,512]{1,0:T(8,128)(2,1)}, bf16[256,512]{1,0:T(8,128)(2,1)}, u32[]{:S(2)}, u32[]{:S(2)}) collective-permute-start(bf16[256,512]{1,0:T(8,128)(2,1)} %collective-permute-done.4.refs_2_), channel_id=1, source_target_pairs={{0,4},{4,0},{8,12},{12,8},{16,20},{20,16},{24,28},{28,24},{1,5},{5... | collective-permute-start | bytes 786440 | tf_op jit(solution)/shard_map/ppermute | solution.py:951
  34.8 26.6 %collective-permute-start.15 = (bf16[4,8,16,512]{3,2,1,0:T(8,128)(2,1)S(1)}, bf16[4,8,16,512]{3,2,1,0:T(8,128)(2,1)S(1)}, u32[]{:S(2)}, u32[]{:S(2)}) collective-permute-start(bf16[4,8,16,512]{3,2,1,0:T(8,128)(2,1)S(1)} %all-to-all-done.refs_0_), channel_id=1, source_target_pairs={{0,24},{4,28},{8,16},{12,20},{16,8},{20,12},{24,0},{28,4},{1,25},{... | collective-permute-start | bytes 1572872 | tf_op jit(solution)/shard_map/ppermute | solution.py:955
  36.9 24.0 %collective-permute-start.13 = (bf16[4,8,16,512]{3,2,1,0:T(8,128)(2,1)S(1)}, bf16[4,8,16,512]{3,2,1,0:T(8,128)(2,1)S(1)}, u32[]{:S(2)}, u32[]{:S(2)}) collective-permute-start(bf16[4,8,16,512]{3,2,1,0:T(8,128)(2,1)S(1)} %all-to-all-done.refs_0_), channel_id=1, source_target_pairs={{0,16},{4,20},{8,24},{12,28},{16,0},{20,4},{24,8},{28,12},{1,17},{... | collective-permute-start | bytes 1572872 | tf_op jit(solution)/shard_map/ppermute | solution.py:955
  37.8 23.2 %collective-permute-start.11 = (bf16[4,8,16,512]{3,2,1,0:T(8,128)(2,1)S(1)}, bf16[4,8,16,512]{3,2,1,0:T(8,128)(2,1)S(1)}, u32[]{:S(2)}, u32[]{:S(2)}) collective-permute-start(bf16[4,8,16,512]{3,2,1,0:T(8,128)(2,1)S(1)} %all-to-all-done.refs_0_), channel_id=1, source_target_pairs={{0,8},{4,12},{8,0},{12,4},{16,24},{20,28},{24,16},{28,20},{1,9},{5... | collective-permute-start | bytes 1572872 | tf_op jit(solution)/shard_map/ppermute | solution.py:955
  53.1 1.4 copy-start.7
  54.5 1.0 copy-start.8
  55.5 31.3 %copy-start.9 = (f32[16,512]{1,0:T(8,128)}, f32[16,512]{1,0:T(8,128)S(1)}, u32[]{:S(2)}) copy-start(f32[16,512]{1,0:T(8,128)S(1)} %get-tuple-element.75.rows_ref) | copy-start | bytes 98308
  55.5 6.8 %collective-permute-start.10 = (bf16[4,8,16,512]{3,2,1,0:T(8,128)(2,1)S(1)}, bf16[4,8,16,512]{3,2,1,0:T(8,128)(2,1)S(1)}, u32[]{:S(2)}, u32[]{:S(2)}) collective-permute-start(bf16[4,8,16,512]{3,2,1,0:T(8,128)(2,1)S(1)} %all-to-all-done.refs_0_), channel_id=1, source_target_pairs={{0,4},{4,0},{8,12},{12,8},{16,20},{20,16},{24,28},{28,24},{1,5},{5... | collective-permute-start | bytes 1572872 | tf_op jit(solution)/shard_map/ppermute | solution.py:951
  60.9 1.9 %collective-permute-start.14 = (bf16[4,8,16,512]{3,2,1,0:T(8,128)(2,1)S(1)}, bf16[4,8,16,512]{3,2,1,0:T(8,128)(2,1)S(1)}, u32[]{:S(2)}, u32[]{:S(2)}) collective-permute-start(bf16[4,8,16,512]{3,2,1,0:T(8,128)(2,1)S(1)} %collective-permute-done.13.refs_4_), channel_id=1, source_target_pairs={{0,4},{4,0},{8,12},{12,8},{16,20},{20,16},{24,28},{28,24},{1,5},{5... | collective-permute-start | bytes 1572872 | tf_op jit(solution)/shard_map/ppermute | solution.py:951
  61.0 2.6 %collective-permute-start.12 = (bf16[4,8,16,512]{3,2,1,0:T(8,128)(2,1)S(1)}, bf16[4,8,16,512]{3,2,1,0:T(8,128)(2,1)S(1)}, u32[]{:S(2)}, u32[]{:S(2)}) collective-permute-start(bf16[4,8,16,512]{3,2,1,0:T(8,128)(2,1)S(1)} %collective-permute-done.11.refs_2_), channel_id=1, source_target_pairs={{0,4},{4,0},{8,12},{12,8},{16,20},{20,16},{24,28},{28,24},{1,5},{5... | collective-permute-start | bytes 1572872 | tf_op jit(solution)/shard_map/ppermute | solution.py:951
  62.2 2.1 %collective-permute-start.16 = (bf16[4,8,16,512]{3,2,1,0:T(8,128)(2,1)S(1)}, bf16[4,8,16,512]{3,2,1,0:T(8,128)(2,1)S(1)}, u32[]{:S(2)}, u32[]{:S(2)}) collective-permute-start(bf16[4,8,16,512]{3,2,1,0:T(8,128)(2,1)S(1)} %multiply_convert_fusion.refs_6_), channel_id=1, source_target_pairs={{0,4},{4,0},{8,12},{12,8},{16,20},{20,16},{24,28},{28,24},{1,5},{5... | collective-permute-start | bytes 1572872 | tf_op jit(solution)/shard_map/ppermute | solution.py:951
  64.3 22.7 %copy-start.3 = (bf16[4,640,512]{2,1,0:T(8,128)(2,1)S(1)}, bf16[4,640,512]{2,1,0:T(8,128)(2,1)}, u32[]{:S(2)}) copy-start(bf16[4,640,512]{2,1,0:T(8,128)(2,1)} %get-tuple-element.85.weight_ref.refs_1_) | copy-start | bytes 7864324
  86.8 1.5 copy-start.4
  86.8 1.5 copy-start.10
  86.8 4.4 %collective-permute-start.17 = (bf16[4,4,4,2,16,512]{5,4,3,2,1,0:T(8,128)(2,1)}, bf16[4,4,4,2,16,512]{5,4,3,2,1,0:T(8,128)(2,1)S(1)}, u32[]{:S(2)}, u32[]{:S(2)}) collective-permute-start(bf16[4,4,4,2,16,512]{5,4,3,2,1,0:T(8,128)(2,1)} %get-tuple-element.84), channel_id=1, source_target_pairs={{0,4},{4,0},{8,12},{12,8},{16,20},{20,16},{24,28},{28,24},{1,5},{5... | collective-permute-start | bytes 6291464 | tf_op jit(solution)/shard_map/ppermute | solution.py:951
  88.4 1.0 copy-start.5
  89.3 0.8 copy-start.6
  93.6 31.4 %all-to-all-start.1 = ((bf16[4,4,4,2,16,512]{5,4,3,2,1,0:T(8,128)(2,1)}), bf16[4,4,4,2,16,512]{5,4,3,2,1,0:T(8,128)(2,1)S(1)}, u32[]{:S(2)}, u32[]{:S(2)}) async-start(bf16[4,4,4,2,16,512]{5,4,3,2,1,0:T(8,128)(2,1)} %add_convert_fusion.refs_0_), calls=%async_computation.1 | async-start | bytes 4194304 | tf_op jit(solution)/shard_map/all_to_all | solution.py:964
  121.5 1.9 %collective-permute-start.18 = (bf16[272,640]{1,0:T(8,128)(2,1)}, bf16[272,640]{1,0:T(8,128)(2,1)S(1)}, u32[]{:S(2)}, u32[]{:S(2)}) collective-permute-start(bf16[272,640]{1,0:T(8,128)(2,1)} %get-tuple-element.100), channel_id=1, source_target_pairs={{0,4},{4,0},{8,12},{12,8},{16,20},{20,16},{24,28},{28,24},{1,5},{5... | collective-permute-start | bytes 1044488 | tf_op jit(solution)/shard_map/ppermute | solution.py:951
  121.7 2.2 %collective-permute-start.19 = (bf16[272,640]{1,0:T(8,128)(2,1)}, bf16[272,640]{1,0:T(8,128)(2,1)S(1)}, u32[]{:S(2)}, u32[]{:S(2)}) collective-permute-start(bf16[272,640]{1,0:T(8,128)(2,1)} %get-tuple-element.101), channel_id=1, source_target_pairs={{0,4},{4,0},{8,12},{12,8},{16,20},{20,16},{24,28},{28,24},{1,5},{5... | collective-permute-start | bytes 1044488 | tf_op jit(solution)/shard_map/ppermute | solution.py:951
  122.1 2.4 %collective-permute-start.20 = (bf16[272,640]{1,0:T(8,128)(2,1)}, bf16[272,640]{1,0:T(8,128)(2,1)S(1)}, u32[]{:S(2)}, u32[]{:S(2)}) collective-permute-start(bf16[272,640]{1,0:T(8,128)(2,1)} %get-tuple-element.102), channel_id=1, source_target_pairs={{0,4},{4,0},{8,12},{12,8},{16,20},{20,16},{24,28},{28,24},{1,5},{5... | collective-permute-start | bytes 1044488 | tf_op jit(solution)/shard_map/ppermute | solution.py:951
  122.2 2.7 %collective-permute-start.21 = (bf16[272,640]{1,0:T(8,128)(2,1)}, bf16[272,640]{1,0:T(8,128)(2,1)S(1)}, u32[]{:S(2)}, u32[]{:S(2)}) collective-permute-start(bf16[272,640]{1,0:T(8,128)(2,1)} %get-tuple-element.103), channel_id=1, source_target_pairs={{0,4},{4,0},{8,12},{12,8},{16,20},{20,16},{24,28},{28,24},{1,5},{5... | collective-permute-start | bytes 1044488 | tf_op jit(solution)/shard_map/ppermute | solution.py:951
  124.9 1.3 copy-start.2
  126.9 17.9 %collective-permute-start.22 = (bf16[272,640]{1,0:T(8,128)(2,1)S(1)}, bf16[272,640]{1,0:T(8,128)(2,1)S(1)}, u32[]{:S(2)}, u32[]{:S(2)}) collective-permute-start(bf16[272,640]{1,0:T(8,128)(2,1)S(1)} %get-tuple-element.105), channel_id=1, source_target_pairs={{0,8},{4,12},{8,0},{12,4},{16,24},{20,28},{24,16},{28,20},{1,9},{5... | collective-permute-start | bytes 1044488 | tf_op jit(solution)/shard_map/ppermute | solution.py:968
  128.9 17.4 %collective-permute-start.23 = (bf16[272,640]{1,0:T(8,128)(2,1)S(1)}, bf16[272,640]{1,0:T(8,128)(2,1)S(1)}, u32[]{:S(2)}, u32[]{:S(2)}) collective-permute-start(bf16[272,640]{1,0:T(8,128)(2,1)S(1)} %get-tuple-element.106), channel_id=1, source_target_pairs={{0,16},{4,20},{8,24},{12,28},{16,0},{20,4},{24,8},{28,12},{1,17},{... | collective-permute-start | bytes 1044488 | tf_op jit(solution)/shard_map/ppermute | solution.py:968
  130.4 15.9 %collective-permute-start.24 = (bf16[272,640]{1,0:T(8,128)(2,1)S(1)}, bf16[272,640]{1,0:T(8,128)(2,1)S(1)}, u32[]{:S(2)}, u32[]{:S(2)}) collective-permute-start(bf16[272,640]{1,0:T(8,128)(2,1)S(1)} %get-tuple-element.107), channel_id=1, source_target_pairs={{0,24},{4,28},{8,16},{12,20},{16,8},{20,12},{24,0},{28,4},{1,25},{... | collective-permute-start | bytes 1044488 | tf_op jit(solution)/shard_map/ppermute | solution.py:968
  130.5 8.2 %collective-permute-start.25 = (bf16[4,2,16,512]{3,2,1,0:T(8,128)(2,1)S(1)}, bf16[4,2,16,512]{3,2,1,0:T(8,128)(2,1)S(1)}, u32[]{:S(2)}, u32[]{:S(2)}) collective-permute-start(bf16[4,2,16,512]{3,2,1,0:T(8,128)(2,1)S(1)} %get-tuple-element.108), channel_id=1, source_target_pairs={{0,1},{1,2},{2,3},{3,0},{4,5},{5,6},{6,7},{7,4},{8,9},{9,10},{10,1... | collective-permute-start | bytes 393224 | tf_op jit(solution)/shard_map/ppermute | solution.py:1057
  133.0 9.9 %collective-permute-start.26 = (bf16[4,2,16,512]{3,2,1,0:T(8,128)(2,1)S(1)}, bf16[4,2,16,512]{3,2,1,0:T(8,128)(2,1)S(1)}, u32[]{:S(2)}, u32[]{:S(2)}) collective-permute-start(bf16[4,2,16,512]{3,2,1,0:T(8,128)(2,1)S(1)} %get-tuple-element.109), channel_id=1, source_target_pairs={{0,2},{1,3},{2,0},{3,1},{4,6},{5,7},{6,4},{7,5},{8,10},{9,11},{10,... | collective-permute-start | bytes 393224 | tf_op jit(solution)/shard_map/ppermute | solution.py:1057
  138.7 6.1 %collective-permute-start.27 = (bf16[4,2,16,512]{3,2,1,0:T(8,128)(2,1)S(1)}, bf16[4,2,16,512]{3,2,1,0:T(8,128)(2,1)S(1)}, u32[]{:S(2)}, u32[]{:S(2)}) collective-permute-start(bf16[4,2,16,512]{3,2,1,0:T(8,128)(2,1)S(1)} %get-tuple-element.110), channel_id=1, source_target_pairs={{0,3},{1,0},{2,1},{3,2},{4,7},{5,4},{6,5},{7,6},{8,11},{9,8},{10,9... | collective-permute-start | bytes 393224 | tf_op jit(solution)/shard_map/ppermute | solution.py:1057
  146.9 8.4 %collective-permute-start.28 = (bf16[80,640]{1,0:T(8,128)(2,1)S(1)}, bf16[80,640]{1,0:T(8,128)(2,1)S(1)}, u32[]{:S(2)}, u32[]{:S(2)}) collective-permute-start(bf16[80,640]{1,0:T(8,128)(2,1)S(1)} %get-tuple-element.113), channel_id=1, source_target_pairs={{0,1},{1,2},{2,3},{3,0},{4,5},{5,6},{6,7},{7,4},{8,9},{9,10},{10,1... | collective-permute-start | bytes 307208 | tf_op jit(solution)/shard_map/ppermute | solution.py:1061
  149.5 8.0 %collective-permute-start.29 = (bf16[80,640]{1,0:T(8,128)(2,1)S(1)}, bf16[80,640]{1,0:T(8,128)(2,1)S(1)}, u32[]{:S(2)}, u32[]{:S(2)}) collective-permute-start(bf16[80,640]{1,0:T(8,128)(2,1)S(1)} %get-tuple-element.114), channel_id=1, source_target_pairs={{0,2},{1,3},{2,0},{3,1},{4,6},{5,7},{6,4},{7,5},{8,10},{9,11},{10,... | collective-permute-start | bytes 307208 | tf_op jit(solution)/shard_map/ppermute | solution.py:1061
  151.0 6.5 %collective-permute-start.30 = (bf16[80,640]{1,0:T(8,128)(2,1)S(1)}, bf16[80,640]{1,0:T(8,128)(2,1)S(1)}, u32[]{:S(2)}, u32[]{:S(2)}) collective-permute-start(bf16[80,640]{1,0:T(8,128)(2,1)S(1)} %get-tuple-element.115), channel_id=1, source_target_pairs={{0,3},{1,0},{2,1},{3,2},{4,7},{5,4},{6,5},{7,6},{8,11},{9,8},{10,9... | collective-permute-start | bytes 307208 | tf_op jit(solution)/shard_map/ppermute | solution.py:1061

commit v8 on v7

--- a/solution.py
+++ b/solution.py
@@ -451,27 +451,19 @@
     return copies
 
 
-def ffn_kernel(count, second_ref, rows_ref, cotangent_hbm, residual_hbm, *refs):
+def ffn_kernel(count, second_ref, rows_ref, cotangent_hbm, *refs):
     pieces = refs[:count]
-    result_hbm, branch_hbm, sums_ref = refs[count : count + 3]
-    outs = refs[count + 3 : -13]
-    (weights, grads, residual, cotangent_ref, total, back, result, branch, in_sems, out_sems, residual_sem, tile_sems, cotangent_sems) = refs[-13:]
+    total, back, sums_ref = refs[count : count + 3]
+    outs = refs[count + 3 : -6]
+    weights, grads, cotangent_ref, in_sems, out_sems, cotangent_sems = refs[-6:]
     k = pl.program_id(0)
     length, width = second_ref.shape
     tiles = [slice(r, r + 256) for r in range(0, length, 256)]
-    fetch = pltpu.make_async_copy(residual_hbm, residual, residual_sem)
 
     def arrive(rows):
         return pltpu.make_async_copy(
             cotangent_hbm.at[rows, :], cotangent_ref.at[rows, :], cotangent_sems.at[rows.start // 256]
         )
-
-    def leave(rows):
-        tile = rows.start // 256
-        return [
-            pltpu.make_async_copy(source.at[rows, :], target.at[rows, :], tile_sems.at[i, tile])
-            for i, (source, target) in enumerate([(result, result_hbm), (branch, branch_hbm)])
-        ]
 
     @pl.when(k == 0)
     def _():
@@ -482,7 +474,6 @@
         for block in range(1, 4):
             for copy in weight_copies(block, pieces, weights, in_sems):
                 copy.start()
-        fetch.start()
         total[...] = jnp.zeros_like(total)
         back[...] = jnp.zeros_like(back)
 
@@ -526,108 +517,91 @@
 
     @pl.when(k == 3)
     def _():
-        fetch.wait()
-        gain, bias = rows_ref[2:3, :], rows_ref[4:5, :]
-        gain_grad = jnp.zeros((1, width), F32)
-        shift_grad = jnp.zeros((1, width), F32)
-        outer = jnp.zeros((1, width), F32)
-        for rows in tiles:
-            base = residual[rows, :]
-            result[rows, :] = low(base + total[rows, :] + bias)
-            grad = back[rows, :]
-            normal, rate = norm_parts(base)
-            upstream = cotangent_ref[rows, :].astype(F32)
-            gain_grad = gain_grad + jnp.sum(grad * normal, axis=0, keepdims=True)
-            shift_grad = shift_grad + jnp.sum(grad, axis=0, keepdims=True)
-            outer = outer + jnp.sum(upstream, axis=0, keepdims=True)
-            branch[rows, :] = low(upstream + norm_back(grad, normal, rate, gain))
-            for copy in leave(rows):
-                copy.start()
-        sums_ref[0:2, :] = jnp.zeros((2, width), F32)
-        sums_ref[2:3, :] = gain_grad
-        sums_ref[3:4, :] = shift_grad
-        sums_ref[4:5, :] = outer
-        for rows in tiles:
-            for copy in leave(rows):
-                copy.wait()
         for block in range(4):
             for copy in grad_copies(block, grads, outs, out_sems):
                 copy.wait()
 
 
-def feed_forward(second, rows, cotangent, residual, pieces, grad_shapes):
+def feed_forward(second, rows, cotangent, pieces, grad_shapes):
     length, width = second.shape
     shape = jax.ShapeDtypeStruct
     weights = (4, width // 16, 2, 16, width)
-    outs = [
-        shape((length, width), BF16),
-        shape((length, width), BF16),
-        shape((16, width), F32),
-    ]
+    outs = [shape((length, width), F32), shape((length, width), F32), shape((16, width), F32)]
     return pl.pallas_call(
         functools.partial(ffn_kernel, len(pieces)),
         grid=(4,),
         out_shape=outs + [shape(s, BF16) for s in grad_shapes],
         in_specs=[fixed(o.shape) for o in (second, rows)]
-        + [pl.BlockSpec(memory_space=pltpu.HBM)] * (2 + len(pieces)),
-        out_specs=anywhere(outs[:2]) + [fixed(outs[2].shape)] + anywhere(grad_shapes),
+        + [pl.BlockSpec(memory_space=pltpu.HBM)] * (1 + len(pieces)),
+        out_specs=[fixed(o.shape) for o in outs] + anywhere(grad_shapes),
         scratch_shapes=[
             pltpu.VMEM(weights, BF16),
             pltpu.VMEM(weights, BF16),
-            pltpu.VMEM((length, width), F32),
-            pltpu.VMEM((length, width), BF16),
-            pltpu.VMEM((length, width), F32),
-            pltpu.VMEM((length, width), F32),
-            pltpu.VMEM((length, width), BF16),
             pltpu.VMEM((length, width), BF16),
             pltpu.SemaphoreType.DMA((4, 8)),
             pltpu.SemaphoreType.DMA((4, 8)),
-            pltpu.SemaphoreType.DMA,
-            pltpu.SemaphoreType.DMA((2, length // 256)),
             pltpu.SemaphoreType.DMA((length // 256,)),
         ],
-        compiler_params=params(44),
-        cost_estimate=cost(22),
+        compiler_params=params(36),
+        cost_estimate=cost(21),
         name="feed_forward",
-    )(second, rows, cotangent, residual, *pieces)
-
-
-def heads_kernel(branch_ref, weight_ref, heads_ref, grad_ref, output_grad_ref, mark):
+    )(second, rows, cotangent, *pieces)
+
+
+def heads_kernel(total_ref, back_ref, residual_ref, rows_ref, cotangent_ref, sums_in, weight_ref, heads_ref,
+                 result_ref, branch, sums_ref, grad_ref, output_grad_ref):
     slots = heads_ref.shape[0]
-    weight = weight_ref[...].reshape(slots * PAIR, weight_ref.shape[2])
-    grad = low(nt(branch_ref[...], weight))
-    output_grad = low(tn(branch_ref[...], jnp.concatenate([heads_ref[a] for a in range(slots)], axis=1)))
+    length, width = total_ref.shape
+    gain, bias = rows_ref[2:3, :], rows_ref[4:5, :]
+    gain_grad = jnp.zeros((1, width), F32)
+    shift_grad = jnp.zeros((1, width), F32)
+    outer = jnp.zeros((1, width), F32)
+    for rows in [slice(r, r + 256) for r in range(0, length, 256)]:
+        base = residual_ref[rows, :]
+        result_ref[rows, :] = low(base + total_ref[rows, :] + bias)
+        grad = back_ref[rows, :]
+        normal, rate = norm_parts(base)
+        upstream = cotangent_ref[rows, :].astype(F32)
+        gain_grad = gain_grad + jnp.sum(grad * normal, axis=0, keepdims=True)
+        shift_grad = shift_grad + jnp.sum(grad, axis=0, keepdims=True)
+        outer = outer + jnp.sum(upstream, axis=0, keepdims=True)
+        branch[rows, :] = low(upstream + norm_back(grad, normal, rate, gain))
+    sums_ref[...] = sums_in[...]
+    sums_ref[2:3, :] = gain_grad
+    sums_ref[3:4, :] = shift_grad
+    sums_ref[4:5, :] = outer
+    weight = weight_ref[...].reshape(slots * PAIR, width)
+    grad = low(nt(branch[...], weight))
+    heads = jnp.concatenate([heads_ref[a] for a in range(slots)], axis=1)
+    output_grad = low(tn(branch[...], heads))
     for a in range(slots):
         grad_ref[a] = grad[:, a * PAIR : (a + 1) * PAIR]
         output_grad_ref[a] = output_grad[:, a * PAIR : (a + 1) * PAIR]
-    mark[0] = 1.0
-
-
-def heads_back(branch, weights, heads):
-    slots = heads.shape[0]
-    length, width = branch.shape
+
+
+def heads_back(total, back, residual, rows, cotangent, sums, weights, heads):
+    slots, length, pair = heads.shape
+    width = total.shape[1]
     shape = jax.ShapeDtypeStruct
-    outs = [shape((slots, length, PAIR), BF16), shape((slots, width, PAIR), BF16)]
+    operands = [total, back, residual, rows, cotangent, sums]
+    outs = [
+        shape((length, width), BF16),
+        pltpu.HBM((length, width), BF16),
+        pltpu.HBM(sums.shape, F32),
+        pltpu.HBM((slots, length, pair), BF16),
+        pltpu.HBM((slots, width, pair), BF16),
+    ]
     return pl.pallas_call(
         heads_kernel,
         grid=(1,),
-        out_shape=outs + [MARK],
-        in_specs=[
-            fixed((length, width)),
-            pl.BlockSpec((slots, PAIR, width), lambda a: (0, width // PAIR, 0)),
-        ]
-        + [fixed(heads.shape)],
-        out_specs=[fixed(o.shape) for o in outs] + [mark_spec()],
-        compiler_params=params(16),
+        out_shape=outs,
+        in_specs=[fixed(o.shape) for o in operands]
+        + [pl.BlockSpec((slots, pair, width), lambda a: (0, width // pair, 0)), fixed(heads.shape)],
+        out_specs=[fixed(o.shape) for o in outs],
+        compiler_params=params(28),
         cost_estimate=cost(4),
         name="heads_back",
-    )(branch, weights, heads)
-
-
-def pair_grads(grad_ref, output_grad_ref, normed_ref, kept, backs, made):
-    attend_backward(grad_ref, kept, backs)
-    made[:, : 4 * PAIR] = low(tn(normed_ref[...], backs[...]))
-    made[:, 4 * PAIR :] = output_grad_ref[...]
+    )(*operands, weights, heads)
 
 
 def leave_copies(slot, made, outs, sems):
@@ -650,11 +624,11 @@
     return copies
 
 
-def back_kernel(waits, parts_out, slots, normed_ref, rows_ref, before_ref, tokens_hbm, residual_grad_hbm, *refs):
+def back_kernel(waits, parts_out, slots, rows_ref, before_ref, normed_hbm, tokens_hbm, residual_grad_hbm, *refs):
     refs = refs[waits:]
     weight, grad_ref, output_grad_ref, kept, refs = refs[0], refs[1], refs[2], refs[3:12], refs[12:]
-    input_grad_ref, sums_ref, outs, mark = refs[0], refs[1], refs[2 : 2 + parts_out], refs[2 + parts_out]
-    backs, made, total, tokens, residual_grad, vector_blocks, sems, out_sems = refs[3 + parts_out :]
+    input_grad_hbm, sums_ref, outs, mark = refs[0], refs[1], refs[2 : 2 + parts_out], refs[2 + parts_out]
+    (backs, made, total, input_grad_ref, normed_ref, tokens, residual_grad, vector_blocks, sems, out_sems, tile_sems) = refs[3 + parts_out :]
     length, width = normed_ref.shape
     devices = sums_ref.shape[0]
     share = width // devices
@@ -663,9 +637,11 @@
         pltpu.make_async_copy(tokens_hbm, tokens, sems.at[0]),
         pltpu.make_async_copy(residual_grad_hbm, residual_grad, sems.at[1]),
     ]
+    fetch = pltpu.make_async_copy(normed_hbm, normed_ref, tile_sems.at[length // 256])
 
     @pl.when(step == 0)
     def _():
+        fetch.start()
         for copy in copies:
             copy.start()
         total[...] = jnp.zeros_like(total)
@@ -678,7 +654,14 @@
         for copy in leave_copies(step - 2, made.at[parity], outs, out_sems.at[parity]):
             copy.wait()
 
-    pair_grads(grad_ref, output_grad_ref, normed_ref, kept, backs, made.at[parity])
+    attend_backward(grad_ref, kept, backs)
+
+    @pl.when(step == 0)
+    def _():
+        fetch.wait()
+
+    made[parity, :, : 4 * PAIR] = low(tn(normed_ref[...], backs[...]))
+    made[parity, :, 4 * PAIR :] = output_grad_ref[...]
     for copy in leave_copies(step, made.at[parity], outs, out_sems.at[parity]):
         copy.start()
     total[...] += nt(backs[...], weight[:width, :])
@@ -690,12 +673,19 @@
         gain = rows_ref[0:1, :]
         gain_grad = jnp.zeros((1, width), F32)
         shift_grad = jnp.zeros((1, width), F32)
+        left = []
         for rows in [slice(r, r + 256) for r in range(0, length, 256)]:
             grad = total[rows, :]
             normal, rate = norm_parts(tokens[rows, :].astype(F32))
             gain_grad = gain_grad + jnp.sum(grad * normal, axis=0, keepdims=True)
             shift_grad = shift_grad + jnp.sum(grad, axis=0, keepdims=True)
             input_grad_ref[rows, :] = low(residual_grad[rows, :].astype(F32) + norm_back(grad, normal, rate, gain))
+            left.append(
+                pltpu.make_async_copy(
+                    input_grad_ref.at[rows, :], input_grad_hbm.at[rows, :], tile_sems.at[rows.start // 256]
+                )
+            )
+            left[-1].start()
         small = [gain_grad, shift_grad] + [before_ref[i : i + 1, :] for i in range(2, 5)]
         sums_ref[:, :128] = collect(small, devices, share)
         sums_ref[:, 128:] = collect([before_ref[i : i + 1, :] for i in range(5, 9)], devices, share)
@@ -721,7 +711,7 @@
         for last in (steps - 2, steps - 1):
             for copy in leave_copies(last, made.at[last % 2], outs, out_sems.at[last % 2]):
                 copy.wait()
-        for copy in leaving:
+        for copy in leaving + left:
             copy.wait()
 
 
@@ -729,30 +719,32 @@
     length, width = normed.shape
     slots = members[0].shape[0]
     shape = jax.ShapeDtypeStruct
-    outs = [shape((length, width), BF16), shape((devices, 256), F32)]
+    outs = [pltpu.HBM((length, width), BF16), shape((devices, 256), F32)]
     grads = [shape(s, BF16) for s in grad_shapes]
-    large = [tokens, residual_grad]
+    large = [normed, tokens, residual_grad]
     return pl.pallas_call(
         functools.partial(back_kernel, len(waits), len(grad_shapes), slots),
         grid=(slots,),
         out_shape=outs + grads + [MARK],
-        in_specs=[fixed(o.shape) for o in (normed, rows, before)] + anywhere(large + waits) + by_step(members),
-        out_specs=[fixed(o.shape) for o in outs] + anywhere(grads) + [mark_spec()],
+        in_specs=[fixed(o.shape) for o in (rows, before)] + anywhere(large + waits) + by_step(members),
+        out_specs=[pl.BlockSpec(memory_space=pltpu.HBM), fixed(outs[1].shape)] + anywhere(grads) + [mark_spec()],
         scratch_shapes=[
             pltpu.VMEM((length, 4 * PAIR), BF16),
             pltpu.VMEM((2, width, 5 * PAIR), BF16),
             pltpu.VMEM((length, width), F32),
+            pltpu.VMEM((length, width), BF16),
         ]
         + [pltpu.VMEM((length, width), m.dtype) for m in large]
         + [
             pltpu.VMEM((8, 16, 5 * PAIR), BF16),
             pltpu.SemaphoreType.DMA((10,)),
             pltpu.SemaphoreType.DMA((2, 8)),
+            pltpu.SemaphoreType.DMA((length // 256 + 1,)),
         ],
         compiler_params=params(),
         cost_estimate=cost(27),
         name="attend_back",
-    )(normed, rows, before, *large, *waits, *members)
+    )(rows, before, *large, *waits, *members)
 
 
 def after(value, *others):
@@ -810,14 +802,36 @@
     return jnp.concatenate([high, low(values - high.astype(F32)), rest], axis=1)
 
 
-def join_kernel(chips, slots, ffn_ref, keep_ref, *refs):
-    others, ffn_outs, outs = refs[:chips], refs[chips : chips + slots], refs[chips + slots :]
+def halve_kernel(keep_ref, other_ref, out_ref):
+    out_ref[...] = low(add(keep_ref[...], other_ref[...]))
+
+
+def halve(keep, other):
+    return pl.pallas_call(
+        halve_kernel,
+        grid=(keep.shape[0],),
+        out_shape=pltpu.HBM(keep.shape, BF16),
+        in_specs=by_step([keep, other]),
+        out_specs=by_step([keep])[0],
+        compiler_params=params(44),
+        cost_estimate=cost(2),
+        name="halve",
+    )(keep, other)
+
+
+def join_kernel(chips, slots, ffn_ref, keep_hbm, *refs):
+    others, ffn_outs, outs = refs[:chips], refs[chips : chips + slots], refs[chips + slots : -2]
+    keep_ref, sems = refs[-2:]
+    copies = [pltpu.make_async_copy(keep_hbm.at[c], keep_ref.at[c], sems.at[c]) for c in range(chips)]
+    for copy in copies:
+        copy.start()
     z = lax.axis_index("head")
     for a, out in enumerate(ffn_outs):
         place = lax.rem(z + a, slots)
         out[...] = low(add(*[ffn_ref[c, pl.ds(place, 1)][0] for c in range(chips)]))
     body = keep_ref.shape[1] - 16
     for chip, out in enumerate(outs):
+        copies[chip].wait()
         out[:body, :] = low(add(keep_ref[chip, :body, :], others[chip][:body, :]))
         values = vector_values(keep_ref[chip, body:, :]) + vector_values(others[chip][body:, :])
         out[body:, :] = vector_rows(values, out.shape[1])
@@ -826,14 +840,15 @@
 def join(ffn, keep, others):
     shape = jax.ShapeDtypeStruct
     chips, slots = ffn.shape[:2]
-    operands = [ffn, keep, *others]
+    operands = [ffn, pltpu.with_memory_space_constraint(keep, pltpu.HBM), *others]
     outs = [shape(ffn.shape[2:], BF16)] * slots + [shape(keep.shape[1:], BF16)] * chips
     made = pl.pallas_call(
         functools.partial(join_kernel, chips, slots),
         grid=(1,),
         out_shape=outs,
-        in_specs=[fixed(o.shape) for o in operands],
+        in_specs=[fixed(ffn.shape), pl.BlockSpec(memory_space=pltpu.HBM)] + [fixed(o.shape) for o in others],
         out_specs=[fixed(o.shape) for o in outs],
+        scratch_shapes=[pltpu.VMEM(keep.shape, BF16), pltpu.SemaphoreType.DMA((chips,))],
         compiler_params=params(44),
         cost_estimate=cost(3),
         name="join",
@@ -1038,14 +1053,14 @@
     )
     if direct:
         ffn_pieces = over_cores(held[:-1] + [low(held[-1].astype(F32) * mark[0])], seqs)
-    result, branch, sums, *ffn_grads = feed_forward(
-        second, rows, cotangent, residual, ffn_pieces, ffn_shapes
-    )
-    heads_grad, output_grad, _ = heads_back(branch, weights, heads)
+    total, back, sums, *ffn_grads = feed_forward(second, rows, cotangent, ffn_pieces, ffn_shapes)
+    result, branch, sums, heads_grad, output_grad = heads_back(
+        total, back, residual, rows, cotangent, sums, weights, heads
+    )
     members = [weights, heads_grad, output_grad, *members]
     waits = []
     if direct:
-        ffn_mine = low(add(ffn_grads[0], to_mate(ffn_grads[1], seqs)))
+        ffn_mine = halve(ffn_grads[0], to_mate(ffn_grads[1], seqs))
         waits = [ffn_mine]
     input_grad, sums, *pair_grads, _ = backward(
         normed, rows, sums, inputs, branch, devices, waits, members, pair_shapes

time: 159 us -> 156 us (0.981)
  local copies, waits for them, and re-layouts: 9.35 us -> 4.87 us
  Pallas kernels: 66.6 us -> 70 us
  other arithmetic: 5.14 us -> 2.86 us
    unnamed x26 -> x14, local copies, waits for them, and re-layouts: 7.23 us -> 2.74 us
    pallas_call x1 -> x2, Pallas kernels: 1.29 us -> 5.68 us  [the longest x1 3.59 us: heads_back(): pl.pallas_call(heads_kernel, grid=(1,), out_shape=outs, in_specs=[fixed(o...]
    convert_element_type x2 -> x1, other arithmetic: 3.04 us -> 0.75 us  [low(): return v.astype(BF16)]
  transfers between devices with their start and end apart: 33 -> 33, of which waited for: 19 -> 19; matrix products, arithmetic and copies ran while one was open for 3% -> 3% of each run, Pallas kernels for 26% -> 28%
where the time goes in v8:
time: 156 us; the launch traced here: 155 us
  Pallas kernels  70 us (45%)
  starting transfers between devices  39.1 us (25%)
  waiting for transfers between devices  37.6 us (24%)
  local copies, waits for them, and re-layouts  4.87 us (3%)
  other arithmetic  2.86 us (2%)
    pallas_call x1, Pallas kernels, backward(): pl.pallas_call(functools.partial(back_kernel, len(waits), len(grad_shapes...  23.8 us
    pallas_call x1, Pallas kernels, feed_forward(): pl.pallas_call(functools.partial(ffn_kernel, len(pieces)), grid=(4,), out...  21.1 us
    ppermute x6, waiting for transfers between devices, over_chips(): lax.ppermute(shares, 'seq', flip(seqs, 2 * r))  16.9 us
    pallas_call x1, Pallas kernels, forward(): pl.pallas_call(functools.partial(forward_kernel, len(pieces), slots), gri...  14.8 us
    ppermute x3, waiting for transfers between devices, body(): lax.ppermute(ffn[a], 'head', turn(slots, a))  9.14 us
    ppermute x3, starting transfers between devices, body(): lax.ppermute(piece, 'head', turn(slots, a))  7.01 us
    ppermute x6, starting transfers between devices, over_chips(): lax.ppermute(shares, 'seq', flip(seqs, 2 * r))  6.98 us
    ppermute x3, starting transfers between devices, body(): lax.ppermute(m, 'head', turn(slots, slots - 1 - a))  5.62 us
  transfers between devices with their start and end apart: 33, of which 19 were waited for; matrix products, arithmetic and copies ran while one was open for 3% of the time, Pallas kernels for 28%

profile of v8, /device:TPU:0, one launch (start us, length us, event | category | flops | bytes accessed | tf_op | source)
XLA Modules:
  0.0 155.3 jit_solution(15324070296315240422)
XLA Ops:
  0.7 0.8 pad_add_fusion
  1.5 1.2 pad_maximum_fusion.own_ref
  2.8 3.1 %collective-permute-start.2 = (bf16[96,512]{1,0:T(8,128)(2,1)S(1)}, bf16[96,512]{1,0:T(8,128)(2,1)S(1)}, u32[]{:S(2)}, u32[]{:S(2)}) collective-permute-start(bf16[96,512]{1,0:T(8,128)(2,1)S(1)} %pad_maximum_fusion.2), channel_id=1, source_target_pairs={{0,1},{1,2},{2,3},{3,0},{4,5},{5,6},{6,7},{7,4},{8,9},{9,10},{10,1... | collective-permute-start | bytes 294920 | tf_op jit(solution)/shard_map/ppermute | solution.py:1033
  5.9 2.6 %collective-permute-start.1 = (bf16[96,512]{1,0:T(8,128)(2,1)S(1)}, bf16[96,512]{1,0:T(8,128)(2,1)S(1)}, u32[]{:S(2)}, u32[]{:S(2)}) collective-permute-start(bf16[96,512]{1,0:T(8,128)(2,1)S(1)} %pad_maximum_fusion.2), channel_id=1, source_target_pairs={{0,2},{1,3},{2,0},{3,1},{4,6},{5,7},{6,4},{7,5},{8,10},{9,11},{10,... | collective-permute-start | bytes 294920 | tf_op jit(solution)/shard_map/ppermute | solution.py:1033
  8.5 1.3 collective-permute-start
  9.8 1.2 reshape.39
  11.1 0.1 copy.34
  11.2 0.8 stack_reshape.7
  12.0 3.1 %collective-permute-done.1.refs_1_ = bf16[96,512]{1,0:T(8,128)(2,1)S(1)} collective-permute-done((bf16[96,512]{1,0:T(8,128)(2,1)S(1)}, bf16[96,512]{1,0:T(8,128)(2,1)S(1)}, u32[]{:S(2)}, u32[]{:S(2)}) %collective-permute-start.1) | collective-permute-done | bytes 98336 | tf_op jit(solution)/shard_map/ppermute | solution.py:1033
  15.1 0.8 join_near.1
  15.9 4.9 %all-to-all-start = ((bf16[4,8,16,512]{3,2,1,0:T(8,128)(2,1)}), bf16[4,8,16,512]{3,2,1,0:T(8,128)(2,1)S(1)}, u32[]{:S(2)}, u32[]{:S(2)}) async-start(bf16[4,8,16,512]{3,2,1,0:T(8,128)(2,1)} %get-tuple-element.79), calls=%async_computation | async-start | bytes 1048576 | tf_op jit(solution)/shard_map/all_to_all | solution.py:1036
  20.8 2.4 %collective-permute-start.8 = (bf16[256,512]{1,0:T(8,128)(2,1)S(1)}, bf16[256,512]{1,0:T(8,128)(2,1)}, u32[]{:S(2)}, u32[]{:S(2)}) collective-permute-start(bf16[256,512]{1,0:T(8,128)(2,1)S(1)} %get-tuple-element.76.refs_0_), channel_id=1, source_target_pairs={{0,24},{4,28},{8,16},{12,20},{16,8},{20,12},{24,0},{28,4},{1,25},{... | collective-permute-start | bytes 786440 | tf_op jit(solution)/shard_map/ppermute | solution.py:970
  23.3 0.5 collective-permute-start.6
  23.8 0.5 collective-permute-start.4
  24.3 6.8 %collective-permute-done.8.refs_6_ = bf16[256,512]{1,0:T(8,128)(2,1)} collective-permute-done((bf16[256,512]{1,0:T(8,128)(2,1)S(1)}, bf16[256,512]{1,0:T(8,128)(2,1)}, u32[]{:S(2)}, u32[]{:S(2)}) %collective-permute-start.8) | collective-permute-done | bytes 262176 | tf_op jit(solution)/shard_map/ppermute | solution.py:970
  31.1 3.2 %collective-permute-done.6.refs_4_ = bf16[256,512]{1,0:T(8,128)(2,1)} collective-permute-done((bf16[256,512]{1,0:T(8,128)(2,1)S(1)}, bf16[256,512]{1,0:T(8,128)(2,1)}, u32[]{:S(2)}, u32[]{:S(2)}) %collective-permute-start.6) | collective-permute-done | bytes 262176 | tf_op jit(solution)/shard_map/ppermute | solution.py:970
  34.3 0.1 collective-permute-done.4.refs_2_
  34.4 0.4 collective-permute-start.5
  34.8 2.0 %collective-permute-start.15 = (bf16[4,8,16,512]{3,2,1,0:T(8,128)(2,1)S(1)}, bf16[4,8,16,512]{3,2,1,0:T(8,128)(2,1)S(1)}, u32[]{:S(2)}, u32[]{:S(2)}) collective-permute-start(bf16[4,8,16,512]{3,2,1,0:T(8,128)(2,1)S(1)} %all-to-all-done.refs_0_), channel_id=1, source_target_pairs={{0,24},{4,28},{8,16},{12,20},{16,8},{20,12},{24,0},{28,4},{1,25},{... | collective-permute-start | bytes 1572872 | tf_op jit(solution)/shard_map/ppermute | solution.py:970
  36.9 0.9 collective-permute-start.13
  37.8 0.5 collective-permute-start.11
  38.3 14.8 %attend_forward.1 = (bf16[1024,512]{1,0:T(8,128)(2,1)S(1)}, f32[16,512]{1,0:T(8,128)S(1)}, f32[1024,512]{1,0:T(8,128)S(1)}, bf16[1024,512]{1,0:T(8,128)(2,1)S(1)...) custom-call(bf16[1024,512]{1,0:T(8,128)(2,1)S(1)} %copy-done.1, ...), custom_call_target="tpu_custom_call" | custom-call | flops 16999999488 | bytes 17000000 | tf_op jit(solution)/shard_map/attend_forward/pallas_call | solution.py:395
  53.2 1.0 copy-done.4
  54.2 6.7 %collective-permute-done.13.refs_4_ = bf16[4,8,16,512]{3,2,1,0:T(8,128)(2,1)S(1)} collective-permute-done((bf16[4,8,16,512]{3,2,1,0:T(8,128)(2,1)S(1)}, bf16[4,8,16,512]{3,2,1,0:T(8,128)(2,1)S(1)}, u32[]{:S(2)}, u32[]{:S(2)}) %collective-permute-start.13) | collective-permute-done | bytes 524320 | tf_op jit(solution)/shard_map/ppermute | solution.py:970
  61.0 0.4 collective-permute-start.12
  61.4 0.8 multiply_convert_fusion.refs_6_
  62.2 0.1 collective-permute-start.16
  62.3 0.5 collective-permute-done.14.refs_5_
  62.8 0.7 collective-permute-done.12.refs_3_
  63.6 0.7 collective-permute-done.16.refs_7_
  64.3 21.1 %feed_forward.1 = (f32[1024,512]{1,0:T(8,128)S(1)}, f32[1024,512]{1,0:T(8,128)S(1)}, f32[16,512]{1,0:T(8,128)S(1)}, bf16[4,4,4,2,16,512]{5,4,3,2,1,0:T(8,128)(2,1)S(1)}, bf16[4,4,4,2,16,512]{5,4,3,2,1,0:T(8,128)(2,1)S(1)}) custom-call(bf16[1024,512]{1,0:T(8,128)(2,1)S(1)} %get-tuple-element.77.second_ref, f32[16,512]{1,0:T(8,128)S(1)} %get-tuple-element.78.rows_ref, ...), custom_call_target="tpu_custom_call" | custom-call | flops 20999999488 | bytes 21000000 | tf_op jit(solution)/shard_map/feed_forward/pallas_call | solution.py:530
  85.5 0.2 collective-permute-start.17
  85.7 3.6 %heads_back.1 = (bf16[1024,512]{1,0:T(8,128)(2,1)}, bf16[1024,512]{1,0:T(8,128)(2,1)}, f32[16,512]{1,0:T(8,128)}, bf16[4,1024,128]{2,1,0:T(8,128)(2,1)}, bf16[4,512,128]{2,1,0:T(8,128)(2,1)}) custom-call(f32[1024,512]{1,0:T(8,128)S(1)} %get-tuple-element.81.total_ref, f32[1024,512]{1,0:T(8,128)S(1)} %get-tuple-element.82.back_ref, ...), custom_call_target="tpu_custom_call" | custom-call | flops 4000000000 | bytes 4000000 | tf_op jit(solution)/shard_map/heads_back/pallas_call | solution.py:594
  89.3 0.4 collective-permute-done.17.other_ref
  89.7 2.1 %halve.1.refs_0_ = bf16[4,4,4,2,16,512]{5,4,3,2,1,0:T(8,128)(2,1)} custom-call(bf16[4,4,4,2,16,512]{5,4,3,2,1,0:T(8,128)(2,1)S(1)} %get-tuple-element.91.keep_ref, bf16[4,4,4,2,16,512]{5,4,3,2,1,0:T(8,128)(2,1)S(1)} %collective-permute-done.17.other_ref), custom_call_target="tpu_custom_call" | custom-call | flops 2000000000 | bytes 2000000 | tf_op jit(solution)/shard_map/halve/pallas_call | solution.py:810
  91.8 3.6 %all-to-all-start.1 = ((bf16[4,4,4,2,16,512]{5,4,3,2,1,0:T(8,128)(2,1)}), bf16[4,4,4,2,16,512]{5,4,3,2,1,0:T(8,128)(2,1)S(1)}, u32[]{:S(2)}, u32[]{:S(2)}) async-start(bf16[4,4,4,2,16,512]{5,4,3,2,1,0:T(8,128)(2,1)} %halve.1.refs_0_), calls=%async_computation.1 | async-start | bytes 4194304 | tf_op jit(solution)/shard_map/all_to_all | solution.py:979
  95.4 23.8 %attend_back.1 = (bf16[1024,512]{1,0:T(8,128)(2,1)}, f32[32,256]{1,0:T(8,128)}, bf16[4,272,640]{2,1,0:T(8,128)(2,1)}, bf16[272,640]{1,0:T(8,128)(2,1)}, bf16[272...) custom-call(f32[16,512]{1,0:T(8,128)} %copy-done.3, ...), custom_call_target="tpu_custom_call" | custom-call | flops 27000000512 | bytes 27000000 | tf_op jit(solution)/shard_map/attend_back/pallas_call | solution.py:725
  119.2 0.2 collective-permute-start.18
  119.4 0.4 collective-permute-start.19
  119.8 0.1 collective-permute-start.20
  119.9 0.4 collective-permute-start.21
  120.3 0.8 collective-permute-done.18.refs_0_
  121.1 0.5 collective-permute-done.19.refs_1_
  121.6 0.5 collective-permute-done.20.refs_2_
  122.1 0.5 collective-permute-done.21.refs_3_
  122.6 1.4 join.1
  124.1 2.0 %collective-permute-start.22 = (bf16[272,640]{1,0:T(8,128)(2,1)S(1)}, bf16[272,640]{1,0:T(8,128)(2,1)S(1)}, u32[]{:S(2)}, u32[]{:S(2)}) collective-permute-start(bf16[272,640]{1,0:T(8,128)(2,1)S(1)} %get-tuple-element.111), channel_id=1, source_target_pairs={{0,8},{4,12},{8,0},{12,4},{16,24},{20,28},{24,16},{28,20},{1,9},{5... | collective-permute-start | bytes 1044488 | tf_op jit(solution)/shard_map/ppermute | solution.py:983
  126.1 1.5 collective-permute-start.23
  127.6 2.6 %collective-permute-start.25 = (bf16[4,2,16,512]{3,2,1,0:T(8,128)(2,1)S(1)}, bf16[4,2,16,512]{3,2,1,0:T(8,128)(2,1)S(1)}, u32[]{:S(2)}, u32[]{:S(2)}) collective-permute-start(bf16[4,2,16,512]{3,2,1,0:T(8,128)(2,1)S(1)} %get-tuple-element.114), channel_id=1, source_target_pairs={{0,1},{1,2},{2,3},{3,0},{4,5},{5,6},{6,7},{7,4},{8,9},{9,10},{10,1... | collective-permute-start | bytes 393224 | tf_op jit(solution)/shard_map/ppermute | solution.py:1072
  130.2 1.6 %collective-permute-start.26 = (bf16[4,2,16,512]{3,2,1,0:T(8,128)(2,1)S(1)}, bf16[4,2,16,512]{3,2,1,0:T(8,128)(2,1)S(1)}, u32[]{:S(2)}, u32[]{:S(2)}) collective-permute-start(bf16[4,2,16,512]{3,2,1,0:T(8,128)(2,1)S(1)} %get-tuple-element.115), channel_id=1, source_target_pairs={{0,2},{1,3},{2,0},{3,1},{4,6},{5,7},{6,4},{7,5},{8,10},{9,11},{10,... | collective-permute-start | bytes 393224 | tf_op jit(solution)/shard_map/ppermute | solution.py:1072
  131.7 4.1 %collective-permute-done.25.refs_4_.refs_1_ = bf16[4,2,16,512]{3,2,1,0:T(8,128)(2,1)S(1)} collective-permute-done((bf16[4,2,16,512]{3,2,1,0:T(8,128)(2,1)S(1)}, bf16[4,2,16,512]{3,2,1,0:T(8,128)(2,1)S(1)}, u32[]{:S(2)}, u32[]{:S(2)}) %collective-permute-start.25) | collective-permute-done | bytes 131104 | tf_op jit(solution)/shard_map/ppermute | solution.py:1072
  135.9 1.0 collective-permute-start.27
  136.9 3.2 %collective-permute-done.26.refs_5_.refs_2_ = bf16[4,2,16,512]{3,2,1,0:T(8,128)(2,1)S(1)} collective-permute-done((bf16[4,2,16,512]{3,2,1,0:T(8,128)(2,1)S(1)}, bf16[4,2,16,512]{3,2,1,0:T(8,128)(2,1)S(1)}, u32[]{:S(2)}, u32[]{:S(2)}) %collective-permute-start.26) | collective-permute-done | bytes 131104 | tf_op jit(solution)/shard_map/ppermute | solution.py:1072
  140.1 1.8 %collective-permute-done.27.refs_6_.refs_3_ = bf16[4,2,16,512]{3,2,1,0:T(8,128)(2,1)S(1)} collective-permute-done((bf16[4,2,16,512]{3,2,1,0:T(8,128)(2,1)S(1)}, bf16[4,2,16,512]{3,2,1,0:T(8,128)(2,1)S(1)}, u32[]{:S(2)}, u32[]{:S(2)}) %collective-permute-start.27) | collective-permute-done | bytes 131104 | tf_op jit(solution)/shard_map/ppermute | solution.py:1072
  141.9 1.5 collective-permute-done.23.refs_2_
  143.5 0.6 sum_plane.1
  144.0 2.6 %collective-permute-start.28 = (bf16[80,640]{1,0:T(8,128)(2,1)S(1)}, bf16[80,640]{1,0:T(8,128)(2,1)S(1)}, u32[]{:S(2)}, u32[]{:S(2)}) collective-permute-start(bf16[80,640]{1,0:T(8,128)(2,1)S(1)} %get-tuple-element.119), channel_id=1, source_target_pairs={{0,1},{1,2},{2,3},{3,0},{4,5},{5,6},{6,7},{7,4},{8,9},{9,10},{10,1... | collective-permute-start | bytes 307208 | tf_op jit(solution)/shard_map/ppermute | solution.py:1076
  146.6 1.6 %collective-permute-start.29 = (bf16[80,640]{1,0:T(8,128)(2,1)S(1)}, bf16[80,640]{1,0:T(8,128)(2,1)S(1)}, u32[]{:S(2)}, u32[]{:S(2)}) collective-permute-start(bf16[80,640]{1,0:T(8,128)(2,1)S(1)} %get-tuple-element.120), channel_id=1, source_target_pairs={{0,2},{1,3},{2,0},{3,1},{4,6},{5,7},{6,4},{7,5},{8,10},{9,11},{10,... | collective-permute-start | bytes 307208 | tf_op jit(solution)/shard_map/ppermute | solution.py:1076
  148.2 1.5 collective-permute-start.30
  149.7 1.0 settle.1
  150.7 0.8 copy.36
  151.5 1.0 copy.37
  152.5 2.2 %collective-permute-done.29.refs_1_ = bf16[80,640]{1,0:T(8,128)(2,1)S(1)} collective-permute-done((bf16[80,640]{1,0:T(8,128)(2,1)S(1)}, bf16[80,640]{1,0:T(8,128)(2,1)S(1)}, u32[]{:S(2)}, u32[]{:S(2)}) %collective-permute-start.29) | collective-permute-done | bytes 102432 | tf_op jit(solution)/shard_map/ppermute | solution.py:1076
  154.7 0.7 finish.1
  (38 shorter events, 0.3 us)
Async XLA Ops:
  0.6 11.3 %copy-start.5 = (bf16[512,64]{0,1:T(8,128)(2,1)S(1)}, bf16[512,64]{0,1:T(8,128)(2,1)}, u32[]{:S(2)}) copy-start(bf16[512,64]{0,1:T(8,128)(2,1)} %param.25) | copy-start | bytes 196612
  2.8 9.2 %collective-permute-start.2 = (bf16[96,512]{1,0:T(8,128)(2,1)S(1)}, bf16[96,512]{1,0:T(8,128)(2,1)S(1)}, u32[]{:S(2)}, u32[]{:S(2)}) collective-permute-start(bf16[96,512]{1,0:T(8,128)(2,1)S(1)} %pad_maximum_fusion.2), channel_id=1, source_target_pairs={{0,1},{1,2},{2,3},{3,0},{4,5},{5,6},{6,7},{7,4},{8,9},{9,10},{10,1... | collective-permute-start | bytes 294920 | tf_op jit(solution)/shard_map/ppermute | solution.py:1033
  5.9 9.2 %collective-permute-start.1 = (bf16[96,512]{1,0:T(8,128)(2,1)S(1)}, bf16[96,512]{1,0:T(8,128)(2,1)S(1)}, u32[]{:S(2)}, u32[]{:S(2)}) collective-permute-start(bf16[96,512]{1,0:T(8,128)(2,1)S(1)} %pad_maximum_fusion.2), channel_id=1, source_target_pairs={{0,2},{1,3},{2,0},{3,1},{4,6},{5,7},{6,4},{7,5},{8,10},{9,11},{10,... | collective-permute-start | bytes 294920 | tf_op jit(solution)/shard_map/ppermute | solution.py:1033
  8.5 6.6 %collective-permute-start = (bf16[96,512]{1,0:T(8,128)(2,1)S(1)}, bf16[96,512]{1,0:T(8,128)(2,1)S(1)}, u32[]{:S(2)}, u32[]{:S(2)}) collective-permute-start(bf16[96,512]{1,0:T(8,128)(2,1)S(1)} %pad_maximum_fusion.2), channel_id=1, source_target_pairs={{0,3},{1,0},{2,1},{3,2},{4,7},{5,4},{6,5},{7,6},{8,11},{9,8},{10,9... | collective-permute-start | bytes 294920 | tf_op jit(solution)/shard_map/ppermute | solution.py:1033
  15.1 23.2 %copy-start.1 = (bf16[1024,512]{1,0:T(8,128)(2,1)S(1)}, bf16[1024,512]{1,0:T(8,128)(2,1)}, u32[]{:S(2)}) copy-start(bf16[1024,512]{1,0:T(8,128)(2,1)} %tokens_hbm.1) | copy-start | bytes 3145732
  15.9 18.9 %all-to-all-start = ((bf16[4,8,16,512]{3,2,1,0:T(8,128)(2,1)}), bf16[4,8,16,512]{3,2,1,0:T(8,128)(2,1)S(1)}, u32[]{:S(2)}, u32[]{:S(2)}) async-start(bf16[4,8,16,512]{3,2,1,0:T(8,128)(2,1)} %get-tuple-element.79), calls=%async_computation | async-start | bytes 1048576 | tf_op jit(solution)/shard_map/all_to_all | solution.py:1036
  20.8 43.5 %copy-start = (bf16[1024,512]{1,0:T(8,128)(2,1)S(1)}, bf16[1024,512]{1,0:T(8,128)(2,1)}, u32[]{:S(2)}) copy-start(bf16[1024,512]{1,0:T(8,128)(2,1)} %cotangent_ref.1) | copy-start | bytes 3145732
  20.8 10.3 %collective-permute-start.8 = (bf16[256,512]{1,0:T(8,128)(2,1)S(1)}, bf16[256,512]{1,0:T(8,128)(2,1)}, u32[]{:S(2)}, u32[]{:S(2)}) collective-permute-start(bf16[256,512]{1,0:T(8,128)(2,1)S(1)} %get-tuple-element.76.refs_0_), channel_id=1, source_target_pairs={{0,24},{4,28},{8,16},{12,20},{16,8},{20,12},{24,0},{28,4},{1,25},{... | collective-permute-start | bytes 786440 | tf_op jit(solution)/shard_map/ppermute | solution.py:970
  23.3 11.1 %collective-permute-start.6 = (bf16[256,512]{1,0:T(8,128)(2,1)S(1)}, bf16[256,512]{1,0:T(8,128)(2,1)}, u32[]{:S(2)}, u32[]{:S(2)}) collective-permute-start(bf16[256,512]{1,0:T(8,128)(2,1)S(1)} %get-tuple-element.76.refs_0_), channel_id=1, source_target_pairs={{0,16},{4,20},{8,24},{12,28},{16,0},{20,4},{24,8},{28,12},{1,17},{... | collective-permute-start | bytes 786440 | tf_op jit(solution)/shard_map/ppermute | solution.py:970
  23.8 10.7 %collective-permute-start.4 = (bf16[256,512]{1,0:T(8,128)(2,1)S(1)}, bf16[256,512]{1,0:T(8,128)(2,1)}, u32[]{:S(2)}, u32[]{:S(2)}) collective-permute-start(bf16[256,512]{1,0:T(8,128)(2,1)S(1)} %get-tuple-element.76.refs_0_), channel_id=1, source_target_pairs={{0,8},{4,12},{8,0},{12,4},{16,24},{20,28},{24,16},{28,20},{1,9},{5... | collective-permute-start | bytes 786440 | tf_op jit(solution)/shard_map/ppermute | solution.py:970
  24.3 12.6 %collective-permute-start.3 = (bf16[256,512]{1,0:T(8,128)(2,1)S(1)}, bf16[256,512]{1,0:T(8,128)(2,1)}, u32[]{:S(2)}, u32[]{:S(2)}) collective-permute-start(bf16[256,512]{1,0:T(8,128)(2,1)S(1)} %get-tuple-element.76.refs_0_), channel_id=1, source_target_pairs={{0,4},{4,0},{8,12},{12,8},{16,20},{20,16},{24,28},{28,24},{1,5},{5... | collective-permute-start | bytes 786440 | tf_op jit(solution)/shard_map/ppermute | solution.py:966
  31.1 6.7 %collective-permute-start.9 = (bf16[256,512]{1,0:T(8,128)(2,1)}, bf16[256,512]{1,0:T(8,128)(2,1)}, u32[]{:S(2)}, u32[]{:S(2)}) collective-permute-start(bf16[256,512]{1,0:T(8,128)(2,1)} %collective-permute-done.8.refs_6_), channel_id=1, source_target_pairs={{0,4},{4,0},{8,12},{12,8},{16,20},{20,16},{24,28},{28,24},{1,5},{5... | collective-permute-start | bytes 786440 | tf_op jit(solution)/shard_map/ppermute | solution.py:966
  34.3 4.0 %collective-permute-start.7 = (bf16[256,512]{1,0:T(8,128)(2,1)}, bf16[256,512]{1,0:T(8,128)(2,1)}, u32[]{:S(2)}, u32[]{:S(2)}) collective-permute-start(bf16[256,512]{1,0:T(8,128)(2,1)} %collective-permute-done.6.refs_4_), channel_id=1, source_target_pairs={{0,4},{4,0},{8,12},{12,8},{16,20},{20,16},{24,28},{28,24},{1,5},{5... | collective-permute-start | bytes 786440 | tf_op jit(solution)/shard_map/ppermute | solution.py:966
  34.4 3.9 %collective-permute-start.5 = (bf16[256,512]{1,0:T(8,128)(2,1)}, bf16[256,512]{1,0:T(8,128)(2,1)}, u32[]{:S(2)}, u32[]{:S(2)}) collective-permute-start(bf16[256,512]{1,0:T(8,128)(2,1)} %collective-permute-done.4.refs_2_), channel_id=1, source_target_pairs={{0,4},{4,0},{8,12},{12,8},{16,20},{20,16},{24,28},{28,24},{1,5},{5... | collective-permute-start | bytes 786440 | tf_op jit(solution)/shard_map/ppermute | solution.py:966
  34.8 26.6 %collective-permute-start.15 = (bf16[4,8,16,512]{3,2,1,0:T(8,128)(2,1)S(1)}, bf16[4,8,16,512]{3,2,1,0:T(8,128)(2,1)S(1)}, u32[]{:S(2)}, u32[]{:S(2)}) collective-permute-start(bf16[4,8,16,512]{3,2,1,0:T(8,128)(2,1)S(1)} %all-to-all-done.refs_0_), channel_id=1, source_target_pairs={{0,24},{4,28},{8,16},{12,20},{16,8},{20,12},{24,0},{28,4},{1,25},{... | collective-permute-start | bytes 1572872 | tf_op jit(solution)/shard_map/ppermute | solution.py:970
  36.9 24.0 %collective-permute-start.13 = (bf16[4,8,16,512]{3,2,1,0:T(8,128)(2,1)S(1)}, bf16[4,8,16,512]{3,2,1,0:T(8,128)(2,1)S(1)}, u32[]{:S(2)}, u32[]{:S(2)}) collective-permute-start(bf16[4,8,16,512]{3,2,1,0:T(8,128)(2,1)S(1)} %all-to-all-done.refs_0_), channel_id=1, source_target_pairs={{0,16},{4,20},{8,24},{12,28},{16,0},{20,4},{24,8},{28,12},{1,17},{... | collective-permute-start | bytes 1572872 | tf_op jit(solution)/shard_map/ppermute | solution.py:970
  37.8 23.2 %collective-permute-start.11 = (bf16[4,8,16,512]{3,2,1,0:T(8,128)(2,1)S(1)}, bf16[4,8,16,512]{3,2,1,0:T(8,128)(2,1)S(1)}, u32[]{:S(2)}, u32[]{:S(2)}) collective-permute-start(bf16[4,8,16,512]{3,2,1,0:T(8,128)(2,1)S(1)} %all-to-all-done.refs_0_), channel_id=1, source_target_pairs={{0,8},{4,12},{8,0},{12,4},{16,24},{20,28},{24,16},{28,20},{1,9},{5... | collective-permute-start | bytes 1572872 | tf_op jit(solution)/shard_map/ppermute | solution.py:970
  53.2 1.0 copy-start.4
  54.2 31.5 %copy-start.3 = (f32[16,512]{1,0:T(8,128)}, f32[16,512]{1,0:T(8,128)S(1)}, u32[]{:S(2)}) copy-start(f32[16,512]{1,0:T(8,128)S(1)} %get-tuple-element.78.rows_ref) | copy-start | bytes 98308
  54.2 8.1 %collective-permute-start.10 = (bf16[4,8,16,512]{3,2,1,0:T(8,128)(2,1)S(1)}, bf16[4,8,16,512]{3,2,1,0:T(8,128)(2,1)S(1)}, u32[]{:S(2)}, u32[]{:S(2)}) collective-permute-start(bf16[4,8,16,512]{3,2,1,0:T(8,128)(2,1)S(1)} %all-to-all-done.refs_0_), channel_id=1, source_target_pairs={{0,4},{4,0},{8,12},{12,8},{16,20},{20,16},{24,28},{28,24},{1,5},{5... | collective-permute-start | bytes 1572872 | tf_op jit(solution)/shard_map/ppermute | solution.py:966
  60.9 1.9 %collective-permute-start.14 = (bf16[4,8,16,512]{3,2,1,0:T(8,128)(2,1)S(1)}, bf16[4,8,16,512]{3,2,1,0:T(8,128)(2,1)S(1)}, u32[]{:S(2)}, u32[]{:S(2)}) collective-permute-start(bf16[4,8,16,512]{3,2,1,0:T(8,128)(2,1)S(1)} %collective-permute-done.13.refs_4_), channel_id=1, source_target_pairs={{0,4},{4,0},{8,12},{12,8},{16,20},{20,16},{24,28},{28,24},{1,5},{5... | collective-permute-start | bytes 1572872 | tf_op jit(solution)/shard_map/ppermute | solution.py:966
  61.0 2.6 %collective-permute-start.12 = (bf16[4,8,16,512]{3,2,1,0:T(8,128)(2,1)S(1)}, bf16[4,8,16,512]{3,2,1,0:T(8,128)(2,1)S(1)}, u32[]{:S(2)}, u32[]{:S(2)}) collective-permute-start(bf16[4,8,16,512]{3,2,1,0:T(8,128)(2,1)S(1)} %collective-permute-done.11.refs_2_), channel_id=1, source_target_pairs={{0,4},{4,0},{8,12},{12,8},{16,20},{20,16},{24,28},{28,24},{1,5},{5... | collective-permute-start | bytes 1572872 | tf_op jit(solution)/shard_map/ppermute | solution.py:966
  62.2 2.1 %collective-permute-start.16 = (bf16[4,8,16,512]{3,2,1,0:T(8,128)(2,1)S(1)}, bf16[4,8,16,512]{3,2,1,0:T(8,128)(2,1)S(1)}, u32[]{:S(2)}, u32[]{:S(2)}) collective-permute-start(bf16[4,8,16,512]{3,2,1,0:T(8,128)(2,1)S(1)} %multiply_convert_fusion.refs_6_), channel_id=1, source_target_pairs={{0,4},{4,0},{8,12},{12,8},{16,20},{20,16},{24,28},{28,24},{1,5},{5... | collective-permute-start | bytes 1572872 | tf_op jit(solution)/shard_map/ppermute | solution.py:966
  64.3 21.4 %copy-start.2 = (bf16[4,640,512]{2,1,0:T(8,128)(2,1)S(1)}, bf16[4,640,512]{2,1,0:T(8,128)(2,1)}, u32[]{:S(2)}) copy-start(bf16[4,640,512]{2,1,0:T(8,128)(2,1)} %get-tuple-element.85.weight_ref.refs_1_) | copy-start | bytes 7864324
  85.5 4.2 %collective-permute-start.17 = (bf16[4,4,4,2,16,512]{5,4,3,2,1,0:T(8,128)(2,1)S(1)}, bf16[4,4,4,2,16,512]{5,4,3,2,1,0:T(8,128)(2,1)S(1)}, u32[]{:S(2)}, u32[]{:S(2)}) collective-permute-start(bf16[4,4,4,2,16,512]{5,4,3,2,1,0:T(8,128)(2,1)S(1)} %get-tuple-element.92), channel_id=1, source_target_pairs={{0,4},{4,0},{8,12},{12,8},{16,20},{20,16},{24,28},{28,24},{1,5},{5... | collective-permute-start | bytes 6291464 | tf_op jit(solution)/shard_map/ppermute | solution.py:966
  91.8 30.8 %all-to-all-start.1 = ((bf16[4,4,4,2,16,512]{5,4,3,2,1,0:T(8,128)(2,1)}), bf16[4,4,4,2,16,512]{5,4,3,2,1,0:T(8,128)(2,1)S(1)}, u32[]{:S(2)}, u32[]{:S(2)}) async-start(bf16[4,4,4,2,16,512]{5,4,3,2,1,0:T(8,128)(2,1)} %halve.1.refs_0_), calls=%async_computation.1 | async-start | bytes 4194304 | tf_op jit(solution)/shard_map/all_to_all | solution.py:979
  119.2 1.9 %collective-permute-start.18 = (bf16[272,640]{1,0:T(8,128)(2,1)}, bf16[272,640]{1,0:T(8,128)(2,1)S(1)}, u32[]{:S(2)}, u32[]{:S(2)}) collective-permute-start(bf16[272,640]{1,0:T(8,128)(2,1)} %get-tuple-element.106), channel_id=1, source_target_pairs={{0,4},{4,0},{8,12},{12,8},{16,20},{20,16},{24,28},{28,24},{1,5},{5... | collective-permute-start | bytes 1044488 | tf_op jit(solution)/shard_map/ppermute | solution.py:966
  119.4 2.2 %collective-permute-start.19 = (bf16[272,640]{1,0:T(8,128)(2,1)}, bf16[272,640]{1,0:T(8,128)(2,1)S(1)}, u32[]{:S(2)}, u32[]{:S(2)}) collective-permute-start(bf16[272,640]{1,0:T(8,128)(2,1)} %get-tuple-element.107), channel_id=1, source_target_pairs={{0,4},{4,0},{8,12},{12,8},{16,20},{20,16},{24,28},{28,24},{1,5},{5... | collective-permute-start | bytes 1044488 | tf_op jit(solution)/shard_map/ppermute | solution.py:966
  119.8 2.4 %collective-permute-start.20 = (bf16[272,640]{1,0:T(8,128)(2,1)}, bf16[272,640]{1,0:T(8,128)(2,1)S(1)}, u32[]{:S(2)}, u32[]{:S(2)}) collective-permute-start(bf16[272,640]{1,0:T(8,128)(2,1)} %get-tuple-element.108), channel_id=1, source_target_pairs={{0,4},{4,0},{8,12},{12,8},{16,20},{20,16},{24,28},{28,24},{1,5},{5... | collective-permute-start | bytes 1044488 | tf_op jit(solution)/shard_map/ppermute | solution.py:966
  119.9 2.7 %collective-permute-start.21 = (bf16[272,640]{1,0:T(8,128)(2,1)}, bf16[272,640]{1,0:T(8,128)(2,1)S(1)}, u32[]{:S(2)}, u32[]{:S(2)}) collective-permute-start(bf16[272,640]{1,0:T(8,128)(2,1)} %get-tuple-element.109), channel_id=1, source_target_pairs={{0,4},{4,0},{8,12},{12,8},{16,20},{20,16},{24,28},{28,24},{1,5},{5... | collective-permute-start | bytes 1044488 | tf_op jit(solution)/shard_map/ppermute | solution.py:966
  124.1 17.9 %collective-permute-start.22 = (bf16[272,640]{1,0:T(8,128)(2,1)S(1)}, bf16[272,640]{1,0:T(8,128)(2,1)S(1)}, u32[]{:S(2)}, u32[]{:S(2)}) collective-permute-start(bf16[272,640]{1,0:T(8,128)(2,1)S(1)} %get-tuple-element.111), channel_id=1, source_target_pairs={{0,8},{4,12},{8,0},{12,4},{16,24},{20,28},{24,16},{28,20},{1,9},{5... | collective-permute-start | bytes 1044488 | tf_op jit(solution)/shard_map/ppermute | solution.py:983
  126.1 17.4 %collective-permute-start.23 = (bf16[272,640]{1,0:T(8,128)(2,1)S(1)}, bf16[272,640]{1,0:T(8,128)(2,1)S(1)}, u32[]{:S(2)}, u32[]{:S(2)}) collective-permute-start(bf16[272,640]{1,0:T(8,128)(2,1)S(1)} %get-tuple-element.112), channel_id=1, source_target_pairs={{0,16},{4,20},{8,24},{12,28},{16,0},{20,4},{24,8},{28,12},{1,17},{... | collective-permute-start | bytes 1044488 | tf_op jit(solution)/shard_map/ppermute | solution.py:983
  127.6 15.9 %collective-permute-start.24 = (bf16[272,640]{1,0:T(8,128)(2,1)S(1)}, bf16[272,640]{1,0:T(8,128)(2,1)S(1)}, u32[]{:S(2)}, u32[]{:S(2)}) collective-permute-start(bf16[272,640]{1,0:T(8,128)(2,1)S(1)} %get-tuple-element.113), channel_id=1, source_target_pairs={{0,24},{4,28},{8,16},{12,20},{16,8},{20,12},{24,0},{28,4},{1,25},{... | collective-permute-start | bytes 1044488 | tf_op jit(solution)/shard_map/ppermute | solution.py:983
  127.6 8.2 %collective-permute-start.25 = (bf16[4,2,16,512]{3,2,1,0:T(8,128)(2,1)S(1)}, bf16[4,2,16,512]{3,2,1,0:T(8,128)(2,1)S(1)}, u32[]{:S(2)}, u32[]{:S(2)}) collective-permute-start(bf16[4,2,16,512]{3,2,1,0:T(8,128)(2,1)S(1)} %get-tuple-element.114), channel_id=1, source_target_pairs={{0,1},{1,2},{2,3},{3,0},{4,5},{5,6},{6,7},{7,4},{8,9},{9,10},{10,1... | collective-permute-start | bytes 393224 | tf_op jit(solution)/shard_map/ppermute | solution.py:1072
  130.2 9.9 %collective-permute-start.26 = (bf16[4,2,16,512]{3,2,1,0:T(8,128)(2,1)S(1)}, bf16[4,2,16,512]{3,2,1,0:T(8,128)(2,1)S(1)}, u32[]{:S(2)}, u32[]{:S(2)}) collective-permute-start(bf16[4,2,16,512]{3,2,1,0:T(8,128)(2,1)S(1)} %get-tuple-element.115), channel_id=1, source_target_pairs={{0,2},{1,3},{2,0},{3,1},{4,6},{5,7},{6,4},{7,5},{8,10},{9,11},{10,... | collective-permute-start | bytes 393224 | tf_op jit(solution)/shard_map/ppermute | solution.py:1072
  135.9 6.1 %collective-permute-start.27 = (bf16[4,2,16,512]{3,2,1,0:T(8,128)(2,1)S(1)}, bf16[4,2,16,512]{3,2,1,0:T(8,128)(2,1)S(1)}, u32[]{:S(2)}, u32[]{:S(2)}) collective-permute-start(bf16[4,2,16,512]{3,2,1,0:T(8,128)(2,1)S(1)} %get-tuple-element.116), channel_id=1, source_target_pairs={{0,3},{1,0},{2,1},{3,2},{4,7},{5,4},{6,5},{7,6},{8,11},{9,8},{10,9... | collective-permute-start | bytes 393224 | tf_op jit(solution)/shard_map/ppermute | solution.py:1072
  144.0 8.4 %collective-permute-start.28 = (bf16[80,640]{1,0:T(8,128)(2,1)S(1)}, bf16[80,640]{1,0:T(8,128)(2,1)S(1)}, u32[]{:S(2)}, u32[]{:S(2)}) collective-permute-start(bf16[80,640]{1,0:T(8,128)(2,1)S(1)} %get-tuple-element.119), channel_id=1, source_target_pairs={{0,1},{1,2},{2,3},{3,0},{4,5},{5,6},{6,7},{7,4},{8,9},{9,10},{10,1... | collective-permute-start | bytes 307208 | tf_op jit(solution)/shard_map/ppermute | solution.py:1076
  146.6 8.0 %collective-permute-start.29 = (bf16[80,640]{1,0:T(8,128)(2,1)S(1)}, bf16[80,640]{1,0:T(8,128)(2,1)S(1)}, u32[]{:S(2)}, u32[]{:S(2)}) collective-permute-start(bf16[80,640]{1,0:T(8,128)(2,1)S(1)} %get-tuple-element.120), channel_id=1, source_target_pairs={{0,2},{1,3},{2,0},{3,1},{4,6},{5,7},{6,4},{7,5},{8,10},{9,11},{10,... | collective-permute-start | bytes 307208 | tf_op jit(solution)/shard_map/ppermute | solution.py:1076
  148.2 6.5 %collective-permute-start.30 = (bf16[80,640]{1,0:T(8,128)(2,1)S(1)}, bf16[80,640]{1,0:T(8,128)(2,1)S(1)}, u32[]{:S(2)}, u32[]{:S(2)}) collective-permute-start(bf16[80,640]{1,0:T(8,128)(2,1)S(1)} %get-tuple-element.121), channel_id=1, source_target_pairs={{0,3},{1,0},{2,1},{3,2},{4,7},{5,4},{6,5},{7,6},{8,11},{9,8},{10,9... | collective-permute-start | bytes 307208 | tf_op jit(solution)/shard_map/ppermute | solution.py:1076

commit v9 on v8

--- a/solution.py
+++ b/solution.py
@@ -549,8 +549,9 @@
 
 
 def heads_kernel(total_ref, back_ref, residual_ref, rows_ref, cotangent_ref, sums_in, weight_ref, heads_ref,
-                 result_ref, branch, sums_ref, grad_ref, output_grad_ref):
+                 result_ref, branch, sums_ref, grad_ref, *refs):
     slots = heads_ref.shape[0]
+    outs, staged = refs[:-1], refs[-1]
     length, width = total_ref.shape
     gain, bias = rows_ref[2:3, :], rows_ref[4:5, :]
     gain_grad = jnp.zeros((1, width), F32)
@@ -573,13 +574,24 @@
     weight = weight_ref[...].reshape(slots * PAIR, width)
     grad = low(nt(branch[...], weight))
     heads = jnp.concatenate([heads_ref[a] for a in range(slots)], axis=1)
-    output_grad = low(tn(branch[...], heads))
+    staged[...] = low(tn(branch[...], heads))
     for a in range(slots):
         grad_ref[a] = grad[:, a * PAIR : (a + 1) * PAIR]
-        output_grad_ref[a] = output_grad[:, a * PAIR : (a + 1) * PAIR]
-
-
-def heads_back(total, back, residual, rows, cotangent, sums, weights, heads):
+    if len(outs) == 1:
+        outs[0][...] = staged[...]
+        return
+    seq, z = lax.axis_index("seq"), lax.axis_index("head")
+    chips = outs[0].shape[0]
+    for core, out in enumerate(outs):
+        for chip in range(chips):
+            start = pl.multiple_of((2 * chip + ((seq & 1) ^ core)) * 64, 64)
+            for there in range(slots):
+                slot = lax.rem(z + slots - there, slots)
+                block = staged[pl.ds(start, 64), pl.ds(pl.multiple_of(slot * PAIR, PAIR), PAIR)]
+                out[chip, there] = jnp.concatenate([block[16 * i : 16 * i + 16, :] for i in range(4)], axis=1)
+
+
+def heads_back(total, back, residual, rows, cotangent, sums, weights, heads, grad_shapes):
     slots, length, pair = heads.shape
     width = total.shape[1]
     shape = jax.ShapeDtypeStruct
@@ -589,8 +601,8 @@
         pltpu.HBM((length, width), BF16),
         pltpu.HBM(sums.shape, F32),
         pltpu.HBM((slots, length, pair), BF16),
-        pltpu.HBM((slots, width, pair), BF16),
     ]
+    outs += [shape(s, BF16) for s in grad_shapes]
     return pl.pallas_call(
         heads_kernel,
         grid=(1,),
@@ -598,6 +610,7 @@
         in_specs=[fixed(o.shape) for o in operands]
         + [pl.BlockSpec((slots, pair, width), lambda a: (0, width // pair, 0)), fixed(heads.shape)],
         out_specs=[fixed(o.shape) for o in outs],
+        scratch_shapes=[pltpu.VMEM((width, slots * pair), BF16)],
         compiler_params=params(28),
         cost_estimate=cost(4),
         name="heads_back",
@@ -626,7 +639,7 @@
 
 def back_kernel(waits, parts_out, slots, rows_ref, before_ref, normed_hbm, tokens_hbm, residual_grad_hbm, *refs):
     refs = refs[waits:]
-    weight, grad_ref, output_grad_ref, kept, refs = refs[0], refs[1], refs[2], refs[3:12], refs[12:]
+    weight, grad_ref, kept, refs = refs[0], refs[1], refs[2:11], refs[11:]
     input_grad_hbm, sums_ref, outs, mark = refs[0], refs[1], refs[2 : 2 + parts_out], refs[2 + parts_out]
     (backs, made, total, input_grad_ref, normed_ref, tokens, residual_grad, vector_blocks, sems, out_sems, tile_sems) = refs[3 + parts_out :]
     length, width = normed_ref.shape
@@ -660,8 +673,7 @@
     def _():
         fetch.wait()
 
-    made[parity, :, : 4 * PAIR] = low(tn(normed_ref[...], backs[...]))
-    made[parity, :, 4 * PAIR :] = output_grad_ref[...]
+    made[parity] = low(tn(normed_ref[...], backs[...]))
     for copy in leave_copies(step, made.at[parity], outs, out_sems.at[parity]):
         copy.start()
     total[...] += nt(backs[...], weight[:width, :])
@@ -730,13 +742,13 @@
         out_specs=[pl.BlockSpec(memory_space=pltpu.HBM), fixed(outs[1].shape)] + anywhere(grads) + [mark_spec()],
         scratch_shapes=[
             pltpu.VMEM((length, 4 * PAIR), BF16),
-            pltpu.VMEM((2, width, 5 * PAIR), BF16),
+            pltpu.VMEM((2, width, 4 * PAIR), BF16),
             pltpu.VMEM((length, width), F32),
             pltpu.VMEM((length, width), BF16),
         ]
         + [pltpu.VMEM((length, width), m.dtype) for m in large]
         + [
-            pltpu.VMEM((8, 16, 5 * PAIR), BF16),
+            pltpu.VMEM((8, 16, 4 * PAIR), BF16),
             pltpu.SemaphoreType.DMA((10,)),
             pltpu.SemaphoreType.DMA((2, 8)),
             pltpu.SemaphoreType.DMA((length // 256 + 1,)),
@@ -798,25 +810,33 @@
 
 def vector_rows(values, width):
     high = low(values)
-    rest = jnp.zeros((values.shape[0], width - 512), BF16)
-    return jnp.concatenate([high, low(values - high.astype(F32)), rest], axis=1)
-
-
-def halve_kernel(keep_ref, other_ref, out_ref):
-    out_ref[...] = low(add(keep_ref[...], other_ref[...]))
-
-
-def halve(keep, other):
+    return jnp.concatenate([high, low(values - high.astype(F32))], axis=1)
+
+
+def halve_kernel(keep_ref, other_ref, keep_output_ref, other_output_ref, out_ref):
+    slots, width = keep_ref.shape[1], keep_ref.shape[-1]
+    for chip in range(keep_ref.shape[0]):
+        out_ref[chip, :, :8] = low(add(keep_ref[chip], other_ref[chip])).reshape(slots, 8, 16, width)
+        out_ref[chip, :, 8] = low(add(keep_output_ref[chip], other_output_ref[chip]))
+
+
+def halves(shape):
+    return pl.BlockSpec((shape[0] // 2,) + shape[1:], lambda a: (a,) + (0,) * (len(shape) - 1))
+
+
+def halve(keep, other, keep_output, other_output):
+    operands = [keep, other, keep_output, other_output]
+    out = pltpu.HBM(keep.shape[:2] + (9, 16, keep.shape[-1]), BF16)
     return pl.pallas_call(
         halve_kernel,
-        grid=(keep.shape[0],),
-        out_shape=pltpu.HBM(keep.shape, BF16),
-        in_specs=by_step([keep, other]),
-        out_specs=by_step([keep])[0],
+        grid=(2,),
+        out_shape=out,
+        in_specs=[halves(o.shape) for o in operands],
+        out_specs=halves(keep.shape[:2] + (9, 16, keep.shape[-1])),
         compiler_params=params(44),
         cost_estimate=cost(2),
         name="halve",
-    )(keep, other)
+    )(*operands)
 
 
 def join_kernel(chips, slots, ffn_ref, keep_hbm, *refs):
@@ -892,9 +912,12 @@
     )(*pairs, *waits)
 
 
-def settle_kernel(ffn, expand_ref, shrink_ref):
-    blocks, _, share, width = ffn[0].shape
+def settle_kernel(ffn, expand_ref, shrink_ref, output_ref):
+    blocks, (_, share, width) = 4, ffn[0].shape
     total = add(*[f[...] for f in ffn])
+    for i in range(width // PAIR):
+        output_ref[i * share : (i + 1) * share, :] = total[8, :, i * PAIR : (i + 1) * PAIR]
+    total = total[:8].reshape(blocks, 2, share, width)
     expand_ref[...] = total[:, 0].reshape(blocks * share, width).T
     for i in range(blocks):
         shrink_ref[:, i] = total[i, 1].T.reshape(width // share, share, share)
@@ -903,8 +926,9 @@
 def settle(ffn, wait):
     shape = jax.ShapeDtypeStruct
     slots = len(ffn)
-    blocks, _, share, width = ffn[0].shape
+    blocks, (_, share, width) = 4, ffn[0].shape
     outs = [shape((width, blocks * share), F32), shape((width // share, blocks, share, share), F32)]
+    outs += [shape((share * width // PAIR, PAIR), F32)]
 
     def kernel(*refs):
         settle_kernel(refs[:slots], *refs[slots + 1 :])
@@ -922,7 +946,7 @@
 
 
 def finish_kernel(share, hidden_share, mine_ref, sums_ref, *refs):
-    came, parts, vectors = refs[:3], refs[3:8], refs[8:]
+    came, parts, vectors = refs[:3], refs[3:7], refs[7:]
     rows = mine_ref.shape[0]
     total = add(mine_ref[...], *[c[:rows, :] for c in came])
     for i, part in enumerate(parts):
@@ -936,7 +960,7 @@
 def finish(mine, sums, came, share, hidden_share):
     shape = jax.ShapeDtypeStruct
     operands = [mine, sums, *came]
-    outs = [shape((mine.shape[0], PAIR), F32)] * 5 + [shape((share,), F32)] * 5 + [shape((hidden_share,), F32)]
+    outs = [shape((mine.shape[0], PAIR), F32)] * 4 + [shape((share,), F32)] * 5 + [shape((hidden_share,), F32)]
     made = pl.pallas_call(
         functools.partial(finish_kernel, share, hidden_share),
         grid=(1,),
@@ -947,7 +971,7 @@
         cost_estimate=cost(1),
         name="finish",
     )(*operands)
-    return made[:5], made[5:]
+    return made[:4], made[4:]
 
 
 def flip(count, bit):
@@ -1035,7 +1059,8 @@
         pieces, vectors = over_cores(over_chips(near, chips, seqs), seqs), []
         load = lax.all_to_all(loads, "head", 0, 0, tiled=True)
         held = over_chips(load, chips, seqs)
-        tall = (slots * width // seqs + 16, 5 * PAIR)
+        tall = (slots * width // seqs + 16, 4 * PAIR)
+        output_shapes = [(chips, slots, 16, width)] * 2
         pair_shapes = [(chips,) + tall] + [tall] * chips
         ffn_shapes = [(chips, slots, 4, 2, 16, width)] * 2
     else:
@@ -1045,7 +1070,8 @@
         vectors = [lax.all_gather(block, ("seq", "head"), axis=0, tiled=False)]
         both = lax.all_gather(load, ("seq", "head"), axis=2, tiled=True)
         ffn_pieces = [both.reshape(4, 2, width // 16, 16, width).transpose(0, 2, 1, 3, 4)]
-        pair_shapes = [(slots, width, 5 * PAIR)]
+        pair_shapes = [(slots, width, 4 * PAIR)]
+        output_shapes = [(width, slots * PAIR)]
         ffn_shapes = [ffn_pieces[0].shape]
 
     (normed, rows, residual, second, mark), (heads, weights, *members) = forward(
@@ -1054,13 +1080,13 @@
     if direct:
         ffn_pieces = over_cores(held[:-1] + [low(held[-1].astype(F32) * mark[0])], seqs)
     total, back, sums, *ffn_grads = feed_forward(second, rows, cotangent, ffn_pieces, ffn_shapes)
-    result, branch, sums, heads_grad, output_grad = heads_back(
-        total, back, residual, rows, cotangent, sums, weights, heads
-    )
-    members = [weights, heads_grad, output_grad, *members]
+    result, branch, sums, heads_grad, *output_grads = heads_back(
+        total, back, residual, rows, cotangent, sums, weights, heads, output_shapes
+    )
+    members = [weights, heads_grad, *members]
     waits = []
     if direct:
-        ffn_mine = halve(ffn_grads[0], to_mate(ffn_grads[1], seqs))
+        ffn_mine = halve(ffn_grads[0], to_mate(ffn_grads[1], seqs), output_grads[0], to_mate(output_grads[1], seqs))
         waits = [ffn_mine]
     input_grad, sums, *pair_grads, _ = backward(
         normed, rows, sums, inputs, branch, devices, waits, members, pair_shapes
@@ -1072,14 +1098,16 @@
         ffn = [ffn[0]] + [lax.ppermute(ffn[a], "head", turn(slots, a)) for a in range(1, slots)]
         pairs = [pairs[0]] + from_chips(pairs[1:], seqs)
         mine, sums, *sends, wait = sum_plane(pairs, slots, ffn[1:])
-        expand_grad, shrink_grad = settle(ffn, wait)
+        expand_grad, shrink_grad, output_part = settle(ffn, wait)
         came = [lax.ppermute(m, "head", turn(slots, slots - 1 - a)) for a, m in enumerate(sends)]
         parts, vector = finish(mine, sums, came[::-1], share, hidden_share)
+        parts = [*parts, output_part]
     else:
         ffn_sum = lax.psum_scatter(
             ffn_grads[0].astype(F32).transpose(0, 2, 1, 3, 4).reshape(4, 2, width, width), ("seq", "head"), scatter_dimension=2, tiled=True
         )
-        every = pair_grads[0].astype(F32)
+        outputs = output_grads[0].reshape(width, slots, PAIR).transpose(1, 0, 2)
+        every = jnp.concatenate([pair_grads[0], outputs], axis=2).astype(F32)
         every = jnp.stack([every[(z + slots - p) % slots] for p in range(slots)])
         pair_sum = lax.psum_scatter(every, "head", scatter_dimension=0, tiled=False)
         pair_sum = lax.psum_scatter(pair_sum, "seq", scatter_dimension=0, tiled=True)

time: 156 us -> 155 us (level)
    ppermute x3, waiting for transfers between devices: 9.14 us -> 6.26 us  [body(): lax.ppermute(ffn[a], 'head', turn(slots, a))]
    all_to_all x1, waiting for transfers between devices: 0.01 us -> 1.7 us  [to_chips(): lax.all_to_all(shares, 'seq', 0, 0, axis_index_groups=plane, tiled=True)]
    unnamed x14 -> x18, local copies, waits for them, and re-layouts: 2.74 us -> 3.41 us
    ppermute x13 -> x14, waiting for transfers between devices: 4.78 us -> 5.14 us  [to_mate(): return lax.ppermute(shares, 'seq', flip(seqs, 1))]
  transfers between devices with their start and end apart: 33 -> 34, of which waited for: 19 -> 18; matrix products, arithmetic and copies ran while one was open for 3% -> 3% of each run, Pallas kernels for 28% -> 29%
where the time goes in v9:
time: 155 us
  Pallas kernels  70.5 us (45%)
  starting transfers between devices  38.9 us (25%)
  waiting for transfers between devices  36.4 us (23%)
  local copies, waits for them, and re-layouts  5.53 us (4%)
  other arithmetic  2.85 us (2%)
    pallas_call x1, Pallas kernels, backward(): pl.pallas_call(functools.partial(back_kernel, len(waits), len(grad_shapes...  23.7 us
    pallas_call x1, Pallas kernels, feed_forward(): pl.pallas_call(functools.partial(ffn_kernel, len(pieces)), grid=(4,), out...  21.1 us
    ppermute x6, waiting for transfers between devices, over_chips(): lax.ppermute(shares, 'seq', flip(seqs, 2 * r))  17.1 us
    pallas_call x1, Pallas kernels, forward(): pl.pallas_call(functools.partial(forward_kernel, len(pieces), slots), gri...  14.8 us
    ppermute x3, starting transfers between devices, body(): lax.ppermute(piece, 'head', turn(slots, a))  7.01 us
    ppermute x6, starting transfers between devices, over_chips(): lax.ppermute(shares, 'seq', flip(seqs, 2 * r))  6.98 us
    ppermute x3, waiting for transfers between devices, body(): lax.ppermute(ffn[a], 'head', turn(slots, a))  6.26 us
    ppermute x3, starting transfers between devices, body(): lax.ppermute(ffn[a], 'head', turn(slots, a))  5.63 us
  transfers between devices with their start and end apart: 34, of which 18 were waited for; matrix products, arithmetic and copies ran while one was open for 3% of the time, Pallas kernels for 29%

profile of v9, /device:TPU:0, one launch (start us, length us, event | category | flops | bytes accessed | tf_op | source)
XLA Modules:
  0.0 155.0 jit_solution(1994464249493166061)
XLA Ops:
  0.7 0.8 pad_add_fusion
  1.5 1.2 pad_maximum_fusion.own_ref
  2.8 3.1 %collective-permute-start.2 = (bf16[96,512]{1,0:T(8,128)(2,1)S(1)}, bf16[96,512]{1,0:T(8,128)(2,1)S(1)}, u32[]{:S(2)}, u32[]{:S(2)}) collective-permute-start(bf16[96,512]{1,0:T(8,128)(2,1)S(1)} %pad_maximum_fusion.2), channel_id=1, source_target_pairs={{0,1},{1,2},{2,3},{3,0},{4,5},{5,6},{6,7},{7,4},{8,9},{9,10},{10,1... | collective-permute-start | bytes 294920 | tf_op jit(solution)/shard_map/ppermute | solution.py:1057
  5.9 2.6 %collective-permute-start.1 = (bf16[96,512]{1,0:T(8,128)(2,1)S(1)}, bf16[96,512]{1,0:T(8,128)(2,1)S(1)}, u32[]{:S(2)}, u32[]{:S(2)}) collective-permute-start(bf16[96,512]{1,0:T(8,128)(2,1)S(1)} %pad_maximum_fusion.2), channel_id=1, source_target_pairs={{0,2},{1,3},{2,0},{3,1},{4,6},{5,7},{6,4},{7,5},{8,10},{9,11},{10,... | collective-permute-start | bytes 294920 | tf_op jit(solution)/shard_map/ppermute | solution.py:1057
  8.5 1.3 collective-permute-start
  9.8 1.2 reshape.39
  11.2 0.8 stack_reshape.7
  12.0 3.1 %collective-permute-done.1.refs_1_ = bf16[96,512]{1,0:T(8,128)(2,1)S(1)} collective-permute-done((bf16[96,512]{1,0:T(8,128)(2,1)S(1)}, bf16[96,512]{1,0:T(8,128)(2,1)S(1)}, u32[]{:S(2)}, u32[]{:S(2)}) %collective-permute-start.1) | collective-permute-done | bytes 98336 | tf_op jit(solution)/shard_map/ppermute | solution.py:1057
  15.1 0.8 join_near.1
  15.9 0.7 copy-done.2
  16.6 4.9 %all-to-all-start = ((bf16[4,8,16,512]{3,2,1,0:T(8,128)(2,1)}), bf16[4,8,16,512]{3,2,1,0:T(8,128)(2,1)S(1)}, u32[]{:S(2)}, u32[]{:S(2)}) async-start(bf16[4,8,16,512]{3,2,1,0:T(8,128)(2,1)} %get-tuple-element.80), calls=%async_computation | async-start | bytes 1048576 | tf_op jit(solution)/shard_map/all_to_all | solution.py:1060
  21.5 2.4 %collective-permute-start.8 = (bf16[256,512]{1,0:T(8,128)(2,1)}, bf16[256,512]{1,0:T(8,128)(2,1)}, u32[]{:S(2)}, u32[]{:S(2)}) collective-permute-start(bf16[256,512]{1,0:T(8,128)(2,1)} %copy-done.2), channel_id=1, source_target_pairs={{0,24},{4,28},{8,16},{12,20},{16,8},{20,12},{24,0},{28,4},{1,25},{... | collective-permute-start | bytes 786440 | tf_op jit(solution)/shard_map/ppermute | solution.py:994
  24.0 0.5 collective-permute-start.6
  24.5 0.5 collective-permute-start.4
  25.0 7.0 %collective-permute-done.8.refs_6_ = bf16[256,512]{1,0:T(8,128)(2,1)} collective-permute-done((bf16[256,512]{1,0:T(8,128)(2,1)}, bf16[256,512]{1,0:T(8,128)(2,1)}, u32[]{:S(2)}, u32[]{:S(2)}) %collective-permute-start.8) | collective-permute-done | bytes 262176 | tf_op jit(solution)/shard_map/ppermute | solution.py:994
  32.0 3.2 %collective-permute-done.6.refs_4_ = bf16[256,512]{1,0:T(8,128)(2,1)} collective-permute-done((bf16[256,512]{1,0:T(8,128)(2,1)}, bf16[256,512]{1,0:T(8,128)(2,1)}, u32[]{:S(2)}, u32[]{:S(2)}) %collective-permute-start.6) | collective-permute-done | bytes 262176 | tf_op jit(solution)/shard_map/ppermute | solution.py:994
  35.3 0.4 collective-permute-start.5
  35.8 1.8 %collective-permute-start.15 = (bf16[4,8,16,512]{3,2,1,0:T(8,128)(2,1)S(1)}, bf16[4,8,16,512]{3,2,1,0:T(8,128)(2,1)S(1)}, u32[]{:S(2)}, u32[]{:S(2)}) collective-permute-start(bf16[4,8,16,512]{3,2,1,0:T(8,128)(2,1)S(1)} %all-to-all-done.refs_0_), channel_id=1, source_target_pairs={{0,24},{4,28},{8,16},{12,20},{16,8},{20,12},{24,0},{28,4},{1,25},{... | collective-permute-start | bytes 1572872 | tf_op jit(solution)/shard_map/ppermute | solution.py:994
  37.6 1.1 collective-permute-start.13
  38.7 0.5 collective-permute-start.11
  39.3 0.9 copy-done.3
  40.2 14.8 %attend_forward.1 = (bf16[1024,512]{1,0:T(8,128)(2,1)S(1)}, f32[16,512]{1,0:T(8,128)S(1)}, f32[1024,512]{1,0:T(8,128)S(1)}, bf16[1024,512]{1,0:T(8,128)(2,1)S(1)...) custom-call(bf16[1024,512]{1,0:T(8,128)(2,1)S(1)} %copy-done.1, ...), custom_call_target="tpu_custom_call" | custom-call | flops 16999999488 | bytes 17000000 | tf_op jit(solution)/shard_map/attend_forward/pallas_call | solution.py:395
  55.1 6.7 %collective-permute-done.13.refs_4_ = bf16[4,8,16,512]{3,2,1,0:T(8,128)(2,1)S(1)} collective-permute-done((bf16[4,8,16,512]{3,2,1,0:T(8,128)(2,1)S(1)}, bf16[4,8,16,512]{3,2,1,0:T(8,128)(2,1)S(1)}, u32[]{:S(2)}, u32[]{:S(2)}) %collective-permute-start.13) | collective-permute-done | bytes 524320 | tf_op jit(solution)/shard_map/ppermute | solution.py:994
  61.9 0.4 collective-permute-start.12
  62.3 0.7 multiply_convert_fusion.refs_6_
  63.1 0.1 collective-permute-start.16
  63.2 0.5 collective-permute-done.14.refs_5_
  63.7 0.7 collective-permute-done.12.refs_3_
  64.5 0.7 collective-permute-done.16.refs_7_
  65.2 21.1 %feed_forward.1 = (f32[1024,512]{1,0:T(8,128)S(1)}, f32[1024,512]{1,0:T(8,128)S(1)}, f32[16,512]{1,0:T(8,128)S(1)}, bf16[4,4,4,2,16,512]{5,4,3,2,1,0:T(8,128)(2,1)S(1)}, bf16[4,4,4,2,16,512]{5,4,3,2,1,0:T(8,128)(2,1)S(1)}) custom-call(bf16[1024,512]{1,0:T(8,128)(2,1)S(1)} %get-tuple-element.78.second_ref, f32[16,512]{1,0:T(8,128)S(1)} %get-tuple-element.79.rows_ref, ...), custom_call_target="tpu_custom_call" | custom-call | flops 20999999488 | bytes 21000000 | tf_op jit(solution)/shard_map/feed_forward/pallas_call | solution.py:530
  86.4 0.2 collective-permute-start.17
  86.6 4.2 %heads_back.1 = (bf16[1024,512]{1,0:T(8,128)(2,1)}, bf16[1024,512]{1,0:T(8,128)(2,1)}, f32[16,512]{1,0:T(8,128)}, bf16[4,1024,128]{2,1,0:T(8,128)(2,1)}, bf16[4,...) custom-call(f32[1024,512]{1,0:T(8,128)S(1)} %get-tuple-element.82.total_ref, ...), custom_call_target="tpu_custom_call" | custom-call | flops 4000000000 | bytes 4000000 | tf_op jit(solution)/shard_map/heads_back/pallas_call | solution.py:606
  90.8 0.4 collective-permute-start.18
  91.1 1.2 collective-permute-done.18.other_output_ref
  92.3 1.7 %halve.1.refs_0_ = bf16[4,4,9,16,512]{4,3,2,1,0:T(8,128)(2,1)} custom-call(bf16[4,4,4,2,16,512]{5,4,3,2,1,0:T(8,128)(2,1)S(1)} %get-tuple-element.92.keep_ref, bf16[4,4,4,2,16,512]{5,4,3,2,1,0:T(8,128)(2,1)S(1)} %collective-permute-done.17.other_ref, bf16[4,4,16,512]{3,2,1,0:T(8,128)(2,1)S(1)} %get-tuple-element.94.keep_output_ref, ...), custom_call_target="tpu_custom_call" | custom-call | flops 2000000000 | bytes 2000000 | tf_op jit(solution)/shard_map/halve/pallas_call | solution.py:830
  94.0 3.6 %all-to-all-start.1 = ((bf16[4,4,9,16,512]{4,3,2,1,0:T(8,128)(2,1)}), bf16[4,4,9,16,512]{4,3,2,1,0:T(8,128)(2,1)S(1)}, u32[]{:S(2)}, u32[]{:S(2)}) async-start(bf16[4,4,9,16,512]{4,3,2,1,0:T(8,128)(2,1)} %halve.1.refs_0_), calls=%async_computation.1 | async-start | bytes 4718592 | tf_op jit(solution)/shard_map/all_to_all | solution.py:1003
  97.7 23.7 %attend_back.1 = (bf16[1024,512]{1,0:T(8,128)(2,1)}, f32[32,256]{1,0:T(8,128)}, bf16[4,272,512]{2,1,0:T(8,128)(2,1)}, bf16[272,512]{1,0:T(8,128)(2,1)}, bf16[272...) custom-call(f32[16,512]{1,0:T(8,128)} %copy-done.5, ...), custom_call_target="tpu_custom_call" | custom-call | flops 27000000512 | bytes 27000000 | tf_op jit(solution)/shard_map/attend_back/pallas_call | solution.py:737
  121.4 0.5 collective-permute-start.19
  121.9 0.1 collective-permute-start.20
  122.0 0.4 collective-permute-start.21
  122.4 0.1 collective-permute-start.22
  122.5 0.8 collective-permute-done.19.refs_0_
  123.3 0.4 collective-permute-done.20.refs_1_
  123.7 0.4 collective-permute-done.21.refs_2_
  124.1 0.4 collective-permute-done.22.refs_3_
  124.4 1.7 %all-to-all-done.1.ffn_ref = bf16[4,4,9,16,512]{4,3,2,1,0:T(8,128)(2,1)S(1)} async-done(((bf16[4,4,9,16,512]{4,3,2,1,0:T(8,128)(2,1)}), bf16[4,4,9,16,512]{4,3,2,1,0:T(8,128)(2,1)S(1)}, u32[]{:S(2)}, u32[]{:S(2)}) %all-to-all-start.1) | async-done | bytes 2359328 | tf_op jit(solution)/shard_map/all_to_all | solution.py:1003
  126.1 1.3 join.1
  127.5 2.6 %collective-permute-start.26 = (bf16[9,16,512]{2,1,0:T(8,128)(2,1)S(1)}, bf16[9,16,512]{2,1,0:T(8,128)(2,1)S(1)}, u32[]{:S(2)}, u32[]{:S(2)}) collective-permute-start(bf16[9,16,512]{2,1,0:T(8,128)(2,1)S(1)} %get-tuple-element.116), channel_id=1, source_target_pairs={{0,1},{1,2},{2,3},{3,0},{4,5},{5,6},{6,7},{7,4},{8,9},{9,10},{10,1... | collective-permute-start | bytes 442376 | tf_op jit(solution)/shard_map/ppermute | solution.py:1098
  130.1 1.4 collective-permute-start.23
  131.5 0.6 collective-permute-start.24
  132.1 1.5 collective-permute-start.25
  133.6 1.5 collective-permute-start.27
  135.1 1.5 collective-permute-start.28
  136.6 6.3 %collective-permute-done.27.refs_5_.refs_2_ = bf16[9,16,512]{2,1,0:T(8,128)(2,1)S(1)} collective-permute-done((bf16[9,16,512]{2,1,0:T(8,128)(2,1)S(1)}, bf16[9,16,512]{2,1,0:T(8,128)(2,1)S(1)}, u32[]{:S(2)}, u32[]{:S(2)}) %collective-permute-start.27) | collective-permute-done | bytes 147488 | tf_op jit(solution)/shard_map/ppermute | solution.py:1098
  142.8 2.2 %collective-permute-done.24.refs_2_ = bf16[272,512]{1,0:T(8,128)(2,1)S(1)} collective-permute-done((bf16[272,512]{1,0:T(8,128)(2,1)S(1)}, bf16[272,512]{1,0:T(8,128)(2,1)S(1)}, u32[]{:S(2)}, u32[]{:S(2)}) %collective-permute-start.24) | collective-permute-done | bytes 278560 | tf_op jit(solution)/shard_map/ppermute | solution.py:1007
  145.0 0.6 sum_plane.1
  145.6 0.7 collective-permute-start.29
  146.3 1.3 collective-permute-start.30
  147.6 2.6 %collective-permute-start.31 = (bf16[80,512]{1,0:T(8,128)(2,1)S(1)}, bf16[80,512]{1,0:T(8,128)(2,1)S(1)}, u32[]{:S(2)}, u32[]{:S(2)}) collective-permute-start(bf16[80,512]{1,0:T(8,128)(2,1)S(1)} %get-tuple-element.123), channel_id=1, source_target_pairs={{0,3},{1,0},{2,1},{3,2},{4,7},{5,4},{6,5},{7,6},{8,11},{9,8},{10,9... | collective-permute-start | bytes 245768 | tf_op jit(solution)/shard_map/ppermute | solution.py:1102
  150.1 1.6 %settle.1 = (f32[512,64]{1,0:T(8,128)S(1)}, f32[32,4,16,16]{3,2,1,0:T(8,128)S(1)}, f32[64,128]{1,0:T(8,128)}) custom-call(bf16[9,16,512]{2,1,0:T(8,128)(2,1)S(1)} %get-tuple-element.130.refs_0_, bf16[9,16,512]{2,1,0:T(8,128)(2,1)S(1)} %collective-permute-done.26.refs_4_.refs_1_, bf16[9,16,512]{2,1,0:T(8,128)(2,1)S(1)} %collective-permute-done.27.refs_5_.refs_2_, ...), custom_call_target="tpu_custom_call" | custom-call | flops 3000000000 | bytes 3000000 | tf_op jit(solution)/shard_map/settle/pallas_call | solution.py:936
  151.7 0.8 copy.36
  152.5 1.0 copy.37
  153.5 0.9 collective-permute-done.30.refs_1_
  154.3 0.7 finish.1
  (44 shorter events, 0.5 us)
Async XLA Ops:
  0.6 11.3 %copy-start.7 = (bf16[512,64]{0,1:T(8,128)(2,1)S(1)}, bf16[512,64]{0,1:T(8,128)(2,1)}, u32[]{:S(2)}) copy-start(bf16[512,64]{0,1:T(8,128)(2,1)} %param.25) | copy-start | bytes 196612
  2.8 9.2 %collective-permute-start.2 = (bf16[96,512]{1,0:T(8,128)(2,1)S(1)}, bf16[96,512]{1,0:T(8,128)(2,1)S(1)}, u32[]{:S(2)}, u32[]{:S(2)}) collective-permute-start(bf16[96,512]{1,0:T(8,128)(2,1)S(1)} %pad_maximum_fusion.2), channel_id=1, source_target_pairs={{0,1},{1,2},{2,3},{3,0},{4,5},{5,6},{6,7},{7,4},{8,9},{9,10},{10,1... | collective-permute-start | bytes 294920 | tf_op jit(solution)/shard_map/ppermute | solution.py:1057
  5.9 9.2 %collective-permute-start.1 = (bf16[96,512]{1,0:T(8,128)(2,1)S(1)}, bf16[96,512]{1,0:T(8,128)(2,1)S(1)}, u32[]{:S(2)}, u32[]{:S(2)}) collective-permute-start(bf16[96,512]{1,0:T(8,128)(2,1)S(1)} %pad_maximum_fusion.2), channel_id=1, source_target_pairs={{0,2},{1,3},{2,0},{3,1},{4,6},{5,7},{6,4},{7,5},{8,10},{9,11},{10,... | collective-permute-start | bytes 294920 | tf_op jit(solution)/shard_map/ppermute | solution.py:1057
  8.5 6.6 %collective-permute-start = (bf16[96,512]{1,0:T(8,128)(2,1)S(1)}, bf16[96,512]{1,0:T(8,128)(2,1)S(1)}, u32[]{:S(2)}, u32[]{:S(2)}) collective-permute-start(bf16[96,512]{1,0:T(8,128)(2,1)S(1)} %pad_maximum_fusion.2), channel_id=1, source_target_pairs={{0,3},{1,0},{2,1},{3,2},{4,7},{5,4},{6,5},{7,6},{8,11},{9,8},{10,9... | collective-permute-start | bytes 294920 | tf_op jit(solution)/shard_map/ppermute | solution.py:1057
  15.1 24.2 %copy-start.1 = (bf16[1024,512]{1,0:T(8,128)(2,1)S(1)}, bf16[1024,512]{1,0:T(8,128)(2,1)}, u32[]{:S(2)}) copy-start(bf16[1024,512]{1,0:T(8,128)(2,1)} %tokens_hbm.1) | copy-start | bytes 3145732
  15.9 0.7 copy-start.2
  16.6 19.1 %all-to-all-start = ((bf16[4,8,16,512]{3,2,1,0:T(8,128)(2,1)}), bf16[4,8,16,512]{3,2,1,0:T(8,128)(2,1)S(1)}, u32[]{:S(2)}, u32[]{:S(2)}) async-start(bf16[4,8,16,512]{3,2,1,0:T(8,128)(2,1)} %get-tuple-element.80), calls=%async_computation | async-start | bytes 1048576 | tf_op jit(solution)/shard_map/all_to_all | solution.py:1060
  21.5 43.7 %copy-start = (bf16[1024,512]{1,0:T(8,128)(2,1)S(1)}, bf16[1024,512]{1,0:T(8,128)(2,1)}, u32[]{:S(2)}) copy-start(bf16[1024,512]{1,0:T(8,128)(2,1)} %cotangent_ref.1) | copy-start | bytes 3145732
  21.5 10.5 %collective-permute-start.8 = (bf16[256,512]{1,0:T(8,128)(2,1)}, bf16[256,512]{1,0:T(8,128)(2,1)}, u32[]{:S(2)}, u32[]{:S(2)}) collective-permute-start(bf16[256,512]{1,0:T(8,128)(2,1)} %copy-done.2), channel_id=1, source_target_pairs={{0,24},{4,28},{8,16},{12,20},{16,8},{20,12},{24,0},{28,4},{1,25},{... | collective-permute-start | bytes 786440 | tf_op jit(solution)/shard_map/ppermute | solution.py:994
  24.0 11.3 %collective-permute-start.6 = (bf16[256,512]{1,0:T(8,128)(2,1)}, bf16[256,512]{1,0:T(8,128)(2,1)}, u32[]{:S(2)}, u32[]{:S(2)}) collective-permute-start(bf16[256,512]{1,0:T(8,128)(2,1)} %copy-done.2), channel_id=1, source_target_pairs={{0,16},{4,20},{8,24},{12,28},{16,0},{20,4},{24,8},{28,12},{1,17},{... | collective-permute-start | bytes 786440 | tf_op jit(solution)/shard_map/ppermute | solution.py:994
  24.5 10.9 %collective-permute-start.4 = (bf16[256,512]{1,0:T(8,128)(2,1)}, bf16[256,512]{1,0:T(8,128)(2,1)}, u32[]{:S(2)}, u32[]{:S(2)}) collective-permute-start(bf16[256,512]{1,0:T(8,128)(2,1)} %copy-done.2), channel_id=1, source_target_pairs={{0,8},{4,12},{8,0},{12,4},{16,24},{20,28},{24,16},{28,20},{1,9},{5... | collective-permute-start | bytes 786440 | tf_op jit(solution)/shard_map/ppermute | solution.py:994
  25.0 12.6 %collective-permute-start.3 = (bf16[256,512]{1,0:T(8,128)(2,1)}, bf16[256,512]{1,0:T(8,128)(2,1)}, u32[]{:S(2)}, u32[]{:S(2)}) collective-permute-start(bf16[256,512]{1,0:T(8,128)(2,1)} %copy-done.2), channel_id=1, source_target_pairs={{0,4},{4,0},{8,12},{12,8},{16,20},{20,16},{24,28},{28,24},{1,5},{5... | collective-permute-start | bytes 786440 | tf_op jit(solution)/shard_map/ppermute | solution.py:990
  32.0 6.7 %collective-permute-start.9 = (bf16[256,512]{1,0:T(8,128)(2,1)}, bf16[256,512]{1,0:T(8,128)(2,1)}, u32[]{:S(2)}, u32[]{:S(2)}) collective-permute-start(bf16[256,512]{1,0:T(8,128)(2,1)} %collective-permute-done.8.refs_6_), channel_id=1, source_target_pairs={{0,4},{4,0},{8,12},{12,8},{16,20},{20,16},{24,28},{28,24},{1,5},{5... | collective-permute-start | bytes 786440 | tf_op jit(solution)/shard_map/ppermute | solution.py:990
  35.2 4.0 %collective-permute-start.7 = (bf16[256,512]{1,0:T(8,128)(2,1)}, bf16[256,512]{1,0:T(8,128)(2,1)}, u32[]{:S(2)}, u32[]{:S(2)}) collective-permute-start(bf16[256,512]{1,0:T(8,128)(2,1)} %collective-permute-done.6.refs_4_), channel_id=1, source_target_pairs={{0,4},{4,0},{8,12},{12,8},{16,20},{20,16},{24,28},{28,24},{1,5},{5... | collective-permute-start | bytes 786440 | tf_op jit(solution)/shard_map/ppermute | solution.py:990
  35.3 3.9 %collective-permute-start.5 = (bf16[256,512]{1,0:T(8,128)(2,1)}, bf16[256,512]{1,0:T(8,128)(2,1)}, u32[]{:S(2)}, u32[]{:S(2)}) collective-permute-start(bf16[256,512]{1,0:T(8,128)(2,1)} %collective-permute-done.4.refs_2_), channel_id=1, source_target_pairs={{0,4},{4,0},{8,12},{12,8},{16,20},{20,16},{24,28},{28,24},{1,5},{5... | collective-permute-start | bytes 786440 | tf_op jit(solution)/shard_map/ppermute | solution.py:990
  35.8 26.6 %collective-permute-start.15 = (bf16[4,8,16,512]{3,2,1,0:T(8,128)(2,1)S(1)}, bf16[4,8,16,512]{3,2,1,0:T(8,128)(2,1)S(1)}, u32[]{:S(2)}, u32[]{:S(2)}) collective-permute-start(bf16[4,8,16,512]{3,2,1,0:T(8,128)(2,1)S(1)} %all-to-all-done.refs_0_), channel_id=1, source_target_pairs={{0,24},{4,28},{8,16},{12,20},{16,8},{20,12},{24,0},{28,4},{1,25},{... | collective-permute-start | bytes 1572872 | tf_op jit(solution)/shard_map/ppermute | solution.py:994
  37.6 24.2 %collective-permute-start.13 = (bf16[4,8,16,512]{3,2,1,0:T(8,128)(2,1)S(1)}, bf16[4,8,16,512]{3,2,1,0:T(8,128)(2,1)S(1)}, u32[]{:S(2)}, u32[]{:S(2)}) collective-permute-start(bf16[4,8,16,512]{3,2,1,0:T(8,128)(2,1)S(1)} %all-to-all-done.refs_0_), channel_id=1, source_target_pairs={{0,16},{4,20},{8,24},{12,28},{16,0},{20,4},{24,8},{28,12},{1,17},{... | collective-permute-start | bytes 1572872 | tf_op jit(solution)/shard_map/ppermute | solution.py:994
  38.7 23.2 %collective-permute-start.11 = (bf16[4,8,16,512]{3,2,1,0:T(8,128)(2,1)S(1)}, bf16[4,8,16,512]{3,2,1,0:T(8,128)(2,1)S(1)}, u32[]{:S(2)}, u32[]{:S(2)}) collective-permute-start(bf16[4,8,16,512]{3,2,1,0:T(8,128)(2,1)S(1)} %all-to-all-done.refs_0_), channel_id=1, source_target_pairs={{0,8},{4,12},{8,0},{12,4},{16,24},{20,28},{24,16},{28,20},{1,9},{5... | collective-permute-start | bytes 1572872 | tf_op jit(solution)/shard_map/ppermute | solution.py:994
  39.3 1.0 copy-start.3
  55.0 31.4 %copy-start.6 = (bf16[1024,512]{1,0:T(8,128)(2,1)}, bf16[1024,512]{1,0:T(8,128)(2,1)S(1)}, u32[]{:S(2)}) copy-start(bf16[1024,512]{1,0:T(8,128)(2,1)S(1)} %get-tuple-element.90.normed_hbm) | copy-start | bytes 3145732
  55.0 31.6 %copy-start.5 = (f32[16,512]{1,0:T(8,128)}, f32[16,512]{1,0:T(8,128)S(1)}, u32[]{:S(2)}) copy-start(f32[16,512]{1,0:T(8,128)S(1)} %get-tuple-element.79.rows_ref) | copy-start | bytes 98308
  55.0 8.2 %collective-permute-start.10 = (bf16[4,8,16,512]{3,2,1,0:T(8,128)(2,1)S(1)}, bf16[4,8,16,512]{3,2,1,0:T(8,128)(2,1)S(1)}, u32[]{:S(2)}, u32[]{:S(2)}) collective-permute-start(bf16[4,8,16,512]{3,2,1,0:T(8,128)(2,1)S(1)} %all-to-all-done.refs_0_), channel_id=1, source_target_pairs={{0,4},{4,0},{8,12},{12,8},{16,20},{20,16},{24,28},{28,24},{1,5},{5... | collective-permute-start | bytes 1572872 | tf_op jit(solution)/shard_map/ppermute | solution.py:990
  61.8 1.9 %collective-permute-start.14 = (bf16[4,8,16,512]{3,2,1,0:T(8,128)(2,1)S(1)}, bf16[4,8,16,512]{3,2,1,0:T(8,128)(2,1)S(1)}, u32[]{:S(2)}, u32[]{:S(2)}) collective-permute-start(bf16[4,8,16,512]{3,2,1,0:T(8,128)(2,1)S(1)} %collective-permute-done.13.refs_4_), channel_id=1, source_target_pairs={{0,4},{4,0},{8,12},{12,8},{16,20},{20,16},{24,28},{28,24},{1,5},{5... | collective-permute-start | bytes 1572872 | tf_op jit(solution)/shard_map/ppermute | solution.py:990
  61.9 2.6 %collective-permute-start.12 = (bf16[4,8,16,512]{3,2,1,0:T(8,128)(2,1)S(1)}, bf16[4,8,16,512]{3,2,1,0:T(8,128)(2,1)S(1)}, u32[]{:S(2)}, u32[]{:S(2)}) collective-permute-start(bf16[4,8,16,512]{3,2,1,0:T(8,128)(2,1)S(1)} %collective-permute-done.11.refs_2_), channel_id=1, source_target_pairs={{0,4},{4,0},{8,12},{12,8},{16,20},{20,16},{24,28},{28,24},{1,5},{5... | collective-permute-start | bytes 1572872 | tf_op jit(solution)/shard_map/ppermute | solution.py:990
  63.1 2.1 %collective-permute-start.16 = (bf16[4,8,16,512]{3,2,1,0:T(8,128)(2,1)S(1)}, bf16[4,8,16,512]{3,2,1,0:T(8,128)(2,1)S(1)}, u32[]{:S(2)}, u32[]{:S(2)}) collective-permute-start(bf16[4,8,16,512]{3,2,1,0:T(8,128)(2,1)S(1)} %multiply_convert_fusion.refs_6_), channel_id=1, source_target_pairs={{0,4},{4,0},{8,12},{12,8},{16,20},{20,16},{24,28},{28,24},{1,5},{5... | collective-permute-start | bytes 1572872 | tf_op jit(solution)/shard_map/ppermute | solution.py:990
  65.2 21.4 %copy-start.4 = (bf16[4,640,512]{2,1,0:T(8,128)(2,1)S(1)}, bf16[4,640,512]{2,1,0:T(8,128)(2,1)}, u32[]{:S(2)}) copy-start(bf16[4,640,512]{2,1,0:T(8,128)(2,1)} %get-tuple-element.86.weight_ref.refs_1_) | copy-start | bytes 7864324
  86.4 5.9 %collective-permute-start.17 = (bf16[4,4,4,2,16,512]{5,4,3,2,1,0:T(8,128)(2,1)S(1)}, bf16[4,4,4,2,16,512]{5,4,3,2,1,0:T(8,128)(2,1)S(1)}, u32[]{:S(2)}, u32[]{:S(2)}) collective-permute-start(bf16[4,4,4,2,16,512]{5,4,3,2,1,0:T(8,128)(2,1)S(1)} %get-tuple-element.93), channel_id=1, source_target_pairs={{0,4},{4,0},{8,12},{12,8},{16,20},{20,16},{24,28},{28,24},{1,5},{5... | collective-permute-start | bytes 6291464 | tf_op jit(solution)/shard_map/ppermute | solution.py:990
  90.8 1.5 collective-permute-start.18
  94.0 32.1 %all-to-all-start.1 = ((bf16[4,4,9,16,512]{4,3,2,1,0:T(8,128)(2,1)}), bf16[4,4,9,16,512]{4,3,2,1,0:T(8,128)(2,1)S(1)}, u32[]{:S(2)}, u32[]{:S(2)}) async-start(bf16[4,4,9,16,512]{4,3,2,1,0:T(8,128)(2,1)} %halve.1.refs_0_), calls=%async_computation.1 | async-start | bytes 4718592 | tf_op jit(solution)/shard_map/all_to_all | solution.py:1003
  121.4 1.9 %collective-permute-start.19 = (bf16[272,512]{1,0:T(8,128)(2,1)}, bf16[272,512]{1,0:T(8,128)(2,1)S(1)}, u32[]{:S(2)}, u32[]{:S(2)}) collective-permute-start(bf16[272,512]{1,0:T(8,128)(2,1)} %get-tuple-element.108), channel_id=1, source_target_pairs={{0,4},{4,0},{8,12},{12,8},{16,20},{20,16},{24,28},{28,24},{1,5},{5... | collective-permute-start | bytes 835592 | tf_op jit(solution)/shard_map/ppermute | solution.py:990
  121.9 1.8 %collective-permute-start.20 = (bf16[272,512]{1,0:T(8,128)(2,1)}, bf16[272,512]{1,0:T(8,128)(2,1)S(1)}, u32[]{:S(2)}, u32[]{:S(2)}) collective-permute-start(bf16[272,512]{1,0:T(8,128)(2,1)} %get-tuple-element.109), channel_id=1, source_target_pairs={{0,4},{4,0},{8,12},{12,8},{16,20},{20,16},{24,28},{28,24},{1,5},{5... | collective-permute-start | bytes 835592 | tf_op jit(solution)/shard_map/ppermute | solution.py:990
  122.0 2.1 %collective-permute-start.21 = (bf16[272,512]{1,0:T(8,128)(2,1)}, bf16[272,512]{1,0:T(8,128)(2,1)S(1)}, u32[]{:S(2)}, u32[]{:S(2)}) collective-permute-start(bf16[272,512]{1,0:T(8,128)(2,1)} %get-tuple-element.110), channel_id=1, source_target_pairs={{0,4},{4,0},{8,12},{12,8},{16,20},{20,16},{24,28},{28,24},{1,5},{5... | collective-permute-start | bytes 835592 | tf_op jit(solution)/shard_map/ppermute | solution.py:990
  122.4 2.1 %collective-permute-start.22 = (bf16[272,512]{1,0:T(8,128)(2,1)}, bf16[272,512]{1,0:T(8,128)(2,1)S(1)}, u32[]{:S(2)}, u32[]{:S(2)}) collective-permute-start(bf16[272,512]{1,0:T(8,128)(2,1)} %get-tuple-element.111), channel_id=1, source_target_pairs={{0,4},{4,0},{8,12},{12,8},{16,20},{20,16},{24,28},{28,24},{1,5},{5... | collective-permute-start | bytes 835592 | tf_op jit(solution)/shard_map/ppermute | solution.py:990
  127.5 7.7 %collective-permute-start.26 = (bf16[9,16,512]{2,1,0:T(8,128)(2,1)S(1)}, bf16[9,16,512]{2,1,0:T(8,128)(2,1)S(1)}, u32[]{:S(2)}, u32[]{:S(2)}) collective-permute-start(bf16[9,16,512]{2,1,0:T(8,128)(2,1)S(1)} %get-tuple-element.116), channel_id=1, source_target_pairs={{0,1},{1,2},{2,3},{3,0},{4,5},{5,6},{6,7},{7,4},{8,9},{9,10},{10,1... | collective-permute-start | bytes 442376 | tf_op jit(solution)/shard_map/ppermute | solution.py:1098
  130.1 12.8 %collective-permute-start.23 = (bf16[272,512]{1,0:T(8,128)(2,1)S(1)}, bf16[272,512]{1,0:T(8,128)(2,1)S(1)}, u32[]{:S(2)}, u32[]{:S(2)}) collective-permute-start(bf16[272,512]{1,0:T(8,128)(2,1)S(1)} %get-tuple-element.113), channel_id=1, source_target_pairs={{0,8},{4,12},{8,0},{12,4},{16,24},{20,28},{24,16},{28,20},{1,9},{5... | collective-permute-start | bytes 835592 | tf_op jit(solution)/shard_map/ppermute | solution.py:1007
  131.5 13.5 %collective-permute-start.24 = (bf16[272,512]{1,0:T(8,128)(2,1)S(1)}, bf16[272,512]{1,0:T(8,128)(2,1)S(1)}, u32[]{:S(2)}, u32[]{:S(2)}) collective-permute-start(bf16[272,512]{1,0:T(8,128)(2,1)S(1)} %get-tuple-element.114), channel_id=1, source_target_pairs={{0,16},{4,20},{8,24},{12,28},{16,0},{20,4},{24,8},{28,12},{1,17},{... | collective-permute-start | bytes 835592 | tf_op jit(solution)/shard_map/ppermute | solution.py:1007
  132.1 13.0 %collective-permute-start.25 = (bf16[272,512]{1,0:T(8,128)(2,1)S(1)}, bf16[272,512]{1,0:T(8,128)(2,1)S(1)}, u32[]{:S(2)}, u32[]{:S(2)}) collective-permute-start(bf16[272,512]{1,0:T(8,128)(2,1)S(1)} %get-tuple-element.115), channel_id=1, source_target_pairs={{0,24},{4,28},{8,16},{12,20},{16,8},{20,12},{24,0},{28,4},{1,25},{... | collective-permute-start | bytes 835592 | tf_op jit(solution)/shard_map/ppermute | solution.py:1007
  133.6 9.3 %collective-permute-start.27 = (bf16[9,16,512]{2,1,0:T(8,128)(2,1)S(1)}, bf16[9,16,512]{2,1,0:T(8,128)(2,1)S(1)}, u32[]{:S(2)}, u32[]{:S(2)}) collective-permute-start(bf16[9,16,512]{2,1,0:T(8,128)(2,1)S(1)} %get-tuple-element.117), channel_id=1, source_target_pairs={{0,2},{1,3},{2,0},{3,1},{4,6},{5,7},{6,4},{7,5},{8,10},{9,11},{10,... | collective-permute-start | bytes 442376 | tf_op jit(solution)/shard_map/ppermute | solution.py:1098
  135.1 7.7 %collective-permute-start.28 = (bf16[9,16,512]{2,1,0:T(8,128)(2,1)S(1)}, bf16[9,16,512]{2,1,0:T(8,128)(2,1)S(1)}, u32[]{:S(2)}, u32[]{:S(2)}) collective-permute-start(bf16[9,16,512]{2,1,0:T(8,128)(2,1)S(1)} %get-tuple-element.118), channel_id=1, source_target_pairs={{0,3},{1,0},{2,1},{3,2},{4,7},{5,4},{6,5},{7,6},{8,11},{9,8},{10,9... | collective-permute-start | bytes 442376 | tf_op jit(solution)/shard_map/ppermute | solution.py:1098
  145.6 7.9 %collective-permute-start.29 = (bf16[80,512]{1,0:T(8,128)(2,1)S(1)}, bf16[80,512]{1,0:T(8,128)(2,1)S(1)}, u32[]{:S(2)}, u32[]{:S(2)}) collective-permute-start(bf16[80,512]{1,0:T(8,128)(2,1)S(1)} %get-tuple-element.121), channel_id=1, source_target_pairs={{0,1},{1,2},{2,3},{3,0},{4,5},{5,6},{6,7},{7,4},{8,9},{9,10},{10,1... | collective-permute-start | bytes 245768 | tf_op jit(solution)/shard_map/ppermute | solution.py:1102
  146.3 8.0 %collective-permute-start.30 = (bf16[80,512]{1,0:T(8,128)(2,1)S(1)}, bf16[80,512]{1,0:T(8,128)(2,1)S(1)}, u32[]{:S(2)}, u32[]{:S(2)}) collective-permute-start(bf16[80,512]{1,0:T(8,128)(2,1)S(1)} %get-tuple-element.122), channel_id=1, source_target_pairs={{0,2},{1,3},{2,0},{3,1},{4,6},{5,7},{6,4},{7,5},{8,10},{9,11},{10,... | collective-permute-start | bytes 245768 | tf_op jit(solution)/shard_map/ppermute | solution.py:1102
  147.6 6.8 %collective-permute-start.31 = (bf16[80,512]{1,0:T(8,128)(2,1)S(1)}, bf16[80,512]{1,0:T(8,128)(2,1)S(1)}, u32[]{:S(2)}, u32[]{:S(2)}) collective-permute-start(bf16[80,512]{1,0:T(8,128)(2,1)S(1)} %get-tuple-element.123), channel_id=1, source_target_pairs={{0,3},{1,0},{2,1},{3,2},{4,7},{5,4},{6,5},{7,6},{8,11},{9,8},{10,9... | collective-permute-start | bytes 245768 | tf_op jit(solution)/shard_map/ppermute | solution.py:1102
